TPU v7x, 128 devices: a whole 4x4x4 slice. The times are simulated.
128 devices in a mesh: dp: 32 (over y, x_lo, z), tensor: 4 (over x_hi, core).
Axes of the slice: x: 4 (x_hi: 2, x_lo: 2; x = x_hi * 2 + x_lo), y: 4, z: 4, core: 2. Of those that a mesh axis runs over, the one named last changes fastest.
Arguments:
- inputs: bfloat16 [16384, 2048], P(('dp', 'tensor')), may hold values from -6 to 6
- segments: int32 [16384], P('dp'), may hold values from 0 to 2, as said below
- att_routes: int32 [16384, 2], P('dp'), may hold values from 0 to 2, all different within a row; in each aligned block of 512 rows (0 to 511, 512 to 1023, ...) at most 384 rows name the same one
- mlp_routes: int32 [16384, 2], P('dp'), may hold values from 0 to 3, all different within a row; in each aligned block of 512 rows (0 to 511, 512 to 1023, ...) at most 320 rows name the same one
- key_value: bfloat16 [2048, 2, 2048], P('dp', None, 'tensor'), may hold values from -0.125 to 0.125
- query_proj: bfloat16 [3, 2048, 2048], P(None, 'dp', 'tensor'), may hold values from -0.125 to 0.125
- output_proj: bfloat16 [3, 2048, 2048], P(None, 'tensor', 'dp'), may hold values from -1 to 1
- router_att: bfloat16 [2048, 3], P('dp'), may hold values from -0.09375 to 0.09375
- gain_att: bfloat16 [2048], P('dp'), may hold values from 0.5 to 1.5
- gate_up: bfloat16 [4, 2048, 2, 5632], P(None, 'dp', None, 'tensor'), may hold values from -0.125 to 0.125
- down_proj: bfloat16 [4, 5632, 2048], P(None, 'tensor', 'dp'), may hold values from -0.15625 to 0.15625
- router_mlp: bfloat16 [2048, 4], P('dp'), may hold values from -0.09375 to 0.09375
- gain_mlp: bfloat16 [2048], P('dp'), may hold values from 0.5 to 1.5
- out_grad: bfloat16 [16384, 2048], P(('dp', 'tensor')), may hold values from -6 to 6
Outputs:
- output: bfloat16 [16384, 2048], P(('dp', 'tensor'))
- grad_inputs: float32 [16384, 2048], P(('dp', 'tensor'))
- grad_key_value: float32 [2048, 2, 2048], P('dp', None, 'tensor')
- grad_query_proj: float32 [3, 2048, 2048], P(None, 'dp', 'tensor')
- grad_output_proj: float32 [3, 2048, 2048], P(None, 'tensor', 'dp')
- grad_router_att: float32 [2048, 3], P('dp')
- grad_gain_att: float32 [2048], P('dp')
- grad_gate_up: float32 [4, 2048, 2, 5632], P(None, 'dp', None, 'tensor')
- grad_down_proj: float32 [4, 5632, 2048], P(None, 'tensor', 'dp')
- grad_router_mlp: float32 [2048, 4], P('dp')
- grad_gain_mlp: float32 [2048], P('dp')
Inputs may be any that keep to these rules, and one draw needn't show every extreme that they name: `segments`: in each group of 512 consecutive tokens the first 256 have segment 0 (the prompt), then come a run of 1 and a run of 2 (two continuations), together 2 * 128 tokens. `att_routes`: each token names two different experts; within each group of 512 consecutive tokens no expert is named by more than 384 tokens, and in some group one is named by exactly 384. `mlp_routes`: each token names two different experts; within each group of 512 consecutive tokens no expert is named by more than 320 tokens, and in some group one is named by exactly 320.
All inputs are finite; a program needn't handle non-finite values.
Results may differ from a plain program's by a relative error of at most 0.03.
Values may be sent and summed in bfloat16 or wider, within the bound.
A program may use at most 320 MiB of HBM per device.

v0:
```python
import math

import jax
import jax.numpy as jnp
from jax import lax
from jax.sharding import PartitionSpec as P

HD = 128
CAP = 320
ATT_CAP = 384


EPSILON = 1e-06
NEGATIVE = -1e30
ROPE_BASE = 10000.0


def rotate(vectors, places, direction):
    half_size = vectors.shape[-1] // 2
    rungs = jnp.arange(half_size, dtype=jnp.float32)
    frequency = ROPE_BASE ** (-2.0 * rungs / vectors.shape[-1])
    angles = places.astype(jnp.float32)[:, None] * frequency[None, :]
    cosine = jnp.cos(angles)[:, None, :]
    sine_part = direction * jnp.sin(angles)[:, None, :]
    lower_half = vectors[..., :half_size]
    upper_half = vectors[..., half_size:]
    return jnp.concatenate(
        [
            lower_half * cosine - upper_half * sine_part,
            upper_half * cosine + lower_half * sine_part,
        ],
        -1,
    )


def positions(segments):
    seq_index = jnp.arange(segments.shape[0], dtype=jnp.int32)
    before = jnp.sum((segments[None, :] < segments[:, None]).astype(jnp.int32), 1)
    prompt_len = jnp.sum((segments == 0).astype(jnp.int32))
    return jnp.where(segments == 0, seq_index, prompt_len + seq_index - before)


def visible(segments, picked_ids):
    seq_index = jnp.arange(segments.shape[0], dtype=jnp.int32)
    own_segment = segments[picked_ids]
    earlier = seq_index[None, :] <= picked_ids[:, None]
    shared = (segments[None, :] == 0) | (segments[None, :] == own_segment[:, None])
    return earlier & shared


def route_gates(logits, routes, expert_count):
    chosen = jnp.take_along_axis(logits, routes, 1)
    largest = jnp.max(chosen, -1, keepdims=True)
    expsum = jnp.exp(chosen - largest)
    weights = expsum / jnp.sum(expsum, -1, keepdims=True)
    onehot = (
        routes[:, :, None] == jnp.arange(expert_count, dtype=jnp.int32)[None, None, :]
    ).astype(jnp.float32)
    return (weights, onehot, jnp.sum(weights[:, :, None] * onehot, 1))


def router_back(dgate, weights, onehot):
    dchosen = jnp.sum(dgate[:, None, :] * onehot, -1)
    dselect = weights * (dchosen - jnp.sum(weights * dchosen, -1, keepdims=True))
    return jnp.sum(dselect[:, :, None] * onehot, 1).astype(jnp.bfloat16)


def slot_ids(routes, expert, capacity):
    matches = jnp.sum((routes == expert).astype(jnp.int32), 1)
    return jnp.argsort(1 - matches, stable=True)[:capacity]


def normalize(activations):
    inverse = lax.rsqrt(jnp.mean(activations * activations, -1, keepdims=True) + EPSILON)
    return (activations * inverse, inverse)


def norm_back(dunit, normed, inverse, gain):
    dscaled = dunit * gain
    return (
        inverse * (dscaled - normed * jnp.mean(dscaled * normed, -1, keepdims=True)),
        jnp.sum(dunit * normed, 0),
    )


def masked_scores(queries, key_rot, allowed):
    raw_scores = jnp.einsum("chd,khd->hck", queries, key_rot, preferred_element_type=jnp.float32)
    return jnp.where(allowed[None], raw_scores, NEGATIVE)


def swiglu_back(dhidden, gate_pre, linear):
    sigmoid_pre = jax.nn.sigmoid(gate_pre)
    dgate_pre = dhidden * linear * sigmoid_pre * (1.0 + gate_pre * (1.0 - sigmoid_pre))
    dlinear = dhidden * gate_pre * sigmoid_pre
    return jnp.concatenate([dgate_pre, dlinear], 1).astype(jnp.bfloat16)


def on_device(
    inputs,
    segments,
    att_routes,
    mlp_routes,
    key_value,
    query_proj,
    output_proj,
    router_att,
    gain_att,
    gate_up,
    down_proj,
    router_mlp,
    gain_mlp,
    out_grad,
):
    tok_count = inputs.shape[0]
    group = tok_count * lax.axis_size("tensor")
    my_start = lax.axis_index("tensor") * tok_count
    width = inputs.shape[1]
    inner_width = query_proj.shape[2]
    heads_local = inner_width // HD
    hidden_local = down_proj.shape[1]
    att_count = query_proj.shape[0]
    mlp_count = gate_up.shape[0]
    width_share = gate_up.shape[1]
    scale_q = 1.0 / math.sqrt(HD)
    kv_full, query_full, output_full, ratt_full, rmlp_full, gatt_full, gmlp_full = (
        lax.all_gather(key_value, "dp", axis=0, tiled=True),
        lax.all_gather(query_proj, "dp", axis=1, tiled=True),
        lax.all_gather(output_proj, "dp", axis=2, tiled=True),
        lax.all_gather(router_att, "dp", axis=0, tiled=True),
        lax.all_gather(router_mlp, "dp", axis=0, tiled=True),
        lax.all_gather(gain_att, "dp", axis=0, tiled=True),
        lax.all_gather(gain_mlp, "dp", axis=0, tiled=True),
    )
    gain_one = gatt_full.astype(jnp.float32)
    gain_two = gmlp_full.astype(jnp.float32)
    places = positions(segments)
    input_rows = inputs.astype(jnp.float32)
    normed_one, inverse_one = normalize(input_rows)
    own_one = (normed_one * gain_one).astype(jnp.bfloat16)
    unit_one = lax.all_gather(own_one, "tensor", axis=0, tiled=True)
    kv_matrix = kv_full.reshape(width, 2 * inner_width)
    kv_raw = jnp.dot(unit_one, kv_matrix, preferred_element_type=jnp.float32)
    key_rot = rotate(kv_raw[:, :inner_width].reshape(group, heads_local, HD), places, 1.0).astype(
        jnp.bfloat16
    )
    val_rows = kv_raw[:, inner_width:].reshape(group, heads_local, HD).astype(jnp.bfloat16)
    logit_att = jnp.dot(unit_one, ratt_full, preferred_element_type=jnp.float32)
    weights_att, onehot_att, gate_att = route_gates(logit_att, att_routes, att_count)
    attention = jnp.zeros((group, width), jnp.float32)
    kept_att = []
    for expert in range(att_count):
        picked_ids = slot_ids(att_routes, expert, ATT_CAP)
        picked = unit_one[picked_ids]
        query_raw = jnp.dot(picked, query_full[expert], preferred_element_type=jnp.float32)
        queries = (
            rotate(query_raw.reshape(ATT_CAP, heads_local, HD), places[picked_ids], 1.0) * scale_q
        ).astype(jnp.bfloat16)
        allowed = visible(segments, picked_ids)
        masked = masked_scores(queries, key_rot, allowed)
        largest = jnp.max(masked, -1, keepdims=True)
        expsum = jnp.exp(masked - largest)
        totals = jnp.sum(expsum, -1, keepdims=True)
        attn_prob = expsum / totals
        log_total = largest + jnp.log(totals)
        mixed_out = jnp.einsum(
            "hck,khd->chd",
            attn_prob.astype(jnp.bfloat16),
            val_rows,
            preferred_element_type=jnp.float32,
        )
        mixed_out = mixed_out.reshape(ATT_CAP, inner_width).astype(jnp.bfloat16)
        branch = jnp.dot(mixed_out, output_full[expert], preferred_element_type=jnp.float32)
        gate_rows = gate_att[picked_ids, expert]
        attention = attention.at[picked_ids].add(branch * gate_rows[:, None])
        kept_att.append(
            (picked_ids, picked, queries, allowed, log_total, mixed_out, branch, gate_rows)
        )
    attn_rows = lax.psum_scatter(attention, "tensor", scatter_dimension=0, tiled=True)
    middle = input_rows + attn_rows
    normed_two, inverse_two = normalize(middle)
    own_two = (normed_two * gain_two).astype(jnp.bfloat16)
    unit_two, grad_all = (
        lax.all_gather(own_two, "tensor", axis=0, tiled=True),
        lax.all_gather(out_grad, "tensor", axis=0, tiled=True),
    )
    grad_rows = out_grad.astype(jnp.float32)
    logit_mlp = jnp.dot(unit_two, rmlp_full, preferred_element_type=jnp.float32)
    weights_mlp, onehot_mlp, gate_mlp = route_gates(logit_mlp, mlp_routes, mlp_count)
    feed = jnp.zeros((group, width), jnp.float32)
    dunit_two = jnp.zeros((group, width), jnp.float32)
    dgate_two = jnp.zeros((group, mlp_count), jnp.float32)
    dp_count = lax.axis_size("dp")
    replicas = dp_count // mlp_count
    slot_rows = CAP // replicas
    own_up = gate_up.reshape(mlp_count, width_share, 2 * hidden_local)
    own_down = jnp.swapaxes(down_proj, 1, 2)
    own_block = jnp.repeat(jnp.concatenate([own_up, own_down], 2), replicas, axis=0)
    owned = lax.all_to_all(own_block, "dp", split_axis=0, concat_axis=1, tiled=True)[0]
    up_whole = owned[:, : 2 * hidden_local]
    down_whole = owned[:, 2 * hidden_local :]
    ids_flat = jnp.concatenate([slot_ids(mlp_routes, expert, CAP) for expert in range(mlp_count)])
    expert_flat = jnp.repeat(jnp.arange(mlp_count, dtype=jnp.int32), CAP)
    gates_flat = gate_mlp[ids_flat, expert_flat]
    incoming = grad_all[ids_flat].astype(jnp.float32)
    dbranch_out = (incoming * gates_flat[:, None]).astype(jnp.bfloat16)
    rows_out = unit_two[ids_flat]
    rows_in, dbranch_in = (
        lax.all_to_all(
            rows_out.reshape(dp_count, slot_rows, width),
            "dp",
            split_axis=0,
            concat_axis=0,
            tiled=True,
        ),
        lax.all_to_all(
            dbranch_out.reshape(dp_count, slot_rows, width),
            "dp",
            split_axis=0,
            concat_axis=0,
            tiled=True,
        ),
    )
    rows_in = rows_in.reshape(dp_count * slot_rows, width)
    dbranch_in = dbranch_in.reshape(dp_count * slot_rows, width)
    joined = jnp.dot(rows_in, up_whole, preferred_element_type=jnp.float32)
    gate_pre = joined[:, :hidden_local]
    linear = joined[:, hidden_local:]
    hidden = (jax.nn.silu(gate_pre) * linear).astype(jnp.bfloat16)
    branch_part = lax.dot_general(
        hidden, down_whole, (((1,), (1,)), ((), ())), preferred_element_type=jnp.float32
    )
    dhidden = jnp.dot(dbranch_in, down_whole, preferred_element_type=jnp.float32)
    djoined = swiglu_back(dhidden, gate_pre, linear)
    grad_up_whole = jnp.dot(rows_in.T, djoined, preferred_element_type=jnp.float32)
    grad_down_whole = jnp.dot(dbranch_in.T, hidden, preferred_element_type=jnp.float32)
    dunit_part = lax.dot_general(
        djoined, up_whole, (((1,), (1,)), ((), ())), preferred_element_type=jnp.float32
    )
    branch_back, dunit_back = (
        lax.all_to_all(
            branch_part.reshape(dp_count, slot_rows, width).astype(jnp.bfloat16),
            "dp",
            split_axis=0,
            concat_axis=0,
            tiled=True,
        ).astype(jnp.float32),
        lax.all_to_all(
            dunit_part.reshape(dp_count, slot_rows, width).astype(jnp.bfloat16),
            "dp",
            split_axis=0,
            concat_axis=0,
            tiled=True,
        ).astype(jnp.float32),
    )
    branch_back = branch_back.reshape(mlp_count * CAP, width)
    dunit_back = dunit_back.reshape(mlp_count * CAP, width)
    feed = feed.at[ids_flat].add(branch_back * gates_flat[:, None])
    dgate_two = dgate_two.at[ids_flat, expert_flat].add(jnp.sum(incoming * branch_back, -1))
    dunit_two = dunit_two.at[ids_flat].add(dunit_back)
    grad_pieces = lax.all_to_all(
        jnp.concatenate([grad_up_whole, grad_down_whole], 1).astype(jnp.bfloat16),
        "dp",
        split_axis=0,
        concat_axis=0,
        tiled=True,
    ).astype(jnp.float32)
    summed = jnp.sum(grad_pieces.reshape(mlp_count, replicas, width_share, 3 * hidden_local), 1)
    grads_up = summed[:, :, : 2 * hidden_local].reshape(mlp_count, width_share, 2, hidden_local)
    grads_down = jnp.swapaxes(summed[:, :, 2 * hidden_local :], 1, 2)
    feed_rows = lax.psum_scatter(
        feed.astype(jnp.bfloat16), "tensor", scatter_dimension=0, tiled=True
    ).astype(jnp.float32)
    output = (middle + feed_rows).astype(jnp.bfloat16)
    dunit_own, dgate_own = (
        lax.psum_scatter(dunit_two, "tensor", scatter_dimension=0, tiled=True),
        lax.psum_scatter(dgate_two, "tensor", scatter_dimension=0, tiled=True),
    )
    dlogit_mlp = router_back(
        dgate_own,
        lax.dynamic_slice_in_dim(weights_mlp, my_start, tok_count, 0),
        lax.dynamic_slice_in_dim(onehot_mlp, my_start, tok_count, 0),
    )
    grad_rmlp = jnp.dot(own_two.T, dlogit_mlp, preferred_element_type=jnp.float32)
    dunit_own = dunit_own + jnp.dot(dlogit_mlp, rmlp_full.T, preferred_element_type=jnp.float32)
    dnorm_two, grad_gain_two = norm_back(dunit_own, normed_two, inverse_two, gain_two)
    dmiddle = grad_rows + dnorm_two
    dattention = lax.all_gather(dmiddle.astype(jnp.bfloat16), "tensor", axis=0, tiled=True)
    dunit_one = jnp.zeros((group, width), jnp.float32)
    dgate_one = jnp.zeros((group, att_count), jnp.float32)
    grad_keys = jnp.zeros((group, heads_local, HD), jnp.float32)
    grad_values = jnp.zeros((group, heads_local, HD), jnp.float32)
    grads_query = []
    grads_output = []
    for expert in range(att_count):
        picked_ids, picked, queries, allowed, log_total, mixed_out, branch, gate_rows = kept_att[
            expert
        ]
        incoming = dattention[picked_ids].astype(jnp.float32)
        dgate_one = dgate_one.at[picked_ids, expert].add(jnp.sum(incoming * branch, -1))
        dbranch = (incoming * gate_rows[:, None]).astype(jnp.bfloat16)
        grads_output.append(jnp.dot(mixed_out.T, dbranch, preferred_element_type=jnp.float32))
        dmixed = jnp.dot(dbranch, output_full[expert].T, preferred_element_type=jnp.float32)
        dmixed = dmixed.astype(jnp.bfloat16).reshape(ATT_CAP, heads_local, HD)
        attn_prob = jnp.exp(masked_scores(queries, key_rot, allowed) - log_total)
        grad_values = grad_values + jnp.einsum(
            "hck,chd->khd",
            attn_prob.astype(jnp.bfloat16),
            dmixed,
            preferred_element_type=jnp.float32,
        )
        dprob = jnp.einsum("chd,khd->hck", dmixed, val_rows, preferred_element_type=jnp.float32)
        dscores = (attn_prob * (dprob - jnp.sum(attn_prob * dprob, -1, keepdims=True))).astype(
            jnp.bfloat16
        )
        dqueries = jnp.einsum("hck,khd->chd", dscores, key_rot, preferred_element_type=jnp.float32)
        grad_keys = grad_keys + jnp.einsum(
            "hck,chd->khd", dscores, queries, preferred_element_type=jnp.float32
        )
        dquery_raw = (
            rotate(dqueries * scale_q, places[picked_ids], -1.0)
            .reshape(ATT_CAP, inner_width)
            .astype(jnp.bfloat16)
        )
        grads_query.append(jnp.dot(picked.T, dquery_raw, preferred_element_type=jnp.float32))
        dunit_one = dunit_one.at[picked_ids].add(
            jnp.dot(dquery_raw, query_full[expert].T, preferred_element_type=jnp.float32)
        )
    dkv_raw = jnp.concatenate(
        [
            rotate(grad_keys, places, -1.0).reshape(group, inner_width),
            grad_values.reshape(group, inner_width),
        ],
        1,
    ).astype(jnp.bfloat16)
    grad_kv = jnp.dot(unit_one.T, dkv_raw, preferred_element_type=jnp.float32).reshape(
        width, 2, inner_width
    )
    dunit_one = dunit_one + jnp.dot(dkv_raw, kv_matrix.T, preferred_element_type=jnp.float32)
    dunit_first, dgate_first = (
        lax.psum_scatter(
            dunit_one.astype(jnp.bfloat16), "tensor", scatter_dimension=0, tiled=True
        ).astype(jnp.float32),
        lax.psum_scatter(
            dgate_one.astype(jnp.bfloat16), "tensor", scatter_dimension=0, tiled=True
        ).astype(jnp.float32),
    )
    dlogit_att = router_back(
        dgate_first,
        lax.dynamic_slice_in_dim(weights_att, my_start, tok_count, 0),
        lax.dynamic_slice_in_dim(onehot_att, my_start, tok_count, 0),
    )
    grad_ratt = jnp.dot(own_one.T, dlogit_att, preferred_element_type=jnp.float32)
    dunit_first = dunit_first + jnp.dot(dlogit_att, ratt_full.T, preferred_element_type=jnp.float32)
    dnorm_one, grad_gain_one = norm_back(dunit_first, normed_one, inverse_one, gain_one)
    grad_input = dmiddle + dnorm_one
    small_ratt, small_rmlp, small_gone, small_gtwo = (
        lax.psum(grad_ratt.astype(jnp.bfloat16), "tensor").astype(jnp.float32),
        lax.psum(grad_rmlp.astype(jnp.bfloat16), "tensor").astype(jnp.float32),
        lax.psum(grad_gain_one.astype(jnp.bfloat16), "tensor").astype(jnp.float32),
        lax.psum(grad_gain_two.astype(jnp.bfloat16), "tensor").astype(jnp.float32),
    )
    shares = (
        lax.psum_scatter(
            grad_kv.astype(jnp.bfloat16), "dp", scatter_dimension=0, tiled=True
        ).astype(jnp.float32),
        lax.psum_scatter(
            jnp.stack(grads_query).astype(jnp.bfloat16), "dp", scatter_dimension=1, tiled=True
        ).astype(jnp.float32),
        lax.psum_scatter(
            jnp.stack(grads_output).astype(jnp.bfloat16), "dp", scatter_dimension=2, tiled=True
        ).astype(jnp.float32),
        lax.psum_scatter(
            small_ratt.astype(jnp.bfloat16), "dp", scatter_dimension=0, tiled=True
        ).astype(jnp.float32),
        lax.psum_scatter(
            small_rmlp.astype(jnp.bfloat16), "dp", scatter_dimension=0, tiled=True
        ).astype(jnp.float32),
        lax.psum_scatter(
            small_gone.astype(jnp.bfloat16), "dp", scatter_dimension=0, tiled=True
        ).astype(jnp.float32),
        lax.psum_scatter(
            small_gtwo.astype(jnp.bfloat16), "dp", scatter_dimension=0, tiled=True
        ).astype(jnp.float32),
    )
    return (
        output,
        grad_input,
        shares[0],
        shares[1],
        shares[2],
        shares[3],
        shares[5],
        grads_up,
        grads_down,
        shares[4],
        shares[6],
    )


def solution(mesh):
    placed = (
        P(("dp", "tensor"), None),
        P("dp"),
        P("dp", None),
        P("dp", None),
        P("dp", None, "tensor"),
        P(None, "dp", "tensor"),
        P(None, "tensor", "dp"),
        P("dp", None),
        P("dp"),
        P(None, "dp", None, "tensor"),
        P(None, "tensor", "dp"),
        P("dp", None),
        P("dp"),
        P(("dp", "tensor"), None),
    )
    return jax.shard_map(
        on_device,
        mesh=mesh,
        in_specs=placed,
        out_specs=(
            P(("dp", "tensor"), None),
            P(("dp", "tensor"), None),
            P("dp", None, "tensor"),
            P(None, "dp", "tensor"),
            P(None, "tensor", "dp"),
            P("dp", None),
            P("dp"),
            P(None, "dp", None, "tensor"),
            P(None, "tensor", "dp"),
            P("dp", None),
            P("dp"),
        ),
        check_vma=False,
    )
```

profile of v0, /device:TPU:1, one launch (start us, length us, event | category | flops | bytes accessed | tf_op | source)
XLA Modules:
  0.0 2714.1 jit_solution(16837101911662529758)
XLA Ops:
  12.3 72.5 %all-reduce.10 = (bf16[2048]{0:T(1024)(128)(2,1)S(1)}, bf16[2048]{0:T(1024)(128)(2,1)}) all-reduce(bf16[2048]{0:T(1024)(128)(2,1)S(1)} %dynamic-update-slice, bf16[2048]{0:T(1024)(128)(2,1)S(1)} %dynamic-update-slice.1), channel_id=1, replica_groups=mesh['dp'=32,'tensor'=4] {'dp'}, use_global_device_ids=true, to_apply=%add.3 | all-reduce | flops 4096 | bytes 16384
  133.2 260.8 %all-gather = bf16[32,64,3]{1,2,0:T(4,128)(2,1)S(1)} all-gather(bf16[1,64,3]{1,2,0:T(4,128)(2,1)S(1)} %bitcast.283), channel_id=1, replica_groups=mesh['dp'=32,'tensor'=4] {'dp'}, dimensions={0}, use_global_device_ids=true | all-gather | bytes 12672 | tf_op jit(solution)/shard_map/all_gather | solution.py:129
  403.2 9.1 gather_fusion.18
  436.8 10.8 all-gather.12.cloned.1.call-done
  457.5 147.5 %all-gather.14.cloned.1.call-done = bf16[3,2048,512]{2,1,0:T(8,128)(2,1)} async-done(((bf16[3,64,512]{2,1,0:T(8,128)(2,1)}), bf16[3,2048,512]{2,1,0:T(8,128)(2,1)}) %all-gather.14.cloned.1.call-update) | async-done | bytes 6291472 | tf_op jit(solution)/shard_map/all_gather | solution.py:127
  633.2 137.0 %all-gather.16.cloned.1.call-done = bf16[3,512,2048]{1,2,0:T(8,128)(2,1)} async-done(((bf16[3,512,64]{1,2,0:T(8,128)(2,1)}), bf16[3,512,2048]{1,2,0:T(8,128)(2,1)}) %all-gather.16.cloned.1.call-update) | async-done | bytes 6291472 | tf_op jit(solution)/shard_map/all_gather | solution.py:128
  774.7 9.2 scatter_custom_fusion
  789.7 11.3 scatter_custom_fusion.1
  811.9 10.9 scatter_custom_fusion.2
  823.5 70.5 %reduce-scatter.18.cloned.1.call-done = f32[128,2048]{1,0:T(8,128)} async-done(((f32[512,2048]{1,0:T(8,128)}), f32[128,2048]{1,0:T(8,128)}) %reduce-scatter.18.cloned.1.call-update) | async-done | bytes 1048592 | tf_op jit(solution)/shard_map/reduce_scatter | solution.py:178
  913.3 11.1 all-gather.18.cloned.1.call-done
  924.5 12.7 gather_fusion.12
  945.1 139.6 %all-gather.1 = bf16[32,64,4]{1,2,0:T(4,128)(2,1)S(1)} all-gather(bf16[1,64,4]{1,2,0:T(4,128)(2,1)S(1)} %bitcast.284), channel_id=1, replica_groups=mesh['dp'=32,'tensor'=4] {'dp'}, dimensions={0}, use_global_device_ids=true | all-gather | bytes 16896 | tf_op jit(solution)/shard_map/all_gather | solution.py:130
  1085.2 13.2 gather_fusion.14
  1099.1 9.1 gather_fusion.19
  1108.6 10.7 gather_fusion.13
  1130.0 22.2 fusion.6
  1152.2 38.6 %all-to-all-done.3 = bf16[32,40,2048]{2,1,0:T(8,128)(2,1)} async-done(((bf16[32,40,2048]{2,1,0:T(8,128)(2,1)}), bf16[32,40,2048]{2,1,0:T(8,128)(2,1)}, u32[]{:S(2)}, u32[]{:S(2)}) %all-to-all-start.3) | async-done | bytes 5242912 | tf_op jit(solution)/shard_map/all_to_all | solution.py:215
  1190.8 19.1 multiply_convert_fusion.1
  1209.9 14.0 convolution_convert_fusion.1
  1229.8 20.9 fusion.8
  1250.7 41.6 %all-to-all-done.2 = bf16[32,40,2048]{2,1,0:T(8,128)(2,1)} async-done(((bf16[32,40,2048]{2,1,0:T(8,128)(2,1)}), bf16[32,40,2048]{2,1,0:T(8,128)(2,1)}, u32[]{:S(2)}, u32[]{:S(2)}) %all-to-all-start.2) | async-done | bytes 5242912 | tf_op jit(solution)/shard_map/all_to_all | solution.py:240
  1304.7 9.4 scatter_custom_fusion.11
  1315.0 47.3 %all-to-all-done.4 = bf16[32,40,2048]{2,1,0:T(8,128)(2,1)} async-done(((bf16[32,40,2048]{2,1,0:T(8,128)(2,1)}), bf16[32,40,2048]{2,1,0:T(8,128)(2,1)}, u32[]{:S(2)}, u32[]{:S(2)}) %all-to-all-start.4) | async-done | bytes 5242912 | tf_op jit(solution)/shard_map/all_to_all | solution.py:247
  1362.3 23.3 scatter_custom_fusion.4
  1387.0 63.2 %reduce-scatter.22.cloned.1.call-done = f32[128,2048]{1,0:T(8,128)} async-done(((f32[512,2048]{1,0:T(8,128)}), f32[128,2048]{1,0:T(8,128)}) %reduce-scatter.22.cloned.1.call-update) | async-done | bytes 1048592 | tf_op jit(solution)/shard_map/reduce_scatter | solution.py:275
  1455.6 25.6 all-gather.22.cloned.1.call-done
  1503.0 19.8 scatter_fusion.3
  1522.8 19.8 scatter_fusion.4
  1542.7 19.8 scatter_fusion.5
  1634.5 10.9 scatter_fusion
  1645.4 9.4 scatter_fusion.1
  1654.8 11.0 scatter_fusion.2
  1677.0 23.7 scatter_custom_fusion.3
  1704.6 8.0 copy.255
  1712.6 7.9 copy.254
  1720.6 13.0 convolution_convert_fusion.2
  1737.9 11.3 copy.252
  1756.6 14.1 copy.253
  1770.8 21.9 convolution_convert_fusion
  1792.7 11.9 pad_maximum_fusion
  1822.5 227.0 %reduce-scatter.32.cloned.1.call-done = bf16[64,3]{1,0:T(8,128)(2,1)} async-done(((bf16[2048,3]{1,0:T(8,128)(2,1)}), bf16[64,3]{1,0:T(8,128)(2,1)}) %reduce-scatter.32.cloned.1.call-update) | async-done | bytes 400
  2050.3 77.6 %all-to-all-done.5 = bf16[32,64,4224]{2,1,0:T(8,128)(2,1)} async-done(((bf16[32,64,4224]{2,1,0:T(8,128)(2,1)}), bf16[32,64,4224]{2,1,0:T(8,128)(2,1)}, u32[]{:S(2)}, u32[]{:S(2)}) %all-to-all-start.5) | async-done | bytes 17301536 | tf_op jit(solution)/shard_map/all_to_all | solution.py:260
  2127.8 9.5 convert_reduce_fusion
  2149.5 70.8 %all-reduce.9 = (bf16[2048]{0:T(1024)(128)(2,1)S(1)}, bf16[2048]{0:T(1024)(128)(2,1)S(1)}) all-reduce(bf16[2048]{0:T(1024)(128)(2,1)S(1)} %get-tuple-element.82, bf16[2048]{0:T(1024)(128)(2,1)S(1)} %copy-done.161), channel_id=12, replica_groups=mesh['dp'=32,'tensor'=4] {'dp'}, use_global_device_ids=true, to_apply=%region_70.71.clone | all-reduce | flops 4096 | bytes 16384
  2220.4 20.1 all-reduce.12
  2245.7 290.0 %all-reduce.15.cloned.1.call-done = (bf16[2048,2,512]{2,1,0:T(2,128)(2,1)}, bf16[3,512,2048]{1,0,2:T(4,128)(2,1)}) async-done(((bf16[2048,2,512]{2,1,0:T(2,128)(2,1)}, bf16[3,512,2048]{1,0,2:T(4,128)(2,1)}), (bf16[2048,2,512]{2,1,0:T(2,128)(2,1)}, bf16[3,512,2048]{1,0,2:T(4,128)(2,1)})) %all-reduce.15.cloned.1.call-update) | async-done | bytes 10485776
  2539.3 166.3 %reduce-scatter.26.cloned.1.call-done = bf16[3,64,512]{2,1,0:T(8,128)(2,1)} async-done(((bf16[3,2048,512]{2,1,0:T(8,128)(2,1)}), bf16[3,64,512]{2,1,0:T(8,128)(2,1)}) %reduce-scatter.26.cloned.1.call-update) | async-done | bytes 196624 | tf_op jit(solution)/shard_map/reduce_scatter | solution.py:366
  (648 shorter events, 371.0 us)
Async XLA Ops:
  7.2 82.4 %copy-start.87 = (bf16[4,64,2,1408]{3,2,1,0:T(2,128)(2,1)S(1)}, bf16[4,64,2,1408]{3,2,1,0:T(2,128)(2,1)}, u32[]{:S(2)}) copy-start(bf16[4,64,2,1408]{3,2,1,0:T(2,128)(2,1)} %param.23) | copy-start | bytes 4325380
  7.2 393.7 %all-gather.10.cloned.1.call-start = ((), (), s32[]{:S(2)}) async-start(), calls=%async_computation.15 | async-start | bytes 2621440 | tf_op jit(solution)/shard_map/all_gather | solution.py:140
  8.6 80.4 %copy-start.169 = (f32[128]{0:T(128)}, f32[128]{0:T(128)S(1)}, u32[]{:S(2)}) copy-start(f32[128]{0:T(128)S(1)} %add_rsqrt_fusion.1) | copy-start | bytes 1540
  87.5 360.1 %all-gather.12.cloned.1.call-start = ((), (), s32[]{:S(2)}) async-start(), calls=%async_computation.16 | async-start | bytes 4325376 | tf_op jit(solution)/shard_map/all_gather | solution.py:126
  88.2 516.8 %all-gather.14.cloned.1.call-start = ((), (), s32[]{:S(2)}) async-start(), calls=%async_computation.17 | async-start | bytes 6488064 | tf_op jit(solution)/shard_map/all_gather | solution.py:127
  89.0 681.3 %all-gather.16.cloned.1.call-start = ((), (), s32[]{:S(2)}) async-start(), calls=%async_computation.18 | async-start | bytes 6488064 | tf_op jit(solution)/shard_map/all_gather | solution.py:128
  97.9 839.3 %all-to-all-start.1 = ((bf16[32,64,4224]{2,1,0:T(8,128)(2,1)}), bf16[32,64,4224]{2,1,0:T(8,128)(2,1)}, u32[]{:S(2)}, u32[]{:S(2)}) async-start(bf16[32,64,4224]{2,1,0:T(8,128)(2,1)} %bitcast.236), calls=%async_computation.2 | async-start | bytes 34603008 | tf_op jit(solution)/shard_map/all_to_all | solution.py:198
  103.2 790.7 %reduce-scatter.18.cloned.1.call-start = ((), (), s32[]{:S(2)}) async-start(), calls=%async_computation.19 | async-start | bytes 5242880 | tf_op jit(solution)/shard_map/reduce_scatter | solution.py:178
  110.9 283.6 %copy-start.137 = (s32[384]{0:T(512)}, s32[384]{0:T(512)S(1)}, u32[]{:S(2)}) copy-start(s32[384]{0:T(512)S(1)} %get-tuple-element.163) | copy-start | bytes 4612
  110.9 322.6 %copy-start.130 = (s32[1024]{0:T(1024)}, s32[1024]{0:T(1024)S(1)}, u32[]{:S(2)}) copy-start(s32[1024]{0:T(1024)S(1)} %pad_clamp_fusion.1) | copy-start | bytes 12292
  113.7 281.3 %copy-start.139 = (s32[384]{0:T(512)}, s32[384]{0:T(512)S(1)}, u32[]{:S(2)}) copy-start(s32[384]{0:T(512)S(1)} %get-tuple-element.165) | copy-start | bytes 4612
  113.7 316.6 %copy-start.132 = (s32[1024]{0:T(1024)}, s32[1024]{0:T(1024)S(1)}, u32[]{:S(2)}) copy-start(s32[1024]{0:T(1024)S(1)} %pad_clamp_fusion.2) | copy-start | bytes 12292
  127.5 271.9 %copy-start.141 = (s32[384]{0:T(512)}, s32[384]{0:T(512)S(1)}, u32[]{:S(2)}) copy-start(s32[384]{0:T(512)S(1)} %get-tuple-element.167) | copy-start | bytes 4612
  127.5 299.7 %copy-start.134 = (s32[1024]{0:T(1024)}, s32[1024]{0:T(1024)S(1)}, u32[]{:S(2)}) copy-start(s32[1024]{0:T(1024)S(1)} %pad_clamp_fusion.3) | copy-start | bytes 12292
  400.8 229.2 %copy-start.41 = (pred[384,512]{1,0:T(8,128)(4,1)}, pred[384,512]{1,0:T(8,128)(4,1)S(1)}, u32[]{:S(2)}) copy-start(pred[384,512]{1,0:T(8,128)(4,1)S(1)} %get-tuple-element.161) | copy-start | bytes 589828
  400.8 383.0 %copy-start.43 = (pred[384,512]{1,0:T(8,128)(4,1)}, pred[384,512]{1,0:T(8,128)(4,1)S(1)}, u32[]{:S(2)}) copy-start(pred[384,512]{1,0:T(8,128)(4,1)S(1)} %get-tuple-element.160) | copy-start | bytes 589828
  623.4 160.4 %copy-start.124 = (f32[4,384]{1,0:T(4,128)}, f32[4,384]{1,0:T(4,128)S(1)}, u32[]{:S(2)}) copy-start(f32[4,384]{1,0:T(4,128)S(1)} %get-tuple-element.178) | copy-start | bytes 18436
  822.8 71.2 %copy-start.39 = (bf16[128,2048]{1,0:T(8,128)(2,1)S(1)}, bf16[128,2048]{1,0:T(8,128)(2,1)}, u32[]{:S(2)}) copy-start(bf16[128,2048]{1,0:T(8,128)(2,1)} %param.14) | copy-start | bytes 1572868
  822.8 74.6 %copy-start.111 = (s32[512,2]{0,1:T(2,128)S(1)}, s32[512,2]{0,1:T(2,128)}, u32[]{:S(2)}) copy-start(s32[512,2]{0,1:T(2,128)} %param.17) | copy-start | bytes 12292
  822.8 101.7 %all-gather.18.cloned.1.call-start = ((), (), s32[]{:S(2)}) async-start(), calls=%async_computation.20 | async-start | bytes 2621440 | tf_op jit(solution)/shard_map/all_gather | solution.py:183
  823.4 113.7 %copy-start.106 = (f32[2048]{0:T(1024)}, f32[2048]{0:T(1024)S(1)}, u32[]{:S(2)}) copy-start(f32[2048]{0:T(1024)S(1)} %convert_element_type.372) | copy-start | bytes 24580
  937.2 187.9 %all-to-all-start = ((bf16[32,40,2048]{2,1,0:T(8,128)(2,1)}), bf16[32,40,2048]{2,1,0:T(8,128)(2,1)}, u32[]{:S(2)}, u32[]{:S(2)}) async-start(bf16[32,40,2048]{2,1,0:T(8,128)(2,1)} %bitcast.241), calls=%async_computation.1 | async-start | bytes 10485760 | tf_op jit(solution)/shard_map/all_to_all | solution.py:208
  944.4 140.9 %all-gather.20.cloned.1.call-start = ((), (), s32[]{:S(2)}) async-start(), calls=%async_computation.22 | async-start | bytes 2621440 | tf_op jit(solution)/shard_map/all_gather | solution.py:184
  1125.1 65.6 %all-to-all-start.3 = ((bf16[32,40,2048]{2,1,0:T(8,128)(2,1)}), bf16[32,40,2048]{2,1,0:T(8,128)(2,1)}, u32[]{:S(2)}, u32[]{:S(2)}) async-start(bf16[32,40,2048]{2,1,0:T(8,128)(2,1)} %fusion), calls=%async_computation.5 | async-start | bytes 10485760 | tf_op jit(solution)/shard_map/all_to_all | solution.py:215
  1223.9 68.3 %all-to-all-start.2 = ((bf16[32,40,2048]{2,1,0:T(8,128)(2,1)}), bf16[32,40,2048]{2,1,0:T(8,128)(2,1)}, u32[]{:S(2)}, u32[]{:S(2)}) async-start(bf16[32,40,2048]{2,1,0:T(8,128)(2,1)} %bitcast.246), calls=%async_computation.3 | async-start | bytes 10485760 | tf_op jit(solution)/shard_map/all_to_all | solution.py:240
  1292.3 70.0 %all-to-all-start.4 = ((bf16[32,40,2048]{2,1,0:T(8,128)(2,1)}), bf16[32,40,2048]{2,1,0:T(8,128)(2,1)}, u32[]{:S(2)}, u32[]{:S(2)}) async-start(bf16[32,40,2048]{2,1,0:T(8,128)(2,1)} %bitcast.244), calls=%async_computation.6 | async-start | bytes 10485760 | tf_op jit(solution)/shard_map/all_to_all | solution.py:247
  1298.8 87.0 %reduce-scatter.28.cloned.1.call-start = ((), (), s32[]{:S(2)}) async-start(), calls=%async_computation.27 | async-start | bytes 327680
  1315.0 135.2 %reduce-scatter.22.cloned.1.call-start = ((), (), s32[]{:S(2)}) async-start(), calls=%async_computation.23 | async-start | bytes 5242880 | tf_op jit(solution)/shard_map/reduce_scatter | solution.py:275
  1385.7 95.6 %all-gather.22.cloned.1.call-start = ((), (), s32[]{:S(2)}) async-start(), calls=%async_computation.24 | async-start | bytes 2621440 | tf_op jit(solution)/shard_map/all_gather | solution.py:287
  1386.9 68.6 %copy-start.127 = (f32[4,384]{1,0:T(4,128)S(1)}, f32[4,384]{1,0:T(4,128)}, u32[]{:S(2)}) copy-start(f32[4,384]{1,0:T(4,128)} %copy-done.126) | copy-start | bytes 18436
  1386.9 68.7 %copy-start.123 = (f32[4,384]{1,0:T(4,128)S(1)}, f32[4,384]{1,0:T(4,128)}, u32[]{:S(2)}) copy-start(f32[4,384]{1,0:T(4,128)} %copy-done.122) | copy-start | bytes 18436
  1387.0 68.7 %copy-start.147 = (f32[4,384]{1,0:T(4,128)S(1)}, f32[4,384]{1,0:T(4,128)}, u32[]{:S(2)}) copy-start(f32[4,384]{1,0:T(4,128)} %get-tuple-element.192) | copy-start | bytes 18436
  1387.0 94.3 %copy-start.135 = (s32[1024]{0:T(1024)S(1)}, s32[1024]{0:T(1024)}, u32[]{:S(2)}) copy-start(s32[1024]{0:T(1024)} %copy-done.134) | copy-start | bytes 12292
  1454.7 171.6 %reduce-scatter.30.cloned.1.call-start = ((), (), s32[]{:S(2)}) async-start(), calls=%async_computation.28 | async-start | bytes 163840
  1455.6 118.6 %copy-start.114 = (f32[4,384]{1,0:T(4,128)}, f32[4,384]{1,0:T(4,128)S(1)}, u32[]{:S(2)}) copy-start(f32[4,384]{1,0:T(4,128)S(1)} %log_add_fusion.1) | copy-start | bytes 18436
  1563.3 258.4 %reduce-scatter.34.cloned.1.call-start = ((), (), s32[]{:S(2)}) async-start(), calls=%async_computation.30 | async-start | bytes 540672
  1564.7 484.8 %reduce-scatter.32.cloned.1.call-start = ((), (), s32[]{:S(2)}) async-start(), calls=%async_computation.29 | async-start | bytes 540672
  1630.1 516.8 %reduce-scatter.24.cloned.1.call-start = ((), (), s32[]{:S(2)}) async-start(), calls=%async_computation.25 | async-start | bytes 2621440 | tf_op jit(solution)/shard_map/reduce_scatter | solution.py:340
  1669.7 573.0 %reduce-scatter.20.cloned.1.call-start = ((), (), s32[]{:S(2)}) async-start(), calls=%async_computation.21 | async-start | bytes 2621440 | tf_op jit(solution)/shard_map/reduce_scatter | solution.py:270
  1704.6 831.2 %all-reduce.15.cloned.1.call-start = ((), (), s32[]{:S(2)}) async-start(), calls=%async_computation.31 | async-start | bytes 25165824
  1804.6 323.3 %all-to-all-start.5 = ((bf16[32,64,4224]{2,1,0:T(8,128)(2,1)}), bf16[32,64,4224]{2,1,0:T(8,128)(2,1)}, u32[]{:S(2)}, u32[]{:S(2)}) async-start(bf16[32,64,4224]{2,1,0:T(8,128)(2,1)} %pad_maximum_fusion), calls=%async_computation.10 | async-start | bytes 34603008 | tf_op jit(solution)/shard_map/all_to_all | solution.py:260
  1811.9 893.7 %reduce-scatter.26.cloned.1.call-start = ((), (), s32[]{:S(2)}) async-start(), calls=%async_computation.26 | async-start | bytes 6488064 | tf_op jit(solution)/shard_map/reduce_scatter | solution.py:366
  2142.4 100.3 %copy-start.18 = (f32[128,2048]{1,0:T(8,128)S(1)}, f32[128,2048]{1,0:T(8,128)}, u32[]{:S(2)}) copy-start(f32[128,2048]{1,0:T(8,128)} %copy-done.16) | copy-start | bytes 3145732
  2142.4 100.3 %copy-start.34 = (f32[128,2048]{1,0:T(8,128)S(1)}, f32[128,2048]{1,0:T(8,128)}, u32[]{:S(2)}) copy-start(f32[128,2048]{1,0:T(8,128)} %copy-done.33) | copy-start | bytes 3145732
  2142.4 100.3 %copy-start.49 = (bf16[128,2048]{1,0:T(8,128)(2,1)S(1)}, bf16[128,2048]{1,0:T(8,128)(2,1)}, u32[]{:S(2)}) copy-start(bf16[128,2048]{1,0:T(8,128)(2,1)} %param.27) | copy-start | bytes 1572868
  2142.4 100.3 %copy-start.108 = (f32[2048]{0:T(1024)S(1)}, f32[2048]{0:T(1024)}, u32[]{:S(2)}) copy-start(f32[2048]{0:T(1024)} %copy-done.106) | copy-start | bytes 24580
  2142.4 100.3 %copy-start.165 = (f32[128]{0:T(128)S(1)}, f32[128]{0:T(128)}, u32[]{:S(2)}) copy-start(f32[128]{0:T(128)} %copy-done.163) | copy-start | bytes 1540
  2142.5 100.3 %copy-start.172 = (f32[128]{0:T(128)S(1)}, f32[128]{0:T(128)}, u32[]{:S(2)}) copy-start(f32[128]{0:T(128)} %copy-done.171) | copy-start | bytes 1540
  (157 other events, 1421.8 us)
Sparse Core Ops, SparseCore 0:
  87.6 45.7 all-gather.9
  135.0 312.5 all-gather.11
  449.2 155.7 all-gather.13
  606.5 163.6 all-gather.15
  822.9 70.9 reduce-scatter.17
  897.5 26.9 all-gather.17
  947.0 40.2 all-gather.19
  1315.1 49.1 reduce-scatter.27
  1385.8 64.2 reduce-scatter.21
  1454.8 26.4 all-gather.21
  1563.5 25.0 reduce-scatter.29
  1590.8 134.3 reduce-scatter.33
  1728.2 321.2 reduce-scatter.31
  2052.0 94.8 reduce-scatter.23
  2149.6 38.1 reduce-scatter.19
  2190.3 345.4 all-reduce.14
  2538.0 167.5 reduce-scatter.25
where the time goes:
time: 2740 us; the launch traced here: 2710 us
  waiting for transfers between devices  1360 us (50%)
  blocking collectives  564 us (21%)
  other arithmetic  305 us (11%)
  local copies, waits for them, and re-layouts  217 us (8%)
  matrix products  213 us (8%)
  starting transfers between devices  38.3 us (1%)
    unnamed x22, waiting for transfers between devices  520 us
    all_gather x1, blocking collectives, on_device(): lax.all_gather(router_att, 'dp', axis=0, tiled=True)  261 us
    reduce_scatter x1, waiting for transfers between devices, on_device(): lax.psum_scatter(jnp.stack(grads_query).astype(jnp.bfloat16), 'dp', scatt...  166 us
    all_gather x1, waiting for transfers between devices, on_device(): lax.all_gather(query_proj, 'dp', axis=1, tiled=True)  147 us
    unnamed x2, blocking collectives  143 us
    all_gather x1, blocking collectives, on_device(): lax.all_gather(router_mlp, 'dp', axis=0, tiled=True)  140 us
    all_gather x1, waiting for transfers between devices, on_device(): lax.all_gather(output_proj, 'dp', axis=2, tiled=True)  137 us
    all_to_all x1, waiting for transfers between devices, on_device(): lax.all_to_all(jnp.concatenate([grad_up_whole, grad_down_whole], 1).astyp...  77.6 us
  transfers between devices with their start and end apart: 23, of which 15 were waited for; matrix products, arithmetic and copies ran while one was open for 22% of the time, Pallas kernels for 0%

commit v1 on v0

v1 whole, which is shorter than its diff:
```python
import functools
import math

import jax
import jax.numpy as jnp
from jax import lax
from jax.experimental import pallas as pl
from jax.experimental.pallas import tpu as pltpu
from jax.sharding import Mesh, PartitionSpec as P

HD = 128
CAP = 320
EPSILON = 1e-06
NEGATIVE = -1e30
ROPE_BASE = 10000.0
MESH_ID = pl.DeviceIdType.MESH
DP = ("y", "xl", "z")
TP = ("xh", "core")
ALL = DP + TP
F32 = jnp.float32
BF16 = jnp.bfloat16


def mod4(place):
    return lax.rem(place + 4, 4)


def neighbour(axis, step):
    size = 2 if axis == "xl" else 4
    return {axis: lax.rem(lax.axis_index(axis) + step + size, size)}


def gather_body(x_ref, out_ref, loc, xs, xr, s1, r1m, r1p, f1s, f1r, s2, r2m, r2p, f2s, f2r):
    y, xl, z = lax.axis_index("y"), lax.axis_index("xl"), lax.axis_index("z")
    half = x_ref.shape[0] // 2
    quarter = half // 2
    barrier = pltpu.get_barrier_semaphore()
    for axis, step in (("xl", 1), ("y", 1), ("y", -1), ("z", 1), ("z", -1)):
        pl.semaphore_signal(
            barrier, inc=1, device_id=neighbour(axis, step), device_id_type=MESH_ID
        )
    pl.semaphore_wait(barrier, 5)
    rings = (("z", "y"), ("y", "z"))
    place = {"y": y, "z": z}
    other = 1 - xl
    both = pl.ds(0, 2)
    sends = []

    def slot(h, first, second, j, start, count):
        yy, zz = (second, first) if h == 0 else (first, second)
        return out_ref.at[yy, j, zz, pl.ds(start, count)]

    def send(src, dst, send_sem, recv_sem, device):
        copy = pltpu.make_async_remote_copy(
            src_ref=src,
            dst_ref=dst,
            send_sem=send_sem,
            recv_sem=recv_sem,
            device_id=device,
            device_id_type=MESH_ID,
        )
        copy.start()
        sends.append(copy)

    def arrived(ref, sem):
        pltpu.make_async_copy(ref, ref, sem).wait()

    own = pltpu.make_async_copy(x_ref, out_ref.at[y, xl, z], loc)
    own.start()
    for h in (0, 1):
        first, second = place[rings[h][0]], place[rings[h][1]]
        src = x_ref.at[pl.ds(h * half, half)]
        dst = slot(h, first, second, xl, h * half, half)
        send(src, dst, xs.at[h], xr.at[h], neighbour("xl", 1))
        send(src, dst, s1.at[h, 0, 0], r1m.at[h, 0], neighbour(rings[h][0], 1))
        send(src, dst, s1.at[h, 0, 1], r1p.at[h, 0], neighbour(rings[h][0], -1))
    own.wait()

    def send_second(h, k, first):
        block = slot(h, first, place[rings[h][1]], both, h * half, half)
        send(block, block, s2.at[h, k, 0], r2m.at[h, k], neighbour(rings[h][1], 1))
        send(block, block, s2.at[h, k, 1], r2p.at[h, k], neighbour(rings[h][1], -1))

    for h in (0, 1):
        first, second = place[rings[h][0]], place[rings[h][1]]
        block = slot(h, first, second, other, h * half, half)
        arrived(block, xr.at[h])
        send(block, block, s1.at[h, 1, 0], r1m.at[h, 1], neighbour(rings[h][0], 1))
        send(block, block, s1.at[h, 1, 1], r1p.at[h, 1], neighbour(rings[h][0], -1))
        send_second(h, 0, first)
    for j, jx in ((0, xl), (1, other)):
        for h in (0, 1):
            first, second = place[rings[h][0]], place[rings[h][1]]
            arrived(slot(h, mod4(first - 1), second, jx, h * half, half), r1m.at[h, j])
            block = slot(h, mod4(first - 1), second, jx, h * half, quarter)
            send(block, block, f1s.at[h, j, 0], f1r.at[h, j, 0], neighbour(rings[h][0], 1))
            arrived(slot(h, mod4(first + 1), second, jx, h * half, half), r1p.at[h, j])
            block = slot(h, mod4(first + 1), second, jx, h * half + quarter, quarter)
            send(block, block, f1s.at[h, j, 1], f1r.at[h, j, 1], neighbour(rings[h][0], -1))
    for k, step in ((1, -1), (2, 1)):
        for h in (0, 1):
            send_second(h, k, mod4(place[rings[h][0]] + step))
    for h in (0, 1):
        first, second = place[rings[h][0]], place[rings[h][1]]
        for j, jx in ((0, xl), (1, other)):
            for p in (0, 1):
                block = slot(h, mod4(first + 2), second, jx, h * half + p * quarter, quarter)
                arrived(block, f1r.at[h, j, p])
        send_second(h, 3, mod4(first + 2))
    steps = ((0, 0), (1, -1), (2, 1), (3, 2))
    for k, step in steps:
        for h in (0, 1):
            first, second = mod4(place[rings[h][0]] + step), place[rings[h][1]]
            arrived(slot(h, first, mod4(second - 1), both, h * half, half), r2m.at[h, k])
            block = slot(h, first, mod4(second - 1), both, h * half, quarter)
            send(block, block, f2s.at[h, k, 0], f2r.at[h, k, 0], neighbour(rings[h][1], 1))
            arrived(slot(h, first, mod4(second + 1), both, h * half, half), r2p.at[h, k])
            block = slot(h, first, mod4(second + 1), both, h * half + quarter, quarter)
            send(block, block, f2s.at[h, k, 1], f2r.at[h, k, 1], neighbour(rings[h][1], -1))
    for k, step in steps:
        for h in (0, 1):
            first, second = mod4(place[rings[h][0]] + step), place[rings[h][1]]
            for p in (0, 1):
                block = slot(h, first, mod4(second + 2), both, h * half + p * quarter, quarter)
                arrived(block, f2r.at[h, k, p])
    for copy in sends:
        copy.wait_send()


def gather_dp(shard, collective_id):
    rows, cols = shard.shape
    dma = pltpu.SemaphoreType.DMA
    whole = pl.pallas_call(
        gather_body,
        out_shape=jax.ShapeDtypeStruct((4, 2, 4, rows, cols), shard.dtype),
        in_specs=[pl.BlockSpec(memory_space=pl.ANY)],
        out_specs=pl.BlockSpec(memory_space=pl.ANY),
        scratch_shapes=[
            dma,
            dma((2,)),
            dma((2,)),
            dma((2, 2, 2)),
            dma((2, 2)),
            dma((2, 2)),
            dma((2, 2, 2)),
            dma((2, 2, 2)),
            dma((2, 4, 2)),
            dma((2, 4)),
            dma((2, 4)),
            dma((2, 4, 2)),
            dma((2, 4, 2)),
        ],
        compiler_params=pltpu.CompilerParams(collective_id=collective_id, has_side_effects=True),
        name="gather_weights",
    )(shard)
    return whole.reshape(32 * rows, cols)


def dot(a, b, dims):
    return lax.dot_general(a, b, (dims, ((), ())), preferred_element_type=F32)


def attention_body(
    k_ref, v_ref, q0, q1, q2, cos_ref, sin_ref, col_ref, row_ref, gate_ref,
    key_out, val_out, que_out, mix_out, gmix_out, prob_out,
):
    h = pl.program_id(0)
    cosine, sine = cos_ref[...], sin_ref[...]
    scale = 1.0 / math.sqrt(HD)

    def rotated(v):
        return v * cosine + pltpu.roll(v, HD // 2, 1) * sine

    key = rotated(k_ref[...]).astype(BF16)
    val = v_ref[...].astype(BF16)
    key_out[...] = key
    val_out[...] = val
    tokens = key.shape[0]
    seg_col, seg_row = col_ref[...], row_ref[...]
    at_row = lax.broadcasted_iota(jnp.int32, (tokens, tokens), 0)
    at_col = lax.broadcasted_iota(jnp.int32, (tokens, tokens), 1)
    allowed = (at_col <= at_row) & ((seg_row == 0) | (seg_row == seg_col))
    for e, q_ref in enumerate((q0, q1, q2)):
        query = (rotated(q_ref[...]) * scale).astype(BF16)
        scores = jnp.where(allowed, dot(query, key, ((1,), (1,))), NEGATIVE)
        largest = jnp.max(scores, 1, keepdims=True)
        expsum = jnp.exp(scores - largest)
        prob = (expsum * (1.0 / jnp.sum(expsum, 1, keepdims=True))).astype(BF16)
        prob_out[0, e] = prob
        mixed = dot(prob, val, ((1,), (0,))).astype(BF16)
        at = pl.ds(pl.multiple_of(e * 4 * HD + h * HD, HD), HD)
        que_out[:, at] = query
        mix_out[:, at] = mixed
        gmix_out[:, at] = (mixed.astype(F32) * gate_ref[:, e : e + 1]).astype(BF16)


def attention_forward(joined, cosine, sine, segments, gates):
    tokens = joined.shape[0]
    heads = 4

    def column(start):
        return pl.BlockSpec((tokens, HD), lambda h: (0, start // HD + h))

    def whole(shape):
        return pl.BlockSpec(shape, lambda h: (0,) * len(shape))

    wide = jax.ShapeDtypeStruct((tokens, 12 * HD), BF16)
    narrow = jax.ShapeDtypeStruct((tokens, 4 * HD), BF16)
    return pl.pallas_call(
        attention_body,
        grid=(heads,),
        in_specs=[column(s) for s in (0, 512, 1024, 1536, 2048)]
        + [whole((tokens, HD))] * 2
        + [whole((tokens, 1)), whole((1, tokens)), whole(gates.shape)],
        out_specs=[column(0), column(0)]
        + [whole(wide.shape)] * 3
        + [pl.BlockSpec((1, 3, tokens, tokens), lambda h: (h, 0, 0, 0))],
        out_shape=[narrow, narrow, wide, wide, wide]
        + [jax.ShapeDtypeStruct((heads, 3, tokens, tokens), BF16)],
        compiler_params=pltpu.CompilerParams(vmem_limit_bytes=48 * 1024 * 1024),
        name="attention_forward",
    )(joined, joined, joined, joined, joined, cosine, sine, segments[:, None], segments[None], gates)


def attention_back_body(
    key_ref, val_ref, q0, q1, q2, m0, m1, m2, h0, h1, h2, prob_ref, cos_ref, sin_ref, gate_ref,
    grad_out, dgate_out,
):
    h = pl.program_id(0)
    cosine, sine = cos_ref[...], sin_ref[...]
    scale = 1.0 / math.sqrt(HD)

    def rotated_back(v):
        return v * cosine - pltpu.roll(v, HD // 2, 1) * sine

    key, val = key_ref[...], val_ref[...]
    tokens = key.shape[0]
    dkey = jnp.zeros((tokens, HD), F32)
    dval = jnp.zeros((tokens, HD), F32)
    lane = lax.broadcasted_iota(jnp.int32, (tokens, HD), 1)
    dgates = jnp.zeros((tokens, HD), F32)
    for e, (q_ref, m_ref, h_ref) in enumerate(((q0, m0, h0), (q1, m1, h1), (q2, m2, h2))):
        query, mixed, raw = q_ref[...], m_ref[...].astype(F32), h_ref[...]
        inner = jnp.sum(mixed * raw, 1, keepdims=True)
        dgates = dgates + jnp.where(lane == e, inner, 0.0)
        gate = gate_ref[:, e : e + 1]
        dmixed = (raw * gate).astype(BF16)
        prob = prob_ref[0, e]
        dval = dval + dot(prob, dmixed, ((0,), (0,)))
        dprob = dot(dmixed, val, ((1,), (1,)))
        delta = jnp.sum(dmixed.astype(F32) * mixed, 1, keepdims=True)
        dscores = (prob.astype(F32) * (dprob - delta)).astype(BF16)
        dquery = dot(dscores, key, ((1,), (0,)))
        dkey = dkey + dot(dscores, query, ((0,), (0,)))
        at = pl.ds(pl.multiple_of(1024 + e * 4 * HD + h * HD, HD), HD)
        grad_out[:, at] = rotated_back(dquery * scale).astype(BF16)
    grad_out[:, pl.ds(pl.multiple_of(h * HD, HD), HD)] = rotated_back(dkey).astype(BF16)
    grad_out[:, pl.ds(pl.multiple_of(512 + h * HD, HD), HD)] = dval.astype(BF16)

    @pl.when(h == 0)
    def _():
        dgate_out[...] = dgates

    @pl.when(h > 0)
    def _():
        dgate_out[...] += dgates


def attention_back(key, val, que, mix, raw, prob, cosine, sine, gates):
    tokens = key.shape[0]
    heads = 4

    def column(start):
        return pl.BlockSpec((tokens, HD), lambda h: (0, start // HD + h))

    def whole(shape):
        return pl.BlockSpec(shape, lambda h: (0,) * len(shape))

    thirds = [column(s) for s in (0, 512, 1024)]
    return pl.pallas_call(
        attention_back_body,
        grid=(heads,),
        in_specs=[column(0), column(0)]
        + thirds * 3
        + [pl.BlockSpec((1, 3, tokens, tokens), lambda h: (h, 0, 0, 0))]
        + [whole((tokens, HD))] * 2
        + [whole(gates.shape)],
        out_specs=[whole((tokens, 2560)), whole((tokens, HD))],
        out_shape=[
            jax.ShapeDtypeStruct((tokens, 2560), BF16),
            jax.ShapeDtypeStruct((tokens, HD), F32),
        ],
        compiler_params=pltpu.CompilerParams(vmem_limit_bytes=48 * 1024 * 1024),
        name="attention_back",
    )(key, val, que, que, que, mix, mix, mix, raw, raw, raw, prob, cosine, sine, gates)


def positions(segments):
    index = jnp.arange(segments.shape[0], dtype=jnp.int32)
    prompt = jnp.sum((segments == 0).astype(jnp.int32))
    first = jnp.sum((segments == 1).astype(jnp.int32))
    before = jnp.where(segments == 0, 0, jnp.where(segments == 1, prompt, prompt + first))
    return jnp.where(segments == 0, index, prompt + index - before)


def route_gates(logits, routes, count):
    onehot = (routes[:, :, None] == jnp.arange(count, dtype=jnp.int32)).astype(F32)
    chosen = jnp.sum(onehot * logits[:, None, :], -1)
    expsum = jnp.exp(chosen - jnp.max(chosen, -1, keepdims=True))
    weights = expsum / jnp.sum(expsum, -1, keepdims=True)
    return weights, onehot, jnp.sum(weights[:, :, None] * onehot, 1)


def router_back(dgate, weights, onehot):
    dchosen = jnp.sum(dgate[:, None, :] * onehot, -1)
    dselect = weights * (dchosen - jnp.sum(weights * dchosen, -1, keepdims=True))
    return jnp.sum(dselect[:, :, None] * onehot, 1).astype(BF16)


def normalize(activations):
    inverse = lax.rsqrt(jnp.mean(activations * activations, -1, keepdims=True) + EPSILON)
    return activations * inverse, inverse


def norm_back(dunit, normed, inverse, gain):
    dscaled = dunit * gain
    return inverse * (dscaled - normed * jnp.mean(dscaled * normed, -1, keepdims=True))


def swiglu_back(dhidden, gate_pre, linear):
    sigmoid_pre = jax.nn.sigmoid(gate_pre)
    dgate_pre = dhidden * linear * sigmoid_pre * (1.0 + gate_pre * (1.0 - sigmoid_pre))
    dlinear = dhidden * gate_pre * sigmoid_pre
    return jnp.concatenate([dgate_pre, dlinear], 1).astype(BF16)


def sum_over_tensor(partial):
    rows, width = partial.shape
    pieces = lax.all_to_all(partial.reshape(4, rows // 4, width), TP, 0, 0, tiled=True)
    return jnp.sum(pieces.astype(F32), 0)


def pad_to(array, width):
    return jnp.pad(array, ((0, 0), (0, width - array.shape[1])))


def on_device(
    inputs,
    segments,
    att_routes,
    mlp_routes,
    key_value,
    query_proj,
    output_proj,
    router_att,
    gain_att,
    gate_up,
    down_proj,
    router_mlp,
    gain_mlp,
    out_grad,
):
    width = inputs.shape[1]
    inner = query_proj.shape[2]
    hidden_local = down_proj.shape[1]
    att_count = query_proj.shape[0]
    mlp_count = gate_up.shape[0]
    share = gate_up.shape[1]
    qkv_cols = (2 + att_count) * inner
    small_at = qkv_cols
    out_at = qkv_cols + 128
    small = jnp.concatenate([router_att, router_mlp, gain_att[:, None], gain_mlp[:, None]], 1)
    own_att = jnp.concatenate(
        [
            key_value.reshape(share, 2 * inner),
            jnp.swapaxes(query_proj, 0, 1).reshape(share, att_count * inner),
            pad_to(small, 128),
            jnp.transpose(output_proj, (2, 0, 1)).reshape(share, att_count * inner),
        ],
        1,
    )
    own_mlp = jnp.concatenate(
        [
            gate_up.reshape(mlp_count, share, 2 * hidden_local),
            jnp.swapaxes(down_proj, 1, 2),
        ],
        2,
    )
    x_all = lax.all_gather(inputs, TP, axis=0, tiled=True)
    grad_all = lax.all_gather(out_grad, TP, axis=0, tiled=True)
    weights = gather_dp(own_att, 0)
    owned = lax.all_to_all(jnp.repeat(own_mlp, 8, axis=0), DP, split_axis=0, concat_axis=1, tiled=True)[0]

    tokens = x_all.shape[0]
    match = jnp.sum((mlp_routes[:, :, None] == jnp.arange(mlp_count, dtype=jnp.int32)).astype(BF16), 1)
    index = jnp.arange(tokens, dtype=jnp.int32)
    lower = (index[None, :] < index[:, None]).astype(BF16)
    rank = dot(lower, match, ((1,), (0,)))
    slot = jnp.where(match > 0, rank.astype(jnp.int32), -1)
    pick = (slot.T[:, None, :] == jnp.arange(CAP, dtype=jnp.int32)[None, :, None]).astype(BF16)
    pick_rows = pick.reshape(mlp_count * CAP, tokens)
    grad_rows = dot(pick_rows, grad_all, ((1,), (0,))).astype(BF16)
    grad_in = lax.all_to_all(grad_rows.reshape(mlp_count, CAP, width), "y", 0, 0, tiled=True)
    grad_in = grad_in.reshape(mlp_count * CAP, width)

    small_all = weights[:, small_at : small_at + 128].astype(F32)
    gain_one, gain_two = small_all[:, 7], small_all[:, 8]
    places = positions(segments).astype(F32)
    frequency = ROPE_BASE ** (-2.0 * jnp.arange(HD // 2, dtype=F32) / HD)
    angles = places[:, None] * frequency[None, :]
    cosine = jnp.concatenate([jnp.cos(angles)] * 2, 1)
    sine = jnp.concatenate([-jnp.sin(angles), jnp.sin(angles)], 1)
    normed_one, inverse_one = normalize(x_all.astype(F32))
    unit_one = (normed_one * gain_one).astype(BF16)
    joined_att = dot(unit_one, weights[:, :out_at], ((1,), (0,)))
    weights_att, onehot_att, gate_att = route_gates(
        joined_att[:, small_at : small_at + att_count], att_routes, att_count
    )
    key_rot, val_rows, queries, mixed, gmixed, prob = attention_forward(
        joined_att, cosine, sine, segments, gate_att
    )
    out_weights = weights[:, out_at:]
    attention = dot(gmixed, out_weights, ((1,), (1,))).astype(BF16)
    middle = inputs.astype(F32) + sum_over_tensor(attention)
    normed_two, inverse_two = normalize(middle)
    own_two = (normed_two * gain_two).astype(BF16)
    unit_two = lax.all_gather(own_two, TP, axis=0, tiled=True)

    router_two = weights[:, small_at + att_count : small_at + att_count + mlp_count]
    logit_mlp = dot(unit_two, router_two, ((1,), (0,)))
    weights_mlp, onehot_mlp, gate_mlp = route_gates(logit_mlp, mlp_routes, mlp_count)
    gate_high = gate_mlp.astype(BF16)
    gate_low = (gate_mlp - gate_high.astype(F32)).astype(BF16)
    extended = jnp.concatenate([unit_two, pad_to(jnp.concatenate([gate_high, gate_low], 1), 128)], 1)
    rows_out = dot(pick_rows, extended, ((1,), (0,))).astype(BF16)
    rows_ext = lax.all_to_all(rows_out.reshape(mlp_count, CAP, width + 128), "y", 0, 0, tiled=True)
    rows_ext = rows_ext.reshape(mlp_count * CAP, width + 128)
    rows_in = rows_ext[:, :width]
    gates_ext = rows_ext[:, width : width + 2 * mlp_count].astype(F32)
    mine = (jnp.arange(2 * mlp_count) % mlp_count == lax.axis_index("y")).astype(F32)
    gates_in = jnp.sum(gates_ext * mine, 1, keepdims=True)
    dbranch_in = (grad_in.astype(F32) * gates_in).astype(BF16)
    up_whole = owned[:, : 2 * hidden_local]
    down_whole = owned[:, 2 * hidden_local :]
    joined = dot(rows_in, up_whole, ((1,), (0,)))
    gate_pre = joined[:, :hidden_local]
    linear = joined[:, hidden_local:]
    hidden = (jax.nn.silu(gate_pre) * linear).astype(BF16)
    branch_part = dot(hidden, down_whole, ((1,), (1,))).astype(BF16)
    dhidden = dot(dbranch_in, down_whole, ((1,), (0,)))
    djoined = swiglu_back(dhidden, gate_pre, linear)
    dunit_part = dot(djoined, up_whole, ((1,), (1,))).astype(BF16)
    branch_back = lax.all_to_all(
        branch_part.reshape(mlp_count, CAP, width), "y", 0, 0, tiled=True
    ).reshape(mlp_count * CAP, width)
    dunit_back = lax.all_to_all(
        dunit_part.reshape(mlp_count, CAP, width), "y", 0, 0, tiled=True
    ).reshape(mlp_count * CAP, width)
    grad_up_whole = dot(rows_in, djoined, ((0,), (0,))).astype(BF16)
    grad_down_whole = dot(dbranch_in, hidden, ((0,), (0,))).astype(BF16)
    grad_pieces = lax.all_to_all(
        jnp.concatenate([grad_up_whole, grad_down_whole], 1), DP, 0, 0, tiled=True
    )

    gate_slots = jnp.sum(pick.astype(F32) * gate_mlp.T[:, None, :], -1).reshape(mlp_count * CAP, 1)
    branch_f32 = branch_back.astype(F32)
    feed = dot(pick_rows, (branch_f32 * gate_slots).astype(BF16), ((0,), (0,))).astype(BF16)
    dgate_slots = jnp.sum(grad_rows.astype(F32) * branch_f32, -1).reshape(mlp_count, CAP, 1)
    dgate_two = jnp.sum(pick.astype(F32) * dgate_slots, 1).T
    dlogit_mlp = router_back(dgate_two, weights_mlp, onehot_mlp)
    dunit_two = dot(pick_rows, dunit_back, ((0,), (0,))) + dot(dlogit_mlp, router_two, ((1,), (1,)))
    dunit_own = sum_over_tensor(dunit_two.astype(BF16))
    grad_rmlp = dot(unit_two, dlogit_mlp, ((0,), (0,)))
    grad_gain_two = jnp.sum(dunit_own * normed_two, 0)
    dmiddle = out_grad.astype(F32) + norm_back(dunit_own, normed_two, inverse_two, gain_two)
    dattention = lax.all_gather(dmiddle.astype(BF16), TP, axis=0, tiled=True)

    raw = dot(dattention, out_weights, ((1,), (0,)))
    grad_qkv, dgate_one = attention_back(
        key_rot, val_rows, queries, mixed, raw, prob, cosine, sine, gate_att
    )
    dlogit_att = router_back(dgate_one[:, :att_count], weights_att, onehot_att)
    grad_joined = jnp.concatenate([grad_qkv, pad_to(dlogit_att, 128)], 1)
    dunit_one = dot(grad_joined, weights[:, :out_at], ((1,), (1,)))
    grad_gain_one = jnp.sum(dunit_one * normed_one, 0)
    grad_small = jnp.concatenate(
        [
            dot(unit_one, dlogit_att, ((0,), (0,))),
            grad_rmlp,
            grad_gain_one[:, None],
            grad_gain_two[:, None],
        ],
        1,
    )
    grad_att = jnp.concatenate(
        [
            dot(unit_one, grad_qkv, ((0,), (0,))).astype(BF16),
            pad_to(grad_small, 128).astype(BF16),
            dot(dattention, gmixed, ((0,), (0,))).astype(BF16),
        ],
        1,
    )
    att_pieces = lax.all_to_all(grad_att.reshape(32, share, grad_att.shape[1]), DP, 0, 0, tiled=True)
    dunit_first = sum_over_tensor(dunit_one.astype(BF16))
    my_start = (lax.axis_index("xh") * 2 + lax.axis_index("core")) * inputs.shape[0]
    own_rows = lambda array: lax.dynamic_slice_in_dim(array, my_start, inputs.shape[0], 0)
    grad_input = dmiddle + norm_back(
        dunit_first, own_rows(normed_one), own_rows(inverse_one), gain_one
    )

    summed_mlp = jnp.sum(grad_pieces.reshape(mlp_count, 8, share, 3 * hidden_local).astype(F32), 1)
    grads_up = summed_mlp[:, :, : 2 * hidden_local].reshape(mlp_count, share, 2, hidden_local)
    grads_down = jnp.swapaxes(summed_mlp[:, :, 2 * hidden_local :], 1, 2)
    summed_att = jnp.sum(att_pieces.astype(F32), 0)
    grad_kv = summed_att[:, : 2 * inner].reshape(share, 2, inner)
    grad_query = jnp.swapaxes(
        summed_att[:, 2 * inner : qkv_cols].reshape(share, att_count, inner), 0, 1
    )
    grad_output = jnp.transpose(
        summed_att[:, out_at:].reshape(share, att_count, inner), (1, 2, 0)
    )
    small_sum = lax.psum(summed_att[:, small_at:out_at], TP)

    feed_rows = sum_over_tensor(feed)
    output = (middle + feed_rows).astype(BF16)
    return (
        output,
        grad_input,
        grad_kv,
        grad_query,
        grad_output,
        small_sum[:, :3],
        small_sum[:, 7],
        grads_up,
        grads_down,
        small_sum[:, 3:7],
        small_sum[:, 8],
    )


def solution(mesh):
    fine = Mesh(mesh.devices.reshape(4, 2, 4, 2, 2), ALL)
    return jax.shard_map(
        on_device,
        mesh=fine,
        in_specs=(
            P(ALL, None),
            P(DP),
            P(DP, None),
            P(DP, None),
            P(DP, None, TP),
            P(None, DP, TP),
            P(None, TP, DP),
            P(DP, None),
            P(DP),
            P(None, DP, None, TP),
            P(None, TP, DP),
            P(DP, None),
            P(DP),
            P(ALL, None),
        ),
        out_specs=(
            P(ALL, None),
            P(ALL, None),
            P(DP, None, TP),
            P(None, DP, TP),
            P(None, TP, DP),
            P(DP, None),
            P(DP),
            P(None, DP, None, TP),
            P(None, TP, DP),
            P(DP, None),
            P(DP),
        ),
        check_vma=False,
    )
```

time: 2740 us -> 1720 us (0.63)
  blocking collectives: 564 us -> 86.7 us
  waiting for transfers between devices: 1360 us -> 1090 us
  other arithmetic: 305 us -> 74.6 us
  local copies, waits for them, and re-layouts: 217 us -> 45 us
  Pallas kernels: 0 us -> 144 us
    all_to_all x6 -> x9, waiting for transfers between devices: 205 us -> 1080 us  [the longest x1 305 us: on_device(): lax.all_to_all(jnp.repeat(own_mlp, 8, axis=0), DP, split_axis=0, concat_a...]
    unnamed x22 -> x4, waiting for transfers between devices: 520 us -> 1.41 us
    all_gather x2 -> x0, blocking collectives: 400 us -> none  [the longest x1 261 us: on_device(): lax.all_gather(router_att, 'dp', axis=0, tiled=True)]
    all_gather x7 -> x4, waiting for transfers between devices: 332 us -> 9.85 us  [the longest x1 9.85 us: on_device(): unit_two = lax.all_gather(own_two, TP, axis=0, tiled=True)]
    reduce_scatter x5 -> x0, waiting for transfers between devices: 302 us -> none  [the longest x1 166 us: on_device(): lax.psum_scatter(jnp.stack(grads_query).astype(jnp.bfloat16), 'dp', scatt...]
    scatter-add x11 -> x0, other arithmetic: 169 us -> none  [the longest x3 59.4 us: on_device(): dgate_one.at[picked_ids, expert].add(jnp.sum(incoming * branch, -1))]
    pallas_call x0 -> x3, Pallas kernels: none -> 144 us  [the longest x1 107 us: gather_dp(): pl.pallas_call(gather_body, out_shape=jax.ShapeDtypeStruct((4, 2, 4, rows...]
    unnamed x2 -> x0, blocking collectives: 143 us -> none
  transfers between devices with their start and end apart: 23 -> 13, of which waited for: 15 -> 9; matrix products, arithmetic and copies ran while one was open for 22% -> 13% of each run, Pallas kernels for 0% -> 8%
where the time goes in v1:
time: 1720 us; the launch traced here: 1710 us
  waiting for transfers between devices  1090 us (63%)
  matrix products  195 us (11%)
  Pallas kernels  144 us (8%)
  blocking collectives  86.7 us (5%)
  other arithmetic  74.6 us (4%)
  starting transfers between devices  52.2 us (3%)
  local copies, waits for them, and re-layouts  45 us (3%)
    all_to_all x1, waiting for transfers between devices, on_device(): lax.all_to_all(jnp.repeat(own_mlp, 8, axis=0), DP, split_axis=0, concat_a...  305 us
    all_to_all x1, waiting for transfers between devices, on_device(): lax.all_to_all(jnp.concatenate([grad_up_whole, grad_down_whole], 1), DP,...  296 us
    all_to_all x1, waiting for transfers between devices, on_device(): lax.all_to_all(grad_att.reshape(32, share, grad_att.shape[1]), DP, 0, 0,...  294 us
    dot_general x21, matrix products, dot(): return lax.dot_general(a, b, (dims, ((), ())), preferred_element_type=F32)  195 us
    pallas_call x1, Pallas kernels, gather_dp(): pl.pallas_call(gather_body, out_shape=jax.ShapeDtypeStruct((4, 2, 4, rows...  107 us
    all_to_all x2, blocking collectives, sum_over_tensor(): lax.all_to_all(partial.reshape(4, rows // 4, width), TP, 0, 0, tiled=True)  70.8 us
    all_to_all x1, waiting for transfers between devices, on_device(): lax.all_to_all(rows_out.reshape(mlp_count, CAP, width + 128), 'y', 0, 0,...  54 us
    all_to_all x1, waiting for transfers between devices, on_device(): lax.all_to_all(dunit_part.reshape(mlp_count, CAP, width), 'y', 0, 0, tile...  45.9 us
  transfers between devices with their start and end apart: 13, of which 9 were waited for; matrix products, arithmetic and copies ran while one was open for 13% of the time, Pallas kernels for 8%

profile of v1, /device:TPU:1, one launch (start us, length us, event | category | flops | bytes accessed | tf_op | source)
XLA Modules:
  0.0 1706.1 jit_solution(7566310993550892471)
XLA Ops:
  13.2 107.4 %gather_weights.1 = bf16[4,2,4,64,4224]{4,3,2,1,0:T(8,128)(2,1)} custom-call(bf16[64,4224]{1,0:T(8,128)(2,1)} %fusion.57.x_ref), custom_call_target="tpu_custom_call" | custom-call | tf_op jit(solution)/shard_map/gather_weights/pallas_call | solution.py:133
  130.0 9.9 fusion.12.k_ref.v_ref.q0.q1.q2
  146.8 23.4 %attention_forward.1 = (bf16[512,512]{1,0:T(8,128)(2,1)S(1)}, bf16[512,512]{1,0:T(8,128)(2,1)S(1)}, bf16[512,1536]{1,0:T(8,128)(2,1)S(1)}, bf16[512,1536]{1,0:T(...) custom-call(f32[512,2688]{1,0:T(8,128)} %copy-done.11, f32[512,2688]{1,0:T(8,128)} %copy-done.11, ...), custom_call_target="tpu_custom_call" | custom-call | tf_op jit(solution)/shard_map/attention_forward/pallas_call | solution.py:209
  170.2 7.1 fusion.32
  177.3 32.1 %all_to_all.63 = bf16[4,128,2048]{2,1,0:T(8,128)(2,1)S(1)} all-to-all(bf16[4,128,2048]{2,1,0:T(8,128)(2,1)S(1)} %bitcast.98), channel_id=1, replica_groups=mesh['y'=4,'xl'=2,'z'=4,'xh'=2,'core'=2] {'xh','core'}, dimensions={0} | all-to-all | bytes 4194304 | tf_op jit(solution)/shard_map/all_to_all | solution.py:339
  213.7 7.1 convolution_convert_fusion.5
  220.8 5.1 all-to-all-start.5
  225.8 9.8 all-gather.7.cloned.1.call-done
  241.5 7.5 convolution_convert_fusion.2
  249.0 36.0 %all-to-all-done.5 = bf16[4,320,2048]{2,1,0:T(8,128)(2,1)} async-done(((bf16[4,320,2048]{2,1,0:T(8,128)(2,1)}), bf16[4,320,2048]{2,1,0:T(8,128)(2,1)}, u32[]{:S(2)}, u32[]{:S(2)}) %all-to-all-start.5) | async-done | bytes 5242912 | tf_op jit(solution)/shard_map/all_to_all | solution.py:403
  284.9 5.1 all-to-all-start.1
  290.1 4.5 reshape.356
  297.7 54.0 %all-to-all-done.1 = bf16[4,320,2176]{2,1,0:T(8,128)(2,1)} async-done(((bf16[4,320,2176]{2,1,0:T(8,128)(2,1)}), bf16[4,320,2176]{2,1,0:T(8,128)(2,1)}, u32[]{:S(2)}, u32[]{:S(2)}) %all-to-all-start.1) | async-done | bytes 5570592 | tf_op jit(solution)/shard_map/all_to_all | solution.py:436
  351.8 7.0 broadcast_in_dim.34
  358.8 5.4 all-to-all-start.2
  365.4 5.7 fusion.4
  371.2 305.2 %all-to-all-done.2 = bf16[32,64,4224]{2,1,0:T(8,128)(2,1)} async-done(((bf16[32,64,4224]{2,1,0:T(8,128)(2,1)}), bf16[32,64,4224]{2,1,0:T(8,128)(2,1)}, u32[]{:S(2)}, u32[]{:S(2)}) %all-to-all-start.2) | async-done | bytes 17301536 | tf_op jit(solution)/shard_map/all_to_all | solution.py:392
  676.4 22.2 %fusion.8 = f32[1280,2816]{1,0:T(8,128)} fusion(bf16[2048,4224]{1,0:T(8,128)(2,1)} %bitcast.16, bf16[1280,2176]{1,0:T(8,128)(2,1)} %bitcast.13), kind=kOutput, calls=%fused_computation.19 | convolution fusion | flops 14763950080 | bytes 31195136 | tf_op jit(solution)/shard_map/dot_general | solution.py:160
  698.7 18.0 %multiply_convert_fusion.2 = (bf16[1280,1408]{1,0:T(8,128)(2,1)}, bf16[1280,1408]{1,0:T(8,128)(2,1)}, bf16[1280,1408]{1,0:T(8,128)(2,1)}) fusion(f32[1280,2816]{1,0:T(8,128)} %fusion.8, bf16[1280,2048]{1,0:T(8,128)(2,1)S(1)} %copy-done.20, bf16[2048,4224]{1,0:T(8,128)(2,1)} %bitcast.16), kind=kOutput, calls=%fused_computation.32 | convolution fusion | flops 7410810880 | bytes 36241408 | tf_op jit(solution)/shard_map/dot_general | solution.py:160
  716.7 13.2 convolution_convert_fusion.6
  729.9 5.5 all-to-all-start.3
  735.3 20.9 %fusion.14 = bf16[1280,2048]{1,0:T(8,128)(2,1)} fusion(bf16[2048,4224]{1,0:T(8,128)(2,1)} %bitcast.16, bf16[1280,1408]{1,0:T(8,128)(2,1)} %get-tuple-element.75, bf16[1280,1408]{1,0:T(8,128)(2,1)} %get-tuple-element.74), kind=kOutput, calls=%fused_computation.25 | convolution fusion | flops 14780989440 | bytes 23986176 | tf_op jit(solution)/shard_map/dot_general | solution.py:160
  756.2 36.7 %all-to-all-done.3 = bf16[4,320,2048]{2,1,0:T(8,128)(2,1)} async-done(((bf16[4,320,2048]{2,1,0:T(8,128)(2,1)}), bf16[4,320,2048]{2,1,0:T(8,128)(2,1)}, u32[]{:S(2)}, u32[]{:S(2)}) %all-to-all-start.3) | async-done | bytes 5242912 | tf_op jit(solution)/shard_map/all_to_all | solution.py:453
  792.9 5.0 all-to-all-start.6
  798.0 5.5 fusion.5
  808.6 45.9 %all-to-all-done.6 = bf16[4,320,2048]{2,1,0:T(8,128)(2,1)} async-done(((bf16[4,320,2048]{2,1,0:T(8,128)(2,1)}), bf16[4,320,2048]{2,1,0:T(8,128)(2,1)}, u32[]{:S(2)}, u32[]{:S(2)}) %all-to-all-start.6) | async-done | bytes 5242912 | tf_op jit(solution)/shard_map/all_to_all | solution.py:456
  854.5 6.3 fusion.31
  860.9 38.7 %all_to_all.64 = bf16[4,128,2048]{2,1,0:T(8,128)(2,1)S(1)} all-to-all(bf16[4,128,2048]{2,1,0:T(8,128)(2,1)S(1)} %bitcast.97), channel_id=1, replica_groups=mesh['y'=4,'xl'=2,'z'=4,'xh'=2,'core'=2] {'xh','core'}, dimensions={0} | all-to-all | bytes 4194304 | tf_op jit(solution)/shard_map/all_to_all | solution.py:339
  902.1 22.0 %convolution_convert_fusion = bf16[2048,2816]{1,0:T(8,128)(2,1)} fusion(bf16[1280,1408]{1,0:T(8,128)(2,1)} %get-tuple-element.75, bf16[1280,1408]{1,0:T(8,128)(2,1)} %get-tuple-element.74, bf16[1280,2176]{1,0:T(8,128)(2,1)} %bitcast.13), kind=kOutput, calls=%fused_computation.9 | convolution fusion | flops 14784135168 | bytes 23986176 | tf_op jit(solution)/shard_map/dot_general | solution.py:160
  924.1 12.6 convolution_convert_fusion.3
  936.8 7.0 bitcast_convert_fusion
  943.8 5.5 all-to-all-start.4
  949.3 8.6 fusion.17.h0.h1.h2
  958.0 13.6 attention_back.1
  973.7 11.8 multiply_reduce_fusion
  985.5 4.8 all-to-all-start.8
  990.3 13.9 pad_maximum_fusion
  1004.2 12.4 all-to-all-done.8
  1017.9 10.5 all-to-all-start.10
  1031.5 5.7 convolution_convert_fusion.4
  1037.2 6.2 convolution_convert_fusion.1
  1043.4 6.8 fusion.3
  1050.2 295.8 %all-to-all-done.10 = bf16[32,64,4224]{2,1,0:T(8,128)(2,1)} async-done(((bf16[32,64,4224]{2,1,0:T(8,128)(2,1)}), bf16[32,64,4224]{2,1,0:T(8,128)(2,1)}, u32[]{:S(2)}, u32[]{:S(2)}) %all-to-all-start.10) | async-done | bytes 17301536 | tf_op jit(solution)/shard_map/all_to_all | solution.py:461
  1346.0 5.2 all-to-all-start.9
  1360.0 9.2 convert_reduce_fusion
  1376.8 294.2 %all-to-all-done.9 = bf16[32,64,4224]{2,1,0:T(8,128)(2,1)} async-done(((bf16[32,64,4224]{2,1,0:T(8,128)(2,1)}), bf16[32,64,4224]{2,1,0:T(8,128)(2,1)}, u32[]{:S(2)}, u32[]{:S(2)}) %all-to-all-start.9) | async-done | bytes 17301536 | tf_op jit(solution)/shard_map/all_to_all | solution.py:503
  1670.9 6.9 convert_reduce_fusion.1
  1677.9 15.9 psum.7
  (202 shorter events, 71.0 us)
Async XLA Ops:
  7.2 120.1 %all-gather.5.cloned.1.call-start = ((), (), s32[]{:S(2)}) async-start(), calls=%async_computation.11 | async-start | bytes 2621440 | tf_op jit(solution)/shard_map/all_gather | solution.py:389
  7.9 205.8 %all-gather.9.cloned.1.call-start = ((), (), s32[]{:S(2)}) async-start(), calls=%async_computation.13 | async-start | bytes 2621440 | tf_op jit(solution)/shard_map/all_gather | solution.py:390
  8.7 227.0 %all-gather.7.cloned.1.call-start = ((), (), s32[]{:S(2)}) async-start(), calls=%async_computation.12 | async-start | bytes 2621440 | tf_op jit(solution)/shard_map/all_gather | solution.py:427
  13.2 108.7 %copy-start.10 = (s32[512]{0:T(512)S(1)}, s32[512]{0:T(512)}, u32[]{:S(2)}) copy-start(s32[512]{0:T(512)} %param.15) | copy-start | bytes 6148
  121.9 17.9 %copy-start.30 = (f32[2048,1]{0,1:T(1,128)}, f32[2048,1]{0,1:T(1,128)S(1)}, u32[]{:S(2)}) copy-start(f32[2048,1]{0,1:T(1,128)S(1)} %get-tuple-element.85) | copy-start | bytes 24580
  130.0 12.4 copy-start.32
  139.9 2.4 copy-start.11
  170.2 7.1 copy-start.5
  170.2 7.1 copy-start.7
  177.3 32.5 %copy-start.24 = (bf16[128,2048]{1,0:T(8,128)(2,1)S(1)}, bf16[128,2048]{1,0:T(8,128)(2,1)}, u32[]{:S(2)}) copy-start(bf16[128,2048]{1,0:T(8,128)(2,1)} %param.14) | copy-start | bytes 1572868
  209.5 2.6 copy-start.27
  210.1 10.6 copy-start.44
  212.4 8.4 copy-start.38
  220.8 64.1 %all-to-all-start.5 = ((bf16[4,320,2048]{2,1,0:T(8,128)(2,1)}), bf16[4,320,2048]{2,1,0:T(8,128)(2,1)}, u32[]{:S(2)}, u32[]{:S(2)}) async-start(bf16[4,320,2048]{2,1,0:T(8,128)(2,1)} %bitcast.82), calls=%async_computation.5 | async-start | bytes 10485760 | tf_op jit(solution)/shard_map/all_to_all | solution.py:403
  284.9 66.8 %all-to-all-start.1 = ((bf16[4,320,2176]{2,1,0:T(8,128)(2,1)}), bf16[4,320,2176]{2,1,0:T(8,128)(2,1)}, u32[]{:S(2)}, u32[]{:S(2)}) async-start(bf16[4,320,2176]{2,1,0:T(8,128)(2,1)} %bitcast.90), calls=%async_computation.1 | async-start | bytes 11141120 | tf_op jit(solution)/shard_map/all_to_all | solution.py:436
  358.8 317.6 %all-to-all-start.2 = ((bf16[32,64,4224]{2,1,0:T(8,128)(2,1)}), bf16[32,64,4224]{2,1,0:T(8,128)(2,1)}, u32[]{:S(2)}, u32[]{:S(2)}) async-start(bf16[32,64,4224]{2,1,0:T(8,128)(2,1)} %bitcast.81), calls=%async_computation.2 | async-start | bytes 34603008 | tf_op jit(solution)/shard_map/all_to_all | solution.py:392
  676.4 22.2 %copy-start.20 = (bf16[1280,2048]{1,0:T(8,128)(2,1)S(1)}, bf16[1280,2048]{1,0:T(8,128)(2,1)}, u32[]{:S(2)}) copy-start(bf16[1280,2048]{1,0:T(8,128)(2,1)} %fusion.4) | copy-start | bytes 15728644
  729.9 63.0 %all-to-all-start.3 = ((bf16[4,320,2048]{2,1,0:T(8,128)(2,1)}), bf16[4,320,2048]{2,1,0:T(8,128)(2,1)}, u32[]{:S(2)}, u32[]{:S(2)}) async-start(bf16[4,320,2048]{2,1,0:T(8,128)(2,1)} %bitcast.92), calls=%async_computation.3 | async-start | bytes 10485760 | tf_op jit(solution)/shard_map/all_to_all | solution.py:453
  792.9 61.7 %all-to-all-start.6 = ((bf16[4,320,2048]{2,1,0:T(8,128)(2,1)}), bf16[4,320,2048]{2,1,0:T(8,128)(2,1)}, u32[]{:S(2)}, u32[]{:S(2)}) async-start(bf16[4,320,2048]{2,1,0:T(8,128)(2,1)} %bitcast.91), calls=%async_computation.6 | async-start | bytes 10485760 | tf_op jit(solution)/shard_map/all_to_all | solution.py:456
  797.9 5.7 copy-start.29
  797.9 5.6 copy-start.39
  797.9 6.6 copy-start.37
  798.0 6.6 copy-start.43
  798.0 151.3 %all-gather.11.cloned.1.call-start = ((), (), s32[]{:S(2)}) async-start(), calls=%async_computation.14 | async-start | bytes 2621440 | tf_op jit(solution)/shard_map/all_gather | solution.py:476
  860.8 39.1 %copy-start.13 = (f32[128,2048]{1,0:T(8,128)S(1)}, f32[128,2048]{1,0:T(8,128)}, u32[]{:S(2)}) copy-start(f32[128,2048]{1,0:T(8,128)} %copy-done.12) | copy-start | bytes 3145732
  860.9 39.1 %copy-start.45 = (f32[128]{0:T(128)S(1)}, f32[128]{0:T(128)}, u32[]{:S(2)}) copy-start(f32[128]{0:T(128)} %copy-done.44) | copy-start | bytes 1540
  860.9 40.1 %copy-start.21 = (bf16[128,2048]{1,0:T(8,128)(2,1)S(1)}, bf16[128,2048]{1,0:T(8,128)(2,1)}, u32[]{:S(2)}) copy-start(bf16[128,2048]{1,0:T(8,128)(2,1)} %param.27) | copy-start | bytes 1572868
  902.1 22.0 %copy-start.49 = (bf16[1280,1408]{1,0:T(8,128)(2,1)S(1)}, bf16[1280,1408]{1,0:T(8,128)(2,1)}, u32[]{:S(2)}) copy-start(bf16[1280,1408]{1,0:T(8,128)(2,1)} %get-tuple-element.76) | copy-start | bytes 10813444
  943.8 41.6 %all-to-all-start.4 = ((bf16[4,128,2048]{2,1,0:T(8,128)(2,1)}), bf16[4,128,2048]{2,1,0:T(8,128)(2,1)}, u32[]{:S(2)}, u32[]{:S(2)}) async-start(bf16[4,128,2048]{2,1,0:T(8,128)(2,1)} %bitcast.95), calls=%async_computation.4 | async-start | bytes 4194304 | tf_op jit(solution)/shard_map/all_to_all | solution.py:339
  949.3 8.6 copy-start.1
  949.3 8.6 copy-start.3
  949.3 8.6 copy-start.6
  949.3 8.6 copy-start.8
  957.9 15.5 copy-start.33
  957.9 15.5 copy-start.26
  957.9 15.5 copy-start.35
  957.9 15.5 copy-start.41
  957.9 15.7 copy-start.47
  985.5 31.1 %all-to-all-start.8 = ((bf16[4,128,2048]{2,1,0:T(8,128)(2,1)}), bf16[4,128,2048]{2,1,0:T(8,128)(2,1)S(1)}, u32[]{:S(2)}, u32[]{:S(2)}) async-start(bf16[4,128,2048]{2,1,0:T(8,128)(2,1)} %bitcast.96), calls=%async_computation.8 | async-start | bytes 4194304 | tf_op jit(solution)/shard_map/all_to_all | solution.py:339
  1017.9 10.6 copy-start.18
  1017.9 11.0 copy-start.31
  1017.9 328.1 %all-to-all-start.10 = ((bf16[32,64,4224]{2,1,0:T(8,128)(2,1)}), bf16[32,64,4224]{2,1,0:T(8,128)(2,1)}, u32[]{:S(2)}, u32[]{:S(2)}) async-start(bf16[32,64,4224]{2,1,0:T(8,128)(2,1)} %bitcast.80), calls=%async_computation.10 | async-start | bytes 34603008 | tf_op jit(solution)/shard_map/all_to_all | solution.py:461
  1031.5 5.7 copy-start.23
  1031.5 5.7 copy-start.48
  1346.0 324.9 %all-to-all-start.9 = ((bf16[32,64,4224]{2,1,0:T(8,128)(2,1)}), bf16[32,64,4224]{2,1,0:T(8,128)(2,1)}, u32[]{:S(2)}, u32[]{:S(2)}) async-start(bf16[32,64,4224]{2,1,0:T(8,128)(2,1)} %bitcast.79), calls=%async_computation.9 | async-start | bytes 34603008 | tf_op jit(solution)/shard_map/all_to_all | solution.py:503
  1351.2 6.0 copy-start.14
  1351.2 5.9 copy-start.17
  1351.2 5.9 copy-start.22
  (15 other events, 14.7 us)
Sparse Core Ops, SparseCore 0:
  9.7 36.7 all-gather.4
  48.2 24.5 all-gather.8
  212.2 23.4 all-gather.6
  902.3 29.2 all-gather.10

commit v2 on v1

--- a/solution.py
+++ b/solution.py
@@ -14,6 +14,7 @@
 NEGATIVE = -1e30
 ROPE_BASE = 10000.0
 MESH_ID = pl.DeviceIdType.MESH
+MIB = 1024 * 1024
 DP = ("y", "xl", "z")
 TP = ("xh", "core")
 ALL = DP + TP
@@ -26,31 +27,26 @@
 
 
 def neighbour(axis, step):
-    size = 2 if axis == "xl" else 4
+    size = 4 if axis in ("y", "z") else 2
     return {axis: lax.rem(lax.axis_index(axis) + step + size, size)}
 
 
-def gather_body(x_ref, out_ref, loc, xs, xr, s1, r1m, r1p, f1s, f1r, s2, r2m, r2p, f2s, f2r):
-    y, xl, z = lax.axis_index("y"), lax.axis_index("xl"), lax.axis_index("z")
-    half = x_ref.shape[0] // 2
-    quarter = half // 2
+def greet(*devices):
     barrier = pltpu.get_barrier_semaphore()
-    for axis, step in (("xl", 1), ("y", 1), ("y", -1), ("z", 1), ("z", -1)):
-        pl.semaphore_signal(
-            barrier, inc=1, device_id=neighbour(axis, step), device_id_type=MESH_ID
-        )
-    pl.semaphore_wait(barrier, 5)
-    rings = (("z", "y"), ("y", "z"))
-    place = {"y": y, "z": z}
-    other = 1 - xl
-    both = pl.ds(0, 2)
-    sends = []
-
-    def slot(h, first, second, j, start, count):
-        yy, zz = (second, first) if h == 0 else (first, second)
-        return out_ref.at[yy, j, zz, pl.ds(start, count)]
-
-    def send(src, dst, send_sem, recv_sem, device):
+    for device in devices:
+        pl.semaphore_signal(barrier, inc=1, device_id=device, device_id_type=MESH_ID)
+    pl.semaphore_wait(barrier, len(devices))
+
+
+def arrived(ref, sem):
+    pltpu.make_async_copy(ref, ref, sem).wait()
+
+
+class Sends:
+    def __init__(self):
+        self.copies = []
+
+    def __call__(self, src, dst, send_sem, recv_sem, device):
         copy = pltpu.make_async_remote_copy(
             src_ref=src,
             dst_ref=dst,
@@ -60,13 +56,40 @@
             device_id_type=MESH_ID,
         )
         copy.start()
-        sends.append(copy)
-
-    def arrived(ref, sem):
-        pltpu.make_async_copy(ref, ref, sem).wait()
-
-    own = pltpu.make_async_copy(x_ref, out_ref.at[y, xl, z], loc)
+        self.copies.append(copy)
+
+    def finish(self):
+        for copy in self.copies:
+            copy.wait_send()
+
+
+def gather_body(
+    x_ref, experts_ref, out_ref, expert_ref,
+    loc, xs, xr, s1, r1m, r1p, f1s, f1r, s2, r2m, r2p, f2s, f2r, es, er,
+):
+    y, xl, z = lax.axis_index("y"), lax.axis_index("xl"), lax.axis_index("z")
+    half = x_ref.shape[0] // 2
+    quarter = half // 2
+    greet(
+        neighbour("xl", 1),
+        *(neighbour("y", step) for step in (1, 2, 3)),
+        *(neighbour("z", step) for step in (1, -1)),
+    )
+    rings = (("z", "y"), ("y", "z"))
+    place = {"y": y, "z": z}
+    other = 1 - xl
+    both = pl.ds(0, 2)
+    sends = Sends()
+    send = sends
+
+    def slot(h, first, second, j, start, count):
+        yy, zz = (second, first) if h == 0 else (first, second)
+        return out_ref.at[j, zz, yy, pl.ds(start, count)]
+
+    own = pltpu.make_async_copy(x_ref, out_ref.at[xl, z, y], loc.at[0])
     own.start()
+    expert = pltpu.make_async_copy(experts_ref.at[y], expert_ref.at[y], loc.at[1])
+    expert.start()
     for h in (0, 1):
         first, second = place[rings[h][0]], place[rings[h][1]]
         src = x_ref.at[pl.ds(h * half, half)]
@@ -107,6 +130,14 @@
                 block = slot(h, mod4(first + 2), second, jx, h * half + p * quarter, quarter)
                 arrived(block, f1r.at[h, j, p])
         send_second(h, 3, mod4(first + 2))
+    for step in (1, 3, 2):
+        send(
+            experts_ref.at[mod4(y + step)],
+            expert_ref.at[y],
+            es.at[step - 1],
+            er.at[step - 1],
+            neighbour("y", step),
+        )
     steps = ((0, 0), (1, -1), (2, 1), (3, 2))
     for k, step in steps:
         for h in (0, 1):
@@ -123,20 +154,25 @@
             for p in (0, 1):
                 block = slot(h, first, mod4(second + 2), both, h * half + p * quarter, quarter)
                 arrived(block, f2r.at[h, k, p])
-    for copy in sends:
-        copy.wait_send()
-
-
-def gather_dp(shard, collective_id):
+    for step in (1, 3, 2):
+        arrived(expert_ref.at[mod4(y - step)], er.at[step - 1])
+    expert.wait()
+    sends.finish()
+
+
+def gather_dp(shard, experts):
     rows, cols = shard.shape
     dma = pltpu.SemaphoreType.DMA
-    whole = pl.pallas_call(
+    whole, expert = pl.pallas_call(
         gather_body,
-        out_shape=jax.ShapeDtypeStruct((4, 2, 4, rows, cols), shard.dtype),
-        in_specs=[pl.BlockSpec(memory_space=pl.ANY)],
-        out_specs=pl.BlockSpec(memory_space=pl.ANY),
+        out_shape=[
+            jax.ShapeDtypeStruct((2, 4, 4, rows, cols), shard.dtype),
+            jax.ShapeDtypeStruct(experts.shape, experts.dtype),
+        ],
+        in_specs=[pl.BlockSpec(memory_space=pl.ANY)] * 2,
+        out_specs=[pl.BlockSpec(memory_space=pl.ANY)] * 2,
         scratch_shapes=[
-            dma,
+            dma((2,)),
             dma((2,)),
             dma((2,)),
             dma((2, 2, 2)),
@@ -149,11 +185,459 @@
             dma((2, 4)),
             dma((2, 4, 2)),
             dma((2, 4, 2)),
+            dma((3,)),
+            dma((3,)),
         ],
-        compiler_params=pltpu.CompilerParams(collective_id=collective_id, has_side_effects=True),
+        compiler_params=pltpu.CompilerParams(collective_id=0, has_side_effects=True),
         name="gather_weights",
-    )(shard)
-    return whole.reshape(32 * rows, cols)
+    )(shard, experts)
+    return whole.reshape(32 * rows, cols), expert
+
+
+def reduce_body(scatter_count, part_refs, core_buf, sum_buf, far_buf, core_s, core_r, far_s, far_r, sends):
+    xh, core = lax.axis_index("xh"), lax.axis_index("core")
+    rows = part_refs[0].shape[1]
+    step = rows // scatter_count
+    far, here = 1 - xh, xh
+    for n, chunk in enumerate(range(0, rows, step)):
+        at = pl.ds(chunk, step)
+        for i, part in enumerate(part_refs):
+            sends(
+                part.at[far * 2 + 1 - core, at],
+                core_buf.at[i, 0, at],
+                core_s.at[i, n, 0],
+                core_r.at[i, n, 0],
+                neighbour("core", 1),
+            )
+    for n, chunk in enumerate(range(0, rows, step)):
+        at = pl.ds(chunk, step)
+        for i, part in enumerate(part_refs):
+            sends(
+                part.at[here * 2 + 1 - core, at],
+                core_buf.at[i, 1, at],
+                core_s.at[i, n, 1],
+                core_r.at[i, n, 1],
+                neighbour("core", 1),
+            )
+    for n, chunk in enumerate(range(0, rows, step)):
+        at = pl.ds(chunk, step)
+        for i, part in enumerate(part_refs):
+            arrived(core_buf.at[i, 0, at], core_r.at[i, n, 0])
+            mine = part[far * 2 + core, chunk : chunk + step, :].astype(F32)
+            sum_buf[i, chunk : chunk + step, :] = (
+                mine + core_buf[i, 0, chunk : chunk + step, :].astype(F32)
+            ).astype(BF16)
+            sends(
+                sum_buf.at[i, at],
+                far_buf.at[i, at],
+                far_s.at[i, n],
+                far_r.at[i, n],
+                neighbour("xh", 1),
+            )
+
+    def total(i, n):
+        chunk = n * step
+        at = pl.ds(chunk, step)
+        arrived(core_buf.at[i, 1, at], core_r.at[i, n, 1])
+        near = part_refs[i][here * 2 + core, chunk : chunk + step, :].astype(F32)
+        near = near + core_buf[i, 1, chunk : chunk + step, :].astype(F32)
+        arrived(far_buf.at[i, at], far_r.at[i, n])
+        return near + far_buf[i, chunk : chunk + step, :].astype(F32)
+
+    return total
+
+
+CHUNKS = 4
+
+
+def reduce_scratch(count, rows, width):
+    dma = pltpu.SemaphoreType.DMA
+    return [
+        pltpu.VMEM((count, 2, rows, width), BF16),
+        pltpu.VMEM((count, rows, width), BF16),
+        pltpu.VMEM((count, rows, width), BF16),
+        dma((count, CHUNKS, 2)),
+        dma((count, CHUNKS, 2)),
+        dma((count, CHUNKS)),
+        dma((count, CHUNKS)),
+    ]
+
+
+def spread_chunk(out_ref, n, step, sems, sends):
+    xh, core = lax.axis_index("xh"), lax.axis_index("core")
+    at = pl.ds(n * step, step)
+    mine = out_ref.at[xh * 2 + core, at]
+    far_s, far_r, core_s, core_r = sems
+    sends(mine, mine, far_s.at[n], far_r.at[n], neighbour("xh", 1))
+    sends(mine, mine, core_s.at[n, 0], core_r.at[n, 0], neighbour("core", 1))
+
+
+def spread_finish(out_ref, step, sems, sends):
+    xh, core = lax.axis_index("xh"), lax.axis_index("core")
+    far_s, far_r, core_s, core_r = sems
+    for n in range(CHUNKS):
+        at = pl.ds(n * step, step)
+        theirs = out_ref.at[(1 - xh) * 2 + core, at]
+        arrived(theirs, far_r.at[n])
+        sends(theirs, theirs, core_s.at[n, 1], core_r.at[n, 1], neighbour("core", 1))
+    for n in range(CHUNKS):
+        at = pl.ds(n * step, step)
+        arrived(out_ref.at[xh * 2 + 1 - core, at], core_r.at[n, 0])
+        arrived(out_ref.at[(1 - xh) * 2 + 1 - core, at], core_r.at[n, 1])
+
+
+def spread_scratch():
+    dma = pltpu.SemaphoreType.DMA
+    return [dma((CHUNKS,)), dma((CHUNKS,)), dma((CHUNKS, 2)), dma((CHUNKS, 2))]
+
+
+def middle_body(part_ref, x_ref, gain_ref, middle_ref, unit_ref, *scratch):
+    sends = Sends()
+    greet(neighbour("core", 1), neighbour("xh", 1))
+    total = reduce_body(CHUNKS, [part_ref], *scratch[:7], sends)
+    me = lax.axis_index("xh") * 2 + lax.axis_index("core")
+    step = x_ref.shape[0] // CHUNKS
+    for n in range(CHUNKS):
+        rows = slice(n * step, (n + 1) * step)
+        middle = x_ref[rows, :].astype(F32) + total(0, n)
+        middle_ref[rows, :] = middle
+        inverse = lax.rsqrt(jnp.mean(middle * middle, 1, keepdims=True) + EPSILON)
+        unit_ref[me, rows, :] = (middle * inverse * gain_ref[...]).astype(BF16)
+        spread_chunk(unit_ref, n, step, scratch[7:], sends)
+    spread_finish(unit_ref, step, scratch[7:], sends)
+    sends.finish()
+
+
+def vmem(count):
+    return [pl.BlockSpec(memory_space=pltpu.VMEM)] * count
+
+
+def middle_and_unit(part, x, gain):
+    rows, width = x.shape
+    middle, unit = pl.pallas_call(
+        middle_body,
+        out_shape=[
+            jax.ShapeDtypeStruct((rows, width), F32),
+            jax.ShapeDtypeStruct((4, rows, width), BF16),
+        ],
+        in_specs=vmem(3),
+        out_specs=vmem(2),
+        scratch_shapes=reduce_scratch(1, rows, width) + spread_scratch(),
+        compiler_params=pltpu.CompilerParams(
+            collective_id=1, has_side_effects=True, vmem_limit_bytes=32 * MIB
+        ),
+        name="middle_and_unit",
+    )(part.reshape(4, rows, width), x, gain[None])
+    return middle, unit.reshape(4 * rows, width)
+
+
+def back_body(part_ref, middle_ref, grad_ref, gain_ref, dmiddle_ref, dgain_ref, spread_ref, *scratch):
+    sends = Sends()
+    greet(neighbour("core", 1), neighbour("xh", 1))
+    total = reduce_body(CHUNKS, [part_ref], *scratch[:7], sends)
+    me = lax.axis_index("xh") * 2 + lax.axis_index("core")
+    step = middle_ref.shape[0] // CHUNKS
+    for n in range(CHUNKS):
+        rows = slice(n * step, (n + 1) * step)
+        middle = middle_ref[rows, :]
+        inverse = lax.rsqrt(jnp.mean(middle * middle, 1, keepdims=True) + EPSILON)
+        normed = middle * inverse
+        dunit = total(0, n)
+        product = dunit * normed
+        dgain = jnp.sum(product, 0, keepdims=True)
+        if n == 0:
+            dgain_ref[...] = dgain
+        else:
+            dgain_ref[...] += dgain
+        mean = jnp.mean(product * gain_ref[...], 1, keepdims=True)
+        dmiddle = grad_ref[rows, :].astype(F32) + inverse * (dunit * gain_ref[...] - normed * mean)
+        dmiddle_ref[rows, :] = dmiddle
+        spread_ref[me, rows, :] = dmiddle.astype(BF16)
+        spread_chunk(spread_ref, n, step, scratch[7:], sends)
+    spread_finish(spread_ref, step, scratch[7:], sends)
+    sends.finish()
+
+
+def middle_back(part, middle, grad, gain):
+    rows, width = middle.shape
+    dmiddle, dgain, spread = pl.pallas_call(
+        back_body,
+        out_shape=[
+            jax.ShapeDtypeStruct((rows, width), F32),
+            jax.ShapeDtypeStruct((1, width), F32),
+            jax.ShapeDtypeStruct((4, rows, width), BF16),
+        ],
+        in_specs=vmem(4),
+        out_specs=vmem(3),
+        scratch_shapes=reduce_scratch(1, rows, width) + spread_scratch(),
+        compiler_params=pltpu.CompilerParams(
+            collective_id=2, has_side_effects=True, vmem_limit_bytes=32 * MIB
+        ),
+        name="middle_back",
+    )(part.reshape(4, rows, width), middle, grad, gain[None])
+    return dmiddle, dgain[0], spread.reshape(4 * rows, width)
+
+
+def last_body(
+    part_ref, feed_ref, x_ref, middle_ref, dmiddle_ref, gain_ref, small_ref,
+    output_ref, dinput_ref, small_out, *scratch,
+):
+    sends = Sends()
+    xh, core = lax.axis_index("xh"), lax.axis_index("core")
+    peers = ({"xh": xh, "core": 1 - core}, {"xh": 1 - xh, "core": core}, {"xh": 1 - xh, "core": 1 - core})
+    greet(*peers)
+    small_buf, small_s, small_r = scratch[7:]
+    for n, peer in enumerate(peers):
+        sends(small_ref, small_buf.at[n], small_s.at[n], small_r.at[n], peer)
+    total = reduce_body(CHUNKS, [part_ref, feed_ref], *scratch[:7], sends)
+    step = x_ref.shape[0] // CHUNKS
+    for n in range(CHUNKS):
+        rows = slice(n * step, (n + 1) * step)
+        x = x_ref[rows, :].astype(F32)
+        inverse = lax.rsqrt(jnp.mean(x * x, 1, keepdims=True) + EPSILON)
+        normed = x * inverse
+        dscaled = total(0, n) * gain_ref[...]
+        mean = jnp.mean(dscaled * normed, 1, keepdims=True)
+        dinput_ref[rows, :] = dmiddle_ref[rows, :] + inverse * (dscaled - normed * mean)
+        output_ref[rows, :] = (middle_ref[rows, :] + total(1, n)).astype(BF16)
+    for n in range(3):
+        arrived(small_buf.at[n], small_r.at[n])
+    small_out[...] = (small_ref[...] + small_buf[1]) + (small_buf[0] + small_buf[2])
+    sends.finish()
+
+
+def last_sums(part, feed, x, middle, dmiddle, gain, small):
+    rows, width = x.shape
+    dma = pltpu.SemaphoreType.DMA
+    return pl.pallas_call(
+        last_body,
+        out_shape=[
+            jax.ShapeDtypeStruct((rows, width), BF16),
+            jax.ShapeDtypeStruct((rows, width), F32),
+            jax.ShapeDtypeStruct(small.shape, F32),
+        ],
+        in_specs=vmem(7),
+        out_specs=vmem(3),
+        scratch_shapes=reduce_scratch(2, rows, width)
+        + [pltpu.VMEM((3, *small.shape), F32), dma((3,)), dma((3,))],
+        compiler_params=pltpu.CompilerParams(
+            collective_id=3, has_side_effects=True, vmem_limit_bytes=40 * MIB
+        ),
+        name="last_sums",
+    )(part.reshape(4, rows, width), feed.reshape(4, rows, width), x, middle, dmiddle, gain[None], small)
+
+
+def rows_body(rows_ref, out_ref, loc, far_s, far_r, core_s, core_r):
+    y, core = lax.axis_index("y"), lax.axis_index("core")
+    half = rows_ref.shape[1] // 2
+    sends = Sends()
+    greet(neighbour("core", 1), *(neighbour("y", step) for step in (1, 2, 3)))
+    at = pl.ds(pl.multiple_of(core * half, half), half)
+    own = pltpu.make_async_copy(rows_ref.at[y], out_ref.at[y], loc)
+    own.start()
+    for step in (2, 1, 3):
+        target = mod4(y + step)
+        sends(
+            rows_ref.at[target, at],
+            out_ref.at[y, at],
+            far_s.at[step - 1],
+            far_r.at[step - 1],
+            neighbour("y", step),
+        )
+    for step in (1, 3, 2):
+        source = mod4(y - step)
+        block = out_ref.at[source, at]
+        arrived(block, far_r.at[step - 1])
+        sends(block, block, core_s.at[step - 1], core_r.at[step - 1], neighbour("core", 1))
+    own.wait()
+    other = pl.ds(pl.multiple_of((1 - core) * half, half), half)
+    for step in (1, 3, 2):
+        arrived(out_ref.at[mod4(y - step), other], core_r.at[step - 1])
+    sends.finish()
+
+
+def rows_to_experts(rows):
+    dma = pltpu.SemaphoreType.DMA
+    return pl.pallas_call(
+        rows_body,
+        out_shape=jax.ShapeDtypeStruct(rows.shape, rows.dtype),
+        in_specs=[pl.BlockSpec(memory_space=pl.ANY)],
+        out_specs=pl.BlockSpec(memory_space=pl.ANY),
+        scratch_shapes=[dma, dma((3,)), dma((3,)), dma((3,)), dma((3,))],
+        compiler_params=pltpu.CompilerParams(collective_id=4, has_side_effects=True),
+        name="rows_to_experts",
+    )(rows)
+
+
+STEPS = (2, 1, -1, 0)
+
+
+def scatter_body(
+    qkv_ref, small_ref, o_ref, out_ref, g_ref, loc, t_buf, r_buf, tb_buf, rb_buf, c_buf,
+    t_s, t_r, r_s, r_r, tb_s, tb_r, rb_s, rb_r, c_s, c_r,
+):
+    xl = lax.axis_index("xl")
+    place = {"y": lax.axis_index("y"), "z": lax.axis_index("z")}
+    half = g_ref.shape[3] // 2
+    quarter = half // 2
+    rings = (("z", "y"), ("y", "z"))
+    sends = Sends()
+    column = 0
+    parts = []
+    for n, ref in enumerate((qkv_ref, small_ref, o_ref)):
+        cols = ref.shape[-1]
+        parts.append(pltpu.make_async_copy(ref, g_ref.at[..., pl.ds(column, cols)], loc.at[n]))
+        parts[-1].start()
+        column += cols
+    greet(neighbour("xl", 1), *(neighbour(axis, step) for axis in ("y", "z") for step in (1, -1)))
+    both = slice(0, 2)
+    for part in parts:
+        part.wait()
+
+    def grad_ref(h, first, second, start):
+        zz, yy = (first, second) if h == 0 else (second, first)
+        return g_ref.at[both, zz, yy, pl.ds(h * half + start, quarter)]
+
+    def grad(h, first, second, j, start, count):
+        zz, yy = (first, second) if h == 0 else (second, first)
+        return g_ref[j, zz, yy, h * half + start : h * half + start + count, :].astype(F32)
+
+    def firsts(h, k):
+        return mod4(place[rings[h][0]] + STEPS[k])
+
+    for k in range(4):
+        for h in (0, 1):
+            second = place[rings[h][1]]
+            for d, way in ((0, 1), (1, -1)):
+                sends(
+                    grad_ref(h, firsts(h, k), mod4(second + 2), d * quarter),
+                    t_buf.at[h, d, k],
+                    t_s.at[h, d, k],
+                    t_r.at[h, d, k],
+                    neighbour(rings[h][1], way),
+                )
+    for k in range(4):
+        for h in (0, 1):
+            second = place[rings[h][1]]
+            for d, way in ((0, 1), (1, -1)):
+                sends(
+                    grad_ref(h, firsts(h, k), mod4(second + way), (1 - d) * quarter),
+                    r_buf.at[h, d, k, both, pl.ds((1 - d) * quarter, quarter)],
+                    r_s.at[h, d, k, 0],
+                    r_r.at[h, d, k, 0],
+                    neighbour(rings[h][1], way),
+                )
+    for k in range(4):
+        for h in (0, 1):
+            second = place[rings[h][1]]
+            for d, way in ((0, 1), (1, -1)):
+                arrived(t_buf.at[h, d, k], t_r.at[h, d, k])
+                for j in (0, 1):
+                    t_buf[h, d, k, j] = (
+                        t_buf[h, d, k, j].astype(F32)
+                        + grad(h, firsts(h, k), mod4(second + way), j, d * quarter, quarter)
+                    ).astype(BF16)
+                sends(
+                    t_buf.at[h, d, k],
+                    r_buf.at[h, d, k, both, pl.ds(d * quarter, quarter)],
+                    r_s.at[h, d, k, 1],
+                    r_r.at[h, d, k, 1],
+                    neighbour(rings[h][1], way),
+                )
+    for k in range(4):
+        for h in (0, 1):
+            second = place[rings[h][1]]
+            for d in (0, 1):
+                arrived(r_buf.at[h, d, k, both, pl.ds((1 - d) * quarter, quarter)], r_r.at[h, d, k, 0])
+                arrived(r_buf.at[h, d, k, both, pl.ds(d * quarter, quarter)], r_r.at[h, d, k, 1])
+            for j in (0, 1):
+                r_buf[h, 0, k, j] = (
+                    r_buf[h, 0, k, j].astype(F32)
+                    + r_buf[h, 1, k, j].astype(F32)
+                    + grad(h, firsts(h, k), second, j, 0, half)
+                ).astype(BF16)
+            for d, way in ((0, 1), (1, -1)):
+                device = neighbour(rings[h][0], way)
+                if k == 0:
+                    sends(
+                        r_buf.at[h, 0, 0, both, pl.ds(d * quarter, quarter)],
+                        tb_buf.at[h, d],
+                        tb_s.at[h, d],
+                        tb_r.at[h, d],
+                        device,
+                    )
+                if k == 1 + d:
+                    sends(
+                        r_buf.at[h, 0, k, both, pl.ds((1 - d) * quarter, quarter)],
+                        rb_buf.at[h, d, both, pl.ds((1 - d) * quarter, quarter)],
+                        rb_s.at[h, d, 0],
+                        rb_r.at[h, d, 0],
+                        device,
+                    )
+                    arrived(tb_buf.at[h, d], tb_r.at[h, d])
+                    for j in (0, 1):
+                        tb_buf[h, d, j] = (
+                            tb_buf[h, d, j].astype(F32)
+                            + r_buf[h, 0, k, j, d * quarter : (d + 1) * quarter, :].astype(F32)
+                        ).astype(BF16)
+                    sends(
+                        tb_buf.at[h, d],
+                        rb_buf.at[h, d, both, pl.ds(d * quarter, quarter)],
+                        rb_s.at[h, d, 1],
+                        rb_r.at[h, d, 1],
+                        device,
+                    )
+    for h in (0, 1):
+        for d in (0, 1):
+            arrived(rb_buf.at[h, d, both, pl.ds((1 - d) * quarter, quarter)], rb_r.at[h, d, 0])
+            arrived(rb_buf.at[h, d, both, pl.ds(d * quarter, quarter)], rb_r.at[h, d, 1])
+        for j in (0, 1):
+            rb_buf[h, 0, j] = (
+                rb_buf[h, 0, j].astype(F32)
+                + rb_buf[h, 1, j].astype(F32)
+                + r_buf[h, 0, 3, j].astype(F32)
+            ).astype(BF16)
+        sends(rb_buf.at[h, 0, 1 - xl], c_buf.at[h], c_s.at[h], c_r.at[h], neighbour("xl", 1))
+    for h in (0, 1):
+        arrived(c_buf.at[h], c_r.at[h])
+        out_ref[h * half : (h + 1) * half, :] = rb_buf[h, 0, xl].astype(F32) + c_buf[h].astype(F32)
+    sends.finish()
+
+
+def scatter_dp(*grads):
+    rows, cols = grads[0].shape[0], sum(grad.shape[1] for grad in grads)
+    share = rows // 32
+    half, quarter = share // 2, share // 4
+    dma = pltpu.SemaphoreType.DMA
+    return pl.pallas_call(
+        scatter_body,
+        out_shape=jax.ShapeDtypeStruct((share, cols), F32),
+        in_specs=[pl.BlockSpec(memory_space=pl.ANY)] * 3,
+        out_specs=pl.BlockSpec(memory_space=pltpu.VMEM),
+        scratch_shapes=[
+            pltpu.VMEM((2, 4, 4, share, cols), BF16),
+            dma((3,)),
+            pltpu.VMEM((2, 2, 4, 2, quarter, cols), BF16),
+            pltpu.VMEM((2, 2, 4, 2, half, cols), BF16),
+            pltpu.VMEM((2, 2, 2, quarter, cols), BF16),
+            pltpu.VMEM((2, 2, 2, half, cols), BF16),
+            pltpu.VMEM((2, half, cols), BF16),
+            dma((2, 2, 4)),
+            dma((2, 2, 4)),
+            dma((2, 2, 4, 2)),
+            dma((2, 2, 4, 2)),
+            dma((2, 2)),
+            dma((2, 2)),
+            dma((2, 2, 2)),
+            dma((2, 2, 2)),
+            dma((2,)),
+            dma((2,)),
+        ],
+        compiler_params=pltpu.CompilerParams(
+            collective_id=5, has_side_effects=True, vmem_limit_bytes=56 * MIB
+        ),
+        name="scatter_grads",
+    )(*(grad.reshape(2, 4, 4, share, grad.shape[1]) for grad in grads))
 
 
 def dot(a, b, dims):
@@ -217,7 +701,7 @@
         + [pl.BlockSpec((1, 3, tokens, tokens), lambda h: (h, 0, 0, 0))],
         out_shape=[narrow, narrow, wide, wide, wide]
         + [jax.ShapeDtypeStruct((heads, 3, tokens, tokens), BF16)],
-        compiler_params=pltpu.CompilerParams(vmem_limit_bytes=48 * 1024 * 1024),
+        compiler_params=pltpu.CompilerParams(vmem_limit_bytes=48 * MIB),
         name="attention_forward",
     )(joined, joined, joined, joined, joined, cosine, sine, segments[:, None], segments[None], gates)
 
@@ -290,7 +774,7 @@
             jax.ShapeDtypeStruct((tokens, 2560), BF16),
             jax.ShapeDtypeStruct((tokens, HD), F32),
         ],
-        compiler_params=pltpu.CompilerParams(vmem_limit_bytes=48 * 1024 * 1024),
+        compiler_params=pltpu.CompilerParams(vmem_limit_bytes=48 * MIB),
         name="attention_back",
     )(key, val, que, que, que, mix, mix, mix, raw, raw, raw, prob, cosine, sine, gates)
 
@@ -322,11 +806,6 @@
     return activations * inverse, inverse
 
 
-def norm_back(dunit, normed, inverse, gain):
-    dscaled = dunit * gain
-    return inverse * (dscaled - normed * jnp.mean(dscaled * normed, -1, keepdims=True))
-
-
 def swiglu_back(dhidden, gate_pre, linear):
     sigmoid_pre = jax.nn.sigmoid(gate_pre)
     dgate_pre = dhidden * linear * sigmoid_pre * (1.0 + gate_pre * (1.0 - sigmoid_pre))
@@ -334,10 +813,14 @@
     return jnp.concatenate([dgate_pre, dlinear], 1).astype(BF16)
 
 
-def sum_over_tensor(partial):
-    rows, width = partial.shape
-    pieces = lax.all_to_all(partial.reshape(4, rows // 4, width), TP, 0, 0, tiled=True)
-    return jnp.sum(pieces.astype(F32), 0)
+def reorder(rows):
+    count, width = rows.shape
+    return jnp.swapaxes(rows.reshape(count, 4, 8, width // 32), 1, 2).reshape(count, width)
+
+
+def order_back(rows):
+    count, width = rows.shape
+    return jnp.swapaxes(rows.reshape(count, 8, 4, width // 32), 1, 2).reshape(count, width)
 
 
 def pad_to(array, width):
@@ -386,10 +869,14 @@
         ],
         2,
     )
+    inputs = reorder(inputs)
+    out_grad = reorder(out_grad)
     x_all = lax.all_gather(inputs, TP, axis=0, tiled=True)
     grad_all = lax.all_gather(out_grad, TP, axis=0, tiled=True)
-    weights = gather_dp(own_att, 0)
-    owned = lax.all_to_all(jnp.repeat(own_mlp, 8, axis=0), DP, split_axis=0, concat_axis=1, tiled=True)[0]
+    weights, own_expert = gather_dp(own_att, own_mlp)
+    own_expert = own_expert.reshape(mlp_count * share, 3 * hidden_local)
+    up_whole = lax.all_gather(own_expert[:, : 2 * hidden_local], ("xl", "z"), axis=0, tiled=True)
+    down_whole = lax.all_gather(own_expert[:, 2 * hidden_local :], ("xl", "z"), axis=0, tiled=True)
 
     tokens = x_all.shape[0]
     match = jnp.sum((mlp_routes[:, :, None] == jnp.arange(mlp_count, dtype=jnp.int32)).astype(BF16), 1)
@@ -421,10 +908,7 @@
     )
     out_weights = weights[:, out_at:]
     attention = dot(gmixed, out_weights, ((1,), (1,))).astype(BF16)
-    middle = inputs.astype(F32) + sum_over_tensor(attention)
-    normed_two, inverse_two = normalize(middle)
-    own_two = (normed_two * gain_two).astype(BF16)
-    unit_two = lax.all_gather(own_two, TP, axis=0, tiled=True)
+    middle, unit_two = middle_and_unit(attention, inputs, gain_two)
 
     router_two = weights[:, small_at + att_count : small_at + att_count + mlp_count]
     logit_mlp = dot(unit_two, router_two, ((1,), (0,)))
@@ -433,47 +917,54 @@
     gate_low = (gate_mlp - gate_high.astype(F32)).astype(BF16)
     extended = jnp.concatenate([unit_two, pad_to(jnp.concatenate([gate_high, gate_low], 1), 128)], 1)
     rows_out = dot(pick_rows, extended, ((1,), (0,))).astype(BF16)
-    rows_ext = lax.all_to_all(rows_out.reshape(mlp_count, CAP, width + 128), "y", 0, 0, tiled=True)
+    rows_ext = rows_to_experts(rows_out.reshape(mlp_count, CAP, width + 128))
     rows_ext = rows_ext.reshape(mlp_count * CAP, width + 128)
     rows_in = rows_ext[:, :width]
     gates_ext = rows_ext[:, width : width + 2 * mlp_count].astype(F32)
     mine = (jnp.arange(2 * mlp_count) % mlp_count == lax.axis_index("y")).astype(F32)
     gates_in = jnp.sum(gates_ext * mine, 1, keepdims=True)
-    dbranch_in = (grad_in.astype(F32) * gates_in).astype(BF16)
-    up_whole = owned[:, : 2 * hidden_local]
-    down_whole = owned[:, 2 * hidden_local :]
     joined = dot(rows_in, up_whole, ((1,), (0,)))
     gate_pre = joined[:, :hidden_local]
     linear = joined[:, hidden_local:]
-    hidden = (jax.nn.silu(gate_pre) * linear).astype(BF16)
+    hidden_f32 = jax.nn.silu(gate_pre) * linear
+    hidden = hidden_f32.astype(BF16)
+    dhidden = dot(grad_in, down_whole, ((1,), (0,)))
+    dgate_in = jnp.sum(hidden_f32 * dhidden, 1, keepdims=True)
+    djoined = swiglu_back(dhidden * gates_in, gate_pre, linear)
+    grad_down_whole = dot(
+        grad_in, (hidden_f32 * gates_in).astype(BF16), ((0,), (0,))
+    ).astype(BF16)
+    djoined, grad_down_whole = lax.optimization_barrier((djoined, grad_down_whole))
+    grad_down_sum = lax.psum_scatter(grad_down_whole, ("xl", "z"), scatter_dimension=0, tiled=True)
+    dunit_part = dot(djoined, up_whole, ((1,), (1,))).astype(BF16)
+    dgate_high = dgate_in.astype(BF16)
+    dgate_low = (dgate_in - dgate_high.astype(F32)).astype(BF16)
+    dunit_ext = jnp.concatenate(
+        [dunit_part, pad_to(jnp.concatenate([dgate_high, dgate_low], 1), 128)], 1
+    )
+    dunit_back = lax.all_to_all(dunit_ext.reshape(mlp_count, CAP, width + 128), "y", 0, 0, tiled=True)
+    djoined, dunit_ext = lax.optimization_barrier((djoined, dunit_ext))
+    grad_up_whole = dot(rows_in, djoined, ((0,), (0,))).astype(BF16)
+    hidden, grad_up_whole = lax.optimization_barrier((hidden, grad_up_whole))
+    grad_up_sum = lax.psum_scatter(grad_up_whole, ("xl", "z"), scatter_dimension=0, tiled=True)
     branch_part = dot(hidden, down_whole, ((1,), (1,))).astype(BF16)
-    dhidden = dot(dbranch_in, down_whole, ((1,), (0,)))
-    djoined = swiglu_back(dhidden, gate_pre, linear)
-    dunit_part = dot(djoined, up_whole, ((1,), (1,))).astype(BF16)
+    dunit_back, branch_part = lax.optimization_barrier((dunit_back, branch_part))
     branch_back = lax.all_to_all(
         branch_part.reshape(mlp_count, CAP, width), "y", 0, 0, tiled=True
     ).reshape(mlp_count * CAP, width)
-    dunit_back = lax.all_to_all(
-        dunit_part.reshape(mlp_count, CAP, width), "y", 0, 0, tiled=True
-    ).reshape(mlp_count * CAP, width)
-    grad_up_whole = dot(rows_in, djoined, ((0,), (0,))).astype(BF16)
-    grad_down_whole = dot(dbranch_in, hidden, ((0,), (0,))).astype(BF16)
-    grad_pieces = lax.all_to_all(
-        jnp.concatenate([grad_up_whole, grad_down_whole], 1), DP, 0, 0, tiled=True
-    )
-
-    gate_slots = jnp.sum(pick.astype(F32) * gate_mlp.T[:, None, :], -1).reshape(mlp_count * CAP, 1)
-    branch_f32 = branch_back.astype(F32)
-    feed = dot(pick_rows, (branch_f32 * gate_slots).astype(BF16), ((0,), (0,))).astype(BF16)
-    dgate_slots = jnp.sum(grad_rows.astype(F32) * branch_f32, -1).reshape(mlp_count, CAP, 1)
+    dunit_back = dunit_back.reshape(mlp_count * CAP, width + 128)
+    dgate_slots = (
+        dunit_back[:, width : width + 1].astype(F32) + dunit_back[:, width + 1 : width + 2].astype(F32)
+    ).reshape(mlp_count, CAP, 1)
     dgate_two = jnp.sum(pick.astype(F32) * dgate_slots, 1).T
     dlogit_mlp = router_back(dgate_two, weights_mlp, onehot_mlp)
-    dunit_two = dot(pick_rows, dunit_back, ((0,), (0,))) + dot(dlogit_mlp, router_two, ((1,), (1,)))
-    dunit_own = sum_over_tensor(dunit_two.astype(BF16))
+    dunit_two = dot(pick_rows, dunit_back[:, :width], ((0,), (0,))) + dot(
+        dlogit_mlp, router_two, ((1,), (1,))
+    )
     grad_rmlp = dot(unit_two, dlogit_mlp, ((0,), (0,)))
-    grad_gain_two = jnp.sum(dunit_own * normed_two, 0)
-    dmiddle = out_grad.astype(F32) + norm_back(dunit_own, normed_two, inverse_two, gain_two)
-    dattention = lax.all_gather(dmiddle.astype(BF16), TP, axis=0, tiled=True)
+    dmiddle, grad_gain_two, dattention = middle_back(
+        dunit_two.astype(BF16), middle, out_grad, gain_two
+    )
 
     raw = dot(dattention, out_weights, ((1,), (0,)))
     grad_qkv, dgate_one = attention_back(
@@ -492,26 +983,16 @@
         ],
         1,
     )
-    grad_att = jnp.concatenate(
-        [
-            dot(unit_one, grad_qkv, ((0,), (0,))).astype(BF16),
-            pad_to(grad_small, 128).astype(BF16),
-            dot(dattention, gmixed, ((0,), (0,))).astype(BF16),
-        ],
-        1,
-    )
-    att_pieces = lax.all_to_all(grad_att.reshape(32, share, grad_att.shape[1]), DP, 0, 0, tiled=True)
-    dunit_first = sum_over_tensor(dunit_one.astype(BF16))
-    my_start = (lax.axis_index("xh") * 2 + lax.axis_index("core")) * inputs.shape[0]
-    own_rows = lambda array: lax.dynamic_slice_in_dim(array, my_start, inputs.shape[0], 0)
-    grad_input = dmiddle + norm_back(
-        dunit_first, own_rows(normed_one), own_rows(inverse_one), gain_one
-    )
-
-    summed_mlp = jnp.sum(grad_pieces.reshape(mlp_count, 8, share, 3 * hidden_local).astype(F32), 1)
-    grads_up = summed_mlp[:, :, : 2 * hidden_local].reshape(mlp_count, share, 2, hidden_local)
-    grads_down = jnp.swapaxes(summed_mlp[:, :, 2 * hidden_local :], 1, 2)
-    summed_att = jnp.sum(att_pieces.astype(F32), 0)
+    gate_slots = jnp.sum(pick.astype(F32) * gate_mlp.T[:, None, :], -1).reshape(mlp_count * CAP, 1)
+    feed = dot(pick_rows, (branch_back.astype(F32) * gate_slots).astype(BF16), ((0,), (0,)))
+    summed_att = scatter_dp(
+        dot(unit_one, grad_qkv, ((0,), (0,))).astype(BF16),
+        pad_to(grad_small, 128).astype(BF16),
+        dot(dattention, gmixed, ((0,), (0,))).astype(BF16),
+    )
+    grad_up_sum, grad_down_sum, summed_att = lax.optimization_barrier(
+        (grad_up_sum, grad_down_sum, summed_att)
+    )
     grad_kv = summed_att[:, : 2 * inner].reshape(share, 2, inner)
     grad_query = jnp.swapaxes(
         summed_att[:, 2 * inner : qkv_cols].reshape(share, att_count, inner), 0, 1
@@ -519,10 +1000,27 @@
     grad_output = jnp.transpose(
         summed_att[:, out_at:].reshape(share, att_count, inner), (1, 2, 0)
     )
-    small_sum = lax.psum(summed_att[:, small_at:out_at], TP)
-
-    feed_rows = sum_over_tensor(feed)
-    output = (middle + feed_rows).astype(BF16)
+    output, grad_input, small_sum = last_sums(
+        dunit_one.astype(BF16),
+        feed.astype(BF16),
+        inputs,
+        middle,
+        dmiddle,
+        gain_one,
+        summed_att[:, small_at:out_at],
+    )
+    output = order_back(output)
+    grad_input = order_back(grad_input)
+
+    summed_mlp = lax.all_to_all(
+        jnp.concatenate([grad_up_sum, grad_down_sum], 1).reshape(mlp_count, share, 3 * hidden_local),
+        "y",
+        0,
+        0,
+        tiled=True,
+    ).astype(F32)
+    grads_up = summed_mlp[:, :, : 2 * hidden_local].reshape(mlp_count, share, 2, hidden_local)
+    grads_down = jnp.swapaxes(summed_mlp[:, :, 2 * hidden_local :], 1, 2)
     return (
         output,
         grad_input,

time: 1720 us -> 837 us (0.49)
  waiting for transfers between devices: 1090 us -> 50.9 us
  Pallas kernels: 144 us -> 461 us
  blocking collectives: 86.7 us -> 0 us
  other arithmetic: 74.6 us -> 33.9 us
  starting transfers between devices: 52.2 us -> 21.7 us
    all_to_all x7 -> x2, waiting for transfers between devices: 1010 us -> 47.8 us  [the longest x1 47.8 us: on_device(): lax.all_to_all(dunit_ext.reshape(mlp_count, CAP, width + 128), 'y', 0, 0,...]
    pallas_call x1 -> x6, Pallas kernels: 107 us -> 424 us  [the longest x1 131 us: gather_dp(): pl.pallas_call(gather_body, out_shape=[jax.ShapeDtypeStruct((2, 4, 4, row...]
    all_to_all x2 -> x0, blocking collectives: 70.8 us -> none  [sum_over_tensor(): lax.all_to_all(partial.reshape(4, rows // 4, width), TP, 0, 0, tiled=True)]
    all_to_all x1, waiting for transfers between devices: 36.7 us -> 0.01 us  [on_device(): lax.all_to_all(branch_part.reshape(mlp_count, CAP, width), 'y', 0, 0, til...]
    all_to_all x1, waiting for transfers between devices: 36 us -> 0.01 us  [on_device(): lax.all_to_all(grad_rows.reshape(mlp_count, CAP, width), 'y', 0, 0, tiled...]
    all_to_all x7 -> x2, starting transfers between devices: 41.6 us -> 10.5 us  [the longest x1 5.3 us: on_device(): lax.all_to_all(jnp.concatenate([grad_up_sum, grad_down_sum], 1).reshape(m...]
    reduce_sum x10 -> x2, other arithmetic: 29.4 us -> 6.79 us  [the longest x1 5.8 us: on_device(): dgate_in = jnp.sum(hidden_f32 * dhidden, 1, keepdims=True)]
  transfers between devices with their start and end apart: 13 -> 10, of which waited for: 9 -> 2; matrix products, arithmetic and copies ran while one was open for 13% -> 26% of each run, Pallas kernels for 8% -> 56%
where the time goes in v2:
time: 837 us; the launch traced here: 830 us
  Pallas kernels  461 us (55%)
  matrix products  198 us (24%)
  waiting for transfers between devices  50.9 us (6%)
  local copies, waits for them, and re-layouts  47.5 us (6%)
  other arithmetic  33.9 us (4%)
  starting transfers between devices  21.7 us (3%)
  between operations  16.8 us (2%)
    dot_general x21, matrix products, dot(): return lax.dot_general(a, b, (dims, ((), ())), preferred_element_type=F32)  198 us
    pallas_call x1, Pallas kernels, gather_dp(): pl.pallas_call(gather_body, out_shape=[jax.ShapeDtypeStruct((2, 4, 4, row...  131 us
    pallas_call x1, Pallas kernels, scatter_dp(): pl.pallas_call(scatter_body, out_shape=jax.ShapeDtypeStruct((share, cols)...  108 us
    pallas_call x1, Pallas kernels, middle_and_unit(): pl.pallas_call(middle_body, out_shape=[jax.ShapeDtypeStruct((rows, width)...  53.7 us
    pallas_call x1, Pallas kernels, middle_back(): pl.pallas_call(back_body, out_shape=[jax.ShapeDtypeStruct((rows, width),...  53.6 us
    all_to_all x1, waiting for transfers between devices, on_device(): lax.all_to_all(dunit_ext.reshape(mlp_count, CAP, width + 128), 'y', 0, 0,...  47.8 us
    pallas_call x1, Pallas kernels, rows_to_experts(): pl.pallas_call(rows_body, out_shape=jax.ShapeDtypeStruct(rows.shape, rows...  46.5 us
    pallas_call x1, Pallas kernels, last_sums(): pl.pallas_call(last_body, out_shape=[jax.ShapeDtypeStruct((rows, width),...  30.9 us
  transfers between devices with their start and end apart: 10, of which 2 were waited for; matrix products, arithmetic and copies ran while one was open for 26% of the time, Pallas kernels for 56%

profile of v2, /device:TPU:1, one launch (start us, length us, event | category | flops | bytes accessed | tf_op | source)
XLA Modules:
  0.0 829.9 jit_solution(14318204185350829917)
XLA Ops:
  7.3 1.5 copy.151
  14.2 2.6 pad_maximum_fusion.1.experts_ref
  16.9 130.6 %gather_weights.1 = (bf16[2,4,4,64,4224]{4,3,2,1,0:T(8,128)(2,1)}, bf16[4,64,4224]{2,1,0:T(8,128)(2,1)}) custom-call(bf16[64,4224]{1,0:T(8,128)(2,1)} %fusion.48.x_ref, bf16[4,64,4224]{2,1,0:T(8,128)(2,1)} %pad_maximum_fusion.1.experts_ref), custom_call_target="tpu_custom_call" | custom-call | tf_op jit(solution)/shard_map/gather_weights/pallas_call | solution.py:166
  147.5 2.6 slice.119
  150.1 2.0 slice.113
  159.9 6.2 convolution_convert_fusion.6
  166.1 5.2 all-to-all-start
  171.6 2.1 fusion.23
  174.3 10.0 %fusion.3.k_ref.v_ref.q0.q1.q2 = f32[512,2688]{1,0:T(8,128)S(1)} fusion(bf16[2048,4224]{1,0:T(8,128)(2,1)} %bitcast.137, bf16[512,2048]{1,0:T(8,128)(2,1)} %all-gather.5.cloned.1.call-done, f32[2048]{0:T(1024)S(1)} %bitcast.146, f32[512]{0:T(512)S(1)} %add_rsqrt_fusion), kind=kOutput, calls=%fused_computation.8 | convolution fusion | flops 5641338880 | bytes 18622464 | tf_op jit(solution)/shard_map/dot_general | solution.py:644
  184.3 2.4 copy-done.23
  191.3 23.8 %attention_forward.1 = (bf16[512,512]{1,0:T(8,128)(2,1)S(1)}, bf16[512,512]{1,0:T(8,128)(2,1)S(1)}, bf16[512,1536]{1,0:T(8,128)(2,1)S(1)}, bf16[512,1536]{1,0:T(...) custom-call(f32[512,2688]{1,0:T(8,128)} %copy-done.23, f32[512,2688]{1,0:T(8,128)} %copy-done.23, ...), custom_call_target="tpu_custom_call" | custom-call | tf_op jit(solution)/shard_map/attention_forward/pallas_call | solution.py:693
  215.1 7.1 fusion.25
  222.3 53.7 %middle_and_unit.1 = (f32[128,2048]{1,0:T(8,128)S(1)}, bf16[4,128,2048]{2,1,0:T(8,128)(2,1)S(1)}) custom-call(bf16[4,128,2048]{2,1,0:T(8,128)(2,1)S(1)} %bitcast.97, bf16[128,2048]{1,0:T(8,128)(2,1)S(1)} %copy-done.2, f32[1,2048]{1,0:T(1,128)S(1)} %get-tuple-element.143.gain_ref), custom_call_target="tpu_custom_call" | custom-call | tf_op jit(solution)/shard_map/middle_and_unit/pallas_call | solution.py:317
  277.3 1.9 fusion.50
  281.4 7.5 convolution_convert_fusion.2
  288.9 46.5 %rows_to_experts.1 = bf16[4,320,2176]{2,1,0:T(8,128)(2,1)} custom-call(bf16[4,320,2176]{2,1,0:T(8,128)(2,1)} %bitcast.113), custom_call_target="tpu_custom_call" | custom-call | tf_op jit(solution)/shard_map/rows_to_experts/pallas_call | solution.py:461
  336.7 22.2 %fusion.18 = f32[1280,2816]{1,0:T(8,128)} fusion(bf16[2048,2816]{1,0:T(8,128)(2,1)} %all-gather.11.cloned.1.call-done, bf16[1280,2176]{1,0:T(8,128)(2,1)} %bitcast.111), kind=kOutput, calls=%fused_computation.38 | convolution fusion | flops 14763950080 | bytes 31195136 | tf_op jit(solution)/shard_map/dot_general | solution.py:644
  358.9 2.9 all-gather.9.cloned.1.call-done
  361.8 22.5 %multiply_convert_fusion.3 = (bf16[1280,1408]{1,0:T(8,128)(2,1)}, bf16[1280,1408]{1,0:T(8,128)(2,1)}, bf16[1280,1408]{1,0:T(8,128)(2,1)}, f32[1280,1408]{1,0:T(8,128)}, f32[1280,1408]{1,0:T(8,128)}) fusion(f32[1280,2816]{1,0:T(8,128)} %fusion.18, f32[1280]{0:T(1024)S(1)} %multiply_reduce_fusion.1, bf16[1280,2048]{1,0:T(8,128)(2,1)} %bitcast.18, ...), kind=kOutput, calls=%fused_computation.20 | convolution fusion | flops 7412613120 | bytes 50664448 | tf_op jit(solution)/shard_map/dot_general | solution.py:644
  384.3 14.2 %convolution_convert_fusion.5 = bf16[2048,1408]{1,0:T(8,128)(2,1)} fusion(bf16[1280,2048]{1,0:T(8,128)(2,1)} %bitcast.18, f32[1280,1408]{1,0:T(8,128)} %get-tuple-element.137, f32[1280]{0:T(1024)S(1)} %multiply_reduce_fusion.1), kind=kOutput, calls=%fused_computation.12 | convolution fusion | flops 7388463104 | bytes 18224128 | tf_op jit(solution)/shard_map/dot_general | solution.py:644
  398.5 6.6 pad_maximum_fusion
  405.2 5.8 multiply_reduce_fusion
  411.9 20.3 %convolution_convert_fusion.4 = bf16[1280,2048]{1,0:T(8,128)(2,1)S(1)} fusion(bf16[1280,2816]{1,0:T(8,128)(2,1)} %pad_maximum_fusion, bf16[2048,2816]{1,0:T(8,128)(2,1)} %all-gather.11.cloned.1.call-done), kind=kOutput, calls=%fused_computation.11 | convolution fusion | flops 14766571520 | bytes 23986176 | tf_op jit(solution)/shard_map/dot_general | solution.py:644
  432.3 3.0 fusion.5
  435.3 21.9 %convolution_convert_fusion.1 = bf16[2048,2816]{1,0:T(8,128)(2,1)} fusion(bf16[1280,2816]{1,0:T(8,128)(2,1)} %pad_maximum_fusion, bf16[1280,2176]{1,0:T(8,128)(2,1)} %bitcast.112), kind=kOutput, calls=%fused_computation.1 | convolution fusion | flops 14769717248 | bytes 23986176 | tf_op jit(solution)/shard_map/dot_general | solution.py:644
  457.2 5.2 all-to-all-start.1
  462.4 2.1 copy.156.grad_ref
  464.5 13.2 %convolution_convert_fusion.7 = bf16[1280,2048]{1,0:T(8,128)(2,1)} fusion(bf16[1280,1408]{1,0:T(8,128)(2,1)} %get-tuple-element.49, bf16[2048,1408]{1,0:T(8,128)(2,1)} %all-gather.9.cloned.1.call-done), kind=kOutput, calls=%fused_computation.14 | convolution fusion | flops 7384596480 | bytes 14614528 | tf_op jit(solution)/shard_map/dot_general | solution.py:644
  477.7 47.8 %all-to-all-done.1 = bf16[4,320,2176]{2,1,0:T(8,128)(2,1)} async-done(((bf16[4,320,2176]{2,1,0:T(8,128)(2,1)}), bf16[4,320,2176]{2,1,0:T(8,128)(2,1)}, u32[]{:S(2)}, u32[]{:S(2)}) %all-to-all-start.1) | async-done | bytes 5570592 | tf_op jit(solution)/shard_map/all_to_all | solution.py:945
  525.5 1.5 add_reduce_fusion
  527.1 5.6 all-to-all-start.2
  533.9 5.1 fusion.12
  539.0 2.1 add_convert_fusion
  541.1 53.6 %middle_back.1 = (f32[128,2048]{1,0:T(8,128)S(1)}, f32[1,2048]{1,0:T(1,128)S(1)}, bf16[4,128,2048]{2,1,0:T(8,128)(2,1)S(1)}) custom-call(bf16[4,128,2048]{2,1,0:T(8,128)(2,1)S(1)} %bitcast.93, f32[128,2048]{1,0:T(8,128)S(1)} %copy-done.5, bf16[128,2048]{1,0:T(8,128)(2,1)S(1)} %copy-done.11, f32[1,2048]{1,0:T(1,128)S(1)} %get-tuple-element.143.gain_ref), custom_call_target="tpu_custom_call" | custom-call | tf_op jit(solution)/shard_map/middle_back/pallas_call | solution.py:363
  594.8 9.0 %fusion.6.h0.h1.h2 = f32[512,1536]{1,0:T(8,128)} fusion(bf16[512,2048]{1,0:T(8,128)(2,1)S(1)} %bitcast.104, bf16[2048,4224]{1,0:T(8,128)(2,1)} %bitcast.141), kind=kOutput, calls=%fused_computation.23 | convolution fusion | flops 3221225472 | bytes 11534336 | tf_op jit(solution)/shard_map/dot_general | solution.py:644
  603.9 13.8 %attention_back.1 = (bf16[512,2560]{1,0:T(8,128)(2,1)}, f32[512,128]{1,0:T(8,128)S(1)}) custom-call(bf16[512,512]{1,0:T(8,128)(2,1)S(1)} %copy-done.16, bf16[512,512]{1,0:T(8,128)(2,1)S(1)} %copy-done.18, bf16[512,1536]{1,0:T(8,128)(2,1)S(1)} %get-tuple-element.42.q0.q1.q2, bf16[512,1536]{1,0:T(8,128)(2,1)S(1)} %get-tuple-element.42.q0.q1.q2, ...), custom_call_target="tpu_custom_call" | custom-call | tf_op jit(solution)/shard_map/attention_back/pallas_call | solution.py:764
  619.8 10.4 %fusion.22 = (bf16[2048]{0:T(1024)(128)(2,1)S(1)}, bf16[512,2048]{1,0:T(8,128)(2,1)S(1)}) fusion(bf16[512,2048]{1,0:T(8,128)(2,1)} %all-gather.5.cloned.1.call-done, f32[512]{0:T(512)S(1)} %copy-done.57, bf16[2048,4224]{1,0:T(8,128)(2,1)} %bitcast.142, bf16[512,3]{1,0:T(8,128)(2,1)S(1)} %copy.159, bf16[512,2560]{1,0:T(8,128)(2,1)} %get-tuple-element.54), kind=kOutput, calls=%fused_computation.43 | convolution fusion | flops 5650642944 | bytes 17835008 | tf_op jit(solution)/shard_map/dot_general | solution.py:644
  632.6 8.3 convolution_convert_fusion.3
  640.9 8.5 %convolution_convert_fusion = bf16[2048,2560]{1,0:T(8,128)(2,1)} fusion(bf16[512,2560]{1,0:T(8,128)(2,1)S(1)} %copy-done.62, bf16[512,2048]{1,0:T(8,128)(2,1)S(1)} %copy-done.27, f32[2048]{0:T(1024)S(1)} %bitcast.148, f32[512]{0:T(512)S(1)} %copy-done.57), kind=kOutput, calls=%fused_computation | convolution fusion | flops 5378146304 | bytes 15214592 | tf_op jit(solution)/shard_map/dot_general | solution.py:644
  649.4 108.2 %scatter_grads.1 = f32[64,4224]{1,0:T(8,128)} custom-call(bf16[2,4,4,64,2560]{4,3,2,1,0:T(8,128)(2,1)} %bitcast.107, bf16[2,4,4,64,128]{4,3,2,1,0:T(8,128)(2,1)} %bitcast.124, bf16[2,4,4,64,1536]{4,3,2,1,0:T(8,128)(2,1)} %bitcast.109), custom_call_target="tpu_custom_call" | custom-call | tf_op jit(solution)/shard_map/scatter_grads/pallas_call | solution.py:612
  757.7 3.1 pad_maximum_fusion.2
  760.7 5.3 all-to-all-start.3
  766.1 6.0 bitcast_convert_fusion
  772.2 30.9 %last_sums.1 = (bf16[128,2048]{1,0:T(8,128)(2,1)S(1)}, f32[128,2048]{1,0:T(8,128)S(1)}, f32[64,128]{1,0:T(8,128)S(1)}) custom-call(bf16[4,128,2048]{2,1,0:T(8,128)(2,1)S(1)} %bitcast.98, bf16[4,128,2048]{2,1,0:T(8,128)(2,1)S(1)} %bitcast.99, bf16[128,2048]{1,0:T(8,128)(2,1)S(1)} %copy-done.3, f32[128,2048]{1,0:T(8,128)S(1)} %copy-done.6, ...), custom_call_target="tpu_custom_call" | custom-call | tf_op jit(solution)/shard_map/last_sums/pallas_call | solution.py:412
  806.2 2.0 copy.166
  815.4 1.6 slice.125
  817.0 2.8 reshape.404
  819.8 1.9 convert_element_type.208
  (233 shorter events, 40.0 us)
Async XLA Ops:
  7.3 152.6 %all-gather.7.cloned.1.call-start = ((), (), s32[]{:S(2)}) async-start(), calls=%async_computation.7 | async-start | bytes 2621440 | tf_op jit(solution)/shard_map/all_gather | solution.py:875
  9.6 162.0 %all-gather.5.cloned.1.call-start = ((), (), s32[]{:S(2)}) async-start(), calls=%async_computation.6 | async-start | bytes 2621440 | tf_op jit(solution)/shard_map/all_gather | solution.py:874
  12.1 324.6 %all-gather.11.cloned.1.call-start = ((), (), s32[]{:S(2)}) async-start(), calls=%async_computation.9 | async-start | bytes 12976128 | tf_op jit(solution)/shard_map/all_gather | solution.py:878
  16.9 135.3 %copy-start.21 = (s32[512]{0:T(512)S(1)}, s32[512]{0:T(512)}, u32[]{:S(2)}) copy-start(s32[512]{0:T(512)} %param.15) | copy-start | bytes 6148
  16.9 136.0 %copy-start.38 = (s32[512,2]{0,1:T(2,128)S(1)}, s32[512,2]{0,1:T(2,128)}, u32[]{:S(2)}) copy-start(s32[512,2]{0,1:T(2,128)} %param.17) | copy-start | bytes 12292
  150.1 211.7 %all-gather.9.cloned.1.call-start = ((), (), s32[]{:S(2)}) async-start(), calls=%async_computation.8 | async-start | bytes 6488064 | tf_op jit(solution)/shard_map/all_gather | solution.py:879
  154.4 19.3 %copy-start.54 = (f32[2048,1]{0,1:T(1,128)}, f32[2048,1]{0,1:T(1,128)S(1)}, u32[]{:S(2)}) copy-start(f32[2048,1]{0,1:T(1,128)S(1)} %slice.110) | copy-start | bytes 24580
  157.2 8.9 %copy-start.30 = (pred[1280,512]{1,0:T(32,128)(4,1)}, pred[1280,512]{1,0:T(32,128)(4,1)S(1)}, u32[]{:S(2)}) copy-start(pred[1280,512]{1,0:T(32,128)(4,1)S(1)} %bitcast_compare_fusion) | copy-start | bytes 1966084
  166.1 192.8 %all-to-all-start = ((bf16[4,320,2048]{2,1,0:T(8,128)(2,1)}), bf16[4,320,2048]{2,1,0:T(8,128)(2,1)}, u32[]{:S(2)}, u32[]{:S(2)}) async-start(bf16[4,320,2048]{2,1,0:T(8,128)(2,1)} %bitcast.115), calls=%async_computation | async-start | bytes 10485760 | tf_op jit(solution)/shard_map/all_to_all | solution.py:890
  171.3 586.3 %reduce-scatter.5.cloned.1.call-start = ((), (), s32[]{:S(2)}) async-start(), calls=%async_computation.11 | async-start | bytes 6488064 | tf_op jit(solution)/shard_map/reduce_scatter | solution.py:938
  174.3 12.5 %copy-start.42 = (s32[512,2]{0,1:T(2,128)S(1)}, s32[512,2]{0,1:T(2,128)}, u32[]{:S(2)}) copy-start(s32[512,2]{0,1:T(2,128)} %param.16) | copy-start | bytes 12292
  215.1 7.2 copy-start.15
  215.1 7.2 copy-start.17
  215.1 7.2 copy-start.2
  279.3 9.6 %copy-start.35 = (f32[512,2]{0,1:T(2,128)}, f32[512,2]{0,1:T(2,128)S(1)}, u32[]{:S(2)}) copy-start(f32[512,2]{0,1:T(2,128)S(1)} %select_reduce_fusion.3) | copy-start | bytes 12292
  279.3 9.6 %copy-start.46 = (f32[512]{0:T(512)}, f32[512]{0:T(512)S(1)}, u32[]{:S(2)}) copy-start(f32[512]{0:T(512)S(1)} %reduce_max.19) | copy-start | bytes 6148
  405.1 352.5 %reduce-scatter.3.cloned.1.call-start = ((), (), s32[]{:S(2)}) async-start(), calls=%async_computation.10 | async-start | bytes 12976128 | tf_op jit(solution)/shard_map/reduce_scatter | solution.py:949
  411.9 20.3 %copy-start.29 = (bf16[1280,2]{1,0:T(8,128)(2,1)S(1)}, bf16[1280,2]{1,0:T(8,128)(2,1)}, u32[]{:S(2)}) copy-start(bf16[1280,2]{1,0:T(8,128)(2,1)} %copy.155) | copy-start | bytes 15364
  457.2 68.3 %all-to-all-start.1 = ((bf16[4,320,2176]{2,1,0:T(8,128)(2,1)}), bf16[4,320,2176]{2,1,0:T(8,128)(2,1)}, u32[]{:S(2)}, u32[]{:S(2)}) async-start(bf16[4,320,2176]{2,1,0:T(8,128)(2,1)} %bitcast.106), calls=%async_computation.1 | async-start | bytes 11141120 | tf_op jit(solution)/shard_map/all_to_all | solution.py:945
  527.1 5.7 copy-start.49
  527.1 6.7 copy-start.39
  527.1 6.7 copy-start.36
  527.1 6.7 copy-start.47
  527.1 6.7 copy-start.53
  527.1 233.6 %all-to-all-start.2 = ((bf16[4,320,2048]{2,1,0:T(8,128)(2,1)}), bf16[4,320,2048]{2,1,0:T(8,128)(2,1)}, u32[]{:S(2)}, u32[]{:S(2)}) async-start(bf16[4,320,2048]{2,1,0:T(8,128)(2,1)} %bitcast.114), calls=%async_computation.2 | async-start | bytes 10485760 | tf_op jit(solution)/shard_map/all_to_all | solution.py:952
  594.7 9.1 %copy-start.13 = (f32[128,2048]{1,0:T(8,128)}, f32[128,2048]{1,0:T(8,128)S(1)}, u32[]{:S(2)}) copy-start(f32[128,2048]{1,0:T(8,128)S(1)} %get-tuple-element.57.dmiddle_ref) | copy-start | bytes 3145732
  594.7 9.1 %copy-start.22 = (bf16[4,128,2048]{2,1,0:T(8,128)(2,1)}, bf16[4,128,2048]{2,1,0:T(8,128)(2,1)S(1)}, u32[]{:S(2)}) copy-start(bf16[4,128,2048]{2,1,0:T(8,128)(2,1)S(1)} %get-tuple-element.52) | copy-start | bytes 6291460
  594.7 9.1 %copy-start.8 = (f32[512,128]{1,0:T(8,128)S(1)}, f32[512,128]{1,0:T(8,128)}, u32[]{:S(2)}) copy-start(f32[512,128]{1,0:T(8,128)} %get-tuple-element.152.sin_ref) | copy-start | bytes 786436
  594.7 9.1 %copy-start.10 = (f32[512,3]{1,0:T(8,128)S(1)}, f32[512,3]{1,0:T(8,128)}, u32[]{:S(2)}) copy-start(f32[512,3]{1,0:T(8,128)} %copy.150.gate_ref) | copy-start | bytes 18436
  594.7 9.1 %copy-start.16 = (bf16[512,512]{1,0:T(8,128)(2,1)S(1)}, bf16[512,512]{1,0:T(8,128)(2,1)}, u32[]{:S(2)}) copy-start(bf16[512,512]{1,0:T(8,128)(2,1)} %copy-done.15) | copy-start | bytes 1572868
  594.8 9.1 %copy-start.18 = (bf16[512,512]{1,0:T(8,128)(2,1)S(1)}, bf16[512,512]{1,0:T(8,128)(2,1)}, u32[]{:S(2)}) copy-start(bf16[512,512]{1,0:T(8,128)(2,1)} %copy-done.17) | copy-start | bytes 1572868
  603.8 15.6 %copy-start.43 = (s32[512,2]{0,1:T(2,128)S(1)}, s32[512,2]{0,1:T(2,128)}, u32[]{:S(2)}) copy-start(s32[512,2]{0,1:T(2,128)} %param.16) | copy-start | bytes 12292
  603.8 15.6 %copy-start.34 = (f32[512,2]{0,1:T(2,128)S(1)}, f32[512,2]{0,1:T(2,128)}, u32[]{:S(2)}) copy-start(f32[512,2]{0,1:T(2,128)} %copy-done.33) | copy-start | bytes 12292
  603.8 15.6 %copy-start.45 = (f32[512]{0:T(512)S(1)}, f32[512]{0:T(512)}, u32[]{:S(2)}) copy-start(f32[512]{0:T(512)} %copy-done.44) | copy-start | bytes 6148
  603.9 15.6 %copy-start.51 = (f32[512]{0:T(512)S(1)}, f32[512]{0:T(512)}, u32[]{:S(2)}) copy-start(f32[512]{0:T(512)} %copy-done.50) | copy-start | bytes 6148
  603.9 15.9 %copy-start.57 = (f32[512]{0:T(512)S(1)}, f32[512]{0:T(512)}, u32[]{:S(2)}) copy-start(f32[512]{0:T(512)} %copy-done.56) | copy-start | bytes 6148
  619.8 10.5 %copy-start.1 = (bf16[4,128,2048]{2,1,0:T(8,128)(2,1)S(1)}, bf16[4,128,2048]{2,1,0:T(8,128)(2,1)}, u32[]{:S(2)}) copy-start(bf16[4,128,2048]{2,1,0:T(8,128)(2,1)} %copy-done) | copy-start | bytes 6291460
  619.8 10.9 %copy-start.26 = (bf16[512,2048]{1,0:T(8,128)(2,1)S(1)}, bf16[512,2048]{1,0:T(8,128)(2,1)}, u32[]{:S(2)}) copy-start(bf16[512,2048]{1,0:T(8,128)(2,1)} %all-gather.5.cloned.1.call-done) | copy-start | bytes 6291460
  619.8 10.9 %copy-start.55 = (f32[2048,1]{0,1:T(1,128)S(1)}, f32[2048,1]{0,1:T(1,128)}, u32[]{:S(2)}) copy-start(f32[2048,1]{0,1:T(1,128)} %copy-done.54) | copy-start | bytes 24580
  632.6 8.3 copy-start.27
  632.6 8.3 copy-start.62
  760.7 54.6 %all-to-all-start.3 = ((bf16[4,64,4224]{2,1,0:T(8,128)(2,1)}), bf16[4,64,4224]{2,1,0:T(8,128)(2,1)}, u32[]{:S(2)}, u32[]{:S(2)}) async-start(bf16[4,64,4224]{2,1,0:T(8,128)(2,1)} %bitcast.108), calls=%async_computation.5 | async-start | bytes 4325376 | tf_op jit(solution)/shard_map/all_to_all | solution.py:1015
  766.0 6.1 copy-start.24
  766.1 6.1 copy-start.3
  766.1 6.1 copy-start.6
  766.1 6.1 copy-start.14
  772.2 37.4 %slice-start = ((f32[64,4224]{1,0:T(8,128)}), f32[64,1024]{1,0:T(8,128)S(1)}, s32[]{:S(2)}) async-start(f32[64,4224]{1,0:T(8,128)} %scatter_grads.1), calls=%async_computation.12 | async-start | bytes 524288 | tf_op jit(solution)/shard_map/slice | solution.py:996
  803.9 6.6 copy-start.25
  (26 other events, 71.3 us)
Sparse Core Ops, SparseCore 0:
  9.8 40.5 all-gather.6
  52.6 24.5 all-gather.4
  150.2 143.5 all-gather.10
  295.8 65.9 all-gather.8
  405.2 66.8 reduce-scatter.4
  474.4 143.7 reduce-scatter.2

commit v3 on v2

--- a/solution.py
+++ b/solution.py
@@ -9,6 +9,7 @@
 from jax.sharding import Mesh, PartitionSpec as P
 
 HD = 128
+HEADS = 2
 CAP = 320
 EPSILON = 1e-06
 NEGATIVE = -1e30
@@ -31,6 +32,11 @@
     return {axis: lax.rem(lax.axis_index(axis) + step + size, size)}
 
 
+def chip_along(step):
+    at = lax.rem(lax.axis_index("xh") * 2 + lax.axis_index("xl") + step + 4, 4)
+    return {"xh": lax.div(at, 2), "xl": lax.rem(at, 2)}
+
+
 def greet(*devices):
     barrier = pltpu.get_barrier_semaphore()
     for device in devices:
@@ -64,11 +70,11 @@
 
 
 def gather_body(
-    x_ref, experts_ref, out_ref, expert_ref,
-    loc, xs, xr, s1, r1m, r1p, f1s, f1r, s2, r2m, r2p, f2s, f2r, es, er,
+    x_ref, ups_ref, downs_ref, out_ref, up_ref, down_ref,
+    loc, xs, xr, s1, r1m, r1p, f1s, f1r, s2, r2m, r2p, f2s, f2r, es, er, ex, ey,
 ):
     y, xl, z = lax.axis_index("y"), lax.axis_index("xl"), lax.axis_index("z")
-    half = x_ref.shape[0] // 2
+    half = x_ref.shape[1] // 2
     quarter = half // 2
     greet(
         neighbour("xl", 1),
@@ -84,17 +90,29 @@
 
     def slot(h, first, second, j, start, count):
         yy, zz = (second, first) if h == 0 else (first, second)
-        return out_ref.at[j, zz, yy, pl.ds(start, count)]
-
-    own = pltpu.make_async_copy(x_ref, out_ref.at[xl, z, y], loc.at[0])
+        return out_ref.at[zz, j, yy, pl.ds(start, count)]
+
+    own = pltpu.make_async_copy(x_ref.at[xl], out_ref.at[z, xl, y], loc.at[0])
     own.start()
-    expert = pltpu.make_async_copy(experts_ref.at[y], expert_ref.at[y], loc.at[1])
-    expert.start()
+    experts = ((ups_ref, up_ref), (downs_ref, down_ref))
+    kept = []
+    for n, (shards, expert) in enumerate(experts):
+        kept.append(pltpu.make_async_copy(shards.at[y], expert.at[xl, y], loc.at[1 + n]))
+        kept[-1].start()
+        send(shards.at[y], expert.at[xl, y], ex.at[n, 0], ey.at[n, 0], neighbour("xl", 1))
+        for step in (1, 3, 2):
+            send(
+                shards.at[mod4(y + step)],
+                expert.at[xl, y],
+                es.at[n, step - 1],
+                er.at[n, step - 1],
+                neighbour("y", step),
+            )
     for h in (0, 1):
         first, second = place[rings[h][0]], place[rings[h][1]]
-        src = x_ref.at[pl.ds(h * half, half)]
+        src = x_ref.at[xl, pl.ds(h * half, half)]
         dst = slot(h, first, second, xl, h * half, half)
-        send(src, dst, xs.at[h], xr.at[h], neighbour("xl", 1))
+        send(x_ref.at[other, pl.ds(h * half, half)], dst, xs.at[h], xr.at[h], neighbour("xl", 1))
         send(src, dst, s1.at[h, 0, 0], r1m.at[h, 0], neighbour(rings[h][0], 1))
         send(src, dst, s1.at[h, 0, 1], r1p.at[h, 0], neighbour(rings[h][0], -1))
     own.wait()
@@ -123,6 +141,11 @@
     for k, step in ((1, -1), (2, 1)):
         for h in (0, 1):
             send_second(h, k, mod4(place[rings[h][0]] + step))
+    for n, (shards, expert) in enumerate(experts):
+        for step in (1, 3, 2):
+            landed = expert.at[xl, mod4(y - step)]
+            arrived(landed, er.at[n, step - 1])
+            send(landed, landed, ex.at[n, step], ey.at[n, step], neighbour("xl", 1))
     for h in (0, 1):
         first, second = place[rings[h][0]], place[rings[h][1]]
         for j, jx in ((0, xl), (1, other)):
@@ -130,14 +153,6 @@
                 block = slot(h, mod4(first + 2), second, jx, h * half + p * quarter, quarter)
                 arrived(block, f1r.at[h, j, p])
         send_second(h, 3, mod4(first + 2))
-    for step in (1, 3, 2):
-        send(
-            experts_ref.at[mod4(y + step)],
-            expert_ref.at[y],
-            es.at[step - 1],
-            er.at[step - 1],
-            neighbour("y", step),
-        )
     steps = ((0, 0), (1, -1), (2, 1), (3, 2))
     for k, step in steps:
         for h in (0, 1):
@@ -154,25 +169,27 @@
             for p in (0, 1):
                 block = slot(h, first, mod4(second + 2), both, h * half + p * quarter, quarter)
                 arrived(block, f2r.at[h, k, p])
-    for step in (1, 3, 2):
-        arrived(expert_ref.at[mod4(y - step)], er.at[step - 1])
-    expert.wait()
+    for n, (shards, expert) in enumerate(experts):
+        for step in (0, 1, 3, 2):
+            arrived(expert.at[other, mod4(y - step)], ey.at[n, step])
+        kept[n].wait()
     sends.finish()
 
 
-def gather_dp(shard, experts):
-    rows, cols = shard.shape
+def gather_dp(shard, ups, downs):
+    _, rows, cols = shard.shape
     dma = pltpu.SemaphoreType.DMA
-    whole, expert = pl.pallas_call(
+    whole, up, down = pl.pallas_call(
         gather_body,
         out_shape=[
-            jax.ShapeDtypeStruct((2, 4, 4, rows, cols), shard.dtype),
-            jax.ShapeDtypeStruct(experts.shape, experts.dtype),
+            jax.ShapeDtypeStruct((4, 2, 4, rows, cols), shard.dtype),
+            jax.ShapeDtypeStruct((2, *ups.shape), ups.dtype),
+            jax.ShapeDtypeStruct((2, *downs.shape), downs.dtype),
         ],
-        in_specs=[pl.BlockSpec(memory_space=pl.ANY)] * 2,
-        out_specs=[pl.BlockSpec(memory_space=pl.ANY)] * 2,
+        in_specs=[pl.BlockSpec(memory_space=pl.ANY)] * 3,
+        out_specs=[pl.BlockSpec(memory_space=pl.ANY)] * 3,
         scratch_shapes=[
-            dma((2,)),
+            dma((3,)),
             dma((2,)),
             dma((2,)),
             dma((2, 2, 2)),
@@ -185,13 +202,15 @@
             dma((2, 4)),
             dma((2, 4, 2)),
             dma((2, 4, 2)),
-            dma((3,)),
-            dma((3,)),
+            dma((2, 3)),
+            dma((2, 3)),
+            dma((2, 4)),
+            dma((2, 4)),
         ],
         compiler_params=pltpu.CompilerParams(collective_id=0, has_side_effects=True),
         name="gather_weights",
-    )(shard, experts)
-    return whole.reshape(32 * rows, cols), expert
+    )(shard, ups, downs)
+    return whole.reshape(32 * rows, cols), up, down
 
 
 def reduce_body(scatter_count, part_refs, core_buf, sum_buf, far_buf, core_s, core_r, far_s, far_r, sends):
@@ -247,6 +266,119 @@
     return total
 
 
+def ring_reduce_body(part_ref, core_buf, sum_buf, via_buf, far_buf, core_s, core_r, ring_s, ring_r, sends):
+    xl, xh, core = lax.axis_index("xl"), lax.axis_index("xh"), lax.axis_index("core")
+    rows = part_ref.shape[3]
+    half = rows // 2
+    at = xh * 2 + xl
+    chips = [lax.rem(at + step, 4) for step in (2, 1, 3, 0)]
+    chips = [(lax.rem(chip, 2), lax.div(chip, 2)) for chip in chips]
+    for n, (pxl, pxh) in enumerate(chips):
+        sends(
+            part_ref.at[pxl, pxh, 1 - core],
+            core_buf.at[n],
+            core_s.at[n],
+            core_r.at[n],
+            neighbour("core", 1),
+        )
+
+    def own(n, start):
+        pxl, pxh = chips[n]
+        return part_ref[pxl, pxh, core, start : start + half, :].astype(F32)
+
+    def both(n, start):
+        return own(n, start) + core_buf[n, start : start + half, :].astype(F32)
+
+    first, second = pl.ds(0, half), pl.ds(half, half)
+    ahead, behind = chip_along(1), chip_along(-1)
+    arrived(core_buf.at[0], core_r.at[0])
+    sum_buf[0, :half, :] = both(0, 0).astype(BF16)
+    sends(sum_buf.at[0, first], via_buf.at[0], ring_s.at[0], ring_r.at[0], ahead)
+    sum_buf[0, half:, :] = both(0, half).astype(BF16)
+    sends(sum_buf.at[0, second], via_buf.at[1], ring_s.at[1], ring_r.at[1], behind)
+    arrived(core_buf.at[1], core_r.at[1])
+    sum_buf[1, half:, :] = both(1, half).astype(BF16)
+    sends(sum_buf.at[1, second], far_buf.at[0, second], ring_s.at[2], ring_r.at[2], ahead)
+    arrived(core_buf.at[2], core_r.at[2])
+    sum_buf[2, :half, :] = both(2, 0).astype(BF16)
+    sends(sum_buf.at[2, first], far_buf.at[1, first], ring_s.at[3], ring_r.at[3], behind)
+    arrived(via_buf.at[0], ring_r.at[0])
+    sum_buf[1, :half, :] = (both(1, 0) + via_buf[0].astype(F32)).astype(BF16)
+    sends(sum_buf.at[1, first], far_buf.at[0, first], ring_s.at[4], ring_r.at[4], ahead)
+    arrived(via_buf.at[1], ring_r.at[1])
+    sum_buf[2, half:, :] = (both(2, half) + via_buf[1].astype(F32)).astype(BF16)
+    sends(sum_buf.at[2, second], far_buf.at[1, second], ring_s.at[5], ring_r.at[5], behind)
+    arrived(core_buf.at[3], core_r.at[3])
+
+    def total(part):
+        rows_at = first if part == 0 else second
+        start = part * half
+        near = both(3, start)
+        arrived(far_buf.at[0, rows_at], ring_r.at[4 if part == 0 else 2])
+        near = near + far_buf[0, start : start + half, :].astype(F32)
+        arrived(far_buf.at[1, rows_at], ring_r.at[3 if part == 0 else 5])
+        return near + far_buf[1, start : start + half, :].astype(F32)
+
+    return total
+
+
+def ring_reduce_scratch(rows, width):
+    dma = pltpu.SemaphoreType.DMA
+    return [
+        pltpu.VMEM((4, rows, width), BF16),
+        pltpu.VMEM((3, rows, width), BF16),
+        pltpu.VMEM((2, rows // 2, width), BF16),
+        pltpu.VMEM((2, rows, width), BF16),
+        dma((4,)),
+        dma((4,)),
+        dma((6,)),
+        dma((6,)),
+    ]
+
+
+def ring_spread(out_ref, part, ring_s, ring_r, core_s, core_r, sends):
+    xl, xh, core = lax.axis_index("xl"), lax.axis_index("xh"), lax.axis_index("core")
+    half = out_ref.shape[3] // 2
+    mine = out_ref.at[xl, xh, core, pl.ds(part * half, half)]
+    sends(mine, mine, ring_s.at[part, 0], ring_r.at[part, 0], chip_along(1))
+    sends(mine, mine, ring_s.at[part, 1], ring_r.at[part, 1], chip_along(-1))
+    sends(mine, mine, core_s.at[part, 0], core_r.at[part, 0], neighbour("core", 1))
+
+
+def ring_spread_finish(out_ref, ring_s, ring_r, core_s, core_r, sends):
+    xl, xh, core = lax.axis_index("xl"), lax.axis_index("xh"), lax.axis_index("core")
+    half = out_ref.shape[3] // 2
+    at = xh * 2 + xl
+
+    def block(step, part, which):
+        chip = lax.rem(at + step + 4, 4)
+        return out_ref.at[lax.rem(chip, 2), lax.div(chip, 2), which, pl.ds(part * half, half)]
+
+    for part in (0, 1):
+        for n, (step, on) in enumerate(((-1, 1), (1, -1))):
+            landed = block(step, part, core)
+            arrived(landed, ring_r.at[part, n])
+            if part == n:
+                sends(landed, landed, ring_s.at[part, 2], ring_r.at[part, 2], chip_along(on))
+            sends(landed, landed, core_s.at[part, 1 + n], core_r.at[part, 1 + n], neighbour("core", 1))
+    for part in (0, 1):
+        landed = block(2, part, core)
+        arrived(landed, ring_r.at[part, 2])
+        sends(landed, landed, core_s.at[part, 3], core_r.at[part, 3], neighbour("core", 1))
+    for part in (0, 1):
+        for n, step in enumerate((0, -1, 1, 2)):
+            arrived(block(step, part, 1 - core), core_r.at[part, n])
+
+
+def ring_spread_scratch():
+    dma = pltpu.SemaphoreType.DMA
+    return [dma((2, 3)), dma((2, 3)), dma((2, 4)), dma((2, 4))]
+
+
+def along_x():
+    return neighbour("core", 1), neighbour("xh", 1), chip_along(1), chip_along(-1)
+
+
 CHUNKS = 4
 
 
@@ -293,18 +425,20 @@
 
 def middle_body(part_ref, x_ref, gain_ref, middle_ref, unit_ref, *scratch):
     sends = Sends()
-    greet(neighbour("core", 1), neighbour("xh", 1))
-    total = reduce_body(CHUNKS, [part_ref], *scratch[:7], sends)
+    greet(*along_x())
+    total = ring_reduce_body(part_ref, *scratch[:8], sends)
     me = lax.axis_index("xh") * 2 + lax.axis_index("core")
     step = x_ref.shape[0] // CHUNKS
-    for n in range(CHUNKS):
-        rows = slice(n * step, (n + 1) * step)
-        middle = x_ref[rows, :].astype(F32) + total(0, n)
+    half = x_ref.shape[0] // 2
+    for part in (0, 1):
+        rows = slice(part * half, (part + 1) * half)
+        middle = x_ref[rows, :].astype(F32) + total(part)
         middle_ref[rows, :] = middle
         inverse = lax.rsqrt(jnp.mean(middle * middle, 1, keepdims=True) + EPSILON)
         unit_ref[me, rows, :] = (middle * inverse * gain_ref[...]).astype(BF16)
-        spread_chunk(unit_ref, n, step, scratch[7:], sends)
-    spread_finish(unit_ref, step, scratch[7:], sends)
+        for n in range(part * CHUNKS // 2, (part + 1) * CHUNKS // 2):
+            spread_chunk(unit_ref, n, step, scratch[8:], sends)
+    spread_finish(unit_ref, step, scratch[8:], sends)
     sends.finish()
 
 
@@ -322,20 +456,20 @@
         ],
         in_specs=vmem(3),
         out_specs=vmem(2),
-        scratch_shapes=reduce_scratch(1, rows, width) + spread_scratch(),
+        scratch_shapes=ring_reduce_scratch(rows, width) + spread_scratch(),
         compiler_params=pltpu.CompilerParams(
             collective_id=1, has_side_effects=True, vmem_limit_bytes=32 * MIB
         ),
         name="middle_and_unit",
-    )(part.reshape(4, rows, width), x, gain[None])
+    )(part.reshape(2, 2, 2, rows, width), x, gain[None])
     return middle, unit.reshape(4 * rows, width)
 
 
 def back_body(part_ref, middle_ref, grad_ref, gain_ref, dmiddle_ref, dgain_ref, spread_ref, *scratch):
     sends = Sends()
-    greet(neighbour("core", 1), neighbour("xh", 1))
+    greet(*along_x())
     total = reduce_body(CHUNKS, [part_ref], *scratch[:7], sends)
-    me = lax.axis_index("xh") * 2 + lax.axis_index("core")
+    xl, xh, core = lax.axis_index("xl"), lax.axis_index("xh"), lax.axis_index("core")
     step = middle_ref.shape[0] // CHUNKS
     for n in range(CHUNKS):
         rows = slice(n * step, (n + 1) * step)
@@ -352,9 +486,10 @@
         mean = jnp.mean(product * gain_ref[...], 1, keepdims=True)
         dmiddle = grad_ref[rows, :].astype(F32) + inverse * (dunit * gain_ref[...] - normed * mean)
         dmiddle_ref[rows, :] = dmiddle
-        spread_ref[me, rows, :] = dmiddle.astype(BF16)
-        spread_chunk(spread_ref, n, step, scratch[7:], sends)
-    spread_finish(spread_ref, step, scratch[7:], sends)
+        spread_ref[xl, xh, core, rows, :] = dmiddle.astype(BF16)
+        if n % 2 == 1:
+            ring_spread(spread_ref, n // 2, *scratch[7:], sends)
+    ring_spread_finish(spread_ref, *scratch[7:], sends)
     sends.finish()
 
 
@@ -365,17 +500,17 @@
         out_shape=[
             jax.ShapeDtypeStruct((rows, width), F32),
             jax.ShapeDtypeStruct((1, width), F32),
-            jax.ShapeDtypeStruct((4, rows, width), BF16),
+            jax.ShapeDtypeStruct((2, 2, 2, rows, width), BF16),
         ],
         in_specs=vmem(4),
         out_specs=vmem(3),
-        scratch_shapes=reduce_scratch(1, rows, width) + spread_scratch(),
+        scratch_shapes=reduce_scratch(1, rows, width) + ring_spread_scratch(),
         compiler_params=pltpu.CompilerParams(
             collective_id=2, has_side_effects=True, vmem_limit_bytes=32 * MIB
         ),
         name="middle_back",
     )(part.reshape(4, rows, width), middle, grad, gain[None])
-    return dmiddle, dgain[0], spread.reshape(4 * rows, width)
+    return dmiddle, dgain[0], spread.reshape(8 * rows, width)
 
 
 def last_body(
@@ -385,21 +520,25 @@
     sends = Sends()
     xh, core = lax.axis_index("xh"), lax.axis_index("core")
     peers = ({"xh": xh, "core": 1 - core}, {"xh": 1 - xh, "core": core}, {"xh": 1 - xh, "core": 1 - core})
-    greet(*peers)
-    small_buf, small_s, small_r = scratch[7:]
+    greet(*peers, chip_along(1), chip_along(-1))
+    small_buf, small_s, small_r = scratch[15:]
     for n, peer in enumerate(peers):
         sends(small_ref, small_buf.at[n], small_s.at[n], small_r.at[n], peer)
-    total = reduce_body(CHUNKS, [part_ref, feed_ref], *scratch[:7], sends)
+    total = ring_reduce_body(part_ref, *scratch[7:15], sends)
+    feed = reduce_body(CHUNKS, [feed_ref], *scratch[:7], sends)
+    half = x_ref.shape[0] // 2
+    for part in (0, 1):
+        rows = slice(part * half, (part + 1) * half)
+        x = x_ref[rows, :].astype(F32)
+        inverse = lax.rsqrt(jnp.mean(x * x, 1, keepdims=True) + EPSILON)
+        normed = x * inverse
+        dscaled = total(part) * gain_ref[...]
+        mean = jnp.mean(dscaled * normed, 1, keepdims=True)
+        dinput_ref[rows, :] = dmiddle_ref[rows, :] + inverse * (dscaled - normed * mean)
     step = x_ref.shape[0] // CHUNKS
     for n in range(CHUNKS):
         rows = slice(n * step, (n + 1) * step)
-        x = x_ref[rows, :].astype(F32)
-        inverse = lax.rsqrt(jnp.mean(x * x, 1, keepdims=True) + EPSILON)
-        normed = x * inverse
-        dscaled = total(0, n) * gain_ref[...]
-        mean = jnp.mean(dscaled * normed, 1, keepdims=True)
-        dinput_ref[rows, :] = dmiddle_ref[rows, :] + inverse * (dscaled - normed * mean)
-        output_ref[rows, :] = (middle_ref[rows, :] + total(1, n)).astype(BF16)
+        output_ref[rows, :] = (middle_ref[rows, :] + feed(0, n)).astype(BF16)
     for n in range(3):
         arrived(small_buf.at[n], small_r.at[n])
     small_out[...] = (small_ref[...] + small_buf[1]) + (small_buf[0] + small_buf[2])
@@ -418,13 +557,22 @@
         ],
         in_specs=vmem(7),
         out_specs=vmem(3),
-        scratch_shapes=reduce_scratch(2, rows, width)
+        scratch_shapes=reduce_scratch(1, rows, width)
+        + ring_reduce_scratch(rows, width)
         + [pltpu.VMEM((3, *small.shape), F32), dma((3,)), dma((3,))],
         compiler_params=pltpu.CompilerParams(
             collective_id=3, has_side_effects=True, vmem_limit_bytes=40 * MIB
         ),
         name="last_sums",
-    )(part.reshape(4, rows, width), feed.reshape(4, rows, width), x, middle, dmiddle, gain[None], small)
+    )(
+        part.reshape(2, 2, 2, rows, width),
+        feed.reshape(4, rows, width),
+        x,
+        middle,
+        dmiddle,
+        gain[None],
+        small,
+    )
 
 
 def rows_body(rows_ref, out_ref, loc, far_s, far_r, core_s, core_r):
@@ -473,8 +621,8 @@
 
 
 def scatter_body(
-    qkv_ref, small_ref, o_ref, out_ref, g_ref, loc, t_buf, r_buf, tb_buf, rb_buf, c_buf,
-    t_s, t_r, r_s, r_r, tb_s, tb_r, rb_s, rb_r, c_s, c_r,
+    qkv_ref, small_ref, o_ref, up_ref, down_ref, out_ref, up_out, down_out, g_ref, loc, t_buf, r_buf, tb_buf, rb_buf, c_buf,
+    t_s, t_r, r_s, r_r, tb_s, tb_r, rb_s, rb_r, c_s, c_r, up_buf, down_buf, up_sum, down_sum, ex, ey, es, er,
 ):
     xl = lax.axis_index("xl")
     place = {"y": lax.axis_index("y"), "z": lax.axis_index("z")}
@@ -489,18 +637,34 @@
         parts.append(pltpu.make_async_copy(ref, g_ref.at[..., pl.ds(column, cols)], loc.at[n]))
         parts[-1].start()
         column += cols
-    greet(neighbour("xl", 1), *(neighbour(axis, step) for axis in ("y", "z") for step in (1, -1)))
+    greet(
+        neighbour("xl", 1),
+        *(neighbour("y", step) for step in (1, 2, 3)),
+        *(neighbour("z", step) for step in (1, -1)),
+    )
     both = slice(0, 2)
+    experts = ((up_ref, up_buf, up_sum, up_out), (down_ref, down_buf, down_sum, down_out))
+    my_y = place["y"]
+    for n, (grads, buf, _, _) in enumerate(experts):
+        for step in (2, 1, 3, 0):
+            target = mod4(my_y + step)
+            sends(
+                grads.at[1 - xl, target],
+                buf.at[step],
+                ex.at[n, step],
+                ey.at[n, step],
+                neighbour("xl", 1),
+            )
     for part in parts:
         part.wait()
 
     def grad_ref(h, first, second, start):
         zz, yy = (first, second) if h == 0 else (second, first)
-        return g_ref.at[both, zz, yy, pl.ds(h * half + start, quarter)]
+        return g_ref.at[zz, both, yy, pl.ds(h * half + start, quarter)]
 
     def grad(h, first, second, j, start, count):
         zz, yy = (first, second) if h == 0 else (second, first)
-        return g_ref[j, zz, yy, h * half + start : h * half + start + count, :].astype(F32)
+        return g_ref[zz, j, yy, h * half + start : h * half + start + count, :].astype(F32)
 
     def firsts(h, k):
         return mod4(place[rings[h][0]] + STEPS[k])
@@ -543,6 +707,22 @@
                     r_s.at[h, d, k, 1],
                     r_r.at[h, d, k, 1],
                     neighbour(rings[h][1], way),
+                )
+    for n, (grads, buf, total, result) in enumerate(experts):
+        for step in (2, 1, 3, 0):
+            target = mod4(my_y + step)
+            arrived(buf.at[step], ey.at[n, step])
+            value = (grads[xl, target].astype(F32) + buf[step].astype(F32)).astype(BF16)
+            if step == 0:
+                result[my_y] = value
+            else:
+                total[step - 1] = value
+                sends(
+                    total.at[step - 1],
+                    result.at[my_y],
+                    es.at[n, step - 1],
+                    er.at[n, step - 1],
+                    neighbour("y", step),
                 )
     for k in range(4):
         for h in (0, 1):
@@ -598,24 +778,33 @@
                 + r_buf[h, 0, 3, j].astype(F32)
             ).astype(BF16)
         sends(rb_buf.at[h, 0, 1 - xl], c_buf.at[h], c_s.at[h], c_r.at[h], neighbour("xl", 1))
+        out_ref[xl, h * half : (h + 1) * half, :] = rb_buf[h, 0, xl].astype(F32)
     for h in (0, 1):
         arrived(c_buf.at[h], c_r.at[h])
-        out_ref[h * half : (h + 1) * half, :] = rb_buf[h, 0, xl].astype(F32) + c_buf[h].astype(F32)
+        out_ref[1 - xl, h * half : (h + 1) * half, :] = c_buf[h].astype(F32)
+    for n, (_, _, _, result) in enumerate(experts):
+        for step in (1, 3, 2):
+            arrived(result.at[mod4(my_y - step)], er.at[n, step - 1])
     sends.finish()
 
 
-def scatter_dp(*grads):
+def scatter_dp(grads, ups, downs):
     rows, cols = grads[0].shape[0], sum(grad.shape[1] for grad in grads)
     share = rows // 32
     half, quarter = share // 2, share // 4
     dma = pltpu.SemaphoreType.DMA
+    up_cols, down_cols = ups.shape[1], downs.shape[1]
     return pl.pallas_call(
         scatter_body,
-        out_shape=jax.ShapeDtypeStruct((share, cols), F32),
-        in_specs=[pl.BlockSpec(memory_space=pl.ANY)] * 3,
-        out_specs=pl.BlockSpec(memory_space=pltpu.VMEM),
+        out_shape=[
+            jax.ShapeDtypeStruct((2, share, cols), F32),
+            jax.ShapeDtypeStruct((4, share, up_cols), BF16),
+            jax.ShapeDtypeStruct((4, share, down_cols), BF16),
+        ],
+        in_specs=[pl.BlockSpec(memory_space=pl.ANY)] * 3 + vmem(2),
+        out_specs=vmem(3),
         scratch_shapes=[
-            pltpu.VMEM((2, 4, 4, share, cols), BF16),
+            pltpu.VMEM((4, 2, 4, share, cols), BF16),
             dma((3,)),
             pltpu.VMEM((2, 2, 4, 2, quarter, cols), BF16),
             pltpu.VMEM((2, 2, 4, 2, half, cols), BF16),
@@ -632,12 +821,24 @@
             dma((2, 2, 2)),
             dma((2,)),
             dma((2,)),
+            pltpu.VMEM((4, share, up_cols), BF16),
+            pltpu.VMEM((4, share, down_cols), BF16),
+            pltpu.VMEM((3, share, up_cols), BF16),
+            pltpu.VMEM((3, share, down_cols), BF16),
+            dma((2, 4)),
+            dma((2, 4)),
+            dma((2, 3)),
+            dma((2, 3)),
         ],
         compiler_params=pltpu.CompilerParams(
             collective_id=5, has_side_effects=True, vmem_limit_bytes=56 * MIB
         ),
         name="scatter_grads",
-    )(*(grad.reshape(2, 4, 4, share, grad.shape[1]) for grad in grads))
+    )(
+        *(grad.reshape(4, 2, 4, share, grad.shape[1]) for grad in grads),
+        ups.reshape(2, 4, share, up_cols),
+        downs.reshape(2, 4, share, down_cols),
+    )
 
 
 def dot(a, b, dims):
@@ -648,7 +849,7 @@
     k_ref, v_ref, q0, q1, q2, cos_ref, sin_ref, col_ref, row_ref, gate_ref,
     key_out, val_out, que_out, mix_out, gmix_out, prob_out,
 ):
-    h = pl.program_id(0)
+    h = pl.program_id(1)
     cosine, sine = cos_ref[...], sin_ref[...]
     scale = 1.0 / math.sqrt(HD)
 
@@ -660,7 +861,7 @@
     key_out[...] = key
     val_out[...] = val
     tokens = key.shape[0]
-    seg_col, seg_row = col_ref[...], row_ref[...]
+    seg_col, seg_row = col_ref[...], row_ref[0]
     at_row = lax.broadcasted_iota(jnp.int32, (tokens, tokens), 0)
     at_col = lax.broadcasted_iota(jnp.int32, (tokens, tokens), 1)
     allowed = (at_col <= at_row) & ((seg_row == 0) | (seg_row == seg_col))
@@ -670,47 +871,54 @@
         largest = jnp.max(scores, 1, keepdims=True)
         expsum = jnp.exp(scores - largest)
         prob = (expsum * (1.0 / jnp.sum(expsum, 1, keepdims=True))).astype(BF16)
-        prob_out[0, e] = prob
+        prob_out[0, 0, e] = prob
         mixed = dot(prob, val, ((1,), (0,))).astype(BF16)
-        at = pl.ds(pl.multiple_of(e * 4 * HD + h * HD, HD), HD)
+        at = pl.ds(pl.multiple_of((e * HEADS + h) * HD, HD), HD)
         que_out[:, at] = query
         mix_out[:, at] = mixed
         gmix_out[:, at] = (mixed.astype(F32) * gate_ref[:, e : e + 1]).astype(BF16)
 
 
+def block_specs(tokens):
+    def column(n):
+        return pl.BlockSpec((tokens, HD), lambda g, h: (g, n * HEADS + h))
+
+    def rows(width):
+        return pl.BlockSpec((tokens, width), lambda g, h: (g, 0))
+
+    return column, rows
+
+
+def prob_spec(tokens):
+    return pl.BlockSpec((1, 1, 3, tokens, tokens), lambda g, h: (g, h, 0, 0, 0))
+
+
 def attention_forward(joined, cosine, sine, segments, gates):
-    tokens = joined.shape[0]
-    heads = 4
-
-    def column(start):
-        return pl.BlockSpec((tokens, HD), lambda h: (0, start // HD + h))
-
-    def whole(shape):
-        return pl.BlockSpec(shape, lambda h: (0,) * len(shape))
-
-    wide = jax.ShapeDtypeStruct((tokens, 12 * HD), BF16)
-    narrow = jax.ShapeDtypeStruct((tokens, 4 * HD), BF16)
+    groups, tokens = segments.shape
+    column, rows = block_specs(tokens)
+    wide = jax.ShapeDtypeStruct((groups * tokens, 3 * HEADS * HD), BF16)
+    narrow = jax.ShapeDtypeStruct((groups * tokens, HEADS * HD), BF16)
     return pl.pallas_call(
         attention_body,
-        grid=(heads,),
-        in_specs=[column(s) for s in (0, 512, 1024, 1536, 2048)]
-        + [whole((tokens, HD))] * 2
-        + [whole((tokens, 1)), whole((1, tokens)), whole(gates.shape)],
-        out_specs=[column(0), column(0)]
-        + [whole(wide.shape)] * 3
-        + [pl.BlockSpec((1, 3, tokens, tokens), lambda h: (h, 0, 0, 0))],
+        grid=(groups, HEADS),
+        in_specs=[column(n) for n in range(5)]
+        + [rows(HD)] * 2
+        + [rows(1), pl.BlockSpec((1, 1, tokens), lambda g, h: (g, 0, 0)), rows(gates.shape[1])],
+        out_specs=[column(0), column(0)] + [rows(wide.shape[1])] * 3 + [prob_spec(tokens)],
         out_shape=[narrow, narrow, wide, wide, wide]
-        + [jax.ShapeDtypeStruct((heads, 3, tokens, tokens), BF16)],
+        + [jax.ShapeDtypeStruct((groups, HEADS, 3, tokens, tokens), BF16)],
         compiler_params=pltpu.CompilerParams(vmem_limit_bytes=48 * MIB),
         name="attention_forward",
-    )(joined, joined, joined, joined, joined, cosine, sine, segments[:, None], segments[None], gates)
+    )(
+        *[joined] * 5, cosine, sine, segments.reshape(-1, 1), segments[:, None], gates
+    )
 
 
 def attention_back_body(
     key_ref, val_ref, q0, q1, q2, m0, m1, m2, h0, h1, h2, prob_ref, cos_ref, sin_ref, gate_ref,
     grad_out, dgate_out,
 ):
-    h = pl.program_id(0)
+    h = pl.program_id(1)
     cosine, sine = cos_ref[...], sin_ref[...]
     scale = 1.0 / math.sqrt(HD)
 
@@ -729,17 +937,17 @@
         dgates = dgates + jnp.where(lane == e, inner, 0.0)
         gate = gate_ref[:, e : e + 1]
         dmixed = (raw * gate).astype(BF16)
-        prob = prob_ref[0, e]
+        prob = prob_ref[0, 0, e]
         dval = dval + dot(prob, dmixed, ((0,), (0,)))
         dprob = dot(dmixed, val, ((1,), (1,)))
         delta = jnp.sum(dmixed.astype(F32) * mixed, 1, keepdims=True)
         dscores = (prob.astype(F32) * (dprob - delta)).astype(BF16)
         dquery = dot(dscores, key, ((1,), (0,)))
         dkey = dkey + dot(dscores, query, ((0,), (0,)))
-        at = pl.ds(pl.multiple_of(1024 + e * 4 * HD + h * HD, HD), HD)
+        at = pl.ds(pl.multiple_of(((2 + e) * HEADS + h) * HD, HD), HD)
         grad_out[:, at] = rotated_back(dquery * scale).astype(BF16)
     grad_out[:, pl.ds(pl.multiple_of(h * HD, HD), HD)] = rotated_back(dkey).astype(BF16)
-    grad_out[:, pl.ds(pl.multiple_of(512 + h * HD, HD), HD)] = dval.astype(BF16)
+    grad_out[:, pl.ds(pl.multiple_of((HEADS + h) * HD, HD), HD)] = dval.astype(BF16)
 
     @pl.when(h == 0)
     def _():
@@ -751,29 +959,20 @@
 
 
 def attention_back(key, val, que, mix, raw, prob, cosine, sine, gates):
-    tokens = key.shape[0]
-    heads = 4
-
-    def column(start):
-        return pl.BlockSpec((tokens, HD), lambda h: (0, start // HD + h))
-
-    def whole(shape):
-        return pl.BlockSpec(shape, lambda h: (0,) * len(shape))
-
-    thirds = [column(s) for s in (0, 512, 1024)]
+    groups, tokens = prob.shape[0], prob.shape[-1]
+    column, rows = block_specs(tokens)
+    thirds = [column(n) for n in range(3)]
+    grads = jax.ShapeDtypeStruct((groups * tokens, 5 * HEADS * HD), BF16)
     return pl.pallas_call(
         attention_back_body,
-        grid=(heads,),
+        grid=(groups, HEADS),
         in_specs=[column(0), column(0)]
         + thirds * 3
-        + [pl.BlockSpec((1, 3, tokens, tokens), lambda h: (h, 0, 0, 0))]
-        + [whole((tokens, HD))] * 2
-        + [whole(gates.shape)],
-        out_specs=[whole((tokens, 2560)), whole((tokens, HD))],
-        out_shape=[
-            jax.ShapeDtypeStruct((tokens, 2560), BF16),
-            jax.ShapeDtypeStruct((tokens, HD), F32),
-        ],
+        + [prob_spec(tokens)]
+        + [rows(HD)] * 2
+        + [rows(gates.shape[1])],
+        out_specs=[rows(grads.shape[1]), rows(HD)],
+        out_shape=[grads, jax.ShapeDtypeStruct((groups * tokens, HD), F32)],
         compiler_params=pltpu.CompilerParams(vmem_limit_bytes=48 * MIB),
         name="attention_back",
     )(key, val, que, que, que, mix, mix, mix, raw, raw, raw, prob, cosine, sine, gates)
@@ -815,12 +1014,7 @@
 
 def reorder(rows):
     count, width = rows.shape
-    return jnp.swapaxes(rows.reshape(count, 4, 8, width // 32), 1, 2).reshape(count, width)
-
-
-def order_back(rows):
-    count, width = rows.shape
-    return jnp.swapaxes(rows.reshape(count, 8, 4, width // 32), 1, 2).reshape(count, width)
+    return jnp.transpose(rows.reshape(count, 4, 2, 4, width // 32), (0, 3, 2, 1, 4)).reshape(count, width)
 
 
 def pad_to(array, width):
@@ -849,36 +1043,40 @@
     att_count = query_proj.shape[0]
     mlp_count = gate_up.shape[0]
     share = gate_up.shape[1]
-    qkv_cols = (2 + att_count) * inner
+    part = inner // 2
+    qkv_cols = (2 + att_count) * part
     small_at = qkv_cols
     out_at = qkv_cols + 128
     small = jnp.concatenate([router_att, router_mlp, gain_att[:, None], gain_mlp[:, None]], 1)
     own_att = jnp.concatenate(
         [
-            key_value.reshape(share, 2 * inner),
-            jnp.swapaxes(query_proj, 0, 1).reshape(share, att_count * inner),
-            pad_to(small, 128),
-            jnp.transpose(output_proj, (2, 0, 1)).reshape(share, att_count * inner),
-        ],
-        1,
-    )
-    own_mlp = jnp.concatenate(
-        [
-            gate_up.reshape(mlp_count, share, 2 * hidden_local),
-            jnp.swapaxes(down_proj, 1, 2),
+            jnp.transpose(key_value.reshape(share, 2, 2, part), (2, 0, 1, 3)).reshape(2, share, -1),
+            jnp.transpose(query_proj.reshape(att_count, share, 2, part), (2, 1, 0, 3)).reshape(
+                2, share, -1
+            ),
+            jnp.broadcast_to(pad_to(small, 128), (2, share, 128)),
+            jnp.transpose(output_proj.reshape(att_count, 2, part, share), (1, 3, 0, 2)).reshape(
+                2, share, -1
+            ),
         ],
         2,
     )
     inputs = reorder(inputs)
     out_grad = reorder(out_grad)
-    x_all = lax.all_gather(inputs, TP, axis=0, tiled=True)
+    x_all = lax.all_gather(inputs, ("xl", *TP), axis=0, tiled=True)
     grad_all = lax.all_gather(out_grad, TP, axis=0, tiled=True)
-    weights, own_expert = gather_dp(own_att, own_mlp)
-    own_expert = own_expert.reshape(mlp_count * share, 3 * hidden_local)
-    up_whole = lax.all_gather(own_expert[:, : 2 * hidden_local], ("xl", "z"), axis=0, tiled=True)
-    down_whole = lax.all_gather(own_expert[:, 2 * hidden_local :], ("xl", "z"), axis=0, tiled=True)
-
-    tokens = x_all.shape[0]
+    marks = lax.all_gather(jnp.concatenate([segments[:, None], att_routes], 1), "xl", axis=0)
+    weights, up_parts, down_parts = gather_dp(
+        own_att, gate_up.reshape(mlp_count, share, -1), jnp.swapaxes(down_proj, 1, 2)
+    )
+    up_whole = lax.all_gather(
+        up_parts.reshape(2 * mlp_count * share, -1), "z", axis=0, tiled=True
+    )
+    down_whole = lax.all_gather(
+        down_parts.reshape(2 * mlp_count * share, -1), "z", axis=0, tiled=True
+    )
+
+    tokens = segments.shape[0]
     match = jnp.sum((mlp_routes[:, :, None] == jnp.arange(mlp_count, dtype=jnp.int32)).astype(BF16), 1)
     index = jnp.arange(tokens, dtype=jnp.int32)
     lower = (index[None, :] < index[:, None]).astype(BF16)
@@ -892,12 +1090,14 @@
 
     small_all = weights[:, small_at : small_at + 128].astype(F32)
     gain_one, gain_two = small_all[:, 7], small_all[:, 8]
-    places = positions(segments).astype(F32)
+    segments = marks[:, :, 0]
+    att_routes = marks[:, :, 1:].reshape(2 * tokens, 2)
+    places = jax.vmap(positions)(segments).reshape(-1).astype(F32)
     frequency = ROPE_BASE ** (-2.0 * jnp.arange(HD // 2, dtype=F32) / HD)
     angles = places[:, None] * frequency[None, :]
     cosine = jnp.concatenate([jnp.cos(angles)] * 2, 1)
     sine = jnp.concatenate([-jnp.sin(angles), jnp.sin(angles)], 1)
-    normed_one, inverse_one = normalize(x_all.astype(F32))
+    normed_one, _ = normalize(x_all.astype(F32))
     unit_one = (normed_one * gain_one).astype(BF16)
     joined_att = dot(unit_one, weights[:, :out_at], ((1,), (0,)))
     weights_att, onehot_att, gate_att = route_gates(
@@ -935,7 +1135,7 @@
         grad_in, (hidden_f32 * gates_in).astype(BF16), ((0,), (0,))
     ).astype(BF16)
     djoined, grad_down_whole = lax.optimization_barrier((djoined, grad_down_whole))
-    grad_down_sum = lax.psum_scatter(grad_down_whole, ("xl", "z"), scatter_dimension=0, tiled=True)
+    grad_down_sum = lax.psum_scatter(grad_down_whole, "z", scatter_dimension=0, tiled=True)
     dunit_part = dot(djoined, up_whole, ((1,), (1,))).astype(BF16)
     dgate_high = dgate_in.astype(BF16)
     dgate_low = (dgate_in - dgate_high.astype(F32)).astype(BF16)
@@ -946,7 +1146,7 @@
     djoined, dunit_ext = lax.optimization_barrier((djoined, dunit_ext))
     grad_up_whole = dot(rows_in, djoined, ((0,), (0,))).astype(BF16)
     hidden, grad_up_whole = lax.optimization_barrier((hidden, grad_up_whole))
-    grad_up_sum = lax.psum_scatter(grad_up_whole, ("xl", "z"), scatter_dimension=0, tiled=True)
+    grad_up_sum = lax.psum_scatter(grad_up_whole, "z", scatter_dimension=0, tiled=True)
     branch_part = dot(hidden, down_whole, ((1,), (1,))).astype(BF16)
     dunit_back, branch_part = lax.optimization_barrier((dunit_back, branch_part))
     branch_back = lax.all_to_all(
@@ -985,21 +1185,24 @@
     )
     gate_slots = jnp.sum(pick.astype(F32) * gate_mlp.T[:, None, :], -1).reshape(mlp_count * CAP, 1)
     feed = dot(pick_rows, (branch_back.astype(F32) * gate_slots).astype(BF16), ((0,), (0,)))
-    summed_att = scatter_dp(
-        dot(unit_one, grad_qkv, ((0,), (0,))).astype(BF16),
-        pad_to(grad_small, 128).astype(BF16),
-        dot(dattention, gmixed, ((0,), (0,))).astype(BF16),
-    )
-    grad_up_sum, grad_down_sum, summed_att = lax.optimization_barrier(
-        (grad_up_sum, grad_down_sum, summed_att)
-    )
-    grad_kv = summed_att[:, : 2 * inner].reshape(share, 2, inner)
-    grad_query = jnp.swapaxes(
-        summed_att[:, 2 * inner : qkv_cols].reshape(share, att_count, inner), 0, 1
-    )
+    summed_att, ups_sum, downs_sum = scatter_dp(
+        (
+            dot(unit_one, grad_qkv, ((0,), (0,))).astype(BF16),
+            pad_to(grad_small, 128).astype(BF16),
+            dot(dattention, gmixed, ((0,), (0,))).astype(BF16),
+        ),
+        grad_up_sum,
+        grad_down_sum,
+    )
+    grad_kv = jnp.transpose(
+        summed_att[:, :, : 2 * part].reshape(2, share, 2, part), (1, 2, 0, 3)
+    ).reshape(share, 2, inner)
+    grad_query = jnp.transpose(
+        summed_att[:, :, 2 * part : qkv_cols].reshape(2, share, att_count, part), (2, 1, 0, 3)
+    ).reshape(att_count, share, inner)
     grad_output = jnp.transpose(
-        summed_att[:, out_at:].reshape(share, att_count, inner), (1, 2, 0)
-    )
+        summed_att[:, :, out_at:].reshape(2, share, att_count, part), (2, 0, 3, 1)
+    ).reshape(att_count, inner, share)
     output, grad_input, small_sum = last_sums(
         dunit_one.astype(BF16),
         feed.astype(BF16),
@@ -1007,20 +1210,13 @@
         middle,
         dmiddle,
         gain_one,
-        summed_att[:, small_at:out_at],
-    )
-    output = order_back(output)
-    grad_input = order_back(grad_input)
-
-    summed_mlp = lax.all_to_all(
-        jnp.concatenate([grad_up_sum, grad_down_sum], 1).reshape(mlp_count, share, 3 * hidden_local),
-        "y",
-        0,
-        0,
-        tiled=True,
-    ).astype(F32)
-    grads_up = summed_mlp[:, :, : 2 * hidden_local].reshape(mlp_count, share, 2, hidden_local)
-    grads_down = jnp.swapaxes(summed_mlp[:, :, 2 * hidden_local :], 1, 2)
+        jnp.sum(summed_att[:, :, small_at:out_at], 0),
+    )
+    output = reorder(output)
+    grad_input = reorder(grad_input)
+
+    grads_up = ups_sum.astype(F32).reshape(mlp_count, share, 2, hidden_local)
+    grads_down = jnp.swapaxes(downs_sum.astype(F32), 1, 2)
     return (
         output,
         grad_input,

time: 837 us -> 747 us (0.89)
  Pallas kernels: 461 us -> 382 us
    pallas_call x4, Pallas kernels: 276 us -> 214 us  [the longest x1 90.2 us: gather_dp(): pl.pallas_call(gather_body, out_shape=[jax.ShapeDtypeStruct((4, 2, 4, row...]
    pallas_call x1, Pallas kernels: 53.6 us -> 39.1 us  [middle_back(): pl.pallas_call(back_body, out_shape=[jax.ShapeDtypeStruct((rows, width),...]
  transfers between devices with their start and end apart: 10 -> 9, of which waited for: 2 -> 1; matrix products, arithmetic and copies ran while one was open for 26% -> 27% of each run, Pallas kernels for 56% -> 35%
where the time goes in v3:
time: 747 us; the launch traced here: 738 us
  Pallas kernels  382 us (51%)
  matrix products  200 us (27%)
  waiting for transfers between devices  48.5 us (6%)
  local copies, waits for them, and re-layouts  41.4 us (6%)
  other arithmetic  29.7 us (4%)
  starting transfers between devices  16.4 us (2%)
  between operations  15.6 us (2%)
    dot_general x21, matrix products, dot(): return lax.dot_general(a, b, (dims, ((), ())), preferred_element_type=F32)  200 us
    pallas_call x1, Pallas kernels, gather_dp(): pl.pallas_call(gather_body, out_shape=[jax.ShapeDtypeStruct((4, 2, 4, row...  90.2 us
    pallas_call x1, Pallas kernels, scatter_dp(): pl.pallas_call(scatter_body, out_shape=[jax.ShapeDtypeStruct((2, share, c...  87.3 us
    all_to_all x1, waiting for transfers between devices, on_device(): lax.all_to_all(dunit_ext.reshape(mlp_count, CAP, width + 128), 'y', 0, 0,...  47.8 us
    pallas_call x1, Pallas kernels, rows_to_experts(): pl.pallas_call(rows_body, out_shape=jax.ShapeDtypeStruct(rows.shape, rows...  46.5 us
    pallas_call x1, Pallas kernels, middle_and_unit(): pl.pallas_call(middle_body, out_shape=[jax.ShapeDtypeStruct((rows, width)...  45.8 us
    pallas_call x1, Pallas kernels, middle_back(): pl.pallas_call(back_body, out_shape=[jax.ShapeDtypeStruct((rows, width),...  39.1 us
    pallas_call x1, Pallas kernels, last_sums(): pl.pallas_call(last_body, out_shape=[jax.ShapeDtypeStruct((rows, width),...  36.5 us
  transfers between devices with their start and end apart: 9, of which 1 were waited for; matrix products, arithmetic and copies ran while one was open for 27% of the time, Pallas kernels for 35%

profile of v3, /device:TPU:1, one launch (start us, length us, event | category | flops | bytes accessed | tf_op | source)
XLA Modules:
  0.0 738.2 jit_solution(18359236942415268910)
XLA Ops:
  7.3 1.5 copy.149
  9.7 1.3 copy.138
  13.5 1.8 reshape.457.ups_ref
  16.2 90.2 %gather_weights.1 = (bf16[4,2,4,64,2176]{4,3,2,1,0:T(8,128)(2,1)}, bf16[2,4,64,2816]{3,2,1,0:T(8,128)(2,1)}, bf16[2,4,64,1408]{3,2,1,0:T(8,128)(2,1)}) custom-call(bf16[2,64,2176]{2,1,0:T(8,128)(2,1)} %pad_maximum_fusion.1.x_ref, bf16[4,64,2816]{2,1,0:T(8,128)(2,1)} %reshape.457.ups_ref, bf16[4,64,1408]{2,1,0:T(8,128)(2,1)} %bitcast.159), custom_call_target="tpu_custom_call" | custom-call | tf_op jit(solution)/shard_map/gather_weights/pallas_call | solution.py:182
  107.1 4.5 all-gather
  114.8 1.3 bitcast_compare_fusion
  116.1 1.9 fusion.44
  118.4 7.3 convolution_convert_fusion.5
  125.7 5.2 all-to-all-start
  131.5 3.4 fusion.5
  134.9 10.6 %fusion.14.k_ref.v_ref.q0.q1.q2 = f32[1024,1408]{1,0:T(8,128)S(1)} fusion(bf16[2048,2176]{1,0:T(8,128)(2,1)} %bitcast.162, bf16[1024,2048]{1,0:T(8,128)(2,1)} %all-gather.6.cloned.1.call-done, f32[2048]{0:T(1024)S(1)} %bitcast.183, f32[1024]{0:T(1024)S(1)} %add_rsqrt_fusion), kind=kOutput, calls=%fused_computation.33 | convolution fusion | flops 5913968640 | bytes 15740928 | tf_op jit(solution)/shard_map/dot_general | solution.py:845
  145.6 2.5 copy-done.21
  150.4 23.7 %attention_forward.1 = (bf16[1024,256]{1,0:T(8,128)(2,1)S(1)}, bf16[1024,256]{1,0:T(8,128)(2,1)S(1)}, bf16[1024,768]{1,0:T(8,128)(2,1)S(1)}, bf16[1024,768]{1,0:...) custom-call(f32[1024,1408]{1,0:T(8,128)} %copy-done.21, f32[1024,1408]{1,0:T(8,128)} %copy-done.21, ...), custom_call_target="tpu_custom_call" | custom-call | tf_op jit(solution)/shard_map/attention_forward/pallas_call | solution.py:901
  174.1 6.2 convolution_convert_fusion.7
  180.3 45.8 %middle_and_unit.1 = (f32[128,2048]{1,0:T(8,128)S(1)}, bf16[4,128,2048]{2,1,0:T(8,128)(2,1)S(1)}) custom-call(bf16[2,2,2,128,2048]{4,3,2,1,0:T(8,128)(2,1)S(1)} %bitcast.125, bf16[128,2048]{1,0:T(8,128)(2,1)S(1)} %copy-done, f32[1,2048]{1,0:T(1,128)S(1)} %get-tuple-element.145.gain_ref), custom_call_target="tpu_custom_call" | custom-call | tf_op jit(solution)/shard_map/middle_and_unit/pallas_call | solution.py:451
  226.2 1.4 copy-done.2
  227.6 1.9 fusion.42
  231.0 7.6 %convolution_convert_fusion.1 = bf16[1280,2176]{1,0:T(8,128)(2,1)} fusion(pred[1280,512]{1,0:T(32,128)(4,1)} %bitcast_compare_fusion, bf16[512,8]{1,0:T(8,128)(2,1)S(1)} %copy.173, bf16[512,2048]{1,0:T(8,128)(2,1)} %bitcast.122), kind=kOutput, calls=%fused_computation.1 | convolution fusion | flops 2861596672 | bytes 8331264 | tf_op jit(solution)/shard_map/dot_general | solution.py:845
  238.6 46.5 %rows_to_experts.1 = bf16[4,320,2176]{2,1,0:T(8,128)(2,1)} custom-call(bf16[4,320,2176]{2,1,0:T(8,128)(2,1)} %bitcast.135), custom_call_target="tpu_custom_call" | custom-call | tf_op jit(solution)/shard_map/rows_to_experts/pallas_call | solution.py:609
  286.4 22.1 %fusion.17 = f32[1280,2816]{1,0:T(8,128)} fusion(bf16[2048,2816]{1,0:T(8,128)(2,1)} %all-gather.12.cloned.1.call-done, bf16[1280,2176]{1,0:T(8,128)(2,1)} %bitcast.133), kind=kOutput, calls=%fused_computation.36 | convolution fusion | flops 14763950080 | bytes 31195136 | tf_op jit(solution)/shard_map/dot_general | solution.py:845
  308.5 22.3 %multiply_convert_fusion.3 = (bf16[1280,1408]{1,0:T(8,128)(2,1)}, bf16[1280,1408]{1,0:T(8,128)(2,1)}, bf16[1280,1408]{1,0:T(8,128)(2,1)}, f32[1280,1408]{1,0:T(8,128)}, f32[1280,1408]{1,0:T(8,128)}) fusion(f32[1280,2816]{1,0:T(8,128)} %fusion.17, f32[1280]{0:T(1024)S(1)} %multiply_reduce_fusion.1, bf16[1280,2048]{1,0:T(8,128)(2,1)} %bitcast.22, ...), kind=kOutput, calls=%fused_computation.22 | convolution fusion | flops 7412613120 | bytes 50664448 | tf_op jit(solution)/shard_map/dot_general | solution.py:845
  330.8 14.3 %convolution_convert_fusion.4 = bf16[2048,1408]{1,0:T(8,128)(2,1)} fusion(bf16[1280,2048]{1,0:T(8,128)(2,1)} %bitcast.22, f32[1280,1408]{1,0:T(8,128)} %get-tuple-element.139, f32[1280]{0:T(1024)S(1)} %multiply_reduce_fusion.1), kind=kOutput, calls=%fused_computation.14 | convolution fusion | flops 7388463104 | bytes 18224128 | tf_op jit(solution)/shard_map/dot_general | solution.py:845
  345.0 6.5 pad_maximum_fusion
  351.6 5.8 multiply_reduce_fusion
  357.7 20.2 %convolution_convert_fusion.3 = bf16[1280,2048]{1,0:T(8,128)(2,1)S(1)} fusion(bf16[1280,2816]{1,0:T(8,128)(2,1)} %pad_maximum_fusion, bf16[2048,2816]{1,0:T(8,128)(2,1)} %all-gather.12.cloned.1.call-done), kind=kOutput, calls=%fused_computation.13 | convolution fusion | flops 14766571520 | bytes 23986176 | tf_op jit(solution)/shard_map/dot_general | solution.py:845
  377.9 3.0 fusion.7
  380.9 21.9 %convolution_convert_fusion = bf16[2048,2816]{1,0:T(8,128)(2,1)} fusion(bf16[1280,2816]{1,0:T(8,128)(2,1)} %pad_maximum_fusion, bf16[1280,2176]{1,0:T(8,128)(2,1)} %bitcast.134), kind=kOutput, calls=%fused_computation | convolution fusion | flops 14769717248 | bytes 23986176 | tf_op jit(solution)/shard_map/dot_general | solution.py:845
  402.9 5.3 all-to-all-start.1
  408.2 2.0 copy.154.grad_ref
  410.2 13.2 %convolution_convert_fusion.6 = bf16[1280,2048]{1,0:T(8,128)(2,1)} fusion(bf16[1280,1408]{1,0:T(8,128)(2,1)} %get-tuple-element.51, bf16[2048,1408]{1,0:T(8,128)(2,1)} %all-gather.10.cloned.1.call-done), kind=kOutput, calls=%fused_computation.16 | convolution fusion | flops 7384596480 | bytes 14614528 | tf_op jit(solution)/shard_map/dot_general | solution.py:845
  423.4 47.8 %all-to-all-done.1 = bf16[4,320,2176]{2,1,0:T(8,128)(2,1)} async-done(((bf16[4,320,2176]{2,1,0:T(8,128)(2,1)}), bf16[4,320,2176]{2,1,0:T(8,128)(2,1)}, u32[]{:S(2)}, u32[]{:S(2)}) %all-to-all-start.1) | async-done | bytes 5570592 | tf_op jit(solution)/shard_map/all_to_all | solution.py:1145
  471.3 1.5 add_reduce_fusion
  472.8 5.2 all-to-all-start.2
  479.2 5.1 fusion.9
  484.3 2.1 add_convert_fusion
  486.4 39.1 %middle_back.1 = (f32[128,2048]{1,0:T(8,128)S(1)}, f32[1,2048]{1,0:T(1,128)S(1)}, bf16[2,2,2,128,2048]{4,3,2,1,0:T(8,128)(2,1)S(1)}) custom-call(bf16[4,128,2048]{2,1,0:T(8,128)(2,1)S(1)} %bitcast.120, f32[128,2048]{1,0:T(8,128)S(1)} %copy-done.5, bf16[128,2048]{1,0:T(8,128)(2,1)S(1)} %copy-done.9, f32[1,2048]{1,0:T(1,128)S(1)} %get-tuple-element.145.gain_ref), custom_call_target="tpu_custom_call" | custom-call | tf_op jit(solution)/shard_map/middle_back/pallas_call | solution.py:498
  525.5 8.9 %fusion.26.h0.h1.h2 = f32[1024,768]{1,0:T(8,128)} fusion(bf16[1024,2048]{1,0:T(8,128)(2,1)S(1)} %bitcast.129, bf16[2048,2176]{1,0:T(8,128)(2,1)} %bitcast.166), kind=kOutput, calls=%fused_computation.51 | convolution fusion | flops 3221225472 | bytes 10485760 | tf_op jit(solution)/shard_map/dot_general | solution.py:845
  534.4 13.2 %attention_back.1 = (bf16[1024,1280]{1,0:T(8,128)(2,1)}, f32[1024,128]{1,0:T(8,128)S(1)}) custom-call(bf16[1024,256]{1,0:T(8,128)(2,1)S(1)} %copy-done.15, bf16[1024,256]{1,0:T(8,128)(2,1)S(1)} %copy-done.17, bf16[1024,768]{1,0:T(8,128)(2,1)S(1)} %get-tuple-element.43.q0.q1.q2, bf16[1024,768]{1,0:T(8,128)(2,1)S(1)} %get-tuple-element.43.q0.q1.q2, ...), custom_call_target="tpu_custom_call" | custom-call | tf_op jit(solution)/shard_map/attention_back/pallas_call | solution.py:966
  548.4 1.2 copy.156
  550.1 12.6 %fusion.4 = (bf16[2048]{0:T(1024)(128)(2,1)S(1)}, bf16[1024,2048]{1,0:T(8,128)(2,1)}) fusion(bf16[1024,2048]{1,0:T(8,128)(2,1)} %all-gather.6.cloned.1.call-done, f32[1024]{0:T(1024)S(1)} %copy-done.54, bf16[2048,2176]{1,0:T(8,128)(2,1)} %bitcast.167, bf16[1024,3]{1,0:T(8,128)(2,1)S(1)} %copy.157, bf16[1024,1280]{1,0:T(8,128)(2,1)} %get-tuple-element.56), kind=kOutput, calls=%fused_computation.10 | convolution fusion | flops 5924714496 | bytes 16791552 | tf_op jit(solution)/shard_map/dot_general | solution.py:845
  565.6 8.0 %convolution_convert_fusion.8 = bf16[2048,768]{1,0:T(8,128)(2,1)} fusion(bf16[1024,2048]{1,0:T(8,128)(2,1)} %bitcast.130, bf16[1024,768]{1,0:T(8,128)(2,1)} %get-tuple-element.46), kind=kOutput, calls=%fused_computation.44 | convolution fusion | flops 3222798336 | bytes 8912896 | tf_op jit(solution)/shard_map/dot_general | solution.py:845
  573.6 7.8 %convolution_convert_fusion.2 = bf16[2048,1280]{1,0:T(8,128)(2,1)} fusion(bf16[1024,1280]{1,0:T(8,128)(2,1)S(1)} %copy-done.60, bf16[1024,2048]{1,0:T(8,128)(2,1)S(1)} %copy-done.23, f32[2048]{0:T(1024)S(1)} %bitcast.185, f32[1024]{0:T(1024)S(1)} %copy-done.54), kind=kOutput, calls=%fused_computation.12 | convolution fusion | flops 5379719168 | bytes 12070912 | tf_op jit(solution)/shard_map/dot_general | solution.py:845
  581.4 6.0 bitcast_convert_fusion
  587.5 87.3 %scatter_grads.1 = (f32[2,64,2176]{2,1,0:T(8,128)}, bf16[4,64,2816]{2,1,0:T(8,128)(2,1)}, bf16[4,64,1408]{2,1,0:T(8,128)(2,1)}) custom-call(bf16[4,2,4,64,1280]{4,3,2,1,0:T(8,128)(2,1)} %bitcast.136, bf16[4,2,4,64,128]{4,3,2,1,0:T(8,128)(2,1)} %bitcast.148, bf16[4,2,4,64,768]{4,3,2,1,0:T(8,128)(2,1)} %bitcast.143, bf16[2,4,64,2816]{3,2,1,0:T(8,128)(2,1)} %bitcast.145, ...), custom_call_target="tpu_custom_call" | custom-call | tf_op jit(solution)/shard_map/scatter_grads/pallas_call | solution.py:797
  676.9 36.5 %last_sums.1 = (bf16[128,2048]{1,0:T(8,128)(2,1)S(1)}, f32[128,2048]{1,0:T(8,128)S(1)}, f32[64,128]{1,0:T(8,128)S(1)}) custom-call(bf16[2,2,2,128,2048]{4,3,2,1,0:T(8,128)(2,1)S(1)} %bitcast.124, bf16[4,128,2048]{2,1,0:T(8,128)(2,1)S(1)} %bitcast.126, bf16[128,2048]{1,0:T(8,128)(2,1)S(1)} %copy-done.1, f32[128,2048]{1,0:T(8,128)S(1)} %copy-done.6, ...), custom_call_target="tpu_custom_call" | custom-call | tf_op jit(solution)/shard_map/last_sums/pallas_call | solution.py:551
  716.0 1.4 copy.160
  724.3 1.3 copy.168
  725.6 4.3 reshape.494
  (243 shorter events, 32.2 us)
Async XLA Ops:
  7.2 5.3 copy-start.31
  7.2 5.8 copy-start.32
  7.3 6.2 copy-start.24
  7.3 111.1 %all-gather.8.cloned.1.call-start = ((), (), s32[]{:S(2)}) async-start(), calls=%async_computation.6 | async-start | bytes 2621440 | tf_op jit(solution)/shard_map/all_gather | solution.py:1067
  9.7 121.8 %all-gather.6.cloned.1.call-start = ((), (), s32[]{:S(2)}) async-start(), calls=%async_computation.5 | async-start | bytes 4718592 | tf_op jit(solution)/shard_map/all_gather | solution.py:1066
  12.1 274.3 %all-gather.12.cloned.1.call-start = ((), (), s32[]{:S(2)}) async-start(), calls=%async_computation.8 | async-start | bytes 14417920 | tf_op jit(solution)/shard_map/all_gather | solution.py:1072
  13.5 93.5 %copy-start.52 = (s32[512,2]{0,1:T(2,128)S(1)}, s32[512,2]{0,1:T(2,128)}, u32[]{:S(2)}) copy-start(s32[512,2]{0,1:T(2,128)} %param.16) | copy-start | bytes 12292
  13.5 93.5 %copy-start.55 = (s32[512]{0:T(512)S(1)}, s32[512]{0:T(512)}, u32[]{:S(2)}) copy-start(s32[512]{0:T(512)} %param.15) | copy-start | bytes 6148
  16.2 97.1 %copy-start.38 = (s32[512,2]{0,1:T(2,128)S(1)}, s32[512,2]{0,1:T(2,128)}, u32[]{:S(2)}) copy-start(s32[512,2]{0,1:T(2,128)} %param.17) | copy-start | bytes 12292
  106.4 202.1 %all-gather.10.cloned.1.call-start = ((), (), s32[]{:S(2)}) async-start(), calls=%async_computation.7 | async-start | bytes 7208960 | tf_op jit(solution)/shard_map/all_gather | solution.py:1075
  111.6 37.4 %copy-start.29 = (s32[2,512,2]{1,2,0:T(2,128)}, s32[2,512,2]{1,2,0:T(2,128)S(1)}, u32[]{:S(2)}) copy-start(s32[2,512,2]{1,2,0:T(2,128)S(1)} %slice.105) | copy-start | bytes 24580
  113.1 21.8 %copy-start.50 = (f32[2048,1]{0,1:T(1,128)}, f32[2048,1]{0,1:T(1,128)S(1)}, u32[]{:S(2)}) copy-start(f32[2048,1]{0,1:T(1,128)S(1)} %slice.102) | copy-start | bytes 24580
  125.7 182.8 %all-to-all-start = ((bf16[4,320,2048]{2,1,0:T(8,128)(2,1)}), bf16[4,320,2048]{2,1,0:T(8,128)(2,1)}, u32[]{:S(2)}, u32[]{:S(2)}) async-start(bf16[4,320,2048]{2,1,0:T(8,128)(2,1)} %bitcast.138), calls=%async_computation | async-start | bytes 10485760 | tf_op jit(solution)/shard_map/all_to_all | solution.py:1088
  130.9 456.5 %reduce-scatter.5.cloned.1.call-start = ((), (), s32[]{:S(2)}) async-start(), calls=%async_computation.10 | async-start | bytes 7208960 | tf_op jit(solution)/shard_map/reduce_scatter | solution.py:1138
  134.9 10.7 %copy-start.53 = (f32[1024]{0:T(1024)}, f32[1024]{0:T(1024)S(1)}, u32[]{:S(2)}) copy-start(f32[1024]{0:T(1024)S(1)} %add_rsqrt_fusion) | copy-start | bytes 12292
  174.0 6.3 copy-start.14
  174.1 6.3 copy-start.16
  174.1 6.3 copy-start
  229.5 9.1 %copy-start.33 = (f32[512,2]{0,1:T(2,128)}, f32[512,2]{0,1:T(2,128)S(1)}, u32[]{:S(2)}) copy-start(f32[512,2]{0,1:T(2,128)S(1)} %select_reduce_fusion.7) | copy-start | bytes 12292
  351.5 235.9 %reduce-scatter.3.cloned.1.call-start = ((), (), s32[]{:S(2)}) async-start(), calls=%async_computation.9 | async-start | bytes 14417920 | tf_op jit(solution)/shard_map/reduce_scatter | solution.py:1149
  402.9 68.4 %all-to-all-start.1 = ((bf16[4,320,2176]{2,1,0:T(8,128)(2,1)}), bf16[4,320,2176]{2,1,0:T(8,128)(2,1)}, u32[]{:S(2)}, u32[]{:S(2)}) async-start(bf16[4,320,2176]{2,1,0:T(8,128)(2,1)} %bitcast.131), calls=%async_computation.1 | async-start | bytes 11141120 | tf_op jit(solution)/shard_map/all_to_all | solution.py:1145
  472.8 5.3 copy-start.41
  472.8 5.3 copy-start.47
  472.8 6.3 copy-start.39
  472.8 6.3 copy-start.34
  472.8 6.3 copy-start.45
  472.8 6.3 copy-start.49
  472.8 108.5 %all-to-all-start.2 = ((bf16[4,320,2048]{2,1,0:T(8,128)(2,1)}), bf16[4,320,2048]{2,1,0:T(8,128)(2,1)}, u32[]{:S(2)}, u32[]{:S(2)}) async-start(bf16[4,320,2048]{2,1,0:T(8,128)(2,1)} %bitcast.137), calls=%async_computation.2 | async-start | bytes 10485760 | tf_op jit(solution)/shard_map/all_to_all | solution.py:1152
  525.4 8.9 %copy-start.10 = (f32[128,2048]{1,0:T(8,128)}, f32[128,2048]{1,0:T(8,128)S(1)}, u32[]{:S(2)}) copy-start(f32[128,2048]{1,0:T(8,128)S(1)} %get-tuple-element.59.dmiddle_ref) | copy-start | bytes 3145732
  525.5 8.9 %copy-start.20 = (bf16[2,2,2,128,2048]{4,3,2,1,0:T(8,128)(2,1)}, bf16[2,2,2,128,2048]{4,3,2,1,0:T(8,128)(2,1)S(1)}, u32[]{:S(2)}) copy-start(bf16[2,2,2,128,2048]{4,3,2,1,0:T(8,128)(2,1)S(1)} %get-tuple-element.54) | copy-start | bytes 12582916
  525.5 8.9 %copy-start.15 = (bf16[1024,256]{1,0:T(8,128)(2,1)S(1)}, bf16[1024,256]{1,0:T(8,128)(2,1)}, u32[]{:S(2)}) copy-start(bf16[1024,256]{1,0:T(8,128)(2,1)} %copy-done.14) | copy-start | bytes 1572868
  525.5 8.9 %copy-start.17 = (bf16[1024,256]{1,0:T(8,128)(2,1)S(1)}, bf16[1024,256]{1,0:T(8,128)(2,1)}, u32[]{:S(2)}) copy-start(bf16[1024,256]{1,0:T(8,128)(2,1)} %copy-done.16) | copy-start | bytes 1572868
  534.4 15.3 %copy-start.30 = (s32[2,512,2]{1,2,0:T(2,128)S(1)}, s32[2,512,2]{1,2,0:T(2,128)}, u32[]{:S(2)}) copy-start(s32[2,512,2]{1,2,0:T(2,128)} %copy-done.29) | copy-start | bytes 24580
  534.4 15.3 %copy-start.28 = (f32[1024,2]{0,1:T(2,128)S(1)}, f32[1024,2]{0,1:T(2,128)}, u32[]{:S(2)}) copy-start(f32[1024,2]{0,1:T(2,128)} %copy-done.27) | copy-start | bytes 24580
  534.4 15.3 %copy-start.37 = (f32[1024]{0:T(1024)S(1)}, f32[1024]{0:T(1024)}, u32[]{:S(2)}) copy-start(f32[1024]{0:T(1024)} %copy-done.36) | copy-start | bytes 12292
  534.4 15.3 %copy-start.43 = (f32[1024]{0:T(1024)S(1)}, f32[1024]{0:T(1024)}, u32[]{:S(2)}) copy-start(f32[1024]{0:T(1024)} %copy-done.42) | copy-start | bytes 12292
  534.4 15.6 %copy-start.54 = (f32[1024]{0:T(1024)S(1)}, f32[1024]{0:T(1024)}, u32[]{:S(2)}) copy-start(f32[1024]{0:T(1024)} %copy-done.53) | copy-start | bytes 12292
  550.1 12.7 %copy-start.3 = (bf16[4,128,2048]{2,1,0:T(8,128)(2,1)S(1)}, bf16[4,128,2048]{2,1,0:T(8,128)(2,1)}, u32[]{:S(2)}) copy-start(bf16[4,128,2048]{2,1,0:T(8,128)(2,1)} %copy-done.2) | copy-start | bytes 6291460
  550.1 13.0 %copy-start.22 = (bf16[1024,2048]{1,0:T(8,128)(2,1)S(1)}, bf16[1024,2048]{1,0:T(8,128)(2,1)}, u32[]{:S(2)}) copy-start(bf16[1024,2048]{1,0:T(8,128)(2,1)} %all-gather.6.cloned.1.call-done) | copy-start | bytes 12582916
  550.1 13.0 %copy-start.51 = (f32[2048,1]{0,1:T(1,128)S(1)}, f32[2048,1]{0,1:T(1,128)}, u32[]{:S(2)}) copy-start(f32[2048,1]{0,1:T(1,128)} %copy-done.50) | copy-start | bytes 24580
  565.6 8.0 %copy-start.23 = (bf16[1024,2048]{1,0:T(8,128)(2,1)S(1)}, bf16[1024,2048]{1,0:T(8,128)(2,1)}, u32[]{:S(2)}) copy-start(bf16[1024,2048]{1,0:T(8,128)(2,1)} %all-gather.6.cloned.1.call-done) | copy-start | bytes 12582916
  565.6 8.0 %copy-start.60 = (bf16[1024,1280]{1,0:T(8,128)(2,1)S(1)}, bf16[1024,1280]{1,0:T(8,128)(2,1)}, u32[]{:S(2)}) copy-start(bf16[1024,1280]{1,0:T(8,128)(2,1)} %get-tuple-element.56) | copy-start | bytes 7864324
  587.5 88.2 %copy-start.1 = (bf16[128,2048]{1,0:T(8,128)(2,1)S(1)}, bf16[128,2048]{1,0:T(8,128)(2,1)}, u32[]{:S(2)}) copy-start(bf16[128,2048]{1,0:T(8,128)(2,1)} %copy.140.x_ref) | copy-start | bytes 1572868
  587.5 88.2 %copy-start.6 = (f32[128,2048]{1,0:T(8,128)S(1)}, f32[128,2048]{1,0:T(8,128)}, u32[]{:S(2)}) copy-start(f32[128,2048]{1,0:T(8,128)} %copy-done.4) | copy-start | bytes 3145732
  587.5 88.2 %copy-start.7 = (bf16[1024,2048]{1,0:T(8,128)(2,1)S(1)}, bf16[1024,2048]{1,0:T(8,128)(2,1)}, u32[]{:S(2)}) copy-start(bf16[1024,2048]{1,0:T(8,128)(2,1)} %get-tuple-element.141) | copy-start | bytes 12582916
  676.9 39.0 %copy-start.25 = (f32[2,64,2176]{2,1,0:T(8,128)S(1)}, f32[2,64,2176]{2,1,0:T(8,128)}, u32[]{:S(2)}) copy-start(f32[2,64,2176]{2,1,0:T(8,128)} %get-tuple-element.63) | copy-start | bytes 3342340
  715.9 7.9 %copy-start.13 = (f32[128,2048]{1,0:T(8,128)S(1)}, f32[128,2048]{1,0:T(8,128)}, u32[]{:S(2)}) copy-start(f32[128,2048]{1,0:T(8,128)} %copy-done.12) | copy-start | bytes 3145732
  723.9 6.1 copy-start.26
  (22 other events, 49.9 us)
Sparse Core Ops, SparseCore 0:
  9.8 41.7 all-gather.7
  53.8 63.4 all-gather.5
  118.9 106.1 all-gather.11
  226.6 62.4 all-gather.9
  351.7 56.5 reduce-scatter.4
  410.5 105.8 reduce-scatter.2

commit v4 on v3

--- a/solution.py
+++ b/solution.py
@@ -213,7 +213,7 @@
     return whole.reshape(32 * rows, cols), up, down
 
 
-def reduce_body(scatter_count, part_refs, core_buf, sum_buf, far_buf, core_s, core_r, far_s, far_r, sends):
+def reduce_stages(scatter_count, part_refs, core_buf, sum_buf, far_buf, core_s, core_r, far_s, far_r, sends):
     xh, core = lax.axis_index("xh"), lax.axis_index("core")
     rows = part_refs[0].shape[1]
     step = rows // scatter_count
@@ -238,6 +238,7 @@
                 core_r.at[i, n, 1],
                 neighbour("core", 1),
             )
+    yield
     for n, chunk in enumerate(range(0, rows, step)):
         at = pl.ds(chunk, step)
         for i, part in enumerate(part_refs):
@@ -253,6 +254,7 @@
                 far_r.at[i, n],
                 neighbour("xh", 1),
             )
+    yield
 
     def total(i, n):
         chunk = n * step
@@ -263,10 +265,10 @@
         arrived(far_buf.at[i, at], far_r.at[i, n])
         return near + far_buf[i, chunk : chunk + step, :].astype(F32)
 
-    return total
-
-
-def ring_reduce_body(part_ref, core_buf, sum_buf, via_buf, far_buf, core_s, core_r, ring_s, ring_r, sends):
+    yield total
+
+
+def ring_reduce_stages(part_ref, core_buf, sum_buf, via_buf, far_buf, core_s, core_r, ring_s, ring_r, sends):
     xl, xh, core = lax.axis_index("xl"), lax.axis_index("xh"), lax.axis_index("core")
     rows = part_ref.shape[3]
     half = rows // 2
@@ -291,6 +293,7 @@
 
     first, second = pl.ds(0, half), pl.ds(half, half)
     ahead, behind = chip_along(1), chip_along(-1)
+    yield
     arrived(core_buf.at[0], core_r.at[0])
     sum_buf[0, :half, :] = both(0, 0).astype(BF16)
     sends(sum_buf.at[0, first], via_buf.at[0], ring_s.at[0], ring_r.at[0], ahead)
@@ -302,6 +305,7 @@
     arrived(core_buf.at[2], core_r.at[2])
     sum_buf[2, :half, :] = both(2, 0).astype(BF16)
     sends(sum_buf.at[2, first], far_buf.at[1, first], ring_s.at[3], ring_r.at[3], behind)
+    yield
     arrived(via_buf.at[0], ring_r.at[0])
     sum_buf[1, :half, :] = (both(1, 0) + via_buf[0].astype(F32)).astype(BF16)
     sends(sum_buf.at[1, first], far_buf.at[0, first], ring_s.at[4], ring_r.at[4], ahead)
@@ -319,7 +323,7 @@
         arrived(far_buf.at[1, rows_at], ring_r.at[3 if part == 0 else 5])
         return near + far_buf[1, start : start + half, :].astype(F32)
 
-    return total
+    yield total
 
 
 def ring_reduce_scratch(rows, width):
@@ -426,7 +430,7 @@
 def middle_body(part_ref, x_ref, gain_ref, middle_ref, unit_ref, *scratch):
     sends = Sends()
     greet(*along_x())
-    total = ring_reduce_body(part_ref, *scratch[:8], sends)
+    *_, total = ring_reduce_stages(part_ref, *scratch[:8], sends)
     me = lax.axis_index("xh") * 2 + lax.axis_index("core")
     step = x_ref.shape[0] // CHUNKS
     half = x_ref.shape[0] // 2
@@ -468,7 +472,7 @@
 def back_body(part_ref, middle_ref, grad_ref, gain_ref, dmiddle_ref, dgain_ref, spread_ref, *scratch):
     sends = Sends()
     greet(*along_x())
-    total = reduce_body(CHUNKS, [part_ref], *scratch[:7], sends)
+    *_, total = reduce_stages(CHUNKS, [part_ref], *scratch[:7], sends)
     xl, xh, core = lax.axis_index("xl"), lax.axis_index("xh"), lax.axis_index("core")
     step = middle_ref.shape[0] // CHUNKS
     for n in range(CHUNKS):
@@ -511,68 +515,6 @@
         name="middle_back",
     )(part.reshape(4, rows, width), middle, grad, gain[None])
     return dmiddle, dgain[0], spread.reshape(8 * rows, width)
-
-
-def last_body(
-    part_ref, feed_ref, x_ref, middle_ref, dmiddle_ref, gain_ref, small_ref,
-    output_ref, dinput_ref, small_out, *scratch,
-):
-    sends = Sends()
-    xh, core = lax.axis_index("xh"), lax.axis_index("core")
-    peers = ({"xh": xh, "core": 1 - core}, {"xh": 1 - xh, "core": core}, {"xh": 1 - xh, "core": 1 - core})
-    greet(*peers, chip_along(1), chip_along(-1))
-    small_buf, small_s, small_r = scratch[15:]
-    for n, peer in enumerate(peers):
-        sends(small_ref, small_buf.at[n], small_s.at[n], small_r.at[n], peer)
-    total = ring_reduce_body(part_ref, *scratch[7:15], sends)
-    feed = reduce_body(CHUNKS, [feed_ref], *scratch[:7], sends)
-    half = x_ref.shape[0] // 2
-    for part in (0, 1):
-        rows = slice(part * half, (part + 1) * half)
-        x = x_ref[rows, :].astype(F32)
-        inverse = lax.rsqrt(jnp.mean(x * x, 1, keepdims=True) + EPSILON)
-        normed = x * inverse
-        dscaled = total(part) * gain_ref[...]
-        mean = jnp.mean(dscaled * normed, 1, keepdims=True)
-        dinput_ref[rows, :] = dmiddle_ref[rows, :] + inverse * (dscaled - normed * mean)
-    step = x_ref.shape[0] // CHUNKS
-    for n in range(CHUNKS):
-        rows = slice(n * step, (n + 1) * step)
-        output_ref[rows, :] = (middle_ref[rows, :] + feed(0, n)).astype(BF16)
-    for n in range(3):
-        arrived(small_buf.at[n], small_r.at[n])
-    small_out[...] = (small_ref[...] + small_buf[1]) + (small_buf[0] + small_buf[2])
-    sends.finish()
-
-
-def last_sums(part, feed, x, middle, dmiddle, gain, small):
-    rows, width = x.shape
-    dma = pltpu.SemaphoreType.DMA
-    return pl.pallas_call(
-        last_body,
-        out_shape=[
-            jax.ShapeDtypeStruct((rows, width), BF16),
-            jax.ShapeDtypeStruct((rows, width), F32),
-            jax.ShapeDtypeStruct(small.shape, F32),
-        ],
-        in_specs=vmem(7),
-        out_specs=vmem(3),
-        scratch_shapes=reduce_scratch(1, rows, width)
-        + ring_reduce_scratch(rows, width)
-        + [pltpu.VMEM((3, *small.shape), F32), dma((3,)), dma((3,))],
-        compiler_params=pltpu.CompilerParams(
-            collective_id=3, has_side_effects=True, vmem_limit_bytes=40 * MIB
-        ),
-        name="last_sums",
-    )(
-        part.reshape(2, 2, 2, rows, width),
-        feed.reshape(4, rows, width),
-        x,
-        middle,
-        dmiddle,
-        gain[None],
-        small,
-    )
 
 
 def rows_body(rows_ref, out_ref, loc, far_s, far_r, core_s, core_r):
@@ -620,12 +562,17 @@
 STEPS = (2, 1, -1, 0)
 
 
-def scatter_body(
-    qkv_ref, small_ref, o_ref, up_ref, down_ref, out_ref, up_out, down_out, g_ref, loc, t_buf, r_buf, tb_buf, rb_buf, c_buf,
-    t_s, t_r, r_s, r_r, tb_s, tb_r, rb_s, rb_r, c_s, c_r, up_buf, down_buf, up_sum, down_sum, ex, ey, es, er,
+def finish_body(
+    qkv_ref, small_ref, o_ref, ups_ref, downs_ref, part_ref, feed_ref, x_ref, middle_ref, dmiddle_ref, gain_ref,
+    out_ref, up_out, down_out, output_ref, dinput_ref, small_out,
+    g_ref, loc, t_buf, r_buf, tb_buf, rb_buf, c_buf,
+    t_s, t_r, r_s, r_r, tb_s, tb_r, rb_s, rb_r, c_s, c_r,
+    up_own, down_own, up_buf, down_buf, up_sum, down_sum, ex, ey, es, er,
+    small_own, small_buf, small_s, small_r, *scratch,
 ):
-    xl = lax.axis_index("xl")
+    xl, xh, core = lax.axis_index("xl"), lax.axis_index("xh"), lax.axis_index("core")
     place = {"y": lax.axis_index("y"), "z": lax.axis_index("z")}
+    my_y = place["y"]
     half = g_ref.shape[3] // 2
     quarter = half // 2
     rings = (("z", "y"), ("y", "z"))
@@ -637,25 +584,33 @@
         parts.append(pltpu.make_async_copy(ref, g_ref.at[..., pl.ds(column, cols)], loc.at[n]))
         parts[-1].start()
         column += cols
+    for n, (ref, own) in enumerate(((ups_ref, up_own), (downs_ref, down_own))):
+        parts.append(pltpu.make_async_copy(ref.at[xl], own, loc.at[3 + n]))
+        parts[-1].start()
+    peers = ({"xh": xh, "core": 1 - core}, {"xh": 1 - xh, "core": core}, {"xh": 1 - xh, "core": 1 - core})
     greet(
-        neighbour("xl", 1),
+        *peers,
+        chip_along(1),
+        chip_along(-1),
         *(neighbour("y", step) for step in (1, 2, 3)),
         *(neighbour("z", step) for step in (1, -1)),
     )
     both = slice(0, 2)
-    experts = ((up_ref, up_buf, up_sum, up_out), (down_ref, down_buf, down_sum, down_out))
-    my_y = place["y"]
-    for n, (grads, buf, _, _) in enumerate(experts):
+    ring_stages = ring_reduce_stages(part_ref, *scratch[7:15], sends)
+    feed_stages = reduce_stages(CHUNKS, [feed_ref], *scratch[:7], sends)
+    experts = ((ups_ref, up_own, up_buf, up_sum, up_out), (downs_ref, down_own, down_buf, down_sum, down_out))
+    for n, (grads, _, buf, _, _) in enumerate(experts):
         for step in (2, 1, 3, 0):
-            target = mod4(my_y + step)
             sends(
-                grads.at[1 - xl, target],
+                grads.at[1 - xl, mod4(my_y + step)],
                 buf.at[step],
                 ex.at[n, step],
                 ey.at[n, step],
                 neighbour("xl", 1),
             )
-    for part in parts:
+    next(ring_stages)
+    next(feed_stages)
+    for part in parts[:3]:
         part.wait()
 
     def grad_ref(h, first, second, start):
@@ -691,6 +646,8 @@
                     r_r.at[h, d, k, 0],
                     neighbour(rings[h][1], way),
                 )
+    next(ring_stages)
+    next(feed_stages)
     for k in range(4):
         for h in (0, 1):
             second = place[rings[h][1]]
@@ -708,17 +665,20 @@
                     r_r.at[h, d, k, 1],
                     neighbour(rings[h][1], way),
                 )
-    for n, (grads, buf, total, result) in enumerate(experts):
+    total = next(ring_stages)
+    for part in parts[3:]:
+        part.wait()
+    for n, (_, own, buf, summed, result) in enumerate(experts):
         for step in (2, 1, 3, 0):
             target = mod4(my_y + step)
             arrived(buf.at[step], ey.at[n, step])
-            value = (grads[xl, target].astype(F32) + buf[step].astype(F32)).astype(BF16)
+            value = (own[target].astype(F32) + buf[step].astype(F32)).astype(BF16)
             if step == 0:
                 result[my_y] = value
             else:
-                total[step - 1] = value
+                summed[step - 1] = value
                 sends(
-                    total.at[step - 1],
+                    summed.at[step - 1],
                     result.at[my_y],
                     es.at[n, step - 1],
                     er.at[n, step - 1],
@@ -767,6 +727,15 @@
                         rb_r.at[h, d, 1],
                         device,
                     )
+    rows_half = x_ref.shape[0] // 2
+    for part in (0, 1):
+        rows = slice(part * rows_half, (part + 1) * rows_half)
+        x = x_ref[rows, :].astype(F32)
+        inverse = lax.rsqrt(jnp.mean(x * x, 1, keepdims=True) + EPSILON)
+        normed = x * inverse
+        dscaled = total(part) * gain_ref[...]
+        mean = jnp.mean(dscaled * normed, 1, keepdims=True)
+        dinput_ref[rows, :] = dmiddle_ref[rows, :] + inverse * (dscaled - normed * mean)
     for h in (0, 1):
         for d in (0, 1):
             arrived(rb_buf.at[h, d, both, pl.ds((1 - d) * quarter, quarter)], rb_r.at[h, d, 0])
@@ -782,30 +751,48 @@
     for h in (0, 1):
         arrived(c_buf.at[h], c_r.at[h])
         out_ref[1 - xl, h * half : (h + 1) * half, :] = c_buf[h].astype(F32)
-    for n, (_, _, _, result) in enumerate(experts):
+    first, last = qkv_ref.shape[-1], qkv_ref.shape[-1] + small_ref.shape[-1]
+    small_own[...] = out_ref[0, :, first:last] + out_ref[1, :, first:last]
+    for n, peer in enumerate(peers):
+        sends(small_own, small_buf.at[n], small_s.at[n], small_r.at[n], peer)
+    feed = next(feed_stages)
+    step = x_ref.shape[0] // CHUNKS
+    for n in range(CHUNKS):
+        rows = slice(n * step, (n + 1) * step)
+        output_ref[rows, :] = (middle_ref[rows, :] + feed(0, n)).astype(BF16)
+    for n, (_, _, _, _, result) in enumerate(experts):
         for step in (1, 3, 2):
             arrived(result.at[mod4(my_y - step)], er.at[n, step - 1])
+    for n in range(3):
+        arrived(small_buf.at[n], small_r.at[n])
+    small_out[...] = (small_own[...] + small_buf[1]) + (small_buf[0] + small_buf[2])
     sends.finish()
 
 
-def scatter_dp(grads, ups, downs):
+def finish(grads, ups, downs, part, feed, x, middle, dmiddle, gain):
     rows, cols = grads[0].shape[0], sum(grad.shape[1] for grad in grads)
     share = rows // 32
     half, quarter = share // 2, share // 4
     dma = pltpu.SemaphoreType.DMA
     up_cols, down_cols = ups.shape[1], downs.shape[1]
+    small = (share, grads[1].shape[1])
+    own_rows, width = x.shape
+    anywhere = pl.BlockSpec(memory_space=pl.ANY)
     return pl.pallas_call(
-        scatter_body,
+        finish_body,
         out_shape=[
             jax.ShapeDtypeStruct((2, share, cols), F32),
             jax.ShapeDtypeStruct((4, share, up_cols), BF16),
             jax.ShapeDtypeStruct((4, share, down_cols), BF16),
+            jax.ShapeDtypeStruct((own_rows, width), BF16),
+            jax.ShapeDtypeStruct((own_rows, width), F32),
+            jax.ShapeDtypeStruct(small, F32),
         ],
-        in_specs=[pl.BlockSpec(memory_space=pl.ANY)] * 3 + vmem(2),
-        out_specs=vmem(3),
+        in_specs=[anywhere] * 5 + vmem(6),
+        out_specs=vmem(6),
         scratch_shapes=[
             pltpu.VMEM((4, 2, 4, share, cols), BF16),
-            dma((3,)),
+            dma((5,)),
             pltpu.VMEM((2, 2, 4, 2, quarter, cols), BF16),
             pltpu.VMEM((2, 2, 4, 2, half, cols), BF16),
             pltpu.VMEM((2, 2, 2, quarter, cols), BF16),
@@ -823,26 +810,266 @@
             dma((2,)),
             pltpu.VMEM((4, share, up_cols), BF16),
             pltpu.VMEM((4, share, down_cols), BF16),
+            pltpu.VMEM((4, share, up_cols), BF16),
+            pltpu.VMEM((4, share, down_cols), BF16),
             pltpu.VMEM((3, share, up_cols), BF16),
             pltpu.VMEM((3, share, down_cols), BF16),
             dma((2, 4)),
             dma((2, 4)),
             dma((2, 3)),
             dma((2, 3)),
-        ],
+            pltpu.VMEM(small, F32),
+            pltpu.VMEM((3, *small), F32),
+            dma((3,)),
+            dma((3,)),
+        ]
+        + reduce_scratch(1, own_rows, width)
+        + ring_reduce_scratch(own_rows, width),
         compiler_params=pltpu.CompilerParams(
-            collective_id=5, has_side_effects=True, vmem_limit_bytes=56 * MIB
+            collective_id=5, has_side_effects=True, vmem_limit_bytes=60 * MIB
         ),
-        name="scatter_grads",
+        name="finish",
     )(
         *(grad.reshape(4, 2, 4, share, grad.shape[1]) for grad in grads),
         ups.reshape(2, 4, share, up_cols),
         downs.reshape(2, 4, share, down_cols),
+        part.reshape(2, 2, 2, own_rows, width),
+        feed.reshape(4, own_rows, width),
+        x,
+        middle,
+        dmiddle,
+        gain[None],
     )
 
 
 def dot(a, b, dims):
     return lax.dot_general(a, b, (dims, ((), ())), preferred_element_type=F32)
+
+
+LANES = 128
+WIDE = 256
+
+
+def experts_body(
+    rows_ref, grad_ref, up_ref, down_ref, gate_ref, up_rows_ref,
+    djoined_out, hidden_out, gated_out, dgate_out, dunit_out, raw, djoined,
+):
+    j = pl.program_id(0)
+    chunks = djoined.shape[1] // WIDE
+
+    @pl.when(j == 0)
+    def _():
+        dgate_out[...] = jnp.zeros_like(dgate_out)
+
+    @pl.when((j < chunks) & (lax.rem(j, 2) == 0))
+    def _():
+        pair = dot(grad_ref[...], down_ref[...], ((1,), (0,)))
+        raw[0] = pair[:, :LANES]
+        raw[1] = pair[:, LANES:]
+
+    @pl.when(j < chunks)
+    def _():
+        joined = dot(rows_ref[...], up_ref[...], ((1,), (0,)))
+        gate_pre, linear = joined[:, :LANES], joined[:, LANES:]
+        sigmoid = jax.nn.sigmoid(gate_pre)
+        silu = gate_pre * sigmoid
+        hidden = silu * linear
+        dhidden = raw[lax.rem(j, 2)]
+        gate = gate_ref[...]
+        dgate_out[...] += hidden * dhidden
+        dhidden = dhidden * gate
+        hidden_out[...] = hidden.astype(BF16)
+        gated_out[...] = (hidden * gate).astype(BF16)
+        dgate_pre = (dhidden * linear * (sigmoid + silu * (1.0 - sigmoid))).astype(BF16)
+        dlinear = (dhidden * silu).astype(BF16)
+        djoined_out[:, :LANES] = dgate_pre
+        djoined_out[:, LANES:] = dlinear
+        at = pl.multiple_of(j * WIDE, WIDE)
+        djoined[:, pl.ds(at, LANES)] = dgate_pre
+        djoined[:, pl.ds(at + LANES, LANES)] = dlinear
+
+    @pl.when(j >= chunks)
+    def _():
+        dunit_out[...] = dot(djoined[...], up_rows_ref[...], ((1,), (1,))).astype(BF16)
+
+
+def experts(rows, grads, up, down, gates):
+    count, width = grads.shape
+    hidden = down.shape[1]
+    chunks = hidden // LANES
+    steps = chunks + width // WIDE
+
+    def chunk(j):
+        return jnp.minimum(j, chunks - 1)
+
+    def tail(j):
+        return jnp.maximum(j - chunks, 0)
+
+    return pl.pallas_call(
+        experts_body,
+        grid=(steps,),
+        in_specs=[
+            pl.BlockSpec((count, width), lambda j: (0, 0)),
+            pl.BlockSpec((count, width), lambda j: (0, 0)),
+            pl.BlockSpec((width, WIDE), lambda j: (0, chunk(j))),
+            pl.BlockSpec((width, WIDE), lambda j: (0, chunk(j) // 2)),
+            pl.BlockSpec((count, 1), lambda j: (0, 0)),
+            pl.BlockSpec((WIDE, 2 * hidden), lambda j: (tail(j), 0)),
+        ],
+        out_specs=[
+            pl.BlockSpec((count, WIDE), lambda j: (0, chunk(j))),
+            pl.BlockSpec((count, LANES), lambda j: (0, chunk(j))),
+            pl.BlockSpec((count, LANES), lambda j: (0, chunk(j))),
+            pl.BlockSpec((count, LANES), lambda j: (0, 0)),
+            pl.BlockSpec((count, WIDE), lambda j: (0, tail(j))),
+        ],
+        out_shape=[
+            jax.ShapeDtypeStruct((count, 2 * hidden), BF16),
+            jax.ShapeDtypeStruct((count, hidden), BF16),
+            jax.ShapeDtypeStruct((count, hidden), BF16),
+            jax.ShapeDtypeStruct((count, LANES), F32),
+            jax.ShapeDtypeStruct((count, width), BF16),
+        ],
+        scratch_shapes=[
+            pltpu.VMEM((2, count, LANES), F32),
+            pltpu.VMEM((count, 2 * hidden), BF16),
+        ],
+        compiler_params=pltpu.CompilerParams(vmem_limit_bytes=60 * MIB),
+        name="experts",
+    )(rows, grads, up, down, gates, up)
+
+
+def return_body(
+    dunit_ref, dgate_ref, rows_ref, djoined_ref, hidden_ref, down_ref,
+    dunit_out, dgate_out, up_out, branch_out,
+    dunit_own, dgate_own, rows, djoined, hidden, down, dunit_buf, dgate_buf, dunit_sum, dgate_sum, block,
+    loc, core_s, core_r, far_s, far_r, out_sem,
+):
+    y, core = lax.axis_index("y"), lax.axis_index("core")
+    half = dunit_ref.shape[1] // 2
+    sends = Sends()
+    greet(neighbour("core", 1), *(neighbour("y", step) for step in (1, 2, 3)))
+    mine = pl.ds(pl.multiple_of(core * half, half), half)
+    theirs = pl.ds(pl.multiple_of((1 - core) * half, half), half)
+    order = (2, 1, 3, 0)
+    kinds = (
+        (dunit_ref, dunit_own, dunit_buf, dunit_sum, dunit_out),
+        (dgate_ref, dgate_own, dgate_buf, dgate_sum, dgate_out),
+    )
+    for step in order:
+        for n, (whole, _, buf, _, _) in enumerate(kinds):
+            sends(
+                whole.at[mod4(y + step), theirs],
+                buf.at[step],
+                core_s.at[n, step],
+                core_r.at[n, step],
+                neighbour("core", 1),
+            )
+    own = []
+    for step in order:
+        for n, (whole, kept, _, _, _) in enumerate(kinds):
+            copy = pltpu.make_async_copy(whole.at[mod4(y + step), mine], kept.at[step], loc.at[n, step])
+            copy.start()
+            own.append(copy)
+    loads = []
+    for n, (src, dst) in enumerate(
+        ((rows_ref.at[:, pl.ds(0, rows.shape[1])], rows), (djoined_ref, djoined), (hidden_ref, hidden), (down_ref, down))
+    ):
+        loads.append(pltpu.make_async_copy(src, dst, loc.at[2, n]))
+        loads[-1].start()
+    for copy in own:
+        copy.wait()
+    for step in order:
+        for n, (_, kept, buf, summed, result) in enumerate(kinds):
+            arrived(buf.at[step], core_r.at[n, step])
+            value = (kept[step].astype(F32) + buf[step].astype(F32)).astype(summed.dtype)
+            if step == 0:
+                result[y] = value
+            else:
+                summed[step - 1] = value
+                sends(
+                    summed.at[step - 1],
+                    result.at[y],
+                    far_s.at[n, step - 1],
+                    far_r.at[n, step - 1],
+                    neighbour("y", step),
+                )
+    for load in loads:
+        load.wait()
+    blocks = up_out.shape[0] // WIDE
+
+    @pl.loop(0, blocks)
+    def _(j):
+        at = pl.ds(pl.multiple_of(j * WIDE, WIDE), WIDE)
+        slot = lax.rem(j, 2)
+
+        @pl.when(j >= 2)
+        def _():
+            pltpu.make_async_copy(block.at[slot], up_out.at[at], out_sem.at[slot]).wait()
+
+        block[slot] = dot(rows[:, at], djoined[...], ((0,), (0,))).astype(BF16)
+        pltpu.make_async_copy(block.at[slot], up_out.at[at], out_sem.at[slot]).start()
+
+    @pl.loop(0, blocks)
+    def _(j):
+        at = pl.ds(pl.multiple_of(j * WIDE, WIDE), WIDE)
+        branch_out[:, at] = dot(hidden[...], down[at, :], ((1,), (1,))).astype(BF16)
+
+    for slot in (0, 1):
+        pltpu.make_async_copy(block.at[slot], up_out.at[pl.ds(0, WIDE)], out_sem.at[slot]).wait()
+    for n, (_, _, _, _, result) in enumerate(kinds):
+        for step in (1, 3, 2):
+            arrived(result.at[mod4(y - step)], far_r.at[n, step - 1])
+    sends.finish()
+
+
+def return_rows(dunit, dgate, rows, djoined, hidden, down):
+    _, slots, width = dunit.shape
+    half = slots // 2
+    count, wide = djoined.shape
+    hidden_cols = hidden.shape[1]
+    dma = pltpu.SemaphoreType.DMA
+    anywhere = pl.BlockSpec(memory_space=pl.ANY)
+
+    def pair(places):
+        return [
+            pltpu.VMEM((places, half, width), BF16),
+            pltpu.VMEM((places, half, dgate.shape[2]), F32),
+        ]
+
+    return pl.pallas_call(
+        return_body,
+        out_shape=[
+            jax.ShapeDtypeStruct((4, half, width), BF16),
+            jax.ShapeDtypeStruct((4, half, dgate.shape[2]), F32),
+            jax.ShapeDtypeStruct((width, wide), BF16),
+            jax.ShapeDtypeStruct((count, width), BF16),
+        ],
+        in_specs=[anywhere] * 6,
+        out_specs=vmem(2) + [anywhere] + vmem(1),
+        scratch_shapes=pair(4)
+        + [
+            pltpu.VMEM((count, width), BF16),
+            pltpu.VMEM((count, wide), BF16),
+            pltpu.VMEM((count, hidden_cols), BF16),
+            pltpu.VMEM((width, hidden_cols), BF16),
+        ]
+        + pair(4)
+        + pair(3)
+        + [
+            pltpu.VMEM((2, WIDE, wide), BF16),
+            dma((3, 4)),
+            dma((2, 4)),
+            dma((2, 4)),
+            dma((2, 3)),
+            dma((2, 3)),
+            dma((2,)),
+        ],
+        compiler_params=pltpu.CompilerParams(
+            collective_id=3, has_side_effects=True, vmem_limit_bytes=62 * MIB
+        ),
+        name="return_rows",
+    )(dunit, dgate, rows, djoined, hidden, down)
 
 
 def attention_body(
@@ -1003,13 +1230,6 @@
 def normalize(activations):
     inverse = lax.rsqrt(jnp.mean(activations * activations, -1, keepdims=True) + EPSILON)
     return activations * inverse, inverse
-
-
-def swiglu_back(dhidden, gate_pre, linear):
-    sigmoid_pre = jax.nn.sigmoid(gate_pre)
-    dgate_pre = dhidden * linear * sigmoid_pre * (1.0 + gate_pre * (1.0 - sigmoid_pre))
-    dlinear = dhidden * gate_pre * sigmoid_pre
-    return jnp.concatenate([dgate_pre, dlinear], 1).astype(BF16)
 
 
 def reorder(rows):
@@ -1067,7 +1287,9 @@
     grad_all = lax.all_gather(out_grad, TP, axis=0, tiled=True)
     marks = lax.all_gather(jnp.concatenate([segments[:, None], att_routes], 1), "xl", axis=0)
     weights, up_parts, down_parts = gather_dp(
-        own_att, gate_up.reshape(mlp_count, share, -1), jnp.swapaxes(down_proj, 1, 2)
+        own_att,
+        jnp.swapaxes(gate_up.reshape(mlp_count, share, 2, -1, LANES), 2, 3).reshape(mlp_count, share, -1),
+        jnp.swapaxes(down_proj, 1, 2),
     )
     up_whole = lax.all_gather(
         up_parts.reshape(2 * mlp_count * share, -1), "z", axis=0, tiled=True
@@ -1119,48 +1341,33 @@
     rows_out = dot(pick_rows, extended, ((1,), (0,))).astype(BF16)
     rows_ext = rows_to_experts(rows_out.reshape(mlp_count, CAP, width + 128))
     rows_ext = rows_ext.reshape(mlp_count * CAP, width + 128)
-    rows_in = rows_ext[:, :width]
     gates_ext = rows_ext[:, width : width + 2 * mlp_count].astype(F32)
     mine = (jnp.arange(2 * mlp_count) % mlp_count == lax.axis_index("y")).astype(F32)
     gates_in = jnp.sum(gates_ext * mine, 1, keepdims=True)
-    joined = dot(rows_in, up_whole, ((1,), (0,)))
-    gate_pre = joined[:, :hidden_local]
-    linear = joined[:, hidden_local:]
-    hidden_f32 = jax.nn.silu(gate_pre) * linear
-    hidden = hidden_f32.astype(BF16)
-    dhidden = dot(grad_in, down_whole, ((1,), (0,)))
-    dgate_in = jnp.sum(hidden_f32 * dhidden, 1, keepdims=True)
-    djoined = swiglu_back(dhidden * gates_in, gate_pre, linear)
-    grad_down_whole = dot(
-        grad_in, (hidden_f32 * gates_in).astype(BF16), ((0,), (0,))
-    ).astype(BF16)
-    djoined, grad_down_whole = lax.optimization_barrier((djoined, grad_down_whole))
+    djoined, hidden, gated, dgate_part, dunit_part = experts(
+        rows_ext, grad_in, up_whole, down_whole, gates_in
+    )
+    grad_down_whole = dot(grad_in, gated, ((0,), (0,))).astype(BF16)
+    dunit_part, grad_down_whole = lax.optimization_barrier((dunit_part, grad_down_whole))
     grad_down_sum = lax.psum_scatter(grad_down_whole, "z", scatter_dimension=0, tiled=True)
-    dunit_part = dot(djoined, up_whole, ((1,), (1,))).astype(BF16)
-    dgate_high = dgate_in.astype(BF16)
-    dgate_low = (dgate_in - dgate_high.astype(F32)).astype(BF16)
-    dunit_ext = jnp.concatenate(
-        [dunit_part, pad_to(jnp.concatenate([dgate_high, dgate_low], 1), 128)], 1
-    )
-    dunit_back = lax.all_to_all(dunit_ext.reshape(mlp_count, CAP, width + 128), "y", 0, 0, tiled=True)
-    djoined, dunit_ext = lax.optimization_barrier((djoined, dunit_ext))
-    grad_up_whole = dot(rows_in, djoined, ((0,), (0,))).astype(BF16)
-    hidden, grad_up_whole = lax.optimization_barrier((hidden, grad_up_whole))
+    dunit_back, dgate_back, grad_up_whole, branch_part = return_rows(
+        dunit_part.reshape(mlp_count, CAP, width),
+        dgate_part.reshape(mlp_count, CAP, LANES),
+        rows_ext,
+        djoined,
+        hidden,
+        down_whole,
+    )
     grad_up_sum = lax.psum_scatter(grad_up_whole, "z", scatter_dimension=0, tiled=True)
-    branch_part = dot(hidden, down_whole, ((1,), (1,))).astype(BF16)
-    dunit_back, branch_part = lax.optimization_barrier((dunit_back, branch_part))
     branch_back = lax.all_to_all(
         branch_part.reshape(mlp_count, CAP, width), "y", 0, 0, tiled=True
     ).reshape(mlp_count * CAP, width)
-    dunit_back = dunit_back.reshape(mlp_count * CAP, width + 128)
-    dgate_slots = (
-        dunit_back[:, width : width + 1].astype(F32) + dunit_back[:, width + 1 : width + 2].astype(F32)
-    ).reshape(mlp_count, CAP, 1)
-    dgate_two = jnp.sum(pick.astype(F32) * dgate_slots, 1).T
+    pick_half = lax.dynamic_slice_in_dim(pick, lax.axis_index("core") * (CAP // 2), CAP // 2, 1)
+    dgate_two = jnp.sum(pick_half.astype(F32) * jnp.sum(dgate_back, -1, keepdims=True), 1).T
     dlogit_mlp = router_back(dgate_two, weights_mlp, onehot_mlp)
-    dunit_two = dot(pick_rows, dunit_back[:, :width], ((0,), (0,))) + dot(
-        dlogit_mlp, router_two, ((1,), (1,))
-    )
+    dunit_two = dot(
+        pick_half.reshape(-1, tokens), dunit_back.reshape(-1, width), ((0,), (0,))
+    ) + dot(dlogit_mlp, router_two, ((1,), (1,)))
     grad_rmlp = dot(unit_two, dlogit_mlp, ((0,), (0,)))
     dmiddle, grad_gain_two, dattention = middle_back(
         dunit_two.astype(BF16), middle, out_grad, gain_two
@@ -1185,7 +1392,7 @@
     )
     gate_slots = jnp.sum(pick.astype(F32) * gate_mlp.T[:, None, :], -1).reshape(mlp_count * CAP, 1)
     feed = dot(pick_rows, (branch_back.astype(F32) * gate_slots).astype(BF16), ((0,), (0,)))
-    summed_att, ups_sum, downs_sum = scatter_dp(
+    summed_att, ups_sum, downs_sum, output, grad_input, small_sum = finish(
         (
             dot(unit_one, grad_qkv, ((0,), (0,))).astype(BF16),
             pad_to(grad_small, 128).astype(BF16),
@@ -1193,6 +1400,12 @@
         ),
         grad_up_sum,
         grad_down_sum,
+        dunit_one.astype(BF16),
+        feed.astype(BF16),
+        inputs,
+        middle,
+        dmiddle,
+        gain_one,
     )
     grad_kv = jnp.transpose(
         summed_att[:, :, : 2 * part].reshape(2, share, 2, part), (1, 2, 0, 3)
@@ -1203,19 +1416,12 @@
     grad_output = jnp.transpose(
         summed_att[:, :, out_at:].reshape(2, share, att_count, part), (2, 0, 3, 1)
     ).reshape(att_count, inner, share)
-    output, grad_input, small_sum = last_sums(
-        dunit_one.astype(BF16),
-        feed.astype(BF16),
-        inputs,
-        middle,
-        dmiddle,
-        gain_one,
-        jnp.sum(summed_att[:, :, small_at:out_at], 0),
-    )
     output = reorder(output)
     grad_input = reorder(grad_input)
 
-    grads_up = ups_sum.astype(F32).reshape(mlp_count, share, 2, hidden_local)
+    grads_up = jnp.swapaxes(
+        ups_sum.astype(F32).reshape(mlp_count, share, -1, 2, LANES), 2, 3
+    ).reshape(mlp_count, share, 2, hidden_local)
     grads_down = jnp.swapaxes(downs_sum.astype(F32), 1, 2)
     return (
         output,

time: 747 us -> 686 us (0.918)
  matrix products: 200 us -> 95.3 us
  Pallas kernels: 382 us -> 467 us
  waiting for transfers between devices: 48.5 us -> 17.1 us
  other arithmetic: 29.7 us -> 12.5 us
  local copies, waits for them, and re-layouts: 41.4 us -> 57.8 us
    dot_general x21 -> x16, matrix products: 200 us -> 95.3 us  [dot(): return lax.dot_general(a, b, (dims, ((), ())), preferred_element_type=F32)]
    pallas_call x2 -> x3, Pallas kernels: 124 us -> 210 us  [the longest x1 111 us: finish(): pl.pallas_call(finish_body, out_shape=[jax.ShapeDtypeStruct((2, share, co...]
    all_to_all x1 -> x0, waiting for transfers between devices: 47.8 us -> none  [on_device(): lax.all_to_all(dunit_ext.reshape(mlp_count, CAP, width + 128), 'y', 0, 0,...]
    reduce_scatter x1, waiting for transfers between devices: 0.02 us -> 11.4 us  [on_device(): lax.psum_scatter(grad_up_whole, 'z', scatter_dimension=0, tiled=True)]
    concatenate x3 -> x0, other arithmetic: 9.44 us -> none  [the longest x1 6.47 us: swiglu_back(): return jnp.concatenate([dgate_pre, dlinear], 1).astype(BF16)]
    unnamed x138 -> x104, local copies, waits for them, and re-layouts: 18 us -> 19.8 us
  transfers between devices with their start and end apart: 9 -> 8, of which waited for: 1 -> 2; matrix products, arithmetic and copies ran while one was open for 27% -> 17% of each run, Pallas kernels for 35% -> 44%
where the time goes in v4:
time: 686 us; the launch traced here: 679 us
  Pallas kernels  467 us (68%)
  matrix products  95.3 us (14%)
  local copies, waits for them, and re-layouts  57.8 us (8%)
  waiting for transfers between devices  17.1 us (2%)
  between operations  15.4 us (2%)
  other arithmetic  12.5 us (2%)
  starting transfers between devices  10.5 us (2%)
    pallas_call x1, Pallas kernels, finish(): pl.pallas_call(finish_body, out_shape=[jax.ShapeDtypeStruct((2, share, co...  111 us
    pallas_call x1, Pallas kernels, gather_dp(): pl.pallas_call(gather_body, out_shape=[jax.ShapeDtypeStruct((4, 2, 4, row...  96.1 us
    dot_general x16, matrix products, dot(): return lax.dot_general(a, b, (dims, ((), ())), preferred_element_type=F32)  95.3 us
    pallas_call x1, Pallas kernels, experts(): pl.pallas_call(experts_body, grid=(steps,), in_specs=[pl.BlockSpec((count...  55.5 us
    pallas_call x1, Pallas kernels, rows_to_experts(): pl.pallas_call(rows_body, out_shape=jax.ShapeDtypeStruct(rows.shape, rows...  46.6 us
    pallas_call x1, Pallas kernels, return_rows(): pl.pallas_call(return_body, out_shape=[jax.ShapeDtypeStruct((4, half, wid...  43.3 us
    pallas_call x1, Pallas kernels, middle_and_unit(): pl.pallas_call(middle_body, out_shape=[jax.ShapeDtypeStruct((rows, width)...  38.9 us
    pallas_call x1, Pallas kernels, middle_back(): pl.pallas_call(back_body, out_shape=[jax.ShapeDtypeStruct((rows, width),...  38.6 us
  transfers between devices with their start and end apart: 8, of which 2 were waited for; matrix products, arithmetic and copies ran while one was open for 17% of the time, Pallas kernels for 44%

profile of v4, /device:TPU:1, one launch (start us, length us, event | category | flops | bytes accessed | tf_op | source)
XLA Modules:
  0.0 679.1 jit_solution(3925260496322541100)
XLA Ops:
  7.2 1.3 copy.164
  9.5 1.3 copy.149
  12.0 1.5 copy.156
  14.5 2.2 copy.157
  16.8 1.5 reshape.441.ups_ref
  21.3 96.1 %gather_weights.1 = (bf16[4,2,4,64,2176]{4,3,2,1,0:T(8,128)(2,1)}, bf16[2,4,64,2816]{3,2,1,0:T(8,128)(2,1)}, bf16[2,4,64,1408]{3,2,1,0:T(8,128)(2,1)}) custom-call(bf16[2,64,2176]{2,1,0:T(8,128)(2,1)} %pad_maximum_fusion.x_ref, bf16[4,64,2816]{2,1,0:T(8,128)(2,1)} %reshape.441.ups_ref, bf16[4,64,1408]{2,1,0:T(8,128)(2,1)} %bitcast.167), custom_call_target="tpu_custom_call" | custom-call | tf_op jit(solution)/shard_map/gather_weights/pallas_call | solution.py:182
  119.5 3.5 all-gather
  125.3 1.9 fusion.37
  128.3 6.5 convolution_convert_fusion.3
  134.8 5.1 all-to-all-start
  140.0 3.2 fusion.4
  143.5 9.9 %fusion.10.k_ref.v_ref.q0.q1.q2 = f32[1024,1408]{1,0:T(8,128)S(1)} fusion(bf16[2048,2176]{1,0:T(8,128)(2,1)} %bitcast.172, bf16[1024,2048]{1,0:T(8,128)(2,1)S(1)} %copy-done.21, f32[2048]{0:T(1024)S(1)} %bitcast.193, f32[1024]{0:T(1024)S(1)} %add_rsqrt_fusion), kind=kOutput, calls=%fused_computation.18 | convolution fusion | flops 5913968640 | bytes 15740928 | tf_op jit(solution)/shard_map/dot_general | solution.py:846
  153.4 2.5 copy-done.19
  159.4 23.5 %attention_forward.1 = (bf16[1024,256]{1,0:T(8,128)(2,1)S(1)}, bf16[1024,256]{1,0:T(8,128)(2,1)S(1)}, bf16[1024,768]{1,0:T(8,128)(2,1)S(1)}, bf16[1024,768]{1,0:...) custom-call(f32[1024,1408]{1,0:T(8,128)} %copy-done.19, f32[1024,1408]{1,0:T(8,128)} %copy-done.19, ...), custom_call_target="tpu_custom_call" | custom-call | tf_op jit(solution)/shard_map/attention_forward/pallas_call | solution.py:1128
  182.9 6.2 convolution_convert_fusion.4
  189.1 38.9 %middle_and_unit.1 = (f32[128,2048]{1,0:T(8,128)S(1)}, bf16[4,128,2048]{2,1,0:T(8,128)(2,1)S(1)}) custom-call(bf16[2,2,2,128,2048]{4,3,2,1,0:T(8,128)(2,1)S(1)} %bitcast.130, bf16[128,2048]{1,0:T(8,128)(2,1)S(1)} %copy-done, f32[1,2048]{1,0:T(1,128)S(1)} %get-tuple-element.145.gain_ref), custom_call_target="tpu_custom_call" | custom-call | tf_op jit(solution)/shard_map/middle_and_unit/pallas_call | solution.py:455
  228.1 1.3 copy-done.1
  229.4 1.9 fusion.35
  231.6 6.7 convolution_convert_fusion
  238.3 46.6 %rows_to_experts.1 = bf16[4,320,2176]{2,1,0:T(8,128)(2,1)} custom-call(bf16[4,320,2176]{2,1,0:T(8,128)(2,1)} %bitcast.140), custom_call_target="tpu_custom_call" | custom-call | tf_op jit(solution)/shard_map/rows_to_experts/pallas_call | solution.py:551
  284.9 1.2 multiply_reduce_fusion.2
  287.2 5.1 all-gather.10.cloned.1.call-done.up_ref.up_rows_ref
  292.3 55.5 %experts.1 = (bf16[1280,2816]{1,0:T(8,128)(2,1)}, bf16[1280,1408]{1,0:T(8,128)(2,1)}, bf16[1280,1408]{1,0:T(8,128)(2,1)}, f32[1280,128]{1,0:T(8,128)}, bf16[1280,2048]{1,0:T(8,128)(2,1)}) custom-call(bf16[1280,2176]{1,0:T(8,128)(2,1)} %bitcast.136, bf16[1280,2048]{1,0:T(8,128)(2,1)} %bitcast.28.grad_ref, ...), custom_call_target="tpu_custom_call" | custom-call | tf_op jit(solution)/shard_map/experts/pallas_call | solution.py:908
  347.8 13.0 %convolution_convert_fusion.2 = bf16[2048,1408]{1,0:T(8,128)(2,1)} fusion(bf16[1280,2048]{1,0:T(8,128)(2,1)} %bitcast.28.grad_ref, bf16[1280,1408]{1,0:T(8,128)(2,1)} %get-tuple-element.54), kind=kOutput, calls=%fused_computation.10 | convolution fusion | flops 7384858624 | bytes 14614528 | tf_op jit(solution)/shard_map/dot_general | solution.py:846
  360.9 43.3 %return_rows.1 = (bf16[4,160,2048]{2,1,0:T(8,128)(2,1)}, f32[4,160,128]{2,1,0:T(8,128)}, bf16[2048,2816]{1,0:T(8,128)(2,1)}, bf16[1280,2048]{1,0:T(8,128)(2,1)}) custom-call(bf16[4,320,2048]{2,1,0:T(8,128)(2,1)} %bitcast.144, f32[4,320,128]{2,1,0:T(8,128)} %bitcast.168, bf16[1280,2176]{1,0:T(8,128)(2,1)} %bitcast.137, ...), custom_call_target="tpu_custom_call" | custom-call | tf_op jit(solution)/shard_map/return_rows/pallas_call | solution.py:1040
  406.2 1.5 iota_compare_fusion.2
  408.2 5.2 all-to-all-start.1
  413.9 2.1 fusion.33
  416.1 3.1 fusion.13
  419.2 38.6 %middle_back.1 = (f32[128,2048]{1,0:T(8,128)S(1)}, f32[1,2048]{1,0:T(1,128)S(1)}, bf16[2,2,2,128,2048]{4,3,2,1,0:T(8,128)(2,1)S(1)}) custom-call(bf16[4,128,2048]{2,1,0:T(8,128)(2,1)S(1)} %bitcast.131, f32[128,2048]{1,0:T(8,128)S(1)} %copy-done.10, bf16[128,2048]{1,0:T(8,128)(2,1)S(1)} %copy-done.12, f32[1,2048]{1,0:T(1,128)S(1)} %get-tuple-element.145.gain_ref), custom_call_target="tpu_custom_call" | custom-call | tf_op jit(solution)/shard_map/middle_back/pallas_call | solution.py:502
  457.9 8.9 %fusion.19.h0.h1.h2 = f32[1024,768]{1,0:T(8,128)} fusion(bf16[1024,2048]{1,0:T(8,128)(2,1)S(1)} %bitcast.133, bf16[2048,2176]{1,0:T(8,128)(2,1)} %bitcast.176), kind=kOutput, calls=%fused_computation.32 | convolution fusion | flops 3221225472 | bytes 10485760 | tf_op jit(solution)/shard_map/dot_general | solution.py:846
  466.8 13.2 %attention_back.1 = (bf16[1024,1280]{1,0:T(8,128)(2,1)}, f32[1024,128]{1,0:T(8,128)S(1)}) custom-call(bf16[1024,256]{1,0:T(8,128)(2,1)S(1)} %copy-done.15, bf16[1024,256]{1,0:T(8,128)(2,1)S(1)} %copy-done.17, bf16[1024,768]{1,0:T(8,128)(2,1)S(1)} %get-tuple-element.47.q0.q1.q2, bf16[1024,768]{1,0:T(8,128)(2,1)S(1)} %get-tuple-element.47.q0.q1.q2, ...), custom_call_target="tpu_custom_call" | custom-call | tf_op jit(solution)/shard_map/attention_back/pallas_call | solution.py:1193
  480.6 12.7 %fusion.58 = (bf16[1024,2048]{1,0:T(8,128)(2,1)}, bf16[2048]{0:T(1024)(128)(2,1)S(1)}) fusion(f32[1024]{0:T(1024)S(1)} %add_rsqrt_fusion, bf16[1024,2048]{1,0:T(8,128)(2,1)} %all-gather.6.cloned.1.call-done, bf16[2048,2176]{1,0:T(8,128)(2,1)} %bitcast.177, bf16[1024,3]{1,0:T(8,128)(2,1)S(1)} %copy.170, bf16[1024,1280]{1,0:T(8,128)(2,1)} %get-tuple-element.64), kind=kOutput, calls=%fused_computation.124 | convolution fusion | flops 5924714496 | bytes 16791552 | tf_op jit(solution)/shard_map/dot_general | solution.py:846
  496.2 7.6 %convolution_convert_fusion.5 = bf16[2048,768]{1,0:T(8,128)(2,1)} fusion(bf16[1024,2048]{1,0:T(8,128)(2,1)} %bitcast.134, bf16[1024,768]{1,0:T(8,128)(2,1)S(1)} %copy-done.42), kind=kOutput, calls=%fused_computation.27 | convolution fusion | flops 3222798336 | bytes 8912896 | tf_op jit(solution)/shard_map/dot_general | solution.py:846
  503.8 7.9 %convolution_convert_fusion.1 = bf16[2048,1280]{1,0:T(8,128)(2,1)} fusion(bf16[1024,1280]{1,0:T(8,128)(2,1)S(1)} %copy-done.41, bf16[1024,2048]{1,0:T(8,128)(2,1)S(1)} %copy-done.23, f32[2048]{0:T(1024)S(1)} %bitcast.195, f32[1024]{0:T(1024)S(1)} %add_rsqrt_fusion), kind=kOutput, calls=%fused_computation.9 | convolution fusion | flops 5379719168 | bytes 12070912 | tf_op jit(solution)/shard_map/dot_general | solution.py:846
  511.7 7.0 %bitcast_convert_fusion = bf16[512,2048]{1,0:T(8,128)(2,1)} fusion(bf16[4,320,2048]{2,1,0:T(8,128)(2,1)} %all-to-all-done.1, f32[4,320]{1,0:T(4,128)S(1)} %multiply_reduce_fusion, s32[4,512]{1,0:T(4,128)S(1)} %fusion.32), kind=kOutput, calls=%fused_computation.22 | convolution fusion | flops 2693922816 | bytes 7353344 | tf_op jit(solution)/shard_map/dot_general | solution.py:846
  518.7 11.4 %reduce-scatter.3.cloned.1.call-done = bf16[512,2816]{1,0:T(8,128)(2,1)} async-done(((bf16[2048,2816]{1,0:T(8,128)(2,1)}), bf16[512,2816]{1,0:T(8,128)(2,1)}) %reduce-scatter.3.cloned.1.call-update) | async-done | bytes 2883600 | tf_op jit(solution)/shard_map/reduce_scatter | solution.py:1361
  530.0 111.4 %finish.1 = (f32[2,64,2176]{2,1,0:T(8,128)}, bf16[4,64,2816]{2,1,0:T(8,128)(2,1)}, bf16[4,64,1408]{2,1,0:T(8,128)(2,1)}, bf16[128,2048]{1,0:T(8,128)(2,1)}, f32[128,2048]{1,0:T(8,128)}, /*index=5*/f32[64,128]{1,0:T(8,128)}) custom-call(bf16[4,2,4,64,1280]{4,3,2,1,0:T(8,128)(2,1)} %bitcast.141, bf16[4,2,4,64,128]{4,3,2,1,0:T(8,128)(2,1)} %bitcast.156, ...), custom_call_target="tpu_custom_call" | custom-call | tf_op jit(solution)/shard_map/finish/pallas_call | solution.py:781
  641.4 1.9 fusion.59
  644.3 1.4 slice.71
  645.8 1.5 slice_reduce_fusion
  647.3 3.1 reshape.482
  650.4 2.4 copy.199
  652.8 3.3 reshape.479
  656.1 3.8 copy.184
  659.9 1.6 copy.175
  661.6 1.3 copy.182
  666.1 1.3 copy.173
  (201 shorter events, 31.8 us)
Async XLA Ops:
  7.2 121.1 %all-gather.8.cloned.1.call-start = ((), (), s32[]{:S(2)}) async-start(), calls=%async_computation.5 | async-start | bytes 2621440 | tf_op jit(solution)/shard_map/all_gather | solution.py:1287
  9.5 130.5 %all-gather.6.cloned.1.call-start = ((), (), s32[]{:S(2)}) async-start(), calls=%async_computation.4 | async-start | bytes 4718592 | tf_op jit(solution)/shard_map/all_gather | solution.py:1286
  11.9 275.3 %all-gather.12.cloned.1.call-start = ((), (), s32[]{:S(2)}) async-start(), calls=%async_computation.7 | async-start | bytes 7208960 | tf_op jit(solution)/shard_map/all_gather | solution.py:1297
  14.5 5.8 copy-start.36
  14.5 5.8 copy-start.37
  14.5 5.8 copy-start.38
  14.5 5.8 copy-start.39
  16.7 2.9 copy-start.30
  16.8 3.3 copy-start.31
  117.4 2.1 copy-start.34
  117.4 2.1 copy-start.35
  117.4 7.1 %copy-start.33 = (s32[512,2]{0,1:T(2,128)S(1)}, s32[512,2]{0,1:T(2,128)}, u32[]{:S(2)}) copy-start(s32[512,2]{0,1:T(2,128)} %param.17) | copy-start | bytes 12292
  117.5 174.9 %all-gather.10.cloned.1.call-start = ((), (), s32[]{:S(2)}) async-start(), calls=%async_computation.6 | async-start | bytes 14417920 | tf_op jit(solution)/shard_map/all_gather | solution.py:1294
  125.3 9.5 %copy-start.26 = (pred[1280,512]{1,0:T(32,128)(4,1)}, pred[1280,512]{1,0:T(32,128)(4,1)S(1)}, u32[]{:S(2)}) copy-start(pred[1280,512]{1,0:T(32,128)(4,1)S(1)} %bitcast_compare_fusion) | copy-start | bytes 1966084
  127.6 29.7 %copy-start.3 = (f32[1024,128]{1,0:T(8,128)}, f32[1024,128]{1,0:T(8,128)S(1)}, u32[]{:S(2)}) copy-start(f32[1024,128]{1,0:T(8,128)S(1)} %get-tuple-element.153.cos_ref) | copy-start | bytes 1572868
  127.6 29.7 %copy-start.5 = (f32[1024,128]{1,0:T(8,128)}, f32[1024,128]{1,0:T(8,128)S(1)}, u32[]{:S(2)}) copy-start(f32[1024,128]{1,0:T(8,128)S(1)} %get-tuple-element.154.sin_ref) | copy-start | bytes 1572868
  134.8 152.4 %all-to-all-start = ((bf16[4,320,2048]{2,1,0:T(8,128)(2,1)}), bf16[4,320,2048]{2,1,0:T(8,128)(2,1)}, u32[]{:S(2)}, u32[]{:S(2)}) async-start(bf16[4,320,2048]{2,1,0:T(8,128)(2,1)} %bitcast.143), calls=%async_computation | async-start | bytes 10485760 | tf_op jit(solution)/shard_map/all_to_all | solution.py:1310
  139.9 378.8 %reduce-scatter.5.cloned.1.call-start = ((), (), s32[]{:S(2)}) async-start(), calls=%async_computation.9 | async-start | bytes 7208960 | tf_op jit(solution)/shard_map/reduce_scatter | solution.py:1352
  140.0 3.5 copy-start.21
  153.4 2.5 copy-start.19
  182.9 6.2 copy-start.14
  182.9 6.2 copy-start.16
  182.9 6.3 copy-start
  189.1 42.5 %copy-start.27 = (pred[1280,512]{1,0:T(32,128)(4,1)S(1)}, pred[1280,512]{1,0:T(32,128)(4,1)}, u32[]{:S(2)}) copy-start(pred[1280,512]{1,0:T(32,128)(4,1)} %copy-done.26) | copy-start | bytes 1966084
  228.1 1.3 copy-start.1
  228.1 3.2 copy-start.9
  360.8 169.2 %reduce-scatter.3.cloned.1.call-start = ((), (), s32[]{:S(2)}) async-start(), calls=%async_computation.8 | async-start | bytes 14417920 | tf_op jit(solution)/shard_map/reduce_scatter | solution.py:1361
  408.1 5.2 copy-start.29
  408.2 103.5 %all-to-all-start.1 = ((bf16[4,320,2048]{2,1,0:T(8,128)(2,1)}), bf16[4,320,2048]{2,1,0:T(8,128)(2,1)}, u32[]{:S(2)}, u32[]{:S(2)}) async-start(bf16[4,320,2048]{2,1,0:T(8,128)(2,1)} %bitcast.142), calls=%async_computation.3 | async-start | bytes 10485760 | tf_op jit(solution)/shard_map/all_to_all | solution.py:1362
  413.6 2.5 copy-start.40
  416.1 3.1 copy-start.10
  416.1 3.1 copy-start.12
  457.8 9.0 %copy-start.13 = (f32[128,2048]{1,0:T(8,128)}, f32[128,2048]{1,0:T(8,128)S(1)}, u32[]{:S(2)}) copy-start(f32[128,2048]{1,0:T(8,128)S(1)} %get-tuple-element.70.dmiddle_ref) | copy-start | bytes 3145732
  457.8 9.0 %copy-start.18 = (bf16[2,2,2,128,2048]{4,3,2,1,0:T(8,128)(2,1)}, bf16[2,2,2,128,2048]{4,3,2,1,0:T(8,128)(2,1)S(1)}, u32[]{:S(2)}) copy-start(bf16[2,2,2,128,2048]{4,3,2,1,0:T(8,128)(2,1)S(1)} %get-tuple-element.62) | copy-start | bytes 12582916
  457.8 9.0 %copy-start.4 = (f32[1024,128]{1,0:T(8,128)S(1)}, f32[1024,128]{1,0:T(8,128)}, u32[]{:S(2)}) copy-start(f32[1024,128]{1,0:T(8,128)} %copy-done.3) | copy-start | bytes 1572868
  457.8 9.0 %copy-start.6 = (f32[1024,128]{1,0:T(8,128)S(1)}, f32[1024,128]{1,0:T(8,128)}, u32[]{:S(2)}) copy-start(f32[1024,128]{1,0:T(8,128)} %copy-done.5) | copy-start | bytes 1572868
  457.8 9.0 %copy-start.8 = (f32[1024,3]{1,0:T(8,128)S(1)}, f32[1024,3]{1,0:T(8,128)}, u32[]{:S(2)}) copy-start(f32[1024,3]{1,0:T(8,128)} %copy.161.gate_ref) | copy-start | bytes 36868
  457.8 9.0 %copy-start.15 = (bf16[1024,256]{1,0:T(8,128)(2,1)S(1)}, bf16[1024,256]{1,0:T(8,128)(2,1)}, u32[]{:S(2)}) copy-start(bf16[1024,256]{1,0:T(8,128)(2,1)} %copy-done.14) | copy-start | bytes 1572868
  457.8 9.0 %copy-start.17 = (bf16[1024,256]{1,0:T(8,128)(2,1)S(1)}, bf16[1024,256]{1,0:T(8,128)(2,1)}, u32[]{:S(2)}) copy-start(bf16[1024,256]{1,0:T(8,128)(2,1)} %copy-done.16) | copy-start | bytes 1572868
  480.6 12.7 %copy-start.2 = (bf16[4,128,2048]{2,1,0:T(8,128)(2,1)S(1)}, bf16[4,128,2048]{2,1,0:T(8,128)(2,1)}, u32[]{:S(2)}) copy-start(bf16[4,128,2048]{2,1,0:T(8,128)(2,1)} %copy-done.1) | copy-start | bytes 6291460
  480.6 13.1 %copy-start.22 = (bf16[1024,2048]{1,0:T(8,128)(2,1)S(1)}, bf16[1024,2048]{1,0:T(8,128)(2,1)}, u32[]{:S(2)}) copy-start(bf16[1024,2048]{1,0:T(8,128)(2,1)} %all-gather.6.cloned.1.call-done) | copy-start | bytes 12582916
  493.7 2.5 copy-start.42
  496.2 7.6 %copy-start.23 = (bf16[1024,2048]{1,0:T(8,128)(2,1)S(1)}, bf16[1024,2048]{1,0:T(8,128)(2,1)}, u32[]{:S(2)}) copy-start(bf16[1024,2048]{1,0:T(8,128)(2,1)} %all-gather.6.cloned.1.call-done) | copy-start | bytes 12582916
  496.2 7.6 %copy-start.41 = (bf16[1024,1280]{1,0:T(8,128)(2,1)S(1)}, bf16[1024,1280]{1,0:T(8,128)(2,1)}, u32[]{:S(2)}) copy-start(bf16[1024,1280]{1,0:T(8,128)(2,1)} %get-tuple-element.64) | copy-start | bytes 7864324
  659.9 3.0 copy-start.24
  663.0 5.6 copy-start.25
  664.8 5.9 copy-start.32
  664.8 6.5 copy-start.28
  (3 other events, 3.1 us)
Sparse Core Ops, SparseCore 0:
  9.7 38.4 all-gather.7
  50.4 62.8 all-gather.5
  117.6 62.8 all-gather.11
  182.0 110.2 all-gather.9
  360.9 60.8 reduce-scatter.4
  424.2 105.7 reduce-scatter.2

commit v5 on v4

--- a/solution.py
+++ b/solution.py
@@ -70,8 +70,8 @@
 
 
 def gather_body(
-    x_ref, ups_ref, downs_ref, out_ref, up_ref, down_ref,
-    loc, xs, xr, s1, r1m, r1p, f1s, f1r, s2, r2m, r2p, f2s, f2r, es, er, ex, ey,
+    x_ref, ups_ref, downs_ref, marks_ref, out_ref, up_ref, down_ref, marks_out,
+    loc, xs, xr, s1, r1m, r1p, f1s, f1r, s2, r2m, r2p, f2s, f2r, es, er, ex, ey, ms, mr,
 ):
     y, xl, z = lax.axis_index("y"), lax.axis_index("xl"), lax.axis_index("z")
     half = x_ref.shape[1] // 2
@@ -94,6 +94,9 @@
 
     own = pltpu.make_async_copy(x_ref.at[xl], out_ref.at[z, xl, y], loc.at[0])
     own.start()
+    own_marks = pltpu.make_async_copy(marks_ref, marks_out.at[xl], loc.at[3])
+    own_marks.start()
+    send(marks_ref, marks_out.at[xl], ms, mr, neighbour("xl", 1))
     experts = ((ups_ref, up_ref), (downs_ref, down_ref))
     kept = []
     for n, (shards, expert) in enumerate(experts):
@@ -173,23 +176,26 @@
         for step in (0, 1, 3, 2):
             arrived(expert.at[other, mod4(y - step)], ey.at[n, step])
         kept[n].wait()
+    arrived(marks_out.at[other], mr)
+    own_marks.wait()
     sends.finish()
 
 
-def gather_dp(shard, ups, downs):
+def gather_dp(shard, ups, downs, marks):
     _, rows, cols = shard.shape
     dma = pltpu.SemaphoreType.DMA
-    whole, up, down = pl.pallas_call(
+    whole, up, down, marks = pl.pallas_call(
         gather_body,
         out_shape=[
             jax.ShapeDtypeStruct((4, 2, 4, rows, cols), shard.dtype),
             jax.ShapeDtypeStruct((2, *ups.shape), ups.dtype),
             jax.ShapeDtypeStruct((2, *downs.shape), downs.dtype),
+            jax.ShapeDtypeStruct((2, *marks.shape), marks.dtype),
         ],
-        in_specs=[pl.BlockSpec(memory_space=pl.ANY)] * 3,
-        out_specs=[pl.BlockSpec(memory_space=pl.ANY)] * 3,
+        in_specs=[pl.BlockSpec(memory_space=pl.ANY)] * 4,
+        out_specs=[pl.BlockSpec(memory_space=pl.ANY)] * 4,
         scratch_shapes=[
-            dma((3,)),
+            dma((4,)),
             dma((2,)),
             dma((2,)),
             dma((2, 2, 2)),
@@ -206,11 +212,13 @@
             dma((2, 3)),
             dma((2, 4)),
             dma((2, 4)),
+            dma,
+            dma,
         ],
         compiler_params=pltpu.CompilerParams(collective_id=0, has_side_effects=True),
         name="gather_weights",
-    )(shard, ups, downs)
-    return whole.reshape(32 * rows, cols), up, down
+    )(shard, ups, downs, marks)
+    return whole.reshape(32 * rows, cols), up, down, marks
 
 
 def reduce_stages(scatter_count, part_refs, core_buf, sum_buf, far_buf, core_s, core_r, far_s, far_r, sends):
@@ -427,11 +435,40 @@
     return [dma((CHUNKS,)), dma((CHUNKS,)), dma((CHUNKS, 2)), dma((CHUNKS, 2))]
 
 
-def middle_body(part_ref, x_ref, gain_ref, middle_ref, unit_ref, *scratch):
+def middle_body(
+    part_ref, x_ref, gain_ref, pick_ref, grad_ref, middle_ref, unit_ref, rows_out, rows_buf, loc, ys, yr, cs, cr, *scratch
+):
     sends = Sends()
-    greet(*along_x())
-    *_, total = ring_reduce_stages(part_ref, *scratch[:8], sends)
-    me = lax.axis_index("xh") * 2 + lax.axis_index("core")
+    y, core = lax.axis_index("y"), lax.axis_index("core")
+    greet(*along_x(), *(neighbour("y", step) for step in (1, 2, 3)))
+    stages = ring_reduce_stages(part_ref, *scratch[:8], sends)
+    next(stages)
+    slots = pick_ref.shape[1] // 2
+    mine = pl.ds(pl.multiple_of(core * slots, slots), slots)
+
+    def pick(step):
+        target = mod4(y + step)
+        rows_buf[step - 1] = dot(pick_ref[target, mine, :], grad_ref[...], ((1,), (0,))).astype(BF16)
+        sends(
+            rows_buf.at[step - 1],
+            rows_out.at[y, mine],
+            ys.at[step - 1],
+            yr.at[step - 1],
+            neighbour("y", step),
+        )
+
+    pick(2)
+    next(stages)
+    pick(1)
+    pick(3)
+    rows_buf[3] = dot(pick_ref[y, :slots, :], grad_ref[...], ((1,), (0,))).astype(BF16)
+    rows_buf[4] = dot(pick_ref[y, slots:, :], grad_ref[...], ((1,), (0,))).astype(BF16)
+    kept = []
+    for n in (0, 1):
+        kept.append(pltpu.make_async_copy(rows_buf.at[3 + n], rows_out.at[y, pl.ds(n * slots, slots)], loc.at[n]))
+        kept[-1].start()
+    total = next(stages)
+    me = lax.axis_index("xh") * 2 + core
     step = x_ref.shape[0] // CHUNKS
     half = x_ref.shape[0] // 2
     for part in (0, 1):
@@ -443,6 +480,15 @@
         for n in range(part * CHUNKS // 2, (part + 1) * CHUNKS // 2):
             spread_chunk(unit_ref, n, step, scratch[8:], sends)
     spread_finish(unit_ref, step, scratch[8:], sends)
+    for step in (1, 3, 2):
+        block = rows_out.at[mod4(y - step), mine]
+        arrived(block, yr.at[step - 1])
+        sends(block, block, cs.at[step - 1], cr.at[step - 1], neighbour("core", 1))
+    other = pl.ds(pl.multiple_of((1 - core) * slots, slots), slots)
+    for step in (1, 3, 2):
+        arrived(rows_out.at[mod4(y - step), other], cr.at[step - 1])
+    for copy in kept:
+        copy.wait()
     sends.finish()
 
 
@@ -450,30 +496,69 @@
     return [pl.BlockSpec(memory_space=pltpu.VMEM)] * count
 
 
-def middle_and_unit(part, x, gain):
+def middle_and_unit(part, x, gain, pick, grads):
     rows, width = x.shape
-    middle, unit = pl.pallas_call(
+    experts, slots, _ = pick.shape
+    dma = pltpu.SemaphoreType.DMA
+    middle, unit, rows_in = pl.pallas_call(
         middle_body,
         out_shape=[
             jax.ShapeDtypeStruct((rows, width), F32),
             jax.ShapeDtypeStruct((4, rows, width), BF16),
+            jax.ShapeDtypeStruct((experts, slots, width), BF16),
         ],
-        in_specs=vmem(3),
-        out_specs=vmem(2),
-        scratch_shapes=ring_reduce_scratch(rows, width) + spread_scratch(),
+        in_specs=vmem(5),
+        out_specs=vmem(2) + [pl.BlockSpec(memory_space=pl.ANY)],
+        scratch_shapes=[
+            pltpu.VMEM((5, slots // 2, width), BF16),
+            dma((2,)),
+            dma((3,)),
+            dma((3,)),
+            dma((3,)),
+            dma((3,)),
+        ]
+        + ring_reduce_scratch(rows, width)
+        + spread_scratch(),
         compiler_params=pltpu.CompilerParams(
-            collective_id=1, has_side_effects=True, vmem_limit_bytes=32 * MIB
+            collective_id=1, has_side_effects=True, vmem_limit_bytes=48 * MIB
         ),
         name="middle_and_unit",
-    )(part.reshape(2, 2, 2, rows, width), x, gain[None])
-    return middle, unit.reshape(4 * rows, width)
-
-
-def back_body(part_ref, middle_ref, grad_ref, gain_ref, dmiddle_ref, dgain_ref, spread_ref, *scratch):
+    )(part.reshape(2, 2, 2, rows, width), x, gain[None], pick, grads)
+    return middle, unit.reshape(4 * rows, width), rows_in.reshape(experts * slots, width)
+
+
+def back_body(
+    part_ref, middle_ref, grad_ref, gain_ref, hidden_ref, down_ref, dmiddle_ref, dgain_ref, spread_ref, branch_out,
+    hidden, down, branch, branch_buf, branch_sum, loc, cs, cr, ys, yr, *scratch,
+):
     sends = Sends()
-    greet(*along_x())
-    *_, total = reduce_stages(CHUNKS, [part_ref], *scratch[:7], sends)
-    xl, xh, core = lax.axis_index("xl"), lax.axis_index("xh"), lax.axis_index("core")
+    y, core = lax.axis_index("y"), lax.axis_index("core")
+    loads = []
+    for n, (src, dst) in enumerate(((hidden_ref, hidden), (down_ref, down))):
+        loads.append(pltpu.make_async_copy(src, dst, loc.at[n]))
+        loads[-1].start()
+    greet(*along_x(), *(neighbour("y", step) for step in (1, 2, 3)))
+    stages = reduce_stages(CHUNKS, [part_ref], *scratch[:7], sends)
+    next(stages)
+    slots = branch_out.shape[1]
+    mine = pl.ds(pl.multiple_of(core * slots, slots), slots)
+    theirs = pl.ds(pl.multiple_of((1 - core) * slots, slots), slots)
+
+    def output(step):
+        target = mod4(y + step)
+        branch[step] = dot(hidden[target], down[...], ((1,), (1,))).astype(BF16)
+        sends(
+            branch.at[step, theirs], branch_buf.at[step], cs.at[step], cr.at[step], neighbour("core", 1)
+        )
+
+    for load in loads:
+        load.wait()
+    output(2)
+    next(stages)
+    for step in (1, 3, 0):
+        output(step)
+    total = next(stages)
+    xl, xh = lax.axis_index("xl"), lax.axis_index("xh")
     step = middle_ref.shape[0] // CHUNKS
     for n in range(CHUNKS):
         rows = slice(n * step, (n + 1) * step)
@@ -493,38 +578,78 @@
         spread_ref[xl, xh, core, rows, :] = dmiddle.astype(BF16)
         if n % 2 == 1:
             ring_spread(spread_ref, n // 2, *scratch[7:], sends)
+    for step in (2, 1, 3, 0):
+        arrived(branch_buf.at[step], cr.at[step])
+        value = (branch[step, mine, :].astype(F32) + branch_buf[step].astype(F32)).astype(BF16)
+        if step == 0:
+            branch_out[y] = value
+        else:
+            branch_sum[step - 1] = value
+            sends(
+                branch_sum.at[step - 1],
+                branch_out.at[y],
+                ys.at[step - 1],
+                yr.at[step - 1],
+                neighbour("y", step),
+            )
     ring_spread_finish(spread_ref, *scratch[7:], sends)
+    for step in (1, 3, 2):
+        arrived(branch_out.at[mod4(y - step)], yr.at[step - 1])
     sends.finish()
 
 
-def middle_back(part, middle, grad, gain):
+def middle_back(part, middle, grad, gain, hidden, down):
     rows, width = middle.shape
-    dmiddle, dgain, spread = pl.pallas_call(
+    count, inner = hidden.shape
+    slots = count // 4
+    dma = pltpu.SemaphoreType.DMA
+    anywhere = pl.BlockSpec(memory_space=pl.ANY)
+    dmiddle, dgain, spread, branch = pl.pallas_call(
         back_body,
         out_shape=[
             jax.ShapeDtypeStruct((rows, width), F32),
             jax.ShapeDtypeStruct((1, width), F32),
             jax.ShapeDtypeStruct((2, 2, 2, rows, width), BF16),
+            jax.ShapeDtypeStruct((4, slots // 2, width), BF16),
         ],
-        in_specs=vmem(4),
-        out_specs=vmem(3),
-        scratch_shapes=reduce_scratch(1, rows, width) + ring_spread_scratch(),
+        in_specs=vmem(4) + [anywhere] * 2,
+        out_specs=vmem(4),
+        scratch_shapes=[
+            pltpu.VMEM((4, slots, inner), BF16),
+            pltpu.VMEM(down.shape, BF16),
+            pltpu.VMEM((4, slots, width), BF16),
+            pltpu.VMEM((4, slots // 2, width), BF16),
+            pltpu.VMEM((3, slots // 2, width), BF16),
+            dma((2,)),
+            dma((4,)),
+            dma((4,)),
+            dma((3,)),
+            dma((3,)),
+        ]
+        + reduce_scratch(1, rows, width)
+        + ring_spread_scratch(),
         compiler_params=pltpu.CompilerParams(
-            collective_id=2, has_side_effects=True, vmem_limit_bytes=32 * MIB
+            collective_id=2, has_side_effects=True, vmem_limit_bytes=56 * MIB
         ),
         name="middle_back",
-    )(part.reshape(4, rows, width), middle, grad, gain[None])
-    return dmiddle, dgain[0], spread.reshape(8 * rows, width)
-
-
-def rows_body(rows_ref, out_ref, loc, far_s, far_r, core_s, core_r):
+    )(part.reshape(4, rows, width), middle, grad, gain[None], hidden.reshape(4, slots, inner), down)
+    return dmiddle, dgain[0], spread.reshape(8 * rows, width), branch
+
+
+def rows_body(
+    rows_ref, grad_ref, down_ref, out_ref, raw_out, grad, down, block, loc, out_sem, far_s, far_r, core_s, core_r
+):
     y, core = lax.axis_index("y"), lax.axis_index("core")
     half = rows_ref.shape[1] // 2
     sends = Sends()
     greet(neighbour("core", 1), *(neighbour("y", step) for step in (1, 2, 3)))
     at = pl.ds(pl.multiple_of(core * half, half), half)
-    own = pltpu.make_async_copy(rows_ref.at[y], out_ref.at[y], loc)
+    own = pltpu.make_async_copy(rows_ref.at[y], out_ref.at[y], loc.at[0])
     own.start()
+    loads = []
+    for n, (src, dst) in enumerate(((grad_ref, grad), (down_ref, down))):
+        loads.append(pltpu.make_async_copy(src, dst, loc.at[1 + n]))
+        loads[-1].start()
     for step in (2, 1, 3):
         target = mod4(y + step)
         sends(
@@ -534,6 +659,21 @@
             far_r.at[step - 1],
             neighbour("y", step),
         )
+    for load in loads:
+        load.wait()
+    outs = []
+    columns = raw_out.shape[1]
+    for n, start in enumerate(range(0, columns, WIDE)):
+        cols = min(WIDE, columns - start)
+        if n >= 2:
+            outs[n - 2].wait()
+        block[n % 2, :, :cols] = dot(grad[...], down[:, start : start + cols], ((1,), (0,)))
+        outs.append(
+            pltpu.make_async_copy(
+                block.at[n % 2, :, pl.ds(0, cols)], raw_out.at[:, pl.ds(start, cols)], out_sem.at[n % 2]
+            )
+        )
+        outs[-1].start()
     for step in (1, 3, 2):
         source = mod4(y - step)
         block = out_ref.at[source, at]
@@ -543,20 +683,43 @@
     other = pl.ds(pl.multiple_of((1 - core) * half, half), half)
     for step in (1, 3, 2):
         arrived(out_ref.at[mod4(y - step), other], core_r.at[step - 1])
+    for out in outs[-2:]:
+        out.wait()
     sends.finish()
 
 
-def rows_to_experts(rows):
+LANES = 128
+WIDE = 256
+
+
+def rows_to_experts(rows, grads, down):
+    count, hidden = grads.shape[0], down.shape[1]
+    anywhere = pl.BlockSpec(memory_space=pl.ANY)
     dma = pltpu.SemaphoreType.DMA
     return pl.pallas_call(
         rows_body,
-        out_shape=jax.ShapeDtypeStruct(rows.shape, rows.dtype),
-        in_specs=[pl.BlockSpec(memory_space=pl.ANY)],
-        out_specs=pl.BlockSpec(memory_space=pl.ANY),
-        scratch_shapes=[dma, dma((3,)), dma((3,)), dma((3,)), dma((3,))],
-        compiler_params=pltpu.CompilerParams(collective_id=4, has_side_effects=True),
+        out_shape=[
+            jax.ShapeDtypeStruct(rows.shape, rows.dtype),
+            jax.ShapeDtypeStruct((count, hidden), F32),
+        ],
+        in_specs=[anywhere] * 3,
+        out_specs=[anywhere] * 2,
+        scratch_shapes=[
+            pltpu.VMEM(grads.shape, BF16),
+            pltpu.VMEM(down.shape, BF16),
+            pltpu.VMEM((2, count, WIDE), F32),
+            dma((3,)),
+            dma((2,)),
+            dma((3,)),
+            dma((3,)),
+            dma((3,)),
+            dma((3,)),
+        ],
+        compiler_params=pltpu.CompilerParams(
+            collective_id=4, has_side_effects=True, vmem_limit_bytes=40 * MIB
+        ),
         name="rows_to_experts",
-    )(rows)
+    )(rows, grads, down)
 
 
 STEPS = (2, 1, -1, 0)
@@ -567,7 +730,7 @@
     out_ref, up_out, down_out, output_ref, dinput_ref, small_out,
     g_ref, loc, t_buf, r_buf, tb_buf, rb_buf, c_buf,
     t_s, t_r, r_s, r_r, tb_s, tb_r, rb_s, rb_r, c_s, c_r,
-    up_own, down_own, up_buf, down_buf, up_sum, down_sum, ex, ey, es, er,
+    up_own, up_buf, up_sum, ex, ey, es, er,
     small_own, small_buf, small_s, small_r, *scratch,
 ):
     xl, xh, core = lax.axis_index("xl"), lax.axis_index("xh"), lax.axis_index("core")
@@ -584,8 +747,8 @@
         parts.append(pltpu.make_async_copy(ref, g_ref.at[..., pl.ds(column, cols)], loc.at[n]))
         parts[-1].start()
         column += cols
-    for n, (ref, own) in enumerate(((ups_ref, up_own), (downs_ref, down_own))):
-        parts.append(pltpu.make_async_copy(ref.at[xl], own, loc.at[3 + n]))
+    for n, (src, dst) in enumerate(((ups_ref.at[xl], up_own), (downs_ref.at[my_y], down_out.at[my_y]))):
+        parts.append(pltpu.make_async_copy(src, dst, loc.at[3 + n]))
         parts[-1].start()
     peers = ({"xh": xh, "core": 1 - core}, {"xh": 1 - xh, "core": core}, {"xh": 1 - xh, "core": 1 - core})
     greet(
@@ -598,16 +761,14 @@
     both = slice(0, 2)
     ring_stages = ring_reduce_stages(part_ref, *scratch[7:15], sends)
     feed_stages = reduce_stages(CHUNKS, [feed_ref], *scratch[:7], sends)
-    experts = ((ups_ref, up_own, up_buf, up_sum, up_out), (downs_ref, down_own, down_buf, down_sum, down_out))
-    for n, (grads, _, buf, _, _) in enumerate(experts):
-        for step in (2, 1, 3, 0):
-            sends(
-                grads.at[1 - xl, mod4(my_y + step)],
-                buf.at[step],
-                ex.at[n, step],
-                ey.at[n, step],
-                neighbour("xl", 1),
-            )
+    for step in (2, 1, 3, 0):
+        sends(
+            ups_ref.at[1 - xl, mod4(my_y + step)],
+            up_buf.at[step],
+            ex.at[step],
+            ey.at[step],
+            neighbour("xl", 1),
+        )
     next(ring_stages)
     next(feed_stages)
     for part in parts[:3]:
@@ -666,24 +827,31 @@
                     neighbour(rings[h][1], way),
                 )
     total = next(ring_stages)
+    for step in (2, 1, 3):
+        sends(
+            downs_ref.at[mod4(my_y + step)],
+            down_out.at[my_y],
+            es.at[1, step - 1],
+            er.at[1, step - 1],
+            neighbour("y", step),
+        )
     for part in parts[3:]:
         part.wait()
-    for n, (_, own, buf, summed, result) in enumerate(experts):
-        for step in (2, 1, 3, 0):
-            target = mod4(my_y + step)
-            arrived(buf.at[step], ey.at[n, step])
-            value = (own[target].astype(F32) + buf[step].astype(F32)).astype(BF16)
-            if step == 0:
-                result[my_y] = value
-            else:
-                summed[step - 1] = value
-                sends(
-                    summed.at[step - 1],
-                    result.at[my_y],
-                    es.at[n, step - 1],
-                    er.at[n, step - 1],
-                    neighbour("y", step),
-                )
+    for step in (2, 1, 3, 0):
+        target = mod4(my_y + step)
+        arrived(up_buf.at[step], ey.at[step])
+        value = (up_own[target].astype(F32) + up_buf[step].astype(F32)).astype(BF16)
+        if step == 0:
+            up_out[my_y] = value
+        else:
+            up_sum[step - 1] = value
+            sends(
+                up_sum.at[step - 1],
+                up_out.at[my_y],
+                es.at[0, step - 1],
+                er.at[0, step - 1],
+                neighbour("y", step),
+            )
     for k in range(4):
         for h in (0, 1):
             second = place[rings[h][1]]
@@ -760,7 +928,7 @@
     for n in range(CHUNKS):
         rows = slice(n * step, (n + 1) * step)
         output_ref[rows, :] = (middle_ref[rows, :] + feed(0, n)).astype(BF16)
-    for n, (_, _, _, _, result) in enumerate(experts):
+    for n, result in enumerate((up_out, down_out)):
         for step in (1, 3, 2):
             arrived(result.at[mod4(my_y - step)], er.at[n, step - 1])
     for n in range(3):
@@ -809,13 +977,10 @@
             dma((2,)),
             dma((2,)),
             pltpu.VMEM((4, share, up_cols), BF16),
-            pltpu.VMEM((4, share, down_cols), BF16),
             pltpu.VMEM((4, share, up_cols), BF16),
-            pltpu.VMEM((4, share, down_cols), BF16),
             pltpu.VMEM((3, share, up_cols), BF16),
-            pltpu.VMEM((3, share, down_cols), BF16),
-            dma((2, 4)),
-            dma((2, 4)),
+            dma((4,)),
+            dma((4,)),
             dma((2, 3)),
             dma((2, 3)),
             pltpu.VMEM(small, F32),
@@ -832,7 +997,7 @@
     )(
         *(grad.reshape(4, 2, 4, share, grad.shape[1]) for grad in grads),
         ups.reshape(2, 4, share, up_cols),
-        downs.reshape(2, 4, share, down_cols),
+        downs.reshape(4, share, down_cols),
         part.reshape(2, 2, 2, own_rows, width),
         feed.reshape(4, own_rows, width),
         x,
@@ -846,156 +1011,135 @@
     return lax.dot_general(a, b, (dims, ((), ())), preferred_element_type=F32)
 
 
-LANES = 128
-WIDE = 256
-
-
 def experts_body(
-    rows_ref, grad_ref, up_ref, down_ref, gate_ref, up_rows_ref,
-    djoined_out, hidden_out, gated_out, dgate_out, dunit_out, raw, djoined,
+    rows_ref, raw_ref, gate_up_ref, linear_up_ref, gate_ref,
+    dgate_pre_out, dlinear_out, hidden_out, gated_out, dgate_out,
 ):
-    j = pl.program_id(0)
-    chunks = djoined.shape[1] // WIDE
-
-    @pl.when(j == 0)
+    @pl.when(pl.program_id(0) == 0)
     def _():
         dgate_out[...] = jnp.zeros_like(dgate_out)
 
-    @pl.when((j < chunks) & (lax.rem(j, 2) == 0))
-    def _():
-        pair = dot(grad_ref[...], down_ref[...], ((1,), (0,)))
-        raw[0] = pair[:, :LANES]
-        raw[1] = pair[:, LANES:]
-
-    @pl.when(j < chunks)
-    def _():
-        joined = dot(rows_ref[...], up_ref[...], ((1,), (0,)))
-        gate_pre, linear = joined[:, :LANES], joined[:, LANES:]
-        sigmoid = jax.nn.sigmoid(gate_pre)
-        silu = gate_pre * sigmoid
-        hidden = silu * linear
-        dhidden = raw[lax.rem(j, 2)]
-        gate = gate_ref[...]
-        dgate_out[...] += hidden * dhidden
-        dhidden = dhidden * gate
-        hidden_out[...] = hidden.astype(BF16)
-        gated_out[...] = (hidden * gate).astype(BF16)
-        dgate_pre = (dhidden * linear * (sigmoid + silu * (1.0 - sigmoid))).astype(BF16)
-        dlinear = (dhidden * silu).astype(BF16)
-        djoined_out[:, :LANES] = dgate_pre
-        djoined_out[:, LANES:] = dlinear
-        at = pl.multiple_of(j * WIDE, WIDE)
-        djoined[:, pl.ds(at, LANES)] = dgate_pre
-        djoined[:, pl.ds(at + LANES, LANES)] = dlinear
-
-    @pl.when(j >= chunks)
-    def _():
-        dunit_out[...] = dot(djoined[...], up_rows_ref[...], ((1,), (1,))).astype(BF16)
-
-
-def experts(rows, grads, up, down, gates):
-    count, width = grads.shape
-    hidden = down.shape[1]
+    up = jnp.concatenate([gate_up_ref[...], linear_up_ref[...]], 1)
+    joined = dot(rows_ref[...], up, ((1,), (0,)))
+    gate_pre, linear = joined[:, :LANES], joined[:, LANES:]
+    sigmoid = jax.nn.sigmoid(gate_pre)
+    silu = gate_pre * sigmoid
+    hidden = silu * linear
+    dhidden = raw_ref[...]
+    gate = gate_ref[...]
+    dgate_out[...] += hidden * dhidden
+    dhidden = dhidden * gate
+    hidden_out[...] = hidden.astype(BF16)
+    gated_out[...] = (hidden * gate).astype(BF16)
+    dgate_pre_out[...] = (dhidden * linear * (sigmoid + silu * (1.0 - sigmoid))).astype(BF16)
+    dlinear_out[...] = (dhidden * silu).astype(BF16)
+
+
+def experts(rows, raw, up, gates):
+    count, hidden = raw.shape
+    width = up.shape[0]
     chunks = hidden // LANES
-    steps = chunks + width // WIDE
-
-    def chunk(j):
-        return jnp.minimum(j, chunks - 1)
-
-    def tail(j):
-        return jnp.maximum(j - chunks, 0)
-
+    chunk = pl.BlockSpec((count, LANES), lambda j: (0, j))
+    some = jax.ShapeDtypeStruct((count, hidden), BF16)
     return pl.pallas_call(
         experts_body,
-        grid=(steps,),
+        grid=(chunks,),
         in_specs=[
             pl.BlockSpec((count, width), lambda j: (0, 0)),
-            pl.BlockSpec((count, width), lambda j: (0, 0)),
-            pl.BlockSpec((width, WIDE), lambda j: (0, chunk(j))),
-            pl.BlockSpec((width, WIDE), lambda j: (0, chunk(j) // 2)),
+            chunk,
+            pl.BlockSpec((width, LANES), lambda j: (0, j)),
+            pl.BlockSpec((width, LANES), lambda j: (0, chunks + j)),
             pl.BlockSpec((count, 1), lambda j: (0, 0)),
-            pl.BlockSpec((WIDE, 2 * hidden), lambda j: (tail(j), 0)),
         ],
-        out_specs=[
-            pl.BlockSpec((count, WIDE), lambda j: (0, chunk(j))),
-            pl.BlockSpec((count, LANES), lambda j: (0, chunk(j))),
-            pl.BlockSpec((count, LANES), lambda j: (0, chunk(j))),
-            pl.BlockSpec((count, LANES), lambda j: (0, 0)),
-            pl.BlockSpec((count, WIDE), lambda j: (0, tail(j))),
-        ],
-        out_shape=[
-            jax.ShapeDtypeStruct((count, 2 * hidden), BF16),
-            jax.ShapeDtypeStruct((count, hidden), BF16),
-            jax.ShapeDtypeStruct((count, hidden), BF16),
-            jax.ShapeDtypeStruct((count, LANES), F32),
-            jax.ShapeDtypeStruct((count, width), BF16),
-        ],
-        scratch_shapes=[
-            pltpu.VMEM((2, count, LANES), F32),
-            pltpu.VMEM((count, 2 * hidden), BF16),
-        ],
-        compiler_params=pltpu.CompilerParams(vmem_limit_bytes=60 * MIB),
+        out_specs=[chunk] * 4 + [pl.BlockSpec((count, LANES), lambda j: (0, 0))],
+        out_shape=[some] * 4 + [jax.ShapeDtypeStruct((count, LANES), F32)],
+        compiler_params=pltpu.CompilerParams(vmem_limit_bytes=56 * MIB),
         name="experts",
-    )(rows, grads, up, down, gates, up)
+    )(rows, raw, up, up, gates)
 
 
 def return_body(
-    dunit_ref, dgate_ref, rows_ref, djoined_ref, hidden_ref, down_ref,
-    dunit_out, dgate_out, up_out, branch_out,
-    dunit_own, dgate_own, rows, djoined, hidden, down, dunit_buf, dgate_buf, dunit_sum, dgate_sum, block,
+    dgate_pre_ref, dlinear_ref, up_ref, dgate_ref, rows_ref,
+    dunit_out, dgate_out, up_out,
+    djoined, up, rows, dunit, dgate_own, dunit_buf, dgate_buf, dunit_sum, dgate_sum, block,
     loc, core_s, core_r, far_s, far_r, out_sem,
 ):
     y, core = lax.axis_index("y"), lax.axis_index("core")
-    half = dunit_ref.shape[1] // 2
+    slots = dgate_ref.shape[1]
+    half = slots // 2
+    hidden = dgate_pre_ref.shape[1]
     sends = Sends()
+    loads = []
+    for n, (src, dst) in enumerate(
+        (
+            (up_ref, up),
+            (dgate_pre_ref, djoined.at[:, pl.ds(0, hidden)]),
+            (dlinear_ref, djoined.at[:, pl.ds(hidden, hidden)]),
+            (rows_ref.at[:, pl.ds(0, rows.shape[1])], rows),
+        )
+    ):
+        loads.append(pltpu.make_async_copy(src, dst, loc.at[1, n]))
+        loads[-1].start()
     greet(neighbour("core", 1), *(neighbour("y", step) for step in (1, 2, 3)))
     mine = pl.ds(pl.multiple_of(core * half, half), half)
     theirs = pl.ds(pl.multiple_of((1 - core) * half, half), half)
     order = (2, 1, 3, 0)
-    kinds = (
-        (dunit_ref, dunit_own, dunit_buf, dunit_sum, dunit_out),
-        (dgate_ref, dgate_own, dgate_buf, dgate_sum, dgate_out),
-    )
-    for step in order:
-        for n, (whole, _, buf, _, _) in enumerate(kinds):
-            sends(
-                whole.at[mod4(y + step), theirs],
-                buf.at[step],
-                core_s.at[n, step],
-                core_r.at[n, step],
-                neighbour("core", 1),
-            )
     own = []
     for step in order:
-        for n, (whole, kept, _, _, _) in enumerate(kinds):
-            copy = pltpu.make_async_copy(whole.at[mod4(y + step), mine], kept.at[step], loc.at[n, step])
-            copy.start()
-            own.append(copy)
-    loads = []
-    for n, (src, dst) in enumerate(
-        ((rows_ref.at[:, pl.ds(0, rows.shape[1])], rows), (djoined_ref, djoined), (hidden_ref, hidden), (down_ref, down))
-    ):
-        loads.append(pltpu.make_async_copy(src, dst, loc.at[2, n]))
-        loads[-1].start()
+        target = mod4(y + step)
+        sends(
+            dgate_ref.at[target, theirs],
+            dgate_buf.at[step],
+            core_s.at[1, step],
+            core_r.at[1, step],
+            neighbour("core", 1),
+        )
+        own.append(pltpu.make_async_copy(dgate_ref.at[target, mine], dgate_own.at[step], loc.at[0, step]))
+        own[-1].start()
+    for load in loads[:3]:
+        load.wait()
     for copy in own:
         copy.wait()
-    for step in order:
-        for n, (_, kept, buf, summed, result) in enumerate(kinds):
-            arrived(buf.at[step], core_r.at[n, step])
-            value = (kept[step].astype(F32) + buf[step].astype(F32)).astype(summed.dtype)
-            if step == 0:
-                result[y] = value
-            else:
-                summed[step - 1] = value
-                sends(
-                    summed.at[step - 1],
-                    result.at[y],
-                    far_s.at[n, step - 1],
-                    far_r.at[n, step - 1],
-                    neighbour("y", step),
-                )
-    for load in loads:
-        load.wait()
+
+    def compute(step):
+        at = pl.ds(pl.multiple_of(mod4(y + step) * slots, slots), slots)
+        dunit[step] = dot(djoined[at, :], up[...], ((1,), (1,))).astype(BF16)
+        sends(
+            dunit.at[step, theirs],
+            dunit_buf.at[step],
+            core_s.at[0, step],
+            core_r.at[0, step],
+            neighbour("core", 1),
+        )
+
+    def pass_on(step):
+        arrived(dunit_buf.at[step], core_r.at[0, step])
+        arrived(dgate_buf.at[step], core_r.at[1, step])
+        dunit_value = (dunit[step, mine, :].astype(F32) + dunit_buf[step].astype(F32)).astype(BF16)
+        dgate_value = dgate_own[step] + dgate_buf[step]
+        if step == 0:
+            dunit_out[y] = dunit_value
+            dgate_out[y] = dgate_value
+            return
+        dunit_sum[step - 1] = dunit_value
+        dgate_sum[step - 1] = dgate_value
+        for n, (summed, result) in enumerate(((dunit_sum, dunit_out), (dgate_sum, dgate_out))):
+            sends(
+                summed.at[step - 1],
+                result.at[y],
+                far_s.at[n, step - 1],
+                far_r.at[n, step - 1],
+                neighbour("y", step),
+            )
+
+    compute(2)
+    compute(1)
+    pass_on(2)
+    compute(3)
+    pass_on(1)
+    compute(0)
+    pass_on(3)
+    loads[3].wait()
     blocks = up_out.shape[0] // WIDE
 
     @pl.loop(0, blocks)
@@ -1010,55 +1154,43 @@
         block[slot] = dot(rows[:, at], djoined[...], ((0,), (0,))).astype(BF16)
         pltpu.make_async_copy(block.at[slot], up_out.at[at], out_sem.at[slot]).start()
 
-    @pl.loop(0, blocks)
-    def _(j):
-        at = pl.ds(pl.multiple_of(j * WIDE, WIDE), WIDE)
-        branch_out[:, at] = dot(hidden[...], down[at, :], ((1,), (1,))).astype(BF16)
-
+    pass_on(0)
     for slot in (0, 1):
         pltpu.make_async_copy(block.at[slot], up_out.at[pl.ds(0, WIDE)], out_sem.at[slot]).wait()
-    for n, (_, _, _, _, result) in enumerate(kinds):
+    for n, result in enumerate((dunit_out, dgate_out)):
         for step in (1, 3, 2):
             arrived(result.at[mod4(y - step)], far_r.at[n, step - 1])
     sends.finish()
 
 
-def return_rows(dunit, dgate, rows, djoined, hidden, down):
-    _, slots, width = dunit.shape
+def return_rows(dgate_pre, dlinear, up, dgate, rows):
+    _, slots, lanes = dgate.shape
     half = slots // 2
-    count, wide = djoined.shape
-    hidden_cols = hidden.shape[1]
+    width, wide = up.shape
+    count = dlinear.shape[0]
     dma = pltpu.SemaphoreType.DMA
     anywhere = pl.BlockSpec(memory_space=pl.ANY)
-
-    def pair(places):
-        return [
-            pltpu.VMEM((places, half, width), BF16),
-            pltpu.VMEM((places, half, dgate.shape[2]), F32),
-        ]
-
     return pl.pallas_call(
         return_body,
         out_shape=[
             jax.ShapeDtypeStruct((4, half, width), BF16),
-            jax.ShapeDtypeStruct((4, half, dgate.shape[2]), F32),
+            jax.ShapeDtypeStruct((4, half, lanes), F32),
             jax.ShapeDtypeStruct((width, wide), BF16),
-            jax.ShapeDtypeStruct((count, width), BF16),
         ],
-        in_specs=[anywhere] * 6,
-        out_specs=vmem(2) + [anywhere] + vmem(1),
-        scratch_shapes=pair(4)
-        + [
+        in_specs=[anywhere] * 5,
+        out_specs=vmem(2) + [anywhere],
+        scratch_shapes=[
+            pltpu.VMEM((count, wide), BF16),
+            pltpu.VMEM((width, wide), BF16),
             pltpu.VMEM((count, width), BF16),
-            pltpu.VMEM((count, wide), BF16),
-            pltpu.VMEM((count, hidden_cols), BF16),
-            pltpu.VMEM((width, hidden_cols), BF16),
-        ]
-        + pair(4)
-        + pair(3)
-        + [
+            pltpu.VMEM((4, slots, width), BF16),
+            pltpu.VMEM((4, half, lanes), F32),
+            pltpu.VMEM((4, half, width), BF16),
+            pltpu.VMEM((4, half, lanes), F32),
+            pltpu.VMEM((3, half, width), BF16),
+            pltpu.VMEM((3, half, lanes), F32),
             pltpu.VMEM((2, WIDE, wide), BF16),
-            dma((3, 4)),
+            dma((2, 4)),
             dma((2, 4)),
             dma((2, 4)),
             dma((2, 3)),
@@ -1069,7 +1201,7 @@
             collective_id=3, has_side_effects=True, vmem_limit_bytes=62 * MIB
         ),
         name="return_rows",
-    )(dunit, dgate, rows, djoined, hidden, down)
+    )(dgate_pre, dlinear, up, dgate, rows)
 
 
 def attention_body(
@@ -1285,12 +1417,14 @@
     out_grad = reorder(out_grad)
     x_all = lax.all_gather(inputs, ("xl", *TP), axis=0, tiled=True)
     grad_all = lax.all_gather(out_grad, TP, axis=0, tiled=True)
-    marks = lax.all_gather(jnp.concatenate([segments[:, None], att_routes], 1), "xl", axis=0)
-    weights, up_parts, down_parts = gather_dp(
+    marks = pad_to(jnp.concatenate([segments[:, None], att_routes], 1), LANES).astype(BF16)
+    weights, up_parts, down_parts, marks = gather_dp(
         own_att,
-        jnp.swapaxes(gate_up.reshape(mlp_count, share, 2, -1, LANES), 2, 3).reshape(mlp_count, share, -1),
+        gate_up.reshape(mlp_count, share, -1),
         jnp.swapaxes(down_proj, 1, 2),
-    )
+        marks,
+    )
+    marks = marks[:, :, :3].astype(jnp.int32)
     up_whole = lax.all_gather(
         up_parts.reshape(2 * mlp_count * share, -1), "z", axis=0, tiled=True
     )
@@ -1306,10 +1440,6 @@
     slot = jnp.where(match > 0, rank.astype(jnp.int32), -1)
     pick = (slot.T[:, None, :] == jnp.arange(CAP, dtype=jnp.int32)[None, :, None]).astype(BF16)
     pick_rows = pick.reshape(mlp_count * CAP, tokens)
-    grad_rows = dot(pick_rows, grad_all, ((1,), (0,))).astype(BF16)
-    grad_in = lax.all_to_all(grad_rows.reshape(mlp_count, CAP, width), "y", 0, 0, tiled=True)
-    grad_in = grad_in.reshape(mlp_count * CAP, width)
-
     small_all = weights[:, small_at : small_at + 128].astype(F32)
     gain_one, gain_two = small_all[:, 7], small_all[:, 8]
     segments = marks[:, :, 0]
@@ -1330,7 +1460,7 @@
     )
     out_weights = weights[:, out_at:]
     attention = dot(gmixed, out_weights, ((1,), (1,))).astype(BF16)
-    middle, unit_two = middle_and_unit(attention, inputs, gain_two)
+    middle, unit_two, grad_in = middle_and_unit(attention, inputs, gain_two, pick, grad_all)
 
     router_two = weights[:, small_at + att_count : small_at + att_count + mlp_count]
     logit_mlp = dot(unit_two, router_two, ((1,), (0,)))
@@ -1339,29 +1469,21 @@
     gate_low = (gate_mlp - gate_high.astype(F32)).astype(BF16)
     extended = jnp.concatenate([unit_two, pad_to(jnp.concatenate([gate_high, gate_low], 1), 128)], 1)
     rows_out = dot(pick_rows, extended, ((1,), (0,))).astype(BF16)
-    rows_ext = rows_to_experts(rows_out.reshape(mlp_count, CAP, width + 128))
+    rows_ext, raw = rows_to_experts(
+        rows_out.reshape(mlp_count, CAP, width + 128), grad_in, down_whole
+    )
     rows_ext = rows_ext.reshape(mlp_count * CAP, width + 128)
     gates_ext = rows_ext[:, width : width + 2 * mlp_count].astype(F32)
     mine = (jnp.arange(2 * mlp_count) % mlp_count == lax.axis_index("y")).astype(F32)
     gates_in = jnp.sum(gates_ext * mine, 1, keepdims=True)
-    djoined, hidden, gated, dgate_part, dunit_part = experts(
-        rows_ext, grad_in, up_whole, down_whole, gates_in
-    )
+    dgate_pre, dlinear, hidden, gated, dgate_part = experts(rows_ext, raw, up_whole, gates_in)
     grad_down_whole = dot(grad_in, gated, ((0,), (0,))).astype(BF16)
-    dunit_part, grad_down_whole = lax.optimization_barrier((dunit_part, grad_down_whole))
-    grad_down_sum = lax.psum_scatter(grad_down_whole, "z", scatter_dimension=0, tiled=True)
-    dunit_back, dgate_back, grad_up_whole, branch_part = return_rows(
-        dunit_part.reshape(mlp_count, CAP, width),
-        dgate_part.reshape(mlp_count, CAP, LANES),
-        rows_ext,
-        djoined,
-        hidden,
-        down_whole,
+    dgate_part, grad_down_whole = lax.optimization_barrier((dgate_part, grad_down_whole))
+    grad_down_sum = lax.psum_scatter(grad_down_whole, ("z", "xl"), scatter_dimension=0, tiled=True)
+    dunit_back, dgate_back, grad_up_whole = return_rows(
+        dgate_pre, dlinear, up_whole, dgate_part.reshape(mlp_count, CAP, LANES), rows_ext
     )
     grad_up_sum = lax.psum_scatter(grad_up_whole, "z", scatter_dimension=0, tiled=True)
-    branch_back = lax.all_to_all(
-        branch_part.reshape(mlp_count, CAP, width), "y", 0, 0, tiled=True
-    ).reshape(mlp_count * CAP, width)
     pick_half = lax.dynamic_slice_in_dim(pick, lax.axis_index("core") * (CAP // 2), CAP // 2, 1)
     dgate_two = jnp.sum(pick_half.astype(F32) * jnp.sum(dgate_back, -1, keepdims=True), 1).T
     dlogit_mlp = router_back(dgate_two, weights_mlp, onehot_mlp)
@@ -1369,8 +1491,8 @@
         pick_half.reshape(-1, tokens), dunit_back.reshape(-1, width), ((0,), (0,))
     ) + dot(dlogit_mlp, router_two, ((1,), (1,)))
     grad_rmlp = dot(unit_two, dlogit_mlp, ((0,), (0,)))
-    dmiddle, grad_gain_two, dattention = middle_back(
-        dunit_two.astype(BF16), middle, out_grad, gain_two
+    dmiddle, grad_gain_two, dattention, branch_back = middle_back(
+        dunit_two.astype(BF16), middle, out_grad, gain_two, hidden, down_whole
     )
 
     raw = dot(dattention, out_weights, ((1,), (0,)))
@@ -1390,8 +1512,12 @@
         ],
         1,
     )
-    gate_slots = jnp.sum(pick.astype(F32) * gate_mlp.T[:, None, :], -1).reshape(mlp_count * CAP, 1)
-    feed = dot(pick_rows, (branch_back.astype(F32) * gate_slots).astype(BF16), ((0,), (0,)))
+    gate_slots = jnp.sum(pick_half.astype(F32) * gate_mlp.T[:, None, :], -1, keepdims=True)
+    feed = dot(
+        pick_half.reshape(-1, tokens),
+        (branch_back.astype(F32) * gate_slots).astype(BF16).reshape(-1, width),
+        ((0,), (0,)),
+    )
     summed_att, ups_sum, downs_sum, output, grad_input, small_sum = finish(
         (
             dot(unit_one, grad_qkv, ((0,), (0,))).astype(BF16),
@@ -1419,9 +1545,7 @@
     output = reorder(output)
     grad_input = reorder(grad_input)
 
-    grads_up = jnp.swapaxes(
-        ups_sum.astype(F32).reshape(mlp_count, share, -1, 2, LANES), 2, 3
-    ).reshape(mlp_count, share, 2, hidden_local)
+    grads_up = ups_sum.astype(F32).reshape(mlp_count, share, 2, hidden_local)
     grads_down = jnp.swapaxes(downs_sum.astype(F32), 1, 2)
     return (
         output,

time: 686 us -> 710 us (1.035)
  waiting for transfers between devices: 17.1 us -> 72.9 us
  starting transfers between devices: 10.5 us -> 1.17 us
  matrix products: 95.3 us -> 86 us
  local copies, waits for them, and re-layouts: 57.8 us -> 50 us
    reduce_scatter x1, waiting for transfers between devices: 11.4 us -> 65.3 us  [on_device(): lax.psum_scatter(grad_up_whole, 'z', scatter_dimension=0, tiled=True)]
    pallas_call x2, Pallas kernels: 102 us -> 63.9 us  [the longest x1 39 us: rows_to_experts(): pl.pallas_call(rows_body, out_shape=[jax.ShapeDtypeStruct(rows.shape, row...]
    pallas_call x1, Pallas kernels: 38.6 us -> 74.2 us  [middle_back(): pl.pallas_call(back_body, out_shape=[jax.ShapeDtypeStruct((rows, width),...]
    pallas_call x1, Pallas kernels: 111 us -> 94.6 us  [finish(): pl.pallas_call(finish_body, out_shape=[jax.ShapeDtypeStruct((2, share, co...]
    pallas_call x1, Pallas kernels: 43.3 us -> 53.7 us  [return_rows(): pl.pallas_call(return_body, out_shape=[jax.ShapeDtypeStruct((4, half, wid...]
    all_to_all x2 -> x0, starting transfers between devices: 10.2 us -> none  [the longest x1 5.19 us: on_device(): lax.all_to_all(branch_part.reshape(mlp_count, CAP, width), 'y', 0, 0, til...]
    dot_general x16 -> x15, matrix products: 95.3 us -> 86 us  [dot(): return lax.dot_general(a, b, (dims, ((), ())), preferred_element_type=F32)]
    pallas_call x1, Pallas kernels: 38.9 us -> 46.8 us  [middle_and_unit(): pl.pallas_call(middle_body, out_shape=[jax.ShapeDtypeStruct((rows, width)...]
  transfers between devices with their start and end apart: 8 -> 6, of which waited for: 2 -> 2; matrix products, arithmetic and copies ran while one was open for 17% -> 14% of each run, Pallas kernels for 44% -> 49%
where the time goes in v5:
time: 710 us; the launch traced here: 705 us
  Pallas kernels  465 us (65%)
  matrix products  86 us (12%)
  waiting for transfers between devices  72.9 us (10%)
  local copies, waits for them, and re-layouts  50 us (7%)
  between operations  15.3 us (2%)
  other arithmetic  14.2 us (2%)
    pallas_call x1, Pallas kernels, gather_dp(): pl.pallas_call(gather_body, out_shape=[jax.ShapeDtypeStruct((4, 2, 4, row...  94.8 us
    pallas_call x1, Pallas kernels, finish(): pl.pallas_call(finish_body, out_shape=[jax.ShapeDtypeStruct((2, share, co...  94.6 us
    dot_general x15, matrix products, dot(): return lax.dot_general(a, b, (dims, ((), ())), preferred_element_type=F32)  86 us
    pallas_call x1, Pallas kernels, middle_back(): pl.pallas_call(back_body, out_shape=[jax.ShapeDtypeStruct((rows, width),...  74.2 us
    reduce_scatter x1, waiting for transfers between devices, on_device(): lax.psum_scatter(grad_up_whole, 'z', scatter_dimension=0, tiled=True)  65.3 us
    pallas_call x1, Pallas kernels, return_rows(): pl.pallas_call(return_body, out_shape=[jax.ShapeDtypeStruct((4, half, wid...  53.7 us
    pallas_call x1, Pallas kernels, middle_and_unit(): pl.pallas_call(middle_body, out_shape=[jax.ShapeDtypeStruct((rows, width)...  46.8 us
    pallas_call x1, Pallas kernels, rows_to_experts(): pl.pallas_call(rows_body, out_shape=[jax.ShapeDtypeStruct(rows.shape, row...  39 us
  transfers between devices with their start and end apart: 6, of which 2 were waited for; matrix products, arithmetic and copies ran while one was open for 14% of the time, Pallas kernels for 49%

profile of v5, /device:TPU:1, one launch (start us, length us, event | category | flops | bytes accessed | tf_op | source)
XLA Modules:
  0.0 704.7 jit_solution(5598487468352052456)
XLA Ops:
  7.3 1.4 copy.148
  9.9 1.3 copy.161
  14.6 1.8 reshape.415.ups_ref
  17.3 94.8 %gather_weights.1 = (bf16[4,2,4,64,2176]{4,3,2,1,0:T(8,128)(2,1)}, bf16[2,4,64,2816]{3,2,1,0:T(8,128)(2,1)}, bf16[2,4,64,1408]{3,2,1,0:T(8,128)(2,1)}, bf16[2,512,128]{2,1,0:T(8,128)(2,1)}) custom-call(bf16[2,64,2176]{2,1,0:T(8,128)(2,1)} %pad_maximum_fusion.x_ref, bf16[4,64,2816]{2,1,0:T(8,128)(2,1)} %reshape.415.ups_ref, bf16[4,64,1408]{2,1,0:T(8,128)(2,1)} %bitcast.148, ...), custom_call_target="tpu_custom_call" | custom-call | tf_op jit(solution)/shard_map/gather_weights/pallas_call | solution.py:187
  113.2 1.1 slice.77
  116.6 1.3 bitcast_compare_fusion
  118.0 1.9 fusion.37
  120.2 2.0 iota_compare_fusion.2
  122.8 3.7 fusion.4
  127.1 9.4 %fusion.8.k_ref.v_ref.q0.q1.q2 = f32[1024,1408]{1,0:T(8,128)S(1)} fusion(bf16[2048,2176]{1,0:T(8,128)(2,1)} %bitcast.153, bf16[1024,2048]{1,0:T(8,128)(2,1)S(1)} %copy-done.21, f32[2048]{0:T(1024)S(1)} %bitcast.171, f32[1024]{0:T(1024)S(1)} %add_rsqrt_fusion), kind=kOutput, calls=%fused_computation.15 | convolution fusion | flops 5913968640 | bytes 15740928 | tf_op jit(solution)/shard_map/dot_general | solution.py:1011
  136.5 2.5 copy-done.20
  140.4 1.1 copy-done.11
  142.5 23.9 %attention_forward.1 = (bf16[1024,256]{1,0:T(8,128)(2,1)S(1)}, bf16[1024,256]{1,0:T(8,128)(2,1)S(1)}, bf16[1024,768]{1,0:T(8,128)(2,1)S(1)}, bf16[1024,768]{1,0:...) custom-call(f32[1024,1408]{1,0:T(8,128)} %copy-done.20, f32[1024,1408]{1,0:T(8,128)} %copy-done.20, ...), custom_call_target="tpu_custom_call" | custom-call | tf_op jit(solution)/shard_map/attention_forward/pallas_call | solution.py:1260
  168.0 8.0 %convolution_convert_fusion.3 = bf16[1024,2048]{1,0:T(8,128)(2,1)} fusion(bf16[1024,768]{1,0:T(8,128)(2,1)} %get-tuple-element.54, bf16[2048,2176]{1,0:T(8,128)(2,1)} %bitcast.154), kind=kOutput, calls=%fused_computation.22 | convolution fusion | flops 3223322624 | bytes 8912896 | tf_op jit(solution)/shard_map/dot_general | solution.py:1011
  176.0 1.3 copy-done.4
  177.3 46.8 %middle_and_unit.1 = (f32[128,2048]{1,0:T(8,128)S(1)}, bf16[4,128,2048]{2,1,0:T(8,128)(2,1)S(1)}, bf16[4,320,2048]{2,1,0:T(8,128)(2,1)}) custom-call(bf16[2,2,2,128,2048]{4,3,2,1,0:T(8,128)(2,1)} %bitcast.125, bf16[128,2048]{1,0:T(8,128)(2,1)S(1)} %copy-done.1, f32[1,2048]{1,0:T(1,128)S(1)} %get-tuple-element.155.gain_ref, ...), custom_call_target="tpu_custom_call" | custom-call | tf_op jit(solution)/shard_map/middle_and_unit/pallas_call | solution.py:503
  224.1 1.3 copy-done.2
  225.4 1.9 fusion.35
  227.7 6.6 convolution_convert_fusion
  234.2 2.6 copy-done.6
  236.8 39.0 %rows_to_experts.1 = (bf16[4,320,2176]{2,1,0:T(8,128)(2,1)S(1)}, f32[1280,1408]{1,0:T(8,128)}) custom-call(bf16[4,320,2176]{2,1,0:T(8,128)(2,1)} %bitcast.122, bf16[1280,2048]{1,0:T(8,128)(2,1)S(1)} %bitcast.117, bf16[2048,1408]{1,0:T(8,128)(2,1)} %all-gather.9.cloned.1.call-done.down_ref), custom_call_target="tpu_custom_call" | custom-call | tf_op jit(solution)/shard_map/rows_to_experts/pallas_call | solution.py:699
  275.9 2.5 copy-done
  278.6 1.1 broadcast_in_dim.87.gate_ref
  279.7 7.0 all-gather.11.cloned.1.call-done.gate_up_ref.linear_up_ref.up_ref
  286.7 24.9 %experts.1 = (bf16[1280,1408]{1,0:T(8,128)(2,1)}, bf16[1280,1408]{1,0:T(8,128)(2,1)}, bf16[1280,1408]{1,0:T(8,128)(2,1)}, bf16[1280,1408]{1,0:T(8,128)(2,1)}, f32[1280,128]{1,0:T(8,128)}) custom-call(bf16[1280,2176]{1,0:T(8,128)(2,1)} %bitcast.112, f32[1280,1408]{1,0:T(8,128)} %get-tuple-element.59.raw_ref, ...), custom_call_target="tpu_custom_call" | custom-call | tf_op jit(solution)/shard_map/experts/pallas_call | solution.py:1044
  311.6 12.2 %convolution_convert_fusion.2 = bf16[2048,1408]{1,0:T(8,128)(2,1)} fusion(bf16[1280,2048]{1,0:T(8,128)(2,1)S(1)} %bitcast.120, bf16[1280,1408]{1,0:T(8,128)(2,1)} %get-tuple-element.64), kind=kOutput, calls=%fused_computation.9 | convolution fusion | flops 7384858624 | bytes 14614528 | tf_op jit(solution)/shard_map/dot_general | solution.py:1011
  324.4 53.7 %return_rows.1 = (bf16[4,160,2048]{2,1,0:T(8,128)(2,1)}, f32[4,160,128]{2,1,0:T(8,128)}, bf16[2048,2816]{1,0:T(8,128)(2,1)}) custom-call(bf16[1280,1408]{1,0:T(8,128)(2,1)} %get-tuple-element.61.dgate_pre_ref, bf16[1280,1408]{1,0:T(8,128)(2,1)} %get-tuple-element.62.dlinear_ref, ...), custom_call_target="tpu_custom_call" | custom-call | tf_op jit(solution)/shard_map/return_rows/pallas_call | solution.py:1173
  380.1 2.0 fusion.33
  382.1 4.3 fusion.11
  386.3 74.2 %middle_back.1 = (f32[128,2048]{1,0:T(8,128)}, f32[1,2048]{1,0:T(1,128)}, bf16[2,2,2,128,2048]{4,3,2,1,0:T(8,128)(2,1)}, bf16[4,160,2048]{2,1,0:T(8,128)(2,1)}) custom-call(bf16[4,128,2048]{2,1,0:T(8,128)(2,1)} %bitcast.142, f32[128,2048]{1,0:T(8,128)} %copy-done.13, bf16[128,2048]{1,0:T(8,128)(2,1)} %copy.163.grad_ref, f32[1,2048]{1,0:T(1,128)} %copy-done.19, ...), custom_call_target="tpu_custom_call" | custom-call | tf_op jit(solution)/shard_map/middle_back/pallas_call | solution.py:607
  460.6 8.8 %fusion.17.h0.h1.h2 = f32[1024,768]{1,0:T(8,128)} fusion(bf16[1024,2048]{1,0:T(8,128)(2,1)} %bitcast.176, bf16[2048,2176]{1,0:T(8,128)(2,1)} %bitcast.157), kind=kOutput, calls=%fused_computation.28 | convolution fusion | flops 3221225472 | bytes 10485760 | tf_op jit(solution)/shard_map/dot_general | solution.py:1011
  469.5 13.2 %attention_back.1 = (bf16[1024,1280]{1,0:T(8,128)(2,1)}, f32[1024,128]{1,0:T(8,128)S(1)}) custom-call(bf16[1024,256]{1,0:T(8,128)(2,1)S(1)} %copy-done.16, bf16[1024,256]{1,0:T(8,128)(2,1)S(1)} %copy-done.18, bf16[1024,768]{1,0:T(8,128)(2,1)S(1)} %get-tuple-element.52.q0.q1.q2, bf16[1024,768]{1,0:T(8,128)(2,1)S(1)} %get-tuple-element.52.q0.q1.q2, ...), custom_call_target="tpu_custom_call" | custom-call | tf_op jit(solution)/shard_map/attention_back/pallas_call | solution.py:1325
  483.3 13.2 %fusion.60 = (bf16[1024,2048]{1,0:T(8,128)(2,1)}, bf16[2048]{0:T(1024)(128)(2,1)S(1)}) fusion(f32[1024]{0:T(1024)S(1)} %add_rsqrt_fusion, bf16[1024,2048]{1,0:T(8,128)(2,1)} %all-gather.5.cloned.1.call-done, bf16[2048,2176]{1,0:T(8,128)(2,1)} %bitcast.158, bf16[1024,3]{1,0:T(8,128)(2,1)S(1)} %copy.170, bf16[1024,1280]{1,0:T(8,128)(2,1)} %get-tuple-element.72), kind=kOutput, calls=%fused_computation.125 | convolution fusion | flops 5924714496 | bytes 16791552 | tf_op jit(solution)/shard_map/dot_general | solution.py:1011
  496.8 1.2 convolution_convert_fusion.6
  499.3 5.2 bitcast_convert_fusion
  504.4 5.1 convolution_convert_fusion.4
  509.6 7.7 %convolution_convert_fusion.1 = bf16[2048,1280]{1,0:T(8,128)(2,1)} fusion(bf16[1024,1280]{1,0:T(8,128)(2,1)S(1)} %copy-done.43, bf16[1024,2048]{1,0:T(8,128)(2,1)S(1)} %copy-done.23, f32[2048]{0:T(1024)S(1)} %bitcast.173, f32[1024]{0:T(1024)S(1)} %add_rsqrt_fusion), kind=kOutput, calls=%fused_computation.8 | convolution fusion | flops 5379719168 | bytes 12070912 | tf_op jit(solution)/shard_map/dot_general | solution.py:1011
  517.3 65.3 %reduce-scatter.3.cloned.1.call-done = bf16[512,2816]{1,0:T(8,128)(2,1)} async-done(((bf16[2048,2816]{1,0:T(8,128)(2,1)}), bf16[512,2816]{1,0:T(8,128)(2,1)}) %reduce-scatter.3.cloned.1.call-update) | async-done | bytes 2883600 | tf_op jit(solution)/shard_map/reduce_scatter | solution.py:1486
  582.6 94.6 %finish.1 = (f32[2,64,2176]{2,1,0:T(8,128)}, bf16[4,64,2816]{2,1,0:T(8,128)(2,1)}, bf16[4,64,1408]{2,1,0:T(8,128)(2,1)}, bf16[128,2048]{1,0:T(8,128)(2,1)}, f32[128,2048]{1,0:T(8,128)}, /*index=5*/f32[64,128]{1,0:T(8,128)}) custom-call(bf16[4,2,4,64,1280]{4,3,2,1,0:T(8,128)(2,1)} %bitcast.123, bf16[4,2,4,64,128]{4,3,2,1,0:T(8,128)(2,1)} %bitcast.135, ...), custom_call_target="tpu_custom_call" | custom-call | tf_op jit(solution)/shard_map/finish/pallas_call | solution.py:949
  677.2 1.6 slice_reduce_fusion
  680.6 1.2 fusion.61
  681.8 1.3 copy.173
  686.9 1.1 reshape.446
  688.5 1.1 reshape.444
  689.5 1.7 copy.175
  691.3 1.3 copy.181
  692.6 2.3 convert_bitcast_fusion
  694.9 2.7 reshape.450
  (206 shorter events, 25.6 us)
Async XLA Ops:
  7.2 5.2 copy-start.37
  7.2 5.2 copy-start.36
  7.2 5.2 copy-start.40
  7.2 5.2 copy-start.38
  7.2 5.2 copy-start.41
  7.2 5.2 copy-start.39
  7.2 6.2 copy-start.33
  7.3 6.4 copy-start.31
  7.3 115.5 %all-gather.5.cloned.1.call-start = ((), (), s32[]{:S(2)}) async-start(), calls=%async_computation.2 | async-start | bytes 4718592 | tf_op jit(solution)/shard_map/all_gather | solution.py:1418
  8.7 5.4 copy-start.32
  8.8 5.8 copy-start.24
  9.8 166.1 %all-gather.7.cloned.1.call-start = ((), (), s32[]{:S(2)}) async-start(), calls=%async_computation.3 | async-start | bytes 2621440 | tf_op jit(solution)/shard_map/all_gather | solution.py:1419
  12.3 221.9 %all-gather.9.cloned.1.call-start = ((), (), s32[]{:S(2)}) async-start(), calls=%async_computation.4 | async-start | bytes 7208960 | tf_op jit(solution)/shard_map/all_gather | solution.py:1431
  112.1 2.7 copy-start.30
  112.1 4.3 copy-start.34
  112.2 174.5 %all-gather.11.cloned.1.call-start = ((), (), s32[]{:S(2)}) async-start(), calls=%async_computation.5 | async-start | bytes 14417920 | tf_op jit(solution)/shard_map/all_gather | solution.py:1428
  112.7 404.6 %reduce-scatter.5.cloned.1.call-start = ((), (), s32[]{:S(2)}) async-start(), calls=%async_computation.7 | async-start | bytes 6488064 | tf_op jit(solution)/shard_map/reduce_scatter | solution.py:1482
  120.2 20.2 %copy-start.7 = (f32[1024,128]{1,0:T(8,128)}, f32[1024,128]{1,0:T(8,128)S(1)}, u32[]{:S(2)}) copy-start(f32[1024,128]{1,0:T(8,128)S(1)} %get-tuple-element.163.cos_ref) | copy-start | bytes 1572868
  120.2 20.2 %copy-start.9 = (f32[1024,128]{1,0:T(8,128)}, f32[1024,128]{1,0:T(8,128)S(1)}, u32[]{:S(2)}) copy-start(f32[1024,128]{1,0:T(8,128)S(1)} %get-tuple-element.164.sin_ref) | copy-start | bytes 1572868
  122.8 53.2 %copy-start.19 = (f32[1,2048]{1,0:T(1,128)}, f32[1,2048]{1,0:T(1,128)S(1)}, u32[]{:S(2)}) copy-start(f32[1,2048]{1,0:T(1,128)S(1)} %get-tuple-element.155.gain_ref) | copy-start | bytes 24580
  122.8 4.3 copy-start.21
  136.5 2.5 copy-start.20
  168.0 8.0 %copy-start.1 = (bf16[128,2048]{1,0:T(8,128)(2,1)S(1)}, bf16[128,2048]{1,0:T(8,128)(2,1)}, u32[]{:S(2)}) copy-start(bf16[128,2048]{1,0:T(8,128)(2,1)} %copy.150.x_ref) | copy-start | bytes 1572868
  176.0 1.3 copy-start.4
  177.3 50.3 %copy-start.26 = (pred[1280,512]{1,0:T(32,128)(4,1)S(1)}, pred[1280,512]{1,0:T(32,128)(4,1)}, u32[]{:S(2)}) copy-start(pred[1280,512]{1,0:T(32,128)(4,1)} %bitcast_compare_fusion) | copy-start | bytes 1966084
  224.1 1.3 copy-start.2
  224.1 3.2 copy-start.13
  234.2 2.6 copy-start.6
  275.9 2.5 copy-start
  278.4 33.2 %slice-start = ((s8[5242880]{0:T(1024)(128)(4,1)}), s8[1048576]{0:T(1024)(128)(4,1)S(1)}, s32[]{:S(2)}) async-start(s8[5242880]{0:T(1024)(128)(4,1)} %bitcast.118), calls=%async_computation.8 | async-start | bytes 2097152
  286.7 24.9 %slice-start.1 = ((s8[5242880]{0:T(1024)(128)(4,1)}), s8[4194304]{0:T(1024)(128)(4,1)S(1)}, s32[]{:S(2)}) async-start(s8[5242880]{0:T(1024)(128)(4,1)} %bitcast.118), calls=%async_computation.9 | async-start | bytes 8388608
  323.9 258.7 %reduce-scatter.3.cloned.1.call-start = ((), (), s32[]{:S(2)}) async-start(), calls=%async_computation.6 | async-start | bytes 14417920 | tf_op jit(solution)/shard_map/reduce_scatter | solution.py:1486
  378.1 1.4 copy-start.5
  379.3 2.8 copy-start.44
  460.6 8.9 %copy-start.8 = (f32[1024,128]{1,0:T(8,128)S(1)}, f32[1024,128]{1,0:T(8,128)}, u32[]{:S(2)}) copy-start(f32[1024,128]{1,0:T(8,128)} %copy-done.7) | copy-start | bytes 1572868
  460.6 8.9 %copy-start.10 = (f32[1024,128]{1,0:T(8,128)S(1)}, f32[1024,128]{1,0:T(8,128)}, u32[]{:S(2)}) copy-start(f32[1024,128]{1,0:T(8,128)} %copy-done.9) | copy-start | bytes 1572868
  460.6 8.9 %copy-start.12 = (f32[1024,3]{1,0:T(8,128)S(1)}, f32[1024,3]{1,0:T(8,128)}, u32[]{:S(2)}) copy-start(f32[1024,3]{1,0:T(8,128)} %copy.160.gate_ref) | copy-start | bytes 36868
  460.6 8.9 %copy-start.16 = (bf16[1024,256]{1,0:T(8,128)(2,1)S(1)}, bf16[1024,256]{1,0:T(8,128)(2,1)}, u32[]{:S(2)}) copy-start(bf16[1024,256]{1,0:T(8,128)(2,1)} %copy-done.15) | copy-start | bytes 1572868
  460.6 8.9 %copy-start.18 = (bf16[1024,256]{1,0:T(8,128)(2,1)S(1)}, bf16[1024,256]{1,0:T(8,128)(2,1)}, u32[]{:S(2)}) copy-start(bf16[1024,256]{1,0:T(8,128)(2,1)} %copy-done.17) | copy-start | bytes 1572868
  483.2 13.2 %copy-start.3 = (bf16[4,128,2048]{2,1,0:T(8,128)(2,1)S(1)}, bf16[4,128,2048]{2,1,0:T(8,128)(2,1)}, u32[]{:S(2)}) copy-start(bf16[4,128,2048]{2,1,0:T(8,128)(2,1)} %copy-done.2) | copy-start | bytes 6291460
  483.2 13.6 %copy-start.22 = (bf16[1024,2048]{1,0:T(8,128)(2,1)S(1)}, bf16[1024,2048]{1,0:T(8,128)(2,1)}, u32[]{:S(2)}) copy-start(bf16[1024,2048]{1,0:T(8,128)(2,1)} %all-gather.5.cloned.1.call-done) | copy-start | bytes 12582916
  496.8 2.5 copy-start.27
  499.3 5.2 copy-start.42
  499.3 5.2 copy-start.45
  504.4 5.1 copy-start.23
  504.4 5.1 copy-start.43
  677.2 6.9 copy-start.28
  689.5 5.4 copy-start.25
  (6 other events, 5.9 us)
Sparse Core Ops, SparseCore 0:
  10.3 60.5 all-gather.4
  72.6 40.8 all-gather.6
  115.2 59.7 all-gather.8
  176.4 110.2 all-gather.10
  324.0 149.3 reduce-scatter.4
  475.7 106.8 reduce-scatter.2

commit v6 on v5

--- a/solution.py
+++ b/solution.py
@@ -8,6 +8,8 @@
 from jax.experimental.pallas import tpu as pltpu
 from jax.sharding import Mesh, PartitionSpec as P
 
+LANES = 128
+WIDE = 256
 HD = 128
 HEADS = 2
 CAP = 320
@@ -74,8 +76,10 @@
     loc, xs, xr, s1, r1m, r1p, f1s, f1r, s2, r2m, r2p, f2s, f2r, es, er, ex, ey, ms, mr,
 ):
     y, xl, z = lax.axis_index("y"), lax.axis_index("xl"), lax.axis_index("z")
-    half = x_ref.shape[1] // 2
-    quarter = half // 2
+    rows, cols = x_ref.shape[1:]
+    half = rows // 2
+    split = cols // (3 * LANES) * LANES
+    columns = (pl.ds(0, split), pl.ds(split, cols - split))
     greet(
         neighbour("xl", 1),
         *(neighbour("y", step) for step in (1, 2, 3)),
@@ -90,7 +94,7 @@
 
     def slot(h, first, second, j, start, count):
         yy, zz = (second, first) if h == 0 else (first, second)
-        return out_ref.at[zz, j, yy, pl.ds(start, count)]
+        return out_ref.at[zz, j, yy, pl.ds(start, count), columns[h]]
 
     own = pltpu.make_async_copy(x_ref.at[xl], out_ref.at[z, xl, y], loc.at[0])
     own.start()
@@ -113,21 +117,21 @@
             )
     for h in (0, 1):
         first, second = place[rings[h][0]], place[rings[h][1]]
-        src = x_ref.at[xl, pl.ds(h * half, half)]
-        dst = slot(h, first, second, xl, h * half, half)
-        send(x_ref.at[other, pl.ds(h * half, half)], dst, xs.at[h], xr.at[h], neighbour("xl", 1))
+        src = x_ref.at[xl, :, columns[h]]
+        dst = slot(h, first, second, xl, 0, rows)
+        send(x_ref.at[other, :, columns[h]], dst, xs.at[h], xr.at[h], neighbour("xl", 1))
         send(src, dst, s1.at[h, 0, 0], r1m.at[h, 0], neighbour(rings[h][0], 1))
         send(src, dst, s1.at[h, 0, 1], r1p.at[h, 0], neighbour(rings[h][0], -1))
     own.wait()
 
     def send_second(h, k, first):
-        block = slot(h, first, place[rings[h][1]], both, h * half, half)
+        block = slot(h, first, place[rings[h][1]], both, 0, rows)
         send(block, block, s2.at[h, k, 0], r2m.at[h, k], neighbour(rings[h][1], 1))
         send(block, block, s2.at[h, k, 1], r2p.at[h, k], neighbour(rings[h][1], -1))
 
     for h in (0, 1):
         first, second = place[rings[h][0]], place[rings[h][1]]
-        block = slot(h, first, second, other, h * half, half)
+        block = slot(h, first, second, other, 0, rows)
         arrived(block, xr.at[h])
         send(block, block, s1.at[h, 1, 0], r1m.at[h, 1], neighbour(rings[h][0], 1))
         send(block, block, s1.at[h, 1, 1], r1p.at[h, 1], neighbour(rings[h][0], -1))
@@ -135,42 +139,42 @@
     for j, jx in ((0, xl), (1, other)):
         for h in (0, 1):
             first, second = place[rings[h][0]], place[rings[h][1]]
-            arrived(slot(h, mod4(first - 1), second, jx, h * half, half), r1m.at[h, j])
-            block = slot(h, mod4(first - 1), second, jx, h * half, quarter)
+            arrived(slot(h, mod4(first - 1), second, jx, 0, rows), r1m.at[h, j])
+            block = slot(h, mod4(first - 1), second, jx, 0, half)
             send(block, block, f1s.at[h, j, 0], f1r.at[h, j, 0], neighbour(rings[h][0], 1))
-            arrived(slot(h, mod4(first + 1), second, jx, h * half, half), r1p.at[h, j])
-            block = slot(h, mod4(first + 1), second, jx, h * half + quarter, quarter)
+            arrived(slot(h, mod4(first + 1), second, jx, 0, rows), r1p.at[h, j])
+            block = slot(h, mod4(first + 1), second, jx, half, half)
             send(block, block, f1s.at[h, j, 1], f1r.at[h, j, 1], neighbour(rings[h][0], -1))
     for k, step in ((1, -1), (2, 1)):
         for h in (0, 1):
             send_second(h, k, mod4(place[rings[h][0]] + step))
+    for h in (0, 1):
+        first, second = place[rings[h][0]], place[rings[h][1]]
+        for j, jx in ((0, xl), (1, other)):
+            for p in (0, 1):
+                block = slot(h, mod4(first + 2), second, jx, p * half, half)
+                arrived(block, f1r.at[h, j, p])
+        send_second(h, 3, mod4(first + 2))
     for n, (shards, expert) in enumerate(experts):
         for step in (1, 3, 2):
             landed = expert.at[xl, mod4(y - step)]
             arrived(landed, er.at[n, step - 1])
             send(landed, landed, ex.at[n, step], ey.at[n, step], neighbour("xl", 1))
-    for h in (0, 1):
-        first, second = place[rings[h][0]], place[rings[h][1]]
-        for j, jx in ((0, xl), (1, other)):
-            for p in (0, 1):
-                block = slot(h, mod4(first + 2), second, jx, h * half + p * quarter, quarter)
-                arrived(block, f1r.at[h, j, p])
-        send_second(h, 3, mod4(first + 2))
     steps = ((0, 0), (1, -1), (2, 1), (3, 2))
     for k, step in steps:
         for h in (0, 1):
             first, second = mod4(place[rings[h][0]] + step), place[rings[h][1]]
-            arrived(slot(h, first, mod4(second - 1), both, h * half, half), r2m.at[h, k])
-            block = slot(h, first, mod4(second - 1), both, h * half, quarter)
+            arrived(slot(h, first, mod4(second - 1), both, 0, rows), r2m.at[h, k])
+            block = slot(h, first, mod4(second - 1), both, 0, half)
             send(block, block, f2s.at[h, k, 0], f2r.at[h, k, 0], neighbour(rings[h][1], 1))
-            arrived(slot(h, first, mod4(second + 1), both, h * half, half), r2p.at[h, k])
-            block = slot(h, first, mod4(second + 1), both, h * half + quarter, quarter)
+            arrived(slot(h, first, mod4(second + 1), both, 0, rows), r2p.at[h, k])
+            block = slot(h, first, mod4(second + 1), both, half, half)
             send(block, block, f2s.at[h, k, 1], f2r.at[h, k, 1], neighbour(rings[h][1], -1))
     for k, step in steps:
         for h in (0, 1):
             first, second = mod4(place[rings[h][0]] + step), place[rings[h][1]]
             for p in (0, 1):
-                block = slot(h, first, mod4(second + 2), both, h * half + p * quarter, quarter)
+                block = slot(h, first, mod4(second + 2), both, p * half, half)
                 arrived(block, f2r.at[h, k, p])
     for n, (shards, expert) in enumerate(experts):
         for step in (0, 1, 3, 2):
@@ -435,40 +439,11 @@
     return [dma((CHUNKS,)), dma((CHUNKS,)), dma((CHUNKS, 2)), dma((CHUNKS, 2))]
 
 
-def middle_body(
-    part_ref, x_ref, gain_ref, pick_ref, grad_ref, middle_ref, unit_ref, rows_out, rows_buf, loc, ys, yr, cs, cr, *scratch
-):
+def middle_body(part_ref, x_ref, gain_ref, middle_ref, unit_ref, *scratch):
     sends = Sends()
-    y, core = lax.axis_index("y"), lax.axis_index("core")
-    greet(*along_x(), *(neighbour("y", step) for step in (1, 2, 3)))
-    stages = ring_reduce_stages(part_ref, *scratch[:8], sends)
-    next(stages)
-    slots = pick_ref.shape[1] // 2
-    mine = pl.ds(pl.multiple_of(core * slots, slots), slots)
-
-    def pick(step):
-        target = mod4(y + step)
-        rows_buf[step - 1] = dot(pick_ref[target, mine, :], grad_ref[...], ((1,), (0,))).astype(BF16)
-        sends(
-            rows_buf.at[step - 1],
-            rows_out.at[y, mine],
-            ys.at[step - 1],
-            yr.at[step - 1],
-            neighbour("y", step),
-        )
-
-    pick(2)
-    next(stages)
-    pick(1)
-    pick(3)
-    rows_buf[3] = dot(pick_ref[y, :slots, :], grad_ref[...], ((1,), (0,))).astype(BF16)
-    rows_buf[4] = dot(pick_ref[y, slots:, :], grad_ref[...], ((1,), (0,))).astype(BF16)
-    kept = []
-    for n in (0, 1):
-        kept.append(pltpu.make_async_copy(rows_buf.at[3 + n], rows_out.at[y, pl.ds(n * slots, slots)], loc.at[n]))
-        kept[-1].start()
-    total = next(stages)
-    me = lax.axis_index("xh") * 2 + core
+    greet(*along_x())
+    *_, total = ring_reduce_stages(part_ref, *scratch[:8], sends)
+    me = lax.axis_index("xh") * 2 + lax.axis_index("core")
     step = x_ref.shape[0] // CHUNKS
     half = x_ref.shape[0] // 2
     for part in (0, 1):
@@ -480,15 +455,6 @@
         for n in range(part * CHUNKS // 2, (part + 1) * CHUNKS // 2):
             spread_chunk(unit_ref, n, step, scratch[8:], sends)
     spread_finish(unit_ref, step, scratch[8:], sends)
-    for step in (1, 3, 2):
-        block = rows_out.at[mod4(y - step), mine]
-        arrived(block, yr.at[step - 1])
-        sends(block, block, cs.at[step - 1], cr.at[step - 1], neighbour("core", 1))
-    other = pl.ds(pl.multiple_of((1 - core) * slots, slots), slots)
-    for step in (1, 3, 2):
-        arrived(rows_out.at[mod4(y - step), other], cr.at[step - 1])
-    for copy in kept:
-        copy.wait()
     sends.finish()
 
 
@@ -496,69 +462,48 @@
     return [pl.BlockSpec(memory_space=pltpu.VMEM)] * count
 
 
-def middle_and_unit(part, x, gain, pick, grads):
+def middle_and_unit(part, x, gain):
     rows, width = x.shape
-    experts, slots, _ = pick.shape
-    dma = pltpu.SemaphoreType.DMA
-    middle, unit, rows_in = pl.pallas_call(
+    middle, unit = pl.pallas_call(
         middle_body,
         out_shape=[
             jax.ShapeDtypeStruct((rows, width), F32),
             jax.ShapeDtypeStruct((4, rows, width), BF16),
-            jax.ShapeDtypeStruct((experts, slots, width), BF16),
         ],
-        in_specs=vmem(5),
-        out_specs=vmem(2) + [pl.BlockSpec(memory_space=pl.ANY)],
-        scratch_shapes=[
-            pltpu.VMEM((5, slots // 2, width), BF16),
-            dma((2,)),
-            dma((3,)),
-            dma((3,)),
-            dma((3,)),
-            dma((3,)),
-        ]
-        + ring_reduce_scratch(rows, width)
-        + spread_scratch(),
+        in_specs=vmem(3),
+        out_specs=vmem(2),
+        scratch_shapes=ring_reduce_scratch(rows, width) + spread_scratch(),
         compiler_params=pltpu.CompilerParams(
-            collective_id=1, has_side_effects=True, vmem_limit_bytes=48 * MIB
+            collective_id=1, has_side_effects=True, vmem_limit_bytes=32 * MIB
         ),
         name="middle_and_unit",
-    )(part.reshape(2, 2, 2, rows, width), x, gain[None], pick, grads)
-    return middle, unit.reshape(4 * rows, width), rows_in.reshape(experts * slots, width)
+    )(part.reshape(2, 2, 2, rows, width), x, gain[None])
+    return middle, unit.reshape(4 * rows, width)
 
 
 def back_body(
     part_ref, middle_ref, grad_ref, gain_ref, hidden_ref, down_ref, dmiddle_ref, dgain_ref, spread_ref, branch_out,
-    hidden, down, branch, branch_buf, branch_sum, loc, cs, cr, ys, yr, *scratch,
+    hidden, down, branch, loc, out_sem, *scratch,
 ):
     sends = Sends()
-    y, core = lax.axis_index("y"), lax.axis_index("core")
     loads = []
     for n, (src, dst) in enumerate(((hidden_ref, hidden), (down_ref, down))):
         loads.append(pltpu.make_async_copy(src, dst, loc.at[n]))
         loads[-1].start()
-    greet(*along_x(), *(neighbour("y", step) for step in (1, 2, 3)))
+    greet(*along_x())
     stages = reduce_stages(CHUNKS, [part_ref], *scratch[:7], sends)
     next(stages)
-    slots = branch_out.shape[1]
-    mine = pl.ds(pl.multiple_of(core * slots, slots), slots)
-    theirs = pl.ds(pl.multiple_of((1 - core) * slots, slots), slots)
-
-    def output(step):
-        target = mod4(y + step)
-        branch[step] = dot(hidden[target], down[...], ((1,), (1,))).astype(BF16)
-        sends(
-            branch.at[step, theirs], branch_buf.at[step], cs.at[step], cr.at[step], neighbour("core", 1)
-        )
-
+    next(stages)
     for load in loads:
         load.wait()
-    output(2)
-    next(stages)
-    for step in (1, 3, 0):
-        output(step)
+    slots = branch.shape[1]
+    outs = []
+    for n in range(4):
+        branch[n] = dot(hidden[n * slots : (n + 1) * slots, :], down[...], ((1,), (1,))).astype(BF16)
+        outs.append(pltpu.make_async_copy(branch.at[n], branch_out.at[n], out_sem.at[n]))
+        outs[-1].start()
     total = next(stages)
-    xl, xh = lax.axis_index("xl"), lax.axis_index("xh")
+    xl, xh, core = lax.axis_index("xl"), lax.axis_index("xh"), lax.axis_index("core")
     step = middle_ref.shape[0] // CHUNKS
     for n in range(CHUNKS):
         rows = slice(n * step, (n + 1) * step)
@@ -578,23 +523,9 @@
         spread_ref[xl, xh, core, rows, :] = dmiddle.astype(BF16)
         if n % 2 == 1:
             ring_spread(spread_ref, n // 2, *scratch[7:], sends)
-    for step in (2, 1, 3, 0):
-        arrived(branch_buf.at[step], cr.at[step])
-        value = (branch[step, mine, :].astype(F32) + branch_buf[step].astype(F32)).astype(BF16)
-        if step == 0:
-            branch_out[y] = value
-        else:
-            branch_sum[step - 1] = value
-            sends(
-                branch_sum.at[step - 1],
-                branch_out.at[y],
-                ys.at[step - 1],
-                yr.at[step - 1],
-                neighbour("y", step),
-            )
     ring_spread_finish(spread_ref, *scratch[7:], sends)
-    for step in (1, 3, 2):
-        arrived(branch_out.at[mod4(y - step)], yr.at[step - 1])
+    for out in outs:
+        out.wait()
     sends.finish()
 
 
@@ -610,29 +541,24 @@
             jax.ShapeDtypeStruct((rows, width), F32),
             jax.ShapeDtypeStruct((1, width), F32),
             jax.ShapeDtypeStruct((2, 2, 2, rows, width), BF16),
-            jax.ShapeDtypeStruct((4, slots // 2, width), BF16),
+            jax.ShapeDtypeStruct((4, slots, width), BF16),
         ],
         in_specs=vmem(4) + [anywhere] * 2,
-        out_specs=vmem(4),
+        out_specs=vmem(3) + [anywhere],
         scratch_shapes=[
-            pltpu.VMEM((4, slots, inner), BF16),
+            pltpu.VMEM((count, inner), BF16),
             pltpu.VMEM(down.shape, BF16),
             pltpu.VMEM((4, slots, width), BF16),
-            pltpu.VMEM((4, slots // 2, width), BF16),
-            pltpu.VMEM((3, slots // 2, width), BF16),
             dma((2,)),
             dma((4,)),
-            dma((4,)),
-            dma((3,)),
-            dma((3,)),
         ]
         + reduce_scratch(1, rows, width)
         + ring_spread_scratch(),
         compiler_params=pltpu.CompilerParams(
-            collective_id=2, has_side_effects=True, vmem_limit_bytes=56 * MIB
+            collective_id=2, has_side_effects=True, vmem_limit_bytes=48 * MIB
         ),
         name="middle_back",
-    )(part.reshape(4, rows, width), middle, grad, gain[None], hidden.reshape(4, slots, inner), down)
+    )(part.reshape(4, rows, width), middle, grad, gain[None], hidden, down)
     return dmiddle, dgain[0], spread.reshape(8 * rows, width), branch
 
 
@@ -688,10 +614,6 @@
     sends.finish()
 
 
-LANES = 128
-WIDE = 256
-
-
 def rows_to_experts(rows, grads, down):
     count, hidden = grads.shape[0], down.shape[1]
     anywhere = pl.BlockSpec(memory_space=pl.ANY)
@@ -730,7 +652,7 @@
     out_ref, up_out, down_out, output_ref, dinput_ref, small_out,
     g_ref, loc, t_buf, r_buf, tb_buf, rb_buf, c_buf,
     t_s, t_r, r_s, r_r, tb_s, tb_r, rb_s, rb_r, c_s, c_r,
-    up_own, up_buf, up_sum, ex, ey, es, er,
+    up_own, down_own, up_buf, down_buf, up_sum, down_sum, ex, ey, es, er,
     small_own, small_buf, small_s, small_r, *scratch,
 ):
     xl, xh, core = lax.axis_index("xl"), lax.axis_index("xh"), lax.axis_index("core")
@@ -747,8 +669,8 @@
         parts.append(pltpu.make_async_copy(ref, g_ref.at[..., pl.ds(column, cols)], loc.at[n]))
         parts[-1].start()
         column += cols
-    for n, (src, dst) in enumerate(((ups_ref.at[xl], up_own), (downs_ref.at[my_y], down_out.at[my_y]))):
-        parts.append(pltpu.make_async_copy(src, dst, loc.at[3 + n]))
+    for n, (ref, own) in enumerate(((ups_ref, up_own), (downs_ref, down_own))):
+        parts.append(pltpu.make_async_copy(ref.at[xl], own, loc.at[3 + n]))
         parts[-1].start()
     peers = ({"xh": xh, "core": 1 - core}, {"xh": 1 - xh, "core": core}, {"xh": 1 - xh, "core": 1 - core})
     greet(
@@ -761,14 +683,16 @@
     both = slice(0, 2)
     ring_stages = ring_reduce_stages(part_ref, *scratch[7:15], sends)
     feed_stages = reduce_stages(CHUNKS, [feed_ref], *scratch[:7], sends)
-    for step in (2, 1, 3, 0):
-        sends(
-            ups_ref.at[1 - xl, mod4(my_y + step)],
-            up_buf.at[step],
-            ex.at[step],
-            ey.at[step],
-            neighbour("xl", 1),
-        )
+    experts = ((ups_ref, up_own, up_buf, up_sum, up_out), (downs_ref, down_own, down_buf, down_sum, down_out))
+    for n, (grads, _, buf, _, _) in enumerate(experts):
+        for step in (2, 1, 3, 0):
+            sends(
+                grads.at[1 - xl, mod4(my_y + step)],
+                buf.at[step],
+                ex.at[n, step],
+                ey.at[n, step],
+                neighbour("xl", 1),
+            )
     next(ring_stages)
     next(feed_stages)
     for part in parts[:3]:
@@ -827,31 +751,24 @@
                     neighbour(rings[h][1], way),
                 )
     total = next(ring_stages)
-    for step in (2, 1, 3):
-        sends(
-            downs_ref.at[mod4(my_y + step)],
-            down_out.at[my_y],
-            es.at[1, step - 1],
-            er.at[1, step - 1],
-            neighbour("y", step),
-        )
     for part in parts[3:]:
         part.wait()
-    for step in (2, 1, 3, 0):
-        target = mod4(my_y + step)
-        arrived(up_buf.at[step], ey.at[step])
-        value = (up_own[target].astype(F32) + up_buf[step].astype(F32)).astype(BF16)
-        if step == 0:
-            up_out[my_y] = value
-        else:
-            up_sum[step - 1] = value
-            sends(
-                up_sum.at[step - 1],
-                up_out.at[my_y],
-                es.at[0, step - 1],
-                er.at[0, step - 1],
-                neighbour("y", step),
-            )
+    for n, (_, own, buf, summed, result) in enumerate(experts):
+        for step in (2, 1, 3, 0):
+            target = mod4(my_y + step)
+            arrived(buf.at[step], ey.at[n, step])
+            value = (own[target].astype(F32) + buf[step].astype(F32)).astype(BF16)
+            if step == 0:
+                result[my_y] = value
+            else:
+                summed[step - 1] = value
+                sends(
+                    summed.at[step - 1],
+                    result.at[my_y],
+                    es.at[n, step - 1],
+                    er.at[n, step - 1],
+                    neighbour("y", step),
+                )
     for k in range(4):
         for h in (0, 1):
             second = place[rings[h][1]]
@@ -928,7 +845,7 @@
     for n in range(CHUNKS):
         rows = slice(n * step, (n + 1) * step)
         output_ref[rows, :] = (middle_ref[rows, :] + feed(0, n)).astype(BF16)
-    for n, result in enumerate((up_out, down_out)):
+    for n, (_, _, _, _, result) in enumerate(experts):
         for step in (1, 3, 2):
             arrived(result.at[mod4(my_y - step)], er.at[n, step - 1])
     for n in range(3):
@@ -977,10 +894,13 @@
             dma((2,)),
             dma((2,)),
             pltpu.VMEM((4, share, up_cols), BF16),
+            pltpu.VMEM((4, share, down_cols), BF16),
             pltpu.VMEM((4, share, up_cols), BF16),
+            pltpu.VMEM((4, share, down_cols), BF16),
             pltpu.VMEM((3, share, up_cols), BF16),
-            dma((4,)),
-            dma((4,)),
+            pltpu.VMEM((3, share, down_cols), BF16),
+            dma((2, 4)),
+            dma((2, 4)),
             dma((2, 3)),
             dma((2, 3)),
             pltpu.VMEM(small, F32),
@@ -997,7 +917,7 @@
     )(
         *(grad.reshape(4, 2, 4, share, grad.shape[1]) for grad in grads),
         ups.reshape(2, 4, share, up_cols),
-        downs.reshape(4, share, down_cols),
+        downs.reshape(2, 4, share, down_cols),
         part.reshape(2, 2, 2, own_rows, width),
         feed.reshape(4, own_rows, width),
         x,
@@ -1220,22 +1140,28 @@
     key_out[...] = key
     val_out[...] = val
     tokens = key.shape[0]
-    seg_col, seg_row = col_ref[...], row_ref[0]
-    at_row = lax.broadcasted_iota(jnp.int32, (tokens, tokens), 0)
-    at_col = lax.broadcasted_iota(jnp.int32, (tokens, tokens), 1)
-    allowed = (at_col <= at_row) & ((seg_row == 0) | (seg_row == seg_col))
+    half = tokens // 2
+    allowed = []
+    for start in (0, half):
+        seen = start + half
+        at_row = start + lax.broadcasted_iota(jnp.int32, (half, seen), 0)
+        at_col = lax.broadcasted_iota(jnp.int32, (half, seen), 1)
+        seg_row, seg_col = row_ref[0, :, :seen], col_ref[start : start + half, :]
+        allowed.append((at_col <= at_row) & ((seg_row == 0) | (seg_row == seg_col)))
     for e, q_ref in enumerate((q0, q1, q2)):
         query = (rotated(q_ref[...]) * scale).astype(BF16)
-        scores = jnp.where(allowed, dot(query, key, ((1,), (1,))), NEGATIVE)
-        largest = jnp.max(scores, 1, keepdims=True)
-        expsum = jnp.exp(scores - largest)
-        prob = (expsum * (1.0 / jnp.sum(expsum, 1, keepdims=True))).astype(BF16)
-        prob_out[0, 0, e] = prob
-        mixed = dot(prob, val, ((1,), (0,))).astype(BF16)
         at = pl.ds(pl.multiple_of((e * HEADS + h) * HD, HD), HD)
         que_out[:, at] = query
-        mix_out[:, at] = mixed
-        gmix_out[:, at] = (mixed.astype(F32) * gate_ref[:, e : e + 1]).astype(BF16)
+        for n, start in enumerate((0, half)):
+            rows, seen = slice(start, start + half), start + half
+            scores = jnp.where(allowed[n], dot(query[rows], key[:seen], ((1,), (1,))), NEGATIVE)
+            largest = jnp.max(scores, 1, keepdims=True)
+            expsum = jnp.exp(scores - largest)
+            prob = (expsum * (1.0 / jnp.sum(expsum, 1, keepdims=True))).astype(BF16)
+            prob_out[0, 0, e, rows, :seen] = prob
+            mixed = dot(prob, val[:seen], ((1,), (0,))).astype(BF16)
+            mix_out[rows, at] = mixed
+            gmix_out[rows, at] = (mixed.astype(F32) * gate_ref[rows, e : e + 1]).astype(BF16)
 
 
 def block_specs(tokens):
@@ -1286,8 +1212,9 @@
 
     key, val = key_ref[...], val_ref[...]
     tokens = key.shape[0]
-    dkey = jnp.zeros((tokens, HD), F32)
-    dval = jnp.zeros((tokens, HD), F32)
+    half = tokens // 2
+    dkeys = [jnp.zeros((half, HD), F32)] * 2
+    dvals = [jnp.zeros((half, HD), F32)] * 2
     lane = lax.broadcasted_iota(jnp.int32, (tokens, HD), 1)
     dgates = jnp.zeros((tokens, HD), F32)
     for e, (q_ref, m_ref, h_ref) in enumerate(((q0, m0, h0), (q1, m1, h1), (q2, m2, h2))):
@@ -1296,15 +1223,25 @@
         dgates = dgates + jnp.where(lane == e, inner, 0.0)
         gate = gate_ref[:, e : e + 1]
         dmixed = (raw * gate).astype(BF16)
-        prob = prob_ref[0, 0, e]
-        dval = dval + dot(prob, dmixed, ((0,), (0,)))
-        dprob = dot(dmixed, val, ((1,), (1,)))
         delta = jnp.sum(dmixed.astype(F32) * mixed, 1, keepdims=True)
-        dscores = (prob.astype(F32) * (dprob - delta)).astype(BF16)
-        dquery = dot(dscores, key, ((1,), (0,)))
-        dkey = dkey + dot(dscores, query, ((0,), (0,)))
+        dqueries = []
+        for start in (0, half):
+            rows, seen = slice(start, start + half), start + half
+            prob = prob_ref[0, 0, e, rows, :seen]
+            dprob = dot(dmixed[rows], val[:seen], ((1,), (1,)))
+            dscores = (prob.astype(F32) * (dprob - delta[rows])).astype(BF16)
+            dqueries.append(dot(dscores, key[:seen], ((1,), (0,))))
+            dval = dot(prob, dmixed[rows], ((0,), (0,)))
+            dkey = dot(dscores, query[rows], ((0,), (0,)))
+            dvals[0] = dvals[0] + dval[:half]
+            dkeys[0] = dkeys[0] + dkey[:half]
+            if start:
+                dvals[1] = dvals[1] + dval[half:]
+                dkeys[1] = dkeys[1] + dkey[half:]
+        dquery = jnp.concatenate(dqueries, 0)
         at = pl.ds(pl.multiple_of(((2 + e) * HEADS + h) * HD, HD), HD)
         grad_out[:, at] = rotated_back(dquery * scale).astype(BF16)
+    dkey, dval = jnp.concatenate(dkeys, 0), jnp.concatenate(dvals, 0)
     grad_out[:, pl.ds(pl.multiple_of(h * HD, HD), HD)] = rotated_back(dkey).astype(BF16)
     grad_out[:, pl.ds(pl.multiple_of((HEADS + h) * HD, HD), HD)] = dval.astype(BF16)
 
@@ -1440,6 +1377,10 @@
     slot = jnp.where(match > 0, rank.astype(jnp.int32), -1)
     pick = (slot.T[:, None, :] == jnp.arange(CAP, dtype=jnp.int32)[None, :, None]).astype(BF16)
     pick_rows = pick.reshape(mlp_count * CAP, tokens)
+    grad_rows = dot(pick_rows, grad_all, ((1,), (0,))).astype(BF16)
+    grad_in = lax.all_to_all(grad_rows.reshape(mlp_count, CAP, width), "y", 0, 0, tiled=True)
+    grad_in = grad_in.reshape(mlp_count * CAP, width)
+
     small_all = weights[:, small_at : small_at + 128].astype(F32)
     gain_one, gain_two = small_all[:, 7], small_all[:, 8]
     segments = marks[:, :, 0]
@@ -1460,7 +1401,7 @@
     )
     out_weights = weights[:, out_at:]
     attention = dot(gmixed, out_weights, ((1,), (1,))).astype(BF16)
-    middle, unit_two, grad_in = middle_and_unit(attention, inputs, gain_two, pick, grad_all)
+    middle, unit_two = middle_and_unit(attention, inputs, gain_two)
 
     router_two = weights[:, small_at + att_count : small_at + att_count + mlp_count]
     logit_mlp = dot(unit_two, router_two, ((1,), (0,)))
@@ -1479,7 +1420,7 @@
     dgate_pre, dlinear, hidden, gated, dgate_part = experts(rows_ext, raw, up_whole, gates_in)
     grad_down_whole = dot(grad_in, gated, ((0,), (0,))).astype(BF16)
     dgate_part, grad_down_whole = lax.optimization_barrier((dgate_part, grad_down_whole))
-    grad_down_sum = lax.psum_scatter(grad_down_whole, ("z", "xl"), scatter_dimension=0, tiled=True)
+    grad_down_sum = lax.psum_scatter(grad_down_whole, "z", scatter_dimension=0, tiled=True)
     dunit_back, dgate_back, grad_up_whole = return_rows(
         dgate_pre, dlinear, up_whole, dgate_part.reshape(mlp_count, CAP, LANES), rows_ext
     )
@@ -1491,9 +1432,10 @@
         pick_half.reshape(-1, tokens), dunit_back.reshape(-1, width), ((0,), (0,))
     ) + dot(dlogit_mlp, router_two, ((1,), (1,)))
     grad_rmlp = dot(unit_two, dlogit_mlp, ((0,), (0,)))
-    dmiddle, grad_gain_two, dattention, branch_back = middle_back(
+    dmiddle, grad_gain_two, dattention, branch_part = middle_back(
         dunit_two.astype(BF16), middle, out_grad, gain_two, hidden, down_whole
     )
+    branch_back = lax.all_to_all(branch_part, "y", 0, 0, tiled=True)
 
     raw = dot(dattention, out_weights, ((1,), (0,)))
     grad_qkv, dgate_one = attention_back(
@@ -1512,9 +1454,9 @@
         ],
         1,
     )
-    gate_slots = jnp.sum(pick_half.astype(F32) * gate_mlp.T[:, None, :], -1, keepdims=True)
+    gate_slots = jnp.sum(pick.astype(F32) * gate_mlp.T[:, None, :], -1, keepdims=True)
     feed = dot(
-        pick_half.reshape(-1, tokens),
+        pick_rows,
         (branch_back.astype(F32) * gate_slots).astype(BF16).reshape(-1, width),
         ((0,), (0,)),
     )

time: 710 us -> 656 us (0.924)
  waiting for transfers between devices: 72.9 us -> 29.9 us
  Pallas kernels: 465 us -> 439 us
  starting transfers between devices: 1.17 us -> 11.5 us
    reduce_scatter x1, waiting for transfers between devices: 65.3 us -> 0.02 us  [on_device(): lax.psum_scatter(grad_up_whole, 'z', scatter_dimension=0, tiled=True)]
    pallas_call x1, Pallas kernels: 74.2 us -> 40.5 us  [middle_back(): pl.pallas_call(back_body, out_shape=[jax.ShapeDtypeStruct((rows, width),...]
    pallas_call x1, Pallas kernels: 94.6 us -> 111 us  [finish(): pl.pallas_call(finish_body, out_shape=[jax.ShapeDtypeStruct((2, share, co...]
    all_gather x1, waiting for transfers between devices: 6.98 us -> 22.9 us  [on_device(): lax.all_gather(up_parts.reshape(2 * mlp_count * share, -1), 'z', axis=0,...]
    all_to_all x0 -> x2, starting transfers between devices: none -> 10.4 us  [the longest x1 5.25 us: on_device(): branch_back = lax.all_to_all(branch_part, 'y', 0, 0, tiled=True)]
    pallas_call x1, Pallas kernels: 23.9 us -> 15.7 us  [attention_forward(): pl.pallas_call(attention_body, grid=(groups, HEADS), in_specs=[column(n)...]
    pallas_call x1, Pallas kernels: 46.8 us -> 39.2 us  [middle_and_unit(): pl.pallas_call(middle_body, out_shape=[jax.ShapeDtypeStruct((rows, width)...]
    dot_general x15 -> x16, matrix products: 86 us -> 92.9 us  [dot(): return lax.dot_general(a, b, (dims, ((), ())), preferred_element_type=F32)]
  transfers between devices with their start and end apart: 6 -> 8, of which waited for: 2 -> 2; matrix products, arithmetic and copies ran while one was open for 14% -> 16% of each run, Pallas kernels for 49% -> 47%
where the time goes in v6:
time: 656 us; the launch traced here: 647 us
  Pallas kernels  439 us (67%)
  matrix products  92.9 us (14%)
  local copies, waits for them, and re-layouts  47.3 us (7%)
  waiting for transfers between devices  29.9 us (5%)
  between operations  15.4 us (2%)
  starting transfers between devices  11.5 us (2%)
  other arithmetic  11.5 us (2%)
    pallas_call x1, Pallas kernels, finish(): pl.pallas_call(finish_body, out_shape=[jax.ShapeDtypeStruct((2, share, co...  111 us
    pallas_call x1, Pallas kernels, gather_dp(): pl.pallas_call(gather_body, out_shape=[jax.ShapeDtypeStruct((4, 2, 4, row...  101 us
    dot_general x16, matrix products, dot(): return lax.dot_general(a, b, (dims, ((), ())), preferred_element_type=F32)  92.9 us
    pallas_call x1, Pallas kernels, return_rows(): pl.pallas_call(return_body, out_shape=[jax.ShapeDtypeStruct((4, half, wid...  53.8 us
    pallas_call x1, Pallas kernels, middle_back(): pl.pallas_call(back_body, out_shape=[jax.ShapeDtypeStruct((rows, width),...  40.5 us
    pallas_call x1, Pallas kernels, rows_to_experts(): pl.pallas_call(rows_body, out_shape=[jax.ShapeDtypeStruct(rows.shape, row...  39.2 us
    pallas_call x1, Pallas kernels, middle_and_unit(): pl.pallas_call(middle_body, out_shape=[jax.ShapeDtypeStruct((rows, width)...  39.2 us
    pallas_call x1, Pallas kernels, experts(): pl.pallas_call(experts_body, grid=(chunks,), in_specs=[pl.BlockSpec((coun...  24.7 us
  transfers between devices with their start and end apart: 8, of which 2 were waited for; matrix products, arithmetic and copies ran while one was open for 16% of the time, Pallas kernels for 47%

profile of v6, /device:TPU:1, one launch (start us, length us, event | category | flops | bytes accessed | tf_op | source)
XLA Modules:
  0.0 647.4 jit_solution(1844133603855130504)
XLA Ops:
  7.2 1.4 copy.160
  9.6 1.3 copy.145
  13.4 1.8 reshape.414.ups_ref
  17.0 101.5 %gather_weights.1 = (bf16[4,2,4,64,2176]{4,3,2,1,0:T(8,128)(2,1)}, bf16[2,4,64,2816]{3,2,1,0:T(8,128)(2,1)}, bf16[2,4,64,1408]{3,2,1,0:T(8,128)(2,1)}, bf16[2,512,128]{2,1,0:T(8,128)(2,1)}) custom-call(bf16[2,64,2176]{2,1,0:T(8,128)(2,1)} %pad_maximum_fusion.x_ref, bf16[4,64,2816]{2,1,0:T(8,128)(2,1)} %reshape.414.ups_ref, bf16[4,64,1408]{2,1,0:T(8,128)(2,1)} %bitcast.147, ...), custom_call_target="tpu_custom_call" | custom-call | tf_op jit(solution)/shard_map/gather_weights/pallas_call | solution.py:191
  119.1 1.1 slice.77
  123.0 1.9 fusion.37
  126.0 6.3 convolution_convert_fusion.3
  132.3 5.2 all-to-all-start
  138.0 3.2 fusion.4
  141.4 9.4 %fusion.10.k_ref.v_ref.q0.q1.q2 = f32[1024,1408]{1,0:T(8,128)S(1)} fusion(bf16[2048,2176]{1,0:T(8,128)(2,1)} %bitcast.152, bf16[1024,2048]{1,0:T(8,128)(2,1)S(1)} %copy-done.21, f32[2048]{0:T(1024)S(1)} %bitcast.170, f32[1024]{0:T(1024)S(1)} %add_rsqrt_fusion), kind=kOutput, calls=%fused_computation.18 | convolution fusion | flops 5913968640 | bytes 15740928 | tf_op jit(solution)/shard_map/dot_general | solution.py:931
  150.9 2.4 copy-done.19
  155.8 1.1 copy-done.12
  156.8 15.7 %attention_forward.1 = (bf16[1024,256]{1,0:T(8,128)(2,1)S(1)}, bf16[1024,256]{1,0:T(8,128)(2,1)S(1)}, bf16[1024,768]{1,0:T(8,128)(2,1)S(1)}, bf16[1024,768]{1,0:...) custom-call(f32[1024,1408]{1,0:T(8,128)} %copy-done.19, f32[1024,1408]{1,0:T(8,128)} %copy-done.19, ...), custom_call_target="tpu_custom_call" | custom-call | tf_op jit(solution)/shard_map/attention_forward/pallas_call | solution.py:1186
  172.6 6.2 convolution_convert_fusion.4
  178.8 39.2 %middle_and_unit.1 = (f32[128,2048]{1,0:T(8,128)S(1)}, bf16[4,128,2048]{2,1,0:T(8,128)(2,1)S(1)}) custom-call(bf16[2,2,2,128,2048]{4,3,2,1,0:T(8,128)(2,1)S(1)} %bitcast.119, bf16[128,2048]{1,0:T(8,128)(2,1)S(1)} %copy-done.1, f32[1,2048]{1,0:T(1,128)S(1)} %get-tuple-element.151.gain_ref), custom_call_target="tpu_custom_call" | custom-call | tf_op jit(solution)/shard_map/middle_and_unit/pallas_call | solution.py:467
  218.1 1.3 copy-done.2
  219.4 1.9 fusion.35
  221.6 6.7 %convolution_convert_fusion = bf16[1280,2176]{1,0:T(8,128)(2,1)} fusion(pred[1280,512]{1,0:T(32,128)(4,1)S(1)} %copy-done.27, bf16[512,8]{1,0:T(8,128)(2,1)S(1)} %copy.182, bf16[512,2048]{1,0:T(8,128)(2,1)} %bitcast.117), kind=kOutput, calls=%fused_computation | convolution fusion | flops 2861596672 | bytes 8331264 | tf_op jit(solution)/shard_map/dot_general | solution.py:931
  228.3 39.2 %rows_to_experts.1 = (bf16[4,320,2176]{2,1,0:T(8,128)(2,1)S(1)}, f32[1280,1408]{1,0:T(8,128)}) custom-call(bf16[4,320,2176]{2,1,0:T(8,128)(2,1)} %bitcast.122, bf16[1280,2048]{1,0:T(8,128)(2,1)} %bitcast.24.grad_ref, bf16[2048,1408]{1,0:T(8,128)(2,1)} %all-gather.9.cloned.1.call-done.down_ref), custom_call_target="tpu_custom_call" | custom-call | tf_op jit(solution)/shard_map/rows_to_experts/pallas_call | solution.py:621
  267.6 2.5 copy-done
  270.3 1.1 broadcast_in_dim.87.gate_ref
  271.3 22.9 %all-gather.11.cloned.1.call-done.gate_up_ref.linear_up_ref.up_ref = bf16[2048,2816]{1,0:T(8,128)(2,1)} async-done(((bf16[512,2816]{1,0:T(8,128)(2,1)}), bf16[2048,2816]{1,0:T(8,128)(2,1)}) %all-gather.11.cloned.1.call-update) | async-done | bytes 11534352 | tf_op jit(solution)/shard_map/all_gather | solution.py:1365
  294.3 24.7 %experts.1 = (bf16[1280,1408]{1,0:T(8,128)(2,1)}, bf16[1280,1408]{1,0:T(8,128)(2,1)}, bf16[1280,1408]{1,0:T(8,128)(2,1)}, bf16[1280,1408]{1,0:T(8,128)(2,1)}, f32[1280,128]{1,0:T(8,128)}) custom-call(bf16[1280,2176]{1,0:T(8,128)(2,1)} %bitcast.114, f32[1280,1408]{1,0:T(8,128)} %get-tuple-element.57.raw_ref, ...), custom_call_target="tpu_custom_call" | custom-call | tf_op jit(solution)/shard_map/experts/pallas_call | solution.py:964
  319.0 13.0 %convolution_convert_fusion.2 = bf16[2048,1408]{1,0:T(8,128)(2,1)} fusion(bf16[1280,2048]{1,0:T(8,128)(2,1)} %bitcast.24.grad_ref, bf16[1280,1408]{1,0:T(8,128)(2,1)} %get-tuple-element.62), kind=kOutput, calls=%fused_computation.10 | convolution fusion | flops 7384858624 | bytes 14614528 | tf_op jit(solution)/shard_map/dot_general | solution.py:931
  332.4 53.8 %return_rows.1 = (bf16[4,160,2048]{2,1,0:T(8,128)(2,1)}, f32[4,160,128]{2,1,0:T(8,128)}, bf16[2048,2816]{1,0:T(8,128)(2,1)}) custom-call(bf16[1280,1408]{1,0:T(8,128)(2,1)} %get-tuple-element.59.dgate_pre_ref, bf16[1280,1408]{1,0:T(8,128)(2,1)} %get-tuple-element.60.dlinear_ref, ...), custom_call_target="tpu_custom_call" | custom-call | tf_op jit(solution)/shard_map/return_rows/pallas_call | solution.py:1093
  388.3 1.5 iota_compare_fusion.2
  390.8 2.1 fusion.33
  392.9 1.9 fusion.13
  394.8 40.5 %middle_back.1 = (f32[128,2048]{1,0:T(8,128)S(1)}, f32[1,2048]{1,0:T(1,128)S(1)}, bf16[2,2,2,128,2048]{4,3,2,1,0:T(8,128)(2,1)}, bf16[4,320,2048]{2,1,0:T(8,128)(2,1)}) custom-call(bf16[4,128,2048]{2,1,0:T(8,128)(2,1)S(1)} %bitcast.120, f32[128,2048]{1,0:T(8,128)S(1)} %copy-done.11, bf16[128,2048]{1,0:T(8,128)(2,1)S(1)} %copy-done.13, ...), custom_call_target="tpu_custom_call" | custom-call | tf_op jit(solution)/shard_map/middle_back/pallas_call | solution.py:538
  436.3 5.2 all-to-all-start.1
  441.6 8.7 %fusion.19.h0.h1.h2 = f32[1024,768]{1,0:T(8,128)} fusion(bf16[1024,2048]{1,0:T(8,128)(2,1)} %bitcast.175, bf16[2048,2176]{1,0:T(8,128)(2,1)} %bitcast.156), kind=kOutput, calls=%fused_computation.31 | convolution fusion | flops 3221225472 | bytes 10485760 | tf_op jit(solution)/shard_map/dot_general | solution.py:931
  450.3 13.6 %attention_back.1 = (bf16[1024,1280]{1,0:T(8,128)(2,1)}, f32[1024,128]{1,0:T(8,128)S(1)}) custom-call(bf16[1024,256]{1,0:T(8,128)(2,1)S(1)} %copy-done.16, bf16[1024,256]{1,0:T(8,128)(2,1)S(1)} %copy-done.18, bf16[1024,768]{1,0:T(8,128)(2,1)S(1)} %get-tuple-element.51.q0.q1.q2, bf16[1024,768]{1,0:T(8,128)(2,1)S(1)} %get-tuple-element.51.q0.q1.q2, ...), custom_call_target="tpu_custom_call" | custom-call | tf_op jit(solution)/shard_map/attention_back/pallas_call | solution.py:1262
  464.5 12.6 %fusion.58 = (bf16[1024,2048]{1,0:T(8,128)(2,1)}, bf16[2048]{0:T(1024)(128)(2,1)S(1)}) fusion(f32[1024]{0:T(1024)S(1)} %add_rsqrt_fusion, bf16[1024,2048]{1,0:T(8,128)(2,1)} %all-gather.5.cloned.1.call-done, bf16[2048,2176]{1,0:T(8,128)(2,1)} %bitcast.157, bf16[1024,3]{1,0:T(8,128)(2,1)S(1)} %copy.166, bf16[1024,1280]{1,0:T(8,128)(2,1)} %get-tuple-element.70), kind=kOutput, calls=%fused_computation.124 | convolution fusion | flops 5924714496 | bytes 16791552 | tf_op jit(solution)/shard_map/dot_general | solution.py:931
  477.5 1.2 convolution_convert_fusion.7
  479.9 7.6 %convolution_convert_fusion.5 = bf16[2048,768]{1,0:T(8,128)(2,1)} fusion(bf16[1024,2048]{1,0:T(8,128)(2,1)} %bitcast.176, bf16[1024,768]{1,0:T(8,128)(2,1)S(1)} %copy-done.44), kind=kOutput, calls=%fused_computation.26 | convolution fusion | flops 3222798336 | bytes 8912896 | tf_op jit(solution)/shard_map/dot_general | solution.py:931
  487.6 7.8 %convolution_convert_fusion.1 = bf16[2048,1280]{1,0:T(8,128)(2,1)} fusion(bf16[1024,1280]{1,0:T(8,128)(2,1)S(1)} %copy-done.43, bf16[1024,2048]{1,0:T(8,128)(2,1)S(1)} %copy-done.23, f32[2048]{0:T(1024)S(1)} %bitcast.172, f32[1024]{0:T(1024)S(1)} %add_rsqrt_fusion), kind=kOutput, calls=%fused_computation.9 | convolution fusion | flops 5379719168 | bytes 12070912 | tf_op jit(solution)/shard_map/dot_general | solution.py:931
  495.4 6.3 all-to-all-done.1
  501.7 6.9 %bitcast_convert_fusion = bf16[512,2048]{1,0:T(8,128)(2,1)} fusion(bf16[4,320,2048]{2,1,0:T(8,128)(2,1)} %all-to-all-done.1, f32[4,320]{1,0:T(4,128)S(1)} %multiply_reduce_fusion, s32[4,512]{1,0:T(4,128)S(1)} %fusion.32), kind=kOutput, calls=%fused_computation.22 | convolution fusion | flops 2693922816 | bytes 7353344 | tf_op jit(solution)/shard_map/dot_general | solution.py:931
  508.7 110.8 %finish.1 = (f32[2,64,2176]{2,1,0:T(8,128)}, bf16[4,64,2816]{2,1,0:T(8,128)(2,1)}, bf16[4,64,1408]{2,1,0:T(8,128)(2,1)}, bf16[128,2048]{1,0:T(8,128)(2,1)}, f32[128,2048]{1,0:T(8,128)}, /*index=5*/f32[64,128]{1,0:T(8,128)}) custom-call(bf16[4,2,4,64,1280]{4,3,2,1,0:T(8,128)(2,1)} %bitcast.123, bf16[4,2,4,64,128]{4,3,2,1,0:T(8,128)(2,1)} %bitcast.136, ...), custom_call_target="tpu_custom_call" | custom-call | tf_op jit(solution)/shard_map/finish/pallas_call | solution.py:866
  619.5 1.2 fusion.59
  622.5 1.5 slice_reduce_fusion
  624.1 1.5 copy.171
  625.7 1.3 copy.177
  627.0 4.3 reshape.449
  631.9 1.1 reshape.443
  633.5 1.1 reshape.445
  634.6 1.3 copy.169
  636.9 1.2 convert_bitcast_fusion
  (205 shorter events, 26.1 us)
Async XLA Ops:
  7.2 4.9 copy-start.32
  7.2 5.4 copy-start.33
  7.2 118.8 %all-gather.7.cloned.1.call-start = ((), (), s32[]{:S(2)}) async-start(), calls=%async_computation.5 | async-start | bytes 2621440 | tf_op jit(solution)/shard_map/all_gather | solution.py:1356
  8.7 4.4 copy-start.34
  8.7 4.6 copy-start.38
  8.7 4.6 copy-start.39
  8.7 4.6 copy-start.40
  8.7 4.6 copy-start.41
  8.7 4.7 copy-start.24
  9.6 128.4 %all-gather.5.cloned.1.call-start = ((), (), s32[]{:S(2)}) async-start(), calls=%async_computation.4 | async-start | bytes 4718592 | tf_op jit(solution)/shard_map/all_gather | solution.py:1355
  10.9 4.3 copy-start.37
  11.0 4.3 copy-start.36
  12.1 216.3 %all-gather.9.cloned.1.call-start = ((), (), s32[]{:S(2)}) async-start(), calls=%async_computation.6 | async-start | bytes 7208960 | tf_op jit(solution)/shard_map/all_gather | solution.py:1368
  118.5 2.1 copy-start.31
  118.5 3.7 copy-start.35
  118.5 175.7 %all-gather.11.cloned.1.call-start = ((), (), s32[]{:S(2)}) async-start(), calls=%async_computation.7 | async-start | bytes 14417920 | tf_op jit(solution)/shard_map/all_gather | solution.py:1365
  123.0 9.3 %copy-start.26 = (pred[1280,512]{1,0:T(32,128)(4,1)}, pred[1280,512]{1,0:T(32,128)(4,1)S(1)}, u32[]{:S(2)}) copy-start(pred[1280,512]{1,0:T(32,128)(4,1)S(1)} %bitcast_compare_fusion) | copy-start | bytes 1966084
  125.3 29.4 %copy-start.4 = (f32[1024,128]{1,0:T(8,128)}, f32[1024,128]{1,0:T(8,128)S(1)}, u32[]{:S(2)}) copy-start(f32[1024,128]{1,0:T(8,128)S(1)} %get-tuple-element.159.cos_ref) | copy-start | bytes 1572868
  125.3 29.4 %copy-start.6 = (f32[1024,128]{1,0:T(8,128)}, f32[1024,128]{1,0:T(8,128)S(1)}, u32[]{:S(2)}) copy-start(f32[1024,128]{1,0:T(8,128)S(1)} %get-tuple-element.160.sin_ref) | copy-start | bytes 1572868
  132.3 96.0 %all-to-all-start = ((bf16[4,320,2048]{2,1,0:T(8,128)(2,1)}), bf16[4,320,2048]{2,1,0:T(8,128)(2,1)}, u32[]{:S(2)}, u32[]{:S(2)}) async-start(bf16[4,320,2048]{2,1,0:T(8,128)(2,1)} %bitcast.124), calls=%async_computation | async-start | bytes 10485760 | tf_op jit(solution)/shard_map/all_to_all | solution.py:1381
  137.4 371.3 %reduce-scatter.5.cloned.1.call-start = ((), (), s32[]{:S(2)}) async-start(), calls=%async_computation.9 | async-start | bytes 7208960 | tf_op jit(solution)/shard_map/reduce_scatter | solution.py:1423
  138.0 3.5 copy-start.21
  150.9 2.4 copy-start.19
  172.5 6.2 copy-start.15
  172.5 6.2 copy-start.17
  172.5 6.3 copy-start.1
  178.8 42.8 %copy-start.27 = (pred[1280,512]{1,0:T(32,128)(4,1)S(1)}, pred[1280,512]{1,0:T(32,128)(4,1)}, u32[]{:S(2)}) copy-start(pred[1280,512]{1,0:T(32,128)(4,1)} %copy-done.26) | copy-start | bytes 1966084
  218.0 3.2 copy-start.10
  267.5 2.5 copy-start
  332.0 176.7 %reduce-scatter.3.cloned.1.call-start = ((), (), s32[]{:S(2)}) async-start(), calls=%async_computation.8 | async-start | bytes 14417920 | tf_op jit(solution)/shard_map/reduce_scatter | solution.py:1427
  386.2 4.0 copy-start.30
  390.4 2.5 copy-start.28
  390.4 2.5 copy-start.42
  392.9 1.9 copy-start.11
  392.9 1.9 copy-start.13
  436.3 65.5 %all-to-all-start.1 = ((bf16[4,320,2048]{2,1,0:T(8,128)(2,1)}), bf16[4,320,2048]{2,1,0:T(8,128)(2,1)}, u32[]{:S(2)}, u32[]{:S(2)}) async-start(bf16[4,320,2048]{2,1,0:T(8,128)(2,1)} %get-tuple-element.75), calls=%async_computation.3 | async-start | bytes 10485760 | tf_op jit(solution)/shard_map/all_to_all | solution.py:1438
  441.5 8.7 %copy-start.5 = (f32[1024,128]{1,0:T(8,128)S(1)}, f32[1024,128]{1,0:T(8,128)}, u32[]{:S(2)}) copy-start(f32[1024,128]{1,0:T(8,128)} %copy-done.4) | copy-start | bytes 1572868
  441.5 8.7 %copy-start.7 = (f32[1024,128]{1,0:T(8,128)S(1)}, f32[1024,128]{1,0:T(8,128)}, u32[]{:S(2)}) copy-start(f32[1024,128]{1,0:T(8,128)} %copy-done.6) | copy-start | bytes 1572868
  441.5 8.7 %copy-start.9 = (f32[1024,3]{1,0:T(8,128)S(1)}, f32[1024,3]{1,0:T(8,128)}, u32[]{:S(2)}) copy-start(f32[1024,3]{1,0:T(8,128)} %copy.157.gate_ref) | copy-start | bytes 36868
  441.6 8.7 %copy-start.16 = (bf16[1024,256]{1,0:T(8,128)(2,1)S(1)}, bf16[1024,256]{1,0:T(8,128)(2,1)}, u32[]{:S(2)}) copy-start(bf16[1024,256]{1,0:T(8,128)(2,1)} %copy-done.15) | copy-start | bytes 1572868
  441.6 8.7 %copy-start.18 = (bf16[1024,256]{1,0:T(8,128)(2,1)S(1)}, bf16[1024,256]{1,0:T(8,128)(2,1)}, u32[]{:S(2)}) copy-start(bf16[1024,256]{1,0:T(8,128)(2,1)} %copy-done.17) | copy-start | bytes 1572868
  464.4 12.6 %copy-start.3 = (bf16[4,128,2048]{2,1,0:T(8,128)(2,1)S(1)}, bf16[4,128,2048]{2,1,0:T(8,128)(2,1)}, u32[]{:S(2)}) copy-start(bf16[4,128,2048]{2,1,0:T(8,128)(2,1)} %copy-done.2) | copy-start | bytes 6291460
  464.5 13.0 %copy-start.22 = (bf16[1024,2048]{1,0:T(8,128)(2,1)S(1)}, bf16[1024,2048]{1,0:T(8,128)(2,1)}, u32[]{:S(2)}) copy-start(bf16[1024,2048]{1,0:T(8,128)(2,1)} %all-gather.5.cloned.1.call-done) | copy-start | bytes 12582916
  477.5 2.5 copy-start.44
  479.9 7.6 %copy-start.23 = (bf16[1024,2048]{1,0:T(8,128)(2,1)S(1)}, bf16[1024,2048]{1,0:T(8,128)(2,1)}, u32[]{:S(2)}) copy-start(bf16[1024,2048]{1,0:T(8,128)(2,1)} %all-gather.5.cloned.1.call-done) | copy-start | bytes 12582916
  479.9 7.6 %copy-start.43 = (bf16[1024,1280]{1,0:T(8,128)(2,1)S(1)}, bf16[1024,1280]{1,0:T(8,128)(2,1)}, u32[]{:S(2)}) copy-start(bf16[1024,1280]{1,0:T(8,128)(2,1)} %get-tuple-element.70) | copy-start | bytes 7864324
  631.4 5.6 copy-start.25
  633.2 6.5 %copy-start.29 = (f32[64,128]{1,0:T(8,128)S(1)}, f32[64,128]{1,0:T(8,128)}, u32[]{:S(2)}) copy-start(f32[64,128]{1,0:T(8,128)} %get-tuple-element.80) | copy-start | bytes 98308
  (5 other events, 5.4 us)
Sparse Core Ops, SparseCore 0:
  9.7 41.7 all-gather.6
  53.7 60.6 all-gather.4
  118.7 63.7 all-gather.8
  184.0 110.2 all-gather.10
  332.1 60.8 reduce-scatter.4
  395.4 105.8 reduce-scatter.2

commit v7 on v6

--- a/solution.py
+++ b/solution.py
@@ -76,10 +76,8 @@
     loc, xs, xr, s1, r1m, r1p, f1s, f1r, s2, r2m, r2p, f2s, f2r, es, er, ex, ey, ms, mr,
 ):
     y, xl, z = lax.axis_index("y"), lax.axis_index("xl"), lax.axis_index("z")
-    rows, cols = x_ref.shape[1:]
-    half = rows // 2
-    split = cols // (3 * LANES) * LANES
-    columns = (pl.ds(0, split), pl.ds(split, cols - split))
+    half = x_ref.shape[1] // 2
+    quarter = half // 2
     greet(
         neighbour("xl", 1),
         *(neighbour("y", step) for step in (1, 2, 3)),
@@ -94,7 +92,7 @@
 
     def slot(h, first, second, j, start, count):
         yy, zz = (second, first) if h == 0 else (first, second)
-        return out_ref.at[zz, j, yy, pl.ds(start, count), columns[h]]
+        return out_ref.at[zz, j, yy, pl.ds(start, count)]
 
     own = pltpu.make_async_copy(x_ref.at[xl], out_ref.at[z, xl, y], loc.at[0])
     own.start()
@@ -117,65 +115,66 @@
             )
     for h in (0, 1):
         first, second = place[rings[h][0]], place[rings[h][1]]
-        src = x_ref.at[xl, :, columns[h]]
-        dst = slot(h, first, second, xl, 0, rows)
-        send(x_ref.at[other, :, columns[h]], dst, xs.at[h], xr.at[h], neighbour("xl", 1))
+        src = x_ref.at[xl, pl.ds(h * half, half)]
+        dst = slot(h, first, second, xl, h * half, half)
+        send(x_ref.at[other, pl.ds(h * half, half)], dst, xs.at[h], xr.at[h], neighbour("xl", 1))
         send(src, dst, s1.at[h, 0, 0], r1m.at[h, 0], neighbour(rings[h][0], 1))
         send(src, dst, s1.at[h, 0, 1], r1p.at[h, 0], neighbour(rings[h][0], -1))
     own.wait()
 
     def send_second(h, k, first):
-        block = slot(h, first, place[rings[h][1]], both, 0, rows)
-        send(block, block, s2.at[h, k, 0], r2m.at[h, k], neighbour(rings[h][1], 1))
-        send(block, block, s2.at[h, k, 1], r2p.at[h, k], neighbour(rings[h][1], -1))
+        block = slot(h, first, place[rings[h][1]], both, h * half, half)
+        send(block, block, s2.at[k, 0], r2m.at[k], neighbour(rings[h][1], 1))
+        send(block, block, s2.at[k, 1], r2p.at[k], neighbour(rings[h][1], -1))
 
     for h in (0, 1):
         first, second = place[rings[h][0]], place[rings[h][1]]
-        block = slot(h, first, second, other, 0, rows)
+        block = slot(h, first, second, other, h * half, half)
         arrived(block, xr.at[h])
         send(block, block, s1.at[h, 1, 0], r1m.at[h, 1], neighbour(rings[h][0], 1))
         send(block, block, s1.at[h, 1, 1], r1p.at[h, 1], neighbour(rings[h][0], -1))
-        send_second(h, 0, first)
+        if h == 1:
+            send_second(h, 0, first)
     for j, jx in ((0, xl), (1, other)):
         for h in (0, 1):
             first, second = place[rings[h][0]], place[rings[h][1]]
-            arrived(slot(h, mod4(first - 1), second, jx, 0, rows), r1m.at[h, j])
-            block = slot(h, mod4(first - 1), second, jx, 0, half)
+            arrived(slot(h, mod4(first - 1), second, jx, h * half, half), r1m.at[h, j])
+            block = slot(h, mod4(first - 1), second, jx, h * half, quarter)
             send(block, block, f1s.at[h, j, 0], f1r.at[h, j, 0], neighbour(rings[h][0], 1))
-            arrived(slot(h, mod4(first + 1), second, jx, 0, rows), r1p.at[h, j])
-            block = slot(h, mod4(first + 1), second, jx, half, half)
+            arrived(slot(h, mod4(first + 1), second, jx, h * half, half), r1p.at[h, j])
+            block = slot(h, mod4(first + 1), second, jx, h * half + quarter, quarter)
             send(block, block, f1s.at[h, j, 1], f1r.at[h, j, 1], neighbour(rings[h][0], -1))
     for k, step in ((1, -1), (2, 1)):
-        for h in (0, 1):
-            send_second(h, k, mod4(place[rings[h][0]] + step))
-    for h in (0, 1):
-        first, second = place[rings[h][0]], place[rings[h][1]]
-        for j, jx in ((0, xl), (1, other)):
-            for p in (0, 1):
-                block = slot(h, mod4(first + 2), second, jx, p * half, half)
-                arrived(block, f1r.at[h, j, p])
-        send_second(h, 3, mod4(first + 2))
+        send_second(1, k, mod4(place[rings[1][0]] + step))
     for n, (shards, expert) in enumerate(experts):
         for step in (1, 3, 2):
             landed = expert.at[xl, mod4(y - step)]
             arrived(landed, er.at[n, step - 1])
             send(landed, landed, ex.at[n, step], ey.at[n, step], neighbour("xl", 1))
+    for h in (0, 1):
+        first, second = place[rings[h][0]], place[rings[h][1]]
+        for j, jx in ((0, xl), (1, other)):
+            for p in (0, 1):
+                block = slot(h, mod4(first + 2), second, jx, h * half + p * quarter, quarter)
+                arrived(block, f1r.at[h, j, p])
+        if h == 1:
+            send_second(h, 3, mod4(first + 2))
     steps = ((0, 0), (1, -1), (2, 1), (3, 2))
+    h = 1
+    second = place[rings[h][1]]
     for k, step in steps:
-        for h in (0, 1):
-            first, second = mod4(place[rings[h][0]] + step), place[rings[h][1]]
-            arrived(slot(h, first, mod4(second - 1), both, 0, rows), r2m.at[h, k])
-            block = slot(h, first, mod4(second - 1), both, 0, half)
-            send(block, block, f2s.at[h, k, 0], f2r.at[h, k, 0], neighbour(rings[h][1], 1))
-            arrived(slot(h, first, mod4(second + 1), both, 0, rows), r2p.at[h, k])
-            block = slot(h, first, mod4(second + 1), both, half, half)
-            send(block, block, f2s.at[h, k, 1], f2r.at[h, k, 1], neighbour(rings[h][1], -1))
+        first = mod4(place[rings[h][0]] + step)
+        arrived(slot(h, first, mod4(second - 1), both, half, half), r2m.at[k])
+        block = slot(h, first, mod4(second - 1), both, half, quarter)
+        send(block, block, f2s.at[k, 0], f2r.at[k, 0], neighbour(rings[h][1], 1))
+        arrived(slot(h, first, mod4(second + 1), both, half, half), r2p.at[k])
+        block = slot(h, first, mod4(second + 1), both, half + quarter, quarter)
+        send(block, block, f2s.at[k, 1], f2r.at[k, 1], neighbour(rings[h][1], -1))
     for k, step in steps:
-        for h in (0, 1):
-            first, second = mod4(place[rings[h][0]] + step), place[rings[h][1]]
-            for p in (0, 1):
-                block = slot(h, first, mod4(second + 2), both, p * half, half)
-                arrived(block, f2r.at[h, k, p])
+        first = mod4(place[rings[h][0]] + step)
+        for p in (0, 1):
+            block = slot(h, first, mod4(second + 2), both, half + p * quarter, quarter)
+            arrived(block, f2r.at[k, p])
     for n, (shards, expert) in enumerate(experts):
         for step in (0, 1, 3, 2):
             arrived(expert.at[other, mod4(y - step)], ey.at[n, step])
@@ -183,6 +182,55 @@
     arrived(marks_out.at[other], mr)
     own_marks.wait()
     sends.finish()
+
+
+def gather_rest_body(start_ref, out_ref, s2, r2m, r2p, f2s, f2r):
+    y, z = lax.axis_index("y"), lax.axis_index("z")
+    half = out_ref.shape[3] // 2
+    quarter = half // 2
+    ahead, behind = neighbour("y", 1), neighbour("y", -1)
+    greet(ahead, behind)
+    sends = Sends()
+    both = pl.ds(0, 2)
+
+    def slot(ref, zz, yy, start, count):
+        return ref.at[zz, both, yy, pl.ds(start, count)]
+
+    steps = ((0, 0), (1, -1), (2, 1), (3, 2))
+    for k, step in steps:
+        zz = mod4(z + step)
+        src, dst = slot(start_ref, zz, y, 0, half), slot(out_ref, zz, y, 0, half)
+        sends(src, dst, s2.at[k, 0], r2m.at[k], ahead)
+        sends(src, dst, s2.at[k, 1], r2p.at[k], behind)
+    for k, step in steps:
+        zz = mod4(z + step)
+        arrived(slot(out_ref, zz, mod4(y - 1), 0, half), r2m.at[k])
+        block = slot(out_ref, zz, mod4(y - 1), 0, quarter)
+        sends(block, block, f2s.at[k, 0], f2r.at[k, 0], ahead)
+        arrived(slot(out_ref, zz, mod4(y + 1), 0, half), r2p.at[k])
+        block = slot(out_ref, zz, mod4(y + 1), quarter, quarter)
+        sends(block, block, f2s.at[k, 1], f2r.at[k, 1], behind)
+    for k, step in steps:
+        for p in (0, 1):
+            arrived(slot(out_ref, mod4(z + step), mod4(y + 2), p * quarter, quarter), f2r.at[k, p])
+    sends.finish()
+
+
+def gather_rest(whole, rows):
+    dma = pltpu.SemaphoreType.DMA
+    cols = whole.shape[1]
+    anywhere = pl.BlockSpec(memory_space=pl.ANY)
+    out = pl.pallas_call(
+        gather_rest_body,
+        out_shape=jax.ShapeDtypeStruct((4, 2, 4, rows, cols), whole.dtype),
+        in_specs=[anywhere],
+        out_specs=anywhere,
+        scratch_shapes=[dma((4, 2)), dma((4,)), dma((4,)), dma((4, 2)), dma((4, 2))],
+        input_output_aliases={0: 0},
+        compiler_params=pltpu.CompilerParams(collective_id=6, has_side_effects=True),
+        name="gather_rest",
+    )(whole.reshape(4, 2, 4, rows, cols))
+    return out.reshape(whole.shape)
 
 
 def gather_dp(shard, ups, downs, marks):
@@ -207,11 +255,11 @@
             dma((2, 2)),
             dma((2, 2, 2)),
             dma((2, 2, 2)),
-            dma((2, 4, 2)),
-            dma((2, 4)),
-            dma((2, 4)),
-            dma((2, 4, 2)),
-            dma((2, 4, 2)),
+            dma((4, 2)),
+            dma((4,)),
+            dma((4,)),
+            dma((4, 2)),
+            dma((4, 2)),
             dma((2, 3)),
             dma((2, 3)),
             dma((2, 4)),
@@ -652,7 +700,7 @@
     out_ref, up_out, down_out, output_ref, dinput_ref, small_out,
     g_ref, loc, t_buf, r_buf, tb_buf, rb_buf, c_buf,
     t_s, t_r, r_s, r_r, tb_s, tb_r, rb_s, rb_r, c_s, c_r,
-    up_own, down_own, up_buf, down_buf, up_sum, down_sum, ex, ey, es, er,
+    up_own, up_buf, up_sum, ex, ey, es, er,
     small_own, small_buf, small_s, small_r, *scratch,
 ):
     xl, xh, core = lax.axis_index("xl"), lax.axis_index("xh"), lax.axis_index("core")
@@ -669,8 +717,8 @@
         parts.append(pltpu.make_async_copy(ref, g_ref.at[..., pl.ds(column, cols)], loc.at[n]))
         parts[-1].start()
         column += cols
-    for n, (ref, own) in enumerate(((ups_ref, up_own), (downs_ref, down_own))):
-        parts.append(pltpu.make_async_copy(ref.at[xl], own, loc.at[3 + n]))
+    for n, (src, dst) in enumerate(((ups_ref.at[xl], up_own), (downs_ref.at[my_y], down_out.at[my_y]))):
+        parts.append(pltpu.make_async_copy(src, dst, loc.at[3 + n]))
         parts[-1].start()
     peers = ({"xh": xh, "core": 1 - core}, {"xh": 1 - xh, "core": core}, {"xh": 1 - xh, "core": 1 - core})
     greet(
@@ -683,16 +731,14 @@
     both = slice(0, 2)
     ring_stages = ring_reduce_stages(part_ref, *scratch[7:15], sends)
     feed_stages = reduce_stages(CHUNKS, [feed_ref], *scratch[:7], sends)
-    experts = ((ups_ref, up_own, up_buf, up_sum, up_out), (downs_ref, down_own, down_buf, down_sum, down_out))
-    for n, (grads, _, buf, _, _) in enumerate(experts):
-        for step in (2, 1, 3, 0):
-            sends(
-                grads.at[1 - xl, mod4(my_y + step)],
-                buf.at[step],
-                ex.at[n, step],
-                ey.at[n, step],
-                neighbour("xl", 1),
-            )
+    for step in (2, 1, 3, 0):
+        sends(
+            ups_ref.at[1 - xl, mod4(my_y + step)],
+            up_buf.at[step],
+            ex.at[step],
+            ey.at[step],
+            neighbour("xl", 1),
+        )
     next(ring_stages)
     next(feed_stages)
     for part in parts[:3]:
@@ -751,24 +797,31 @@
                     neighbour(rings[h][1], way),
                 )
     total = next(ring_stages)
+    for step in (2, 1, 3):
+        sends(
+            downs_ref.at[mod4(my_y + step)],
+            down_out.at[my_y],
+            es.at[1, step - 1],
+            er.at[1, step - 1],
+            neighbour("y", step),
+        )
     for part in parts[3:]:
         part.wait()
-    for n, (_, own, buf, summed, result) in enumerate(experts):
-        for step in (2, 1, 3, 0):
-            target = mod4(my_y + step)
-            arrived(buf.at[step], ey.at[n, step])
-            value = (own[target].astype(F32) + buf[step].astype(F32)).astype(BF16)
-            if step == 0:
-                result[my_y] = value
-            else:
-                summed[step - 1] = value
-                sends(
-                    summed.at[step - 1],
-                    result.at[my_y],
-                    es.at[n, step - 1],
-                    er.at[n, step - 1],
-                    neighbour("y", step),
-                )
+    for step in (2, 1, 3, 0):
+        target = mod4(my_y + step)
+        arrived(up_buf.at[step], ey.at[step])
+        value = (up_own[target].astype(F32) + up_buf[step].astype(F32)).astype(BF16)
+        if step == 0:
+            up_out[my_y] = value
+        else:
+            up_sum[step - 1] = value
+            sends(
+                up_sum.at[step - 1],
+                up_out.at[my_y],
+                es.at[0, step - 1],
+                er.at[0, step - 1],
+                neighbour("y", step),
+            )
     for k in range(4):
         for h in (0, 1):
             second = place[rings[h][1]]
@@ -845,7 +898,7 @@
     for n in range(CHUNKS):
         rows = slice(n * step, (n + 1) * step)
         output_ref[rows, :] = (middle_ref[rows, :] + feed(0, n)).astype(BF16)
-    for n, (_, _, _, _, result) in enumerate(experts):
+    for n, result in enumerate((up_out, down_out)):
         for step in (1, 3, 2):
             arrived(result.at[mod4(my_y - step)], er.at[n, step - 1])
     for n in range(3):
@@ -894,13 +947,10 @@
             dma((2,)),
             dma((2,)),
             pltpu.VMEM((4, share, up_cols), BF16),
-            pltpu.VMEM((4, share, down_cols), BF16),
             pltpu.VMEM((4, share, up_cols), BF16),
-            pltpu.VMEM((4, share, down_cols), BF16),
             pltpu.VMEM((3, share, up_cols), BF16),
-            pltpu.VMEM((3, share, down_cols), BF16),
-            dma((2, 4)),
-            dma((2, 4)),
+            dma((4,)),
+            dma((4,)),
             dma((2, 3)),
             dma((2, 3)),
             pltpu.VMEM(small, F32),
@@ -917,7 +967,7 @@
     )(
         *(grad.reshape(4, 2, 4, share, grad.shape[1]) for grad in grads),
         ups.reshape(2, 4, share, up_cols),
-        downs.reshape(2, 4, share, down_cols),
+        downs.reshape(4, share, down_cols),
         part.reshape(2, 2, 2, own_rows, width),
         feed.reshape(4, own_rows, width),
         x,
@@ -1361,6 +1411,7 @@
         jnp.swapaxes(down_proj, 1, 2),
         marks,
     )
+    weights, up_parts, down_parts = lax.optimization_barrier((weights, up_parts, down_parts))
     marks = marks[:, :, :3].astype(jnp.int32)
     up_whole = lax.all_gather(
         up_parts.reshape(2 * mlp_count * share, -1), "z", axis=0, tiled=True
@@ -1368,6 +1419,8 @@
     down_whole = lax.all_gather(
         down_parts.reshape(2 * mlp_count * share, -1), "z", axis=0, tiled=True
     )
+
+    weights = gather_rest(weights, share)
 
     tokens = segments.shape[0]
     match = jnp.sum((mlp_routes[:, :, None] == jnp.arange(mlp_count, dtype=jnp.int32)).astype(BF16), 1)
@@ -1425,6 +1478,14 @@
         dgate_pre, dlinear, up_whole, dgate_part.reshape(mlp_count, CAP, LANES), rows_ext
     )
     grad_up_sum = lax.psum_scatter(grad_up_whole, "z", scatter_dimension=0, tiled=True)
+    halves = grad_down_sum.reshape(2, mlp_count * share, hidden_local)
+    xl = lax.axis_index("xl")
+    theirs = lax.ppermute(
+        lax.dynamic_index_in_dim(halves, 1 - xl, 0, keepdims=False), "xl", ((0, 1), (1, 0))
+    )
+    grad_down_sum = (
+        lax.dynamic_index_in_dim(halves, xl, 0, keepdims=False).astype(F32) + theirs.astype(F32)
+    ).astype(BF16)
     pick_half = lax.dynamic_slice_in_dim(pick, lax.axis_index("core") * (CAP // 2), CAP // 2, 1)
     dgate_two = jnp.sum(pick_half.astype(F32) * jnp.sum(dgate_back, -1, keepdims=True), 1).T
     dlogit_mlp = router_back(dgate_two, weights_mlp, onehot_mlp)

time: 656 us -> 657 us (level)
  waiting for transfers between devices: 29.9 us -> 10.3 us
  Pallas kernels: 439 us -> 457 us
    pallas_call x0 -> x1, Pallas kernels: none -> 36 us  [gather_rest(): pl.pallas_call(gather_rest_body, out_shape=jax.ShapeDtypeStruct((4, 2, 4,...]
    all_gather x1, waiting for transfers between devices: 22.9 us -> 0.01 us  [on_device(): lax.all_gather(up_parts.reshape(2 * mlp_count * share, -1), 'z', axis=0,...]
    pallas_call x1, Pallas kernels: 111 us -> 94.4 us  [finish(): pl.pallas_call(finish_body, out_shape=[jax.ShapeDtypeStruct((2, share, co...]
    unnamed x106 -> x108, local copies, waits for them, and re-layouts: 18 us -> 18 us
  transfers between devices with their start and end apart: 8 -> 9, of which waited for: 2 -> 2; matrix products, arithmetic and copies ran while one was open for 16% -> 17% of each run, Pallas kernels for 47% -> 52%
where the time goes in v7:
time: 657 us; the launch traced here: 648 us
  Pallas kernels  457 us (70%)
  matrix products  92.8 us (14%)
  local copies, waits for them, and re-layouts  48.4 us (7%)
  between operations  15.4 us (2%)
  other arithmetic  12.6 us (2%)
  starting transfers between devices  12.1 us (2%)
  waiting for transfers between devices  10.3 us (2%)
    pallas_call x1, Pallas kernels, gather_dp(): pl.pallas_call(gather_body, out_shape=[jax.ShapeDtypeStruct((4, 2, 4, row...  96.1 us
    pallas_call x1, Pallas kernels, finish(): pl.pallas_call(finish_body, out_shape=[jax.ShapeDtypeStruct((2, share, co...  94.4 us
    dot_general x16, matrix products, dot(): return lax.dot_general(a, b, (dims, ((), ())), preferred_element_type=F32)  92.8 us
    pallas_call x1, Pallas kernels, return_rows(): pl.pallas_call(return_body, out_shape=[jax.ShapeDtypeStruct((4, half, wid...  53.4 us
    pallas_call x1, Pallas kernels, middle_and_unit(): pl.pallas_call(middle_body, out_shape=[jax.ShapeDtypeStruct((rows, width)...  44.1 us
    pallas_call x1, Pallas kernels, middle_back(): pl.pallas_call(back_body, out_shape=[jax.ShapeDtypeStruct((rows, width),...  39.5 us
    pallas_call x1, Pallas kernels, rows_to_experts(): pl.pallas_call(rows_body, out_shape=[jax.ShapeDtypeStruct(rows.shape, row...  39.4 us
    pallas_call x1, Pallas kernels, gather_rest(): pl.pallas_call(gather_rest_body, out_shape=jax.ShapeDtypeStruct((4, 2, 4,...  36 us
  transfers between devices with their start and end apart: 9, of which 2 were waited for; matrix products, arithmetic and copies ran while one was open for 17% of the time, Pallas kernels for 52%

profile of v7, /device:TPU:1, one launch (start us, length us, event | category | flops | bytes accessed | tf_op | source)
XLA Modules:
  0.0 648.4 jit_solution(1730347419542460865)
XLA Ops:
  7.2 1.4 copy.161
  9.6 1.3 copy.146
  13.4 1.8 reshape.425.ups_ref
  17.0 96.1 %gather_weights.1 = (bf16[4,2,4,64,2176]{4,3,2,1,0:T(8,128)(2,1)}, bf16[2,4,64,2816]{3,2,1,0:T(8,128)(2,1)}, bf16[2,4,64,1408]{3,2,1,0:T(8,128)(2,1)}, bf16[2,512,128]{2,1,0:T(8,128)(2,1)}) custom-call(bf16[2,64,2176]{2,1,0:T(8,128)(2,1)} %pad_maximum_fusion.x_ref, bf16[4,64,2816]{2,1,0:T(8,128)(2,1)} %reshape.425.ups_ref, bf16[4,64,1408]{2,1,0:T(8,128)(2,1)} %bitcast.164, ...), custom_call_target="tpu_custom_call" | custom-call | tf_op jit(solution)/shard_map/gather_weights/pallas_call | solution.py:239
  113.7 36.0 %gather_rest.1 = bf16[4,2,4,64,2176]{4,3,2,1,0:T(8,128)(2,1)} custom-call(bf16[4,2,4,64,2176]{4,3,2,1,0:T(8,128)(2,1)} %get-tuple-element.50), custom_call_target="tpu_custom_call", output_to_operand_aliasing={{}: (0, {})} | custom-call | tf_op jit(solution)/shard_map/gather_rest/pallas_call | solution.py:223
  149.8 1.1 slice.77
  153.7 1.9 fusion.38
  156.7 6.3 convolution_convert_fusion.3
  163.0 5.0 all-to-all-start
  168.6 3.2 fusion.4
  172.0 9.4 %fusion.10.k_ref.v_ref.q0.q1.q2 = f32[1024,1408]{1,0:T(8,128)S(1)} fusion(bf16[2048,2176]{1,0:T(8,128)(2,1)} %bitcast.131, bf16[1024,2048]{1,0:T(8,128)(2,1)S(1)} %copy-done.21, f32[2048]{0:T(1024)S(1)} %bitcast.180, f32[1024]{0:T(1024)S(1)} %add_rsqrt_fusion), kind=kOutput, calls=%fused_computation.18 | convolution fusion | flops 5913968640 | bytes 15740928 | tf_op jit(solution)/shard_map/dot_general | solution.py:981
  181.4 2.4 copy-done.19
  187.4 15.7 %attention_forward.1 = (bf16[1024,256]{1,0:T(8,128)(2,1)S(1)}, bf16[1024,256]{1,0:T(8,128)(2,1)S(1)}, bf16[1024,768]{1,0:T(8,128)(2,1)S(1)}, bf16[1024,768]{1,0:...) custom-call(f32[1024,1408]{1,0:T(8,128)} %copy-done.19, f32[1024,1408]{1,0:T(8,128)} %copy-done.19, ...), custom_call_target="tpu_custom_call" | custom-call | tf_op jit(solution)/shard_map/attention_forward/pallas_call | solution.py:1236
  203.1 6.2 convolution_convert_fusion.4
  209.3 44.1 %middle_and_unit.1 = (f32[128,2048]{1,0:T(8,128)S(1)}, bf16[4,128,2048]{2,1,0:T(8,128)(2,1)S(1)}) custom-call(bf16[2,2,2,128,2048]{4,3,2,1,0:T(8,128)(2,1)S(1)} %bitcast.127, bf16[128,2048]{1,0:T(8,128)(2,1)S(1)} %copy-done.1, f32[1,2048]{1,0:T(1,128)S(1)} %get-tuple-element.157.gain_ref), custom_call_target="tpu_custom_call" | custom-call | tf_op jit(solution)/shard_map/middle_and_unit/pallas_call | solution.py:515
  253.4 1.3 copy-done.2
  254.7 1.9 fusion.36
  257.0 6.7 %convolution_convert_fusion = bf16[1280,2176]{1,0:T(8,128)(2,1)} fusion(pred[1280,512]{1,0:T(32,128)(4,1)S(1)} %copy-done.28, bf16[512,8]{1,0:T(8,128)(2,1)S(1)} %copy.183, bf16[512,2048]{1,0:T(8,128)(2,1)} %bitcast.125), kind=kOutput, calls=%fused_computation | convolution fusion | flops 2861596672 | bytes 8331264 | tf_op jit(solution)/shard_map/dot_general | solution.py:981
  263.7 39.4 %rows_to_experts.1 = (bf16[4,320,2176]{2,1,0:T(8,128)(2,1)S(1)}, f32[1280,1408]{1,0:T(8,128)}) custom-call(bf16[4,320,2176]{2,1,0:T(8,128)(2,1)} %bitcast.137, bf16[1280,2048]{1,0:T(8,128)(2,1)} %bitcast.26.grad_ref, bf16[2048,1408]{1,0:T(8,128)(2,1)} %all-gather.9.cloned.1.call-done.down_ref), custom_call_target="tpu_custom_call" | custom-call | tf_op jit(solution)/shard_map/rows_to_experts/pallas_call | solution.py:669
  303.1 2.5 copy-done
  305.9 1.1 broadcast_in_dim.87.gate_ref
  307.0 24.7 %experts.1 = (bf16[1280,1408]{1,0:T(8,128)(2,1)}, bf16[1280,1408]{1,0:T(8,128)(2,1)}, bf16[1280,1408]{1,0:T(8,128)(2,1)}, bf16[1280,1408]{1,0:T(8,128)(2,1)}, f32[1280,128]{1,0:T(8,128)}) custom-call(bf16[1280,2176]{1,0:T(8,128)(2,1)} %bitcast.122, f32[1280,1408]{1,0:T(8,128)} %get-tuple-element.63.raw_ref, ...), custom_call_target="tpu_custom_call" | custom-call | tf_op jit(solution)/shard_map/experts/pallas_call | solution.py:1014
  331.7 13.0 %convolution_convert_fusion.2 = bf16[2048,1408]{1,0:T(8,128)(2,1)} fusion(bf16[1280,2048]{1,0:T(8,128)(2,1)} %bitcast.26.grad_ref, bf16[1280,1408]{1,0:T(8,128)(2,1)} %get-tuple-element.68), kind=kOutput, calls=%fused_computation.10 | convolution fusion | flops 7384858624 | bytes 14614528 | tf_op jit(solution)/shard_map/dot_general | solution.py:981
  345.1 53.4 %return_rows.1 = (bf16[4,160,2048]{2,1,0:T(8,128)(2,1)}, f32[4,160,128]{2,1,0:T(8,128)}, bf16[2048,2816]{1,0:T(8,128)(2,1)}) custom-call(bf16[1280,1408]{1,0:T(8,128)(2,1)} %get-tuple-element.65.dgate_pre_ref, bf16[1280,1408]{1,0:T(8,128)(2,1)} %get-tuple-element.66.dlinear_ref, ...), custom_call_target="tpu_custom_call" | custom-call | tf_op jit(solution)/shard_map/return_rows/pallas_call | solution.py:1143
  400.6 1.5 iota_compare_fusion.2
  403.1 2.1 fusion.34
  405.2 1.8 fusion.13
  407.1 39.5 %middle_back.1 = (f32[128,2048]{1,0:T(8,128)S(1)}, f32[1,2048]{1,0:T(1,128)S(1)}, bf16[2,2,2,128,2048]{4,3,2,1,0:T(8,128)(2,1)}, bf16[4,320,2048]{2,1,0:T(8,128)(2,1)}) custom-call(bf16[4,128,2048]{2,1,0:T(8,128)(2,1)S(1)} %bitcast.128, f32[128,2048]{1,0:T(8,128)S(1)} %copy-done.11, bf16[128,2048]{1,0:T(8,128)(2,1)S(1)} %copy-done.13, ...), custom_call_target="tpu_custom_call" | custom-call | tf_op jit(solution)/shard_map/middle_back/pallas_call | solution.py:586
  447.6 5.3 all-to-all-start.1
  453.0 8.6 %fusion.19.h0.h1.h2 = f32[1024,768]{1,0:T(8,128)} fusion(bf16[1024,2048]{1,0:T(8,128)(2,1)} %bitcast.185, bf16[2048,2176]{1,0:T(8,128)(2,1)} %bitcast.135), kind=kOutput, calls=%fused_computation.31 | convolution fusion | flops 3221225472 | bytes 10485760 | tf_op jit(solution)/shard_map/dot_general | solution.py:981
  461.6 13.5 %attention_back.1 = (bf16[1024,1280]{1,0:T(8,128)(2,1)}, f32[1024,128]{1,0:T(8,128)S(1)}) custom-call(bf16[1024,256]{1,0:T(8,128)(2,1)S(1)} %copy-done.16, bf16[1024,256]{1,0:T(8,128)(2,1)S(1)} %copy-done.18, bf16[1024,768]{1,0:T(8,128)(2,1)S(1)} %get-tuple-element.57.q0.q1.q2, bf16[1024,768]{1,0:T(8,128)(2,1)S(1)} %get-tuple-element.57.q0.q1.q2, ...), custom_call_target="tpu_custom_call" | custom-call | tf_op jit(solution)/shard_map/attention_back/pallas_call | solution.py:1312
  475.6 12.6 %fusion.59 = (bf16[1024,2048]{1,0:T(8,128)(2,1)}, bf16[2048]{0:T(1024)(128)(2,1)S(1)}) fusion(f32[1024]{0:T(1024)S(1)} %add_rsqrt_fusion, bf16[1024,2048]{1,0:T(8,128)(2,1)} %all-gather.5.cloned.1.call-done, bf16[2048,2176]{1,0:T(8,128)(2,1)} %bitcast.136, bf16[1024,3]{1,0:T(8,128)(2,1)S(1)} %copy.167, bf16[1024,1280]{1,0:T(8,128)(2,1)} %get-tuple-element.76), kind=kOutput, calls=%fused_computation.127 | convolution fusion | flops 5924714496 | bytes 16791552 | tf_op jit(solution)/shard_map/dot_general | solution.py:981
  488.6 1.2 convolution_convert_fusion.7
  491.1 7.6 %convolution_convert_fusion.5 = bf16[2048,768]{1,0:T(8,128)(2,1)} fusion(bf16[1024,2048]{1,0:T(8,128)(2,1)} %bitcast.186, bf16[1024,768]{1,0:T(8,128)(2,1)S(1)} %copy-done.45), kind=kOutput, calls=%fused_computation.26 | convolution fusion | flops 3222798336 | bytes 8912896 | tf_op jit(solution)/shard_map/dot_general | solution.py:981
  498.7 7.8 %convolution_convert_fusion.1 = bf16[2048,1280]{1,0:T(8,128)(2,1)} fusion(bf16[1024,1280]{1,0:T(8,128)(2,1)S(1)} %copy-done.44, bf16[1024,2048]{1,0:T(8,128)(2,1)S(1)} %copy-done.23, f32[2048]{0:T(1024)S(1)} %bitcast.182, f32[1024]{0:T(1024)S(1)} %add_rsqrt_fusion), kind=kOutput, calls=%fused_computation.9 | convolution fusion | flops 5379719168 | bytes 12070912 | tf_op jit(solution)/shard_map/dot_general | solution.py:981
  506.5 1.2 dynamic-slice_bitcast_fusion
  508.4 4.5 all-to-all-done.1
  512.9 7.0 %bitcast_convert_fusion = bf16[512,2048]{1,0:T(8,128)(2,1)} fusion(bf16[4,320,2048]{2,1,0:T(8,128)(2,1)} %all-to-all-done.1, f32[4,320]{1,0:T(4,128)S(1)} %multiply_reduce_fusion, s32[4,512]{1,0:T(4,128)S(1)} %fusion.33), kind=kOutput, calls=%fused_computation.22 | convolution fusion | flops 2693922816 | bytes 7353344 | tf_op jit(solution)/shard_map/dot_general | solution.py:981
  519.9 5.2 collective-permute-done
  526.1 94.4 %finish.1 = (f32[2,64,2176]{2,1,0:T(8,128)}, bf16[4,64,2816]{2,1,0:T(8,128)(2,1)}, bf16[4,64,1408]{2,1,0:T(8,128)(2,1)}, bf16[128,2048]{1,0:T(8,128)(2,1)}, f32[128,2048]{1,0:T(8,128)}, /*index=5*/f32[64,128]{1,0:T(8,128)}) custom-call(bf16[4,2,4,64,1280]{4,3,2,1,0:T(8,128)(2,1)} %bitcast.139, bf16[4,2,4,64,128]{4,3,2,1,0:T(8,128)(2,1)} %bitcast.152, ...), custom_call_target="tpu_custom_call" | custom-call | tf_op jit(solution)/shard_map/finish/pallas_call | solution.py:919
  620.5 1.2 fusion.60
  623.5 1.5 slice_reduce_fusion
  625.0 1.5 copy.172
  626.7 1.3 copy.178
  628.0 4.3 reshape.464
  632.9 1.1 reshape.457
  635.5 1.3 copy.170
  637.9 1.2 convert_bitcast_fusion
  (212 shorter events, 29.9 us)
Async XLA Ops:
  7.2 4.9 copy-start.33
  7.2 5.4 copy-start.34
  7.2 149.5 %all-gather.7.cloned.1.call-start = ((), (), s32[]{:S(2)}) async-start(), calls=%async_computation.5 | async-start | bytes 2621440 | tf_op jit(solution)/shard_map/all_gather | solution.py:1406
  8.7 4.4 copy-start.35
  8.7 4.6 copy-start.39
  8.7 4.6 copy-start.40
  8.7 4.6 copy-start.41
  8.7 4.6 copy-start.42
  8.7 4.7 copy-start.24
  9.6 159.0 %all-gather.5.cloned.1.call-start = ((), (), s32[]{:S(2)}) async-start(), calls=%async_computation.4 | async-start | bytes 4718592 | tf_op jit(solution)/shard_map/all_gather | solution.py:1405
  11.0 4.3 copy-start.38
  11.0 4.3 copy-start.37
  12.1 251.6 %all-gather.9.cloned.1.call-start = ((), (), s32[]{:S(2)}) async-start(), calls=%async_computation.6 | async-start | bytes 7208960 | tf_op jit(solution)/shard_map/all_gather | solution.py:1419
  113.1 193.8 %all-gather.11.cloned.1.call-start = ((), (), s32[]{:S(2)}) async-start(), calls=%async_computation.7 | async-start | bytes 14417920 | tf_op jit(solution)/shard_map/all_gather | solution.py:1416
  113.7 37.5 %copy-start.32 = (bf16[2,512,128]{2,1,0:T(8,128)(2,1)S(1)}, bf16[2,512,128]{2,1,0:T(8,128)(2,1)}, u32[]{:S(2)}) copy-start(bf16[2,512,128]{2,1,0:T(8,128)(2,1)} %get-tuple-element.54) | copy-start | bytes 786436
  149.8 3.2 copy-start.36
  153.7 9.3 %copy-start.27 = (pred[1280,512]{1,0:T(32,128)(4,1)}, pred[1280,512]{1,0:T(32,128)(4,1)S(1)}, u32[]{:S(2)}) copy-start(pred[1280,512]{1,0:T(32,128)(4,1)S(1)} %bitcast_compare_fusion) | copy-start | bytes 1966084
  156.0 29.3 %copy-start.4 = (f32[1024,128]{1,0:T(8,128)}, f32[1024,128]{1,0:T(8,128)S(1)}, u32[]{:S(2)}) copy-start(f32[1024,128]{1,0:T(8,128)S(1)} %get-tuple-element.165.cos_ref) | copy-start | bytes 1572868
  156.0 29.3 %copy-start.6 = (f32[1024,128]{1,0:T(8,128)}, f32[1024,128]{1,0:T(8,128)S(1)}, u32[]{:S(2)}) copy-start(f32[1024,128]{1,0:T(8,128)S(1)} %get-tuple-element.166.sin_ref) | copy-start | bytes 1572868
  163.0 100.7 %all-to-all-start = ((bf16[4,320,2048]{2,1,0:T(8,128)(2,1)}), bf16[4,320,2048]{2,1,0:T(8,128)(2,1)}, u32[]{:S(2)}, u32[]{:S(2)}) async-start(bf16[4,320,2048]{2,1,0:T(8,128)(2,1)} %bitcast.138), calls=%async_computation | async-start | bytes 10485760 | tf_op jit(solution)/shard_map/all_to_all | solution.py:1434
  168.0 338.5 %reduce-scatter.5.cloned.1.call-start = ((), (), s32[]{:S(2)}) async-start(), calls=%async_computation.9 | async-start | bytes 7208960 | tf_op jit(solution)/shard_map/reduce_scatter | solution.py:1476
  168.6 3.5 copy-start.21
  181.4 2.4 copy-start.19
  203.1 6.2 copy-start.15
  203.1 6.2 copy-start.17
  203.1 6.3 copy-start.1
  209.3 47.7 %copy-start.28 = (pred[1280,512]{1,0:T(32,128)(4,1)S(1)}, pred[1280,512]{1,0:T(32,128)(4,1)}, u32[]{:S(2)}) copy-start(pred[1280,512]{1,0:T(32,128)(4,1)} %copy-done.27) | copy-start | bytes 1966084
  253.4 3.2 copy-start.10
  303.1 2.5 copy-start
  344.7 181.5 %reduce-scatter.3.cloned.1.call-start = ((), (), s32[]{:S(2)}) async-start(), calls=%async_computation.8 | async-start | bytes 14417920 | tf_op jit(solution)/shard_map/reduce_scatter | solution.py:1480
  398.5 4.0 copy-start.31
  402.7 2.5 copy-start.29
  402.7 2.5 copy-start.43
  447.6 65.3 %all-to-all-start.1 = ((bf16[4,320,2048]{2,1,0:T(8,128)(2,1)}), bf16[4,320,2048]{2,1,0:T(8,128)(2,1)}, u32[]{:S(2)}, u32[]{:S(2)}) async-start(bf16[4,320,2048]{2,1,0:T(8,128)(2,1)} %get-tuple-element.81), calls=%async_computation.3 | async-start | bytes 10485760 | tf_op jit(solution)/shard_map/all_to_all | solution.py:1499
  452.9 8.6 %copy-start.5 = (f32[1024,128]{1,0:T(8,128)S(1)}, f32[1024,128]{1,0:T(8,128)}, u32[]{:S(2)}) copy-start(f32[1024,128]{1,0:T(8,128)} %copy-done.4) | copy-start | bytes 1572868
  452.9 8.6 %copy-start.7 = (f32[1024,128]{1,0:T(8,128)S(1)}, f32[1024,128]{1,0:T(8,128)}, u32[]{:S(2)}) copy-start(f32[1024,128]{1,0:T(8,128)} %copy-done.6) | copy-start | bytes 1572868
  452.9 8.6 %copy-start.9 = (f32[1024,3]{1,0:T(8,128)S(1)}, f32[1024,3]{1,0:T(8,128)}, u32[]{:S(2)}) copy-start(f32[1024,3]{1,0:T(8,128)} %copy.158.gate_ref) | copy-start | bytes 36868
  452.9 8.6 %copy-start.16 = (bf16[1024,256]{1,0:T(8,128)(2,1)S(1)}, bf16[1024,256]{1,0:T(8,128)(2,1)}, u32[]{:S(2)}) copy-start(bf16[1024,256]{1,0:T(8,128)(2,1)} %copy-done.15) | copy-start | bytes 1572868
  452.9 8.6 %copy-start.18 = (bf16[1024,256]{1,0:T(8,128)(2,1)S(1)}, bf16[1024,256]{1,0:T(8,128)(2,1)}, u32[]{:S(2)}) copy-start(bf16[1024,256]{1,0:T(8,128)(2,1)} %copy-done.17) | copy-start | bytes 1572868
  475.6 12.6 %copy-start.3 = (bf16[4,128,2048]{2,1,0:T(8,128)(2,1)S(1)}, bf16[4,128,2048]{2,1,0:T(8,128)(2,1)}, u32[]{:S(2)}) copy-start(bf16[4,128,2048]{2,1,0:T(8,128)(2,1)} %copy-done.2) | copy-start | bytes 6291460
  475.6 13.0 %copy-start.22 = (bf16[1024,2048]{1,0:T(8,128)(2,1)S(1)}, bf16[1024,2048]{1,0:T(8,128)(2,1)}, u32[]{:S(2)}) copy-start(bf16[1024,2048]{1,0:T(8,128)(2,1)} %all-gather.5.cloned.1.call-done) | copy-start | bytes 12582916
  488.6 2.5 copy-start.45
  491.1 7.6 %copy-start.23 = (bf16[1024,2048]{1,0:T(8,128)(2,1)S(1)}, bf16[1024,2048]{1,0:T(8,128)(2,1)}, u32[]{:S(2)}) copy-start(bf16[1024,2048]{1,0:T(8,128)(2,1)} %all-gather.5.cloned.1.call-done) | copy-start | bytes 12582916
  491.1 7.6 %copy-start.44 = (bf16[1024,1280]{1,0:T(8,128)(2,1)S(1)}, bf16[1024,1280]{1,0:T(8,128)(2,1)}, u32[]{:S(2)}) copy-start(bf16[1024,1280]{1,0:T(8,128)(2,1)} %get-tuple-element.76) | copy-start | bytes 7864324
  507.7 17.4 %copy-start.25 = (bf16[512,1408]{1,0:T(8,128)(2,1)S(1)}, bf16[512,1408]{1,0:T(8,128)(2,1)}, u32[]{:S(2)}) copy-start(bf16[512,1408]{1,0:T(8,128)(2,1)} %reduce-scatter.5.cloned.1.call-done) | copy-start | bytes 4325380
  507.7 17.4 %collective-permute-start = (bf16[256,1408]{1,0:T(8,128)(2,1)S(1)}, bf16[256,1408]{1,0:T(8,128)(2,1)S(1)}, u32[]{:S(2)}, u32[]{:S(2)}) collective-permute-start(bf16[256,1408]{1,0:T(8,128)(2,1)S(1)} %dynamic-slice_bitcast_fusion), channel_id=1, source_target_pairs={{0,16},{16,0},{1,17},{17,1},{2,18},{18,2},{3,19},{19,3},{4,20},{20... | collective-permute-start | bytes 2162696 | tf_op jit(solution)/shard_map/ppermute | solution.py:1483
  632.3 5.6 copy-start.26
  634.1 6.5 %copy-start.30 = (f32[64,128]{1,0:T(8,128)S(1)}, f32[64,128]{1,0:T(8,128)}, u32[]{:S(2)}) copy-start(f32[64,128]{1,0:T(8,128)} %get-tuple-element.86) | copy-start | bytes 98308
  (7 other events, 9.2 us)
Sparse Core Ops, SparseCore 0:
  9.7 41.7 all-gather.6
  53.7 65.6 all-gather.4
  121.1 57.8 all-gather.8
  180.4 110.2 all-gather.10
  344.8 54.8 reduce-scatter.4
  402.0 105.7 reduce-scatter.2

commit v8 on v7

--- a/solution.py
+++ b/solution.py
@@ -102,13 +102,15 @@
     experts = ((ups_ref, up_ref), (downs_ref, down_ref))
     kept = []
     for n, (shards, expert) in enumerate(experts):
-        kept.append(pltpu.make_async_copy(shards.at[y], expert.at[xl, y], loc.at[1 + n]))
+        place_of = expert.at[xl] if n == 0 else expert
+        kept.append(pltpu.make_async_copy(shards.at[y], place_of.at[y], loc.at[1 + n]))
         kept[-1].start()
-        send(shards.at[y], expert.at[xl, y], ex.at[n, 0], ey.at[n, 0], neighbour("xl", 1))
+        if n == 0:
+            send(shards.at[y], place_of.at[y], ex.at[0], ey.at[0], neighbour("xl", 1))
         for step in (1, 3, 2):
             send(
                 shards.at[mod4(y + step)],
-                expert.at[xl, y],
+                place_of.at[y],
                 es.at[n, step - 1],
                 er.at[n, step - 1],
                 neighbour("y", step),
@@ -124,8 +126,8 @@
 
     def send_second(h, k, first):
         block = slot(h, first, place[rings[h][1]], both, h * half, half)
-        send(block, block, s2.at[k, 0], r2m.at[k], neighbour(rings[h][1], 1))
-        send(block, block, s2.at[k, 1], r2p.at[k], neighbour(rings[h][1], -1))
+        send(block, block, s2.at[h, k, 0], r2m.at[h, k], neighbour(rings[h][1], 1))
+        send(block, block, s2.at[h, k, 1], r2p.at[h, k], neighbour(rings[h][1], -1))
 
     for h in (0, 1):
         first, second = place[rings[h][0]], place[rings[h][1]]
@@ -133,8 +135,7 @@
         arrived(block, xr.at[h])
         send(block, block, s1.at[h, 1, 0], r1m.at[h, 1], neighbour(rings[h][0], 1))
         send(block, block, s1.at[h, 1, 1], r1p.at[h, 1], neighbour(rings[h][0], -1))
-        if h == 1:
-            send_second(h, 0, first)
+        send_second(h, 0, first)
     for j, jx in ((0, xl), (1, other)):
         for h in (0, 1):
             first, second = place[rings[h][0]], place[rings[h][1]]
@@ -145,92 +146,44 @@
             block = slot(h, mod4(first + 1), second, jx, h * half + quarter, quarter)
             send(block, block, f1s.at[h, j, 1], f1r.at[h, j, 1], neighbour(rings[h][0], -1))
     for k, step in ((1, -1), (2, 1)):
-        send_second(1, k, mod4(place[rings[1][0]] + step))
-    for n, (shards, expert) in enumerate(experts):
-        for step in (1, 3, 2):
-            landed = expert.at[xl, mod4(y - step)]
-            arrived(landed, er.at[n, step - 1])
-            send(landed, landed, ex.at[n, step], ey.at[n, step], neighbour("xl", 1))
+        for h in (0, 1):
+            send_second(h, k, mod4(place[rings[h][0]] + step))
     for h in (0, 1):
         first, second = place[rings[h][0]], place[rings[h][1]]
         for j, jx in ((0, xl), (1, other)):
             for p in (0, 1):
                 block = slot(h, mod4(first + 2), second, jx, h * half + p * quarter, quarter)
                 arrived(block, f1r.at[h, j, p])
-        if h == 1:
-            send_second(h, 3, mod4(first + 2))
+        send_second(h, 3, mod4(first + 2))
+    for step in (1, 3, 2):
+        landed = up_ref.at[xl, mod4(y - step)]
+        arrived(landed, er.at[0, step - 1])
+        send(landed, landed, ex.at[step], ey.at[step], neighbour("xl", 1))
     steps = ((0, 0), (1, -1), (2, 1), (3, 2))
-    h = 1
-    second = place[rings[h][1]]
     for k, step in steps:
-        first = mod4(place[rings[h][0]] + step)
-        arrived(slot(h, first, mod4(second - 1), both, half, half), r2m.at[k])
-        block = slot(h, first, mod4(second - 1), both, half, quarter)
-        send(block, block, f2s.at[k, 0], f2r.at[k, 0], neighbour(rings[h][1], 1))
-        arrived(slot(h, first, mod4(second + 1), both, half, half), r2p.at[k])
-        block = slot(h, first, mod4(second + 1), both, half + quarter, quarter)
-        send(block, block, f2s.at[k, 1], f2r.at[k, 1], neighbour(rings[h][1], -1))
+        for h in (0, 1):
+            first, second = mod4(place[rings[h][0]] + step), place[rings[h][1]]
+            arrived(slot(h, first, mod4(second - 1), both, h * half, half), r2m.at[h, k])
+            block = slot(h, first, mod4(second - 1), both, h * half, quarter)
+            send(block, block, f2s.at[h, k, 0], f2r.at[h, k, 0], neighbour(rings[h][1], 1))
+            arrived(slot(h, first, mod4(second + 1), both, h * half, half), r2p.at[h, k])
+            block = slot(h, first, mod4(second + 1), both, h * half + quarter, quarter)
+            send(block, block, f2s.at[h, k, 1], f2r.at[h, k, 1], neighbour(rings[h][1], -1))
     for k, step in steps:
-        first = mod4(place[rings[h][0]] + step)
-        for p in (0, 1):
-            block = slot(h, first, mod4(second + 2), both, half + p * quarter, quarter)
-            arrived(block, f2r.at[k, p])
-    for n, (shards, expert) in enumerate(experts):
-        for step in (0, 1, 3, 2):
-            arrived(expert.at[other, mod4(y - step)], ey.at[n, step])
-        kept[n].wait()
+        for h in (0, 1):
+            first, second = mod4(place[rings[h][0]] + step), place[rings[h][1]]
+            for p in (0, 1):
+                block = slot(h, first, mod4(second + 2), both, h * half + p * quarter, quarter)
+                arrived(block, f2r.at[h, k, p])
+    for step in (0, 1, 3, 2):
+        arrived(up_ref.at[other, mod4(y - step)], ey.at[step])
+    for step in (1, 3, 2):
+        arrived(down_ref.at[mod4(y - step)], er.at[1, step - 1])
+    for copy in kept:
+        copy.wait()
     arrived(marks_out.at[other], mr)
     own_marks.wait()
     sends.finish()
-
-
-def gather_rest_body(start_ref, out_ref, s2, r2m, r2p, f2s, f2r):
-    y, z = lax.axis_index("y"), lax.axis_index("z")
-    half = out_ref.shape[3] // 2
-    quarter = half // 2
-    ahead, behind = neighbour("y", 1), neighbour("y", -1)
-    greet(ahead, behind)
-    sends = Sends()
-    both = pl.ds(0, 2)
-
-    def slot(ref, zz, yy, start, count):
-        return ref.at[zz, both, yy, pl.ds(start, count)]
-
-    steps = ((0, 0), (1, -1), (2, 1), (3, 2))
-    for k, step in steps:
-        zz = mod4(z + step)
-        src, dst = slot(start_ref, zz, y, 0, half), slot(out_ref, zz, y, 0, half)
-        sends(src, dst, s2.at[k, 0], r2m.at[k], ahead)
-        sends(src, dst, s2.at[k, 1], r2p.at[k], behind)
-    for k, step in steps:
-        zz = mod4(z + step)
-        arrived(slot(out_ref, zz, mod4(y - 1), 0, half), r2m.at[k])
-        block = slot(out_ref, zz, mod4(y - 1), 0, quarter)
-        sends(block, block, f2s.at[k, 0], f2r.at[k, 0], ahead)
-        arrived(slot(out_ref, zz, mod4(y + 1), 0, half), r2p.at[k])
-        block = slot(out_ref, zz, mod4(y + 1), quarter, quarter)
-        sends(block, block, f2s.at[k, 1], f2r.at[k, 1], behind)
-    for k, step in steps:
-        for p in (0, 1):
-            arrived(slot(out_ref, mod4(z + step), mod4(y + 2), p * quarter, quarter), f2r.at[k, p])
-    sends.finish()
-
-
-def gather_rest(whole, rows):
-    dma = pltpu.SemaphoreType.DMA
-    cols = whole.shape[1]
-    anywhere = pl.BlockSpec(memory_space=pl.ANY)
-    out = pl.pallas_call(
-        gather_rest_body,
-        out_shape=jax.ShapeDtypeStruct((4, 2, 4, rows, cols), whole.dtype),
-        in_specs=[anywhere],
-        out_specs=anywhere,
-        scratch_shapes=[dma((4, 2)), dma((4,)), dma((4,)), dma((4, 2)), dma((4, 2))],
-        input_output_aliases={0: 0},
-        compiler_params=pltpu.CompilerParams(collective_id=6, has_side_effects=True),
-        name="gather_rest",
-    )(whole.reshape(4, 2, 4, rows, cols))
-    return out.reshape(whole.shape)
 
 
 def gather_dp(shard, ups, downs, marks):
@@ -241,7 +194,7 @@
         out_shape=[
             jax.ShapeDtypeStruct((4, 2, 4, rows, cols), shard.dtype),
             jax.ShapeDtypeStruct((2, *ups.shape), ups.dtype),
-            jax.ShapeDtypeStruct((2, *downs.shape), downs.dtype),
+            jax.ShapeDtypeStruct(downs.shape, downs.dtype),
             jax.ShapeDtypeStruct((2, *marks.shape), marks.dtype),
         ],
         in_specs=[pl.BlockSpec(memory_space=pl.ANY)] * 4,
@@ -255,15 +208,15 @@
             dma((2, 2)),
             dma((2, 2, 2)),
             dma((2, 2, 2)),
-            dma((4, 2)),
+            dma((2, 4, 2)),
+            dma((2, 4)),
+            dma((2, 4)),
+            dma((2, 4, 2)),
+            dma((2, 4, 2)),
+            dma((2, 3)),
+            dma((2, 3)),
             dma((4,)),
             dma((4,)),
-            dma((4, 2)),
-            dma((4, 2)),
-            dma((2, 3)),
-            dma((2, 3)),
-            dma((2, 4)),
-            dma((2, 4)),
             dma,
             dma,
         ],
@@ -610,20 +563,14 @@
     return dmiddle, dgain[0], spread.reshape(8 * rows, width), branch
 
 
-def rows_body(
-    rows_ref, grad_ref, down_ref, out_ref, raw_out, grad, down, block, loc, out_sem, far_s, far_r, core_s, core_r
-):
+def rows_body(rows_ref, out_ref, loc, far_s, far_r, core_s, core_r):
     y, core = lax.axis_index("y"), lax.axis_index("core")
     half = rows_ref.shape[1] // 2
     sends = Sends()
     greet(neighbour("core", 1), *(neighbour("y", step) for step in (1, 2, 3)))
     at = pl.ds(pl.multiple_of(core * half, half), half)
-    own = pltpu.make_async_copy(rows_ref.at[y], out_ref.at[y], loc.at[0])
+    own = pltpu.make_async_copy(rows_ref.at[y], out_ref.at[y], loc)
     own.start()
-    loads = []
-    for n, (src, dst) in enumerate(((grad_ref, grad), (down_ref, down))):
-        loads.append(pltpu.make_async_copy(src, dst, loc.at[1 + n]))
-        loads[-1].start()
     for step in (2, 1, 3):
         target = mod4(y + step)
         sends(
@@ -633,21 +580,6 @@
             far_r.at[step - 1],
             neighbour("y", step),
         )
-    for load in loads:
-        load.wait()
-    outs = []
-    columns = raw_out.shape[1]
-    for n, start in enumerate(range(0, columns, WIDE)):
-        cols = min(WIDE, columns - start)
-        if n >= 2:
-            outs[n - 2].wait()
-        block[n % 2, :, :cols] = dot(grad[...], down[:, start : start + cols], ((1,), (0,)))
-        outs.append(
-            pltpu.make_async_copy(
-                block.at[n % 2, :, pl.ds(0, cols)], raw_out.at[:, pl.ds(start, cols)], out_sem.at[n % 2]
-            )
-        )
-        outs[-1].start()
     for step in (1, 3, 2):
         source = mod4(y - step)
         block = out_ref.at[source, at]
@@ -657,39 +589,20 @@
     other = pl.ds(pl.multiple_of((1 - core) * half, half), half)
     for step in (1, 3, 2):
         arrived(out_ref.at[mod4(y - step), other], core_r.at[step - 1])
-    for out in outs[-2:]:
-        out.wait()
     sends.finish()
 
 
-def rows_to_experts(rows, grads, down):
-    count, hidden = grads.shape[0], down.shape[1]
-    anywhere = pl.BlockSpec(memory_space=pl.ANY)
+def rows_to_experts(rows):
     dma = pltpu.SemaphoreType.DMA
     return pl.pallas_call(
         rows_body,
-        out_shape=[
-            jax.ShapeDtypeStruct(rows.shape, rows.dtype),
-            jax.ShapeDtypeStruct((count, hidden), F32),
-        ],
-        in_specs=[anywhere] * 3,
-        out_specs=[anywhere] * 2,
-        scratch_shapes=[
-            pltpu.VMEM(grads.shape, BF16),
-            pltpu.VMEM(down.shape, BF16),
-            pltpu.VMEM((2, count, WIDE), F32),
-            dma((3,)),
-            dma((2,)),
-            dma((3,)),
-            dma((3,)),
-            dma((3,)),
-            dma((3,)),
-        ],
-        compiler_params=pltpu.CompilerParams(
-            collective_id=4, has_side_effects=True, vmem_limit_bytes=40 * MIB
-        ),
+        out_shape=jax.ShapeDtypeStruct(rows.shape, rows.dtype),
+        in_specs=[pl.BlockSpec(memory_space=pl.ANY)],
+        out_specs=pl.BlockSpec(memory_space=pl.ANY),
+        scratch_shapes=[dma, dma((3,)), dma((3,)), dma((3,)), dma((3,))],
+        compiler_params=pltpu.CompilerParams(collective_id=4, has_side_effects=True),
         name="rows_to_experts",
-    )(rows, grads, down)
+    )(rows)
 
 
 STEPS = (2, 1, -1, 0)
@@ -981,23 +894,50 @@
     return lax.dot_general(a, b, (dims, ((), ())), preferred_element_type=F32)
 
 
+def joined_body(rows_ref, gate_up_ref, linear_up_ref, gate_out, linear_out):
+    up = jnp.concatenate([gate_up_ref[...], linear_up_ref[...]], 1)
+    joined = dot(rows_ref[...], up, ((1,), (0,)))
+    gate_out[...] = joined[:, :LANES]
+    linear_out[...] = joined[:, LANES:]
+
+
+def joined_rows(rows, up):
+    count, width, hidden = rows.shape[0], up.shape[0], up.shape[1] // 2
+    chunks = hidden // LANES
+    chunk = pl.BlockSpec((count, LANES), lambda j: (0, j))
+    return pl.pallas_call(
+        joined_body,
+        grid=(chunks,),
+        in_specs=[
+            pl.BlockSpec((count, width), lambda j: (0, 0)),
+            pl.BlockSpec((width, LANES), lambda j: (0, j)),
+            pl.BlockSpec((width, LANES), lambda j: (0, chunks + j)),
+        ],
+        out_specs=[chunk] * 2,
+        out_shape=[jax.ShapeDtypeStruct((count, hidden), F32)] * 2,
+        compiler_params=pltpu.CompilerParams(vmem_limit_bytes=48 * MIB),
+        name="joined_rows",
+    )(rows, up, up)
+
+
 def experts_body(
-    rows_ref, raw_ref, gate_up_ref, linear_up_ref, gate_ref,
-    dgate_pre_out, dlinear_out, hidden_out, gated_out, dgate_out,
+    grad_ref, down_ref, gate_pre_ref, linear_ref, gate_ref,
+    dgate_pre_out, dlinear_out, hidden_out, gated_out, dgate_out, *, units,
 ):
-    @pl.when(pl.program_id(0) == 0)
+    j = pl.program_id(0)
+
+    @pl.when(j == 0)
     def _():
         dgate_out[...] = jnp.zeros_like(dgate_out)
 
-    up = jnp.concatenate([gate_up_ref[...], linear_up_ref[...]], 1)
-    joined = dot(rows_ref[...], up, ((1,), (0,)))
-    gate_pre, linear = joined[:, :LANES], joined[:, LANES:]
+    dhidden = dot(grad_ref[...], down_ref[...], ((1,), (0,)))
+    gate_pre, linear = gate_pre_ref[...], linear_ref[...]
     sigmoid = jax.nn.sigmoid(gate_pre)
     silu = gate_pre * sigmoid
     hidden = silu * linear
-    dhidden = raw_ref[...]
     gate = gate_ref[...]
-    dgate_out[...] += hidden * dhidden
+    product = hidden * dhidden
+    dgate_out[...] += product[:, :LANES] + jnp.where(j * WIDE + LANES < units, product[:, LANES:], 0.0)
     dhidden = dhidden * gate
     hidden_out[...] = hidden.astype(BF16)
     gated_out[...] = (hidden * gate).astype(BF16)
@@ -1005,27 +945,26 @@
     dlinear_out[...] = (dhidden * silu).astype(BF16)
 
 
-def experts(rows, raw, up, gates):
-    count, hidden = raw.shape
-    width = up.shape[0]
-    chunks = hidden // LANES
-    chunk = pl.BlockSpec((count, LANES), lambda j: (0, j))
+def experts(grads, down, gate_pre, linear, gates):
+    count, hidden = gate_pre.shape
+    width = down.shape[0]
+    chunk = pl.BlockSpec((count, WIDE), lambda j: (0, j))
     some = jax.ShapeDtypeStruct((count, hidden), BF16)
     return pl.pallas_call(
-        experts_body,
-        grid=(chunks,),
+        functools.partial(experts_body, units=hidden),
+        grid=(pl.cdiv(hidden, WIDE),),
         in_specs=[
             pl.BlockSpec((count, width), lambda j: (0, 0)),
+            pl.BlockSpec((width, WIDE), lambda j: (0, j)),
             chunk,
-            pl.BlockSpec((width, LANES), lambda j: (0, j)),
-            pl.BlockSpec((width, LANES), lambda j: (0, chunks + j)),
+            chunk,
             pl.BlockSpec((count, 1), lambda j: (0, 0)),
         ],
         out_specs=[chunk] * 4 + [pl.BlockSpec((count, LANES), lambda j: (0, 0))],
         out_shape=[some] * 4 + [jax.ShapeDtypeStruct((count, LANES), F32)],
         compiler_params=pltpu.CompilerParams(vmem_limit_bytes=56 * MIB),
         name="experts",
-    )(rows, raw, up, up, gates)
+    )(grads, down, gate_pre, linear, gates)
 
 
 def return_body(
@@ -1411,16 +1350,14 @@
         jnp.swapaxes(down_proj, 1, 2),
         marks,
     )
-    weights, up_parts, down_parts = lax.optimization_barrier((weights, up_parts, down_parts))
     marks = marks[:, :, :3].astype(jnp.int32)
     up_whole = lax.all_gather(
         up_parts.reshape(2 * mlp_count * share, -1), "z", axis=0, tiled=True
     )
+    up_parts, down_parts = lax.optimization_barrier((up_parts, down_parts))
     down_whole = lax.all_gather(
-        down_parts.reshape(2 * mlp_count * share, -1), "z", axis=0, tiled=True
-    )
-
-    weights = gather_rest(weights, share)
+        down_parts.reshape(mlp_count * share, -1), ("z", "xl"), axis=0, tiled=True
+    )
 
     tokens = segments.shape[0]
     match = jnp.sum((mlp_routes[:, :, None] == jnp.arange(mlp_count, dtype=jnp.int32)).astype(BF16), 1)
@@ -1463,14 +1400,15 @@
     gate_low = (gate_mlp - gate_high.astype(F32)).astype(BF16)
     extended = jnp.concatenate([unit_two, pad_to(jnp.concatenate([gate_high, gate_low], 1), 128)], 1)
     rows_out = dot(pick_rows, extended, ((1,), (0,))).astype(BF16)
-    rows_ext, raw = rows_to_experts(
-        rows_out.reshape(mlp_count, CAP, width + 128), grad_in, down_whole
-    )
+    rows_ext = rows_to_experts(rows_out.reshape(mlp_count, CAP, width + 128))
     rows_ext = rows_ext.reshape(mlp_count * CAP, width + 128)
     gates_ext = rows_ext[:, width : width + 2 * mlp_count].astype(F32)
     mine = (jnp.arange(2 * mlp_count) % mlp_count == lax.axis_index("y")).astype(F32)
     gates_in = jnp.sum(gates_ext * mine, 1, keepdims=True)
-    dgate_pre, dlinear, hidden, gated, dgate_part = experts(rows_ext, raw, up_whole, gates_in)
+    gate_pre, linear = joined_rows(rows_ext, up_whole)
+    dgate_pre, dlinear, hidden, gated, dgate_part = experts(
+        grad_in, down_whole, gate_pre, linear, gates_in
+    )
     grad_down_whole = dot(grad_in, gated, ((0,), (0,))).astype(BF16)
     dgate_part, grad_down_whole = lax.optimization_barrier((dgate_part, grad_down_whole))
     grad_down_sum = lax.psum_scatter(grad_down_whole, "z", scatter_dimension=0, tiled=True)

time: 657 us -> 692 us (1.053)
  waiting for transfers between devices: 10.3 us -> 68.7 us
  Pallas kernels: 457 us -> 429 us
    all_gather x1, waiting for transfers between devices: 0.01 us -> 58.8 us  [on_device(): lax.all_gather(down_parts.reshape(mlp_count * share, -1), ('z', 'xl'), ax...]
    pallas_call x3, Pallas kernels: 100 us -> 86.1 us  [the longest x1 46.5 us: rows_to_experts(): pl.pallas_call(rows_body, out_shape=jax.ShapeDtypeStruct(rows.shape, rows...]
    pallas_call x1, Pallas kernels: 96.1 us -> 82.9 us  [gather_dp(): pl.pallas_call(gather_body, out_shape=[jax.ShapeDtypeStruct((4, 2, 4, row...]
  transfers between devices with their start and end apart: 9 -> 9, of which waited for: 2 -> 3; matrix products, arithmetic and copies ran while one was open for 17% -> 16% of each run, Pallas kernels for 52% -> 46%
where the time goes in v8:
time: 692 us; the launch traced here: 683 us
  Pallas kernels  429 us (62%)
  matrix products  93.5 us (14%)
  waiting for transfers between devices  68.7 us (10%)
  local copies, waits for them, and re-layouts  49.4 us (7%)
  between operations  15.6 us (2%)
  other arithmetic  14.1 us (2%)
  starting transfers between devices  12.5 us (2%)
    pallas_call x1, Pallas kernels, finish(): pl.pallas_call(finish_body, out_shape=[jax.ShapeDtypeStruct((2, share, co...  95.7 us
    dot_general x16, matrix products, dot(): return lax.dot_general(a, b, (dims, ((), ())), preferred_element_type=F32)  93.5 us
    pallas_call x1, Pallas kernels, gather_dp(): pl.pallas_call(gather_body, out_shape=[jax.ShapeDtypeStruct((4, 2, 4, row...  82.9 us
    all_gather x1, waiting for transfers between devices, on_device(): lax.all_gather(down_parts.reshape(mlp_count * share, -1), ('z', 'xl'), ax...  58.8 us
    pallas_call x1, Pallas kernels, return_rows(): pl.pallas_call(return_body, out_shape=[jax.ShapeDtypeStruct((4, half, wid...  53.8 us
    pallas_call x1, Pallas kernels, rows_to_experts(): pl.pallas_call(rows_body, out_shape=jax.ShapeDtypeStruct(rows.shape, rows...  46.5 us
    pallas_call x1, Pallas kernels, middle_and_unit(): pl.pallas_call(middle_body, out_shape=[jax.ShapeDtypeStruct((rows, width)...  41.5 us
    pallas_call x1, Pallas kernels, middle_back(): pl.pallas_call(back_body, out_shape=[jax.ShapeDtypeStruct((rows, width),...  40.3 us
  transfers between devices with their start and end apart: 9, of which 3 were waited for; matrix products, arithmetic and copies ran while one was open for 16% of the time, Pallas kernels for 46%

profile of v8, /device:TPU:1, one launch (start us, length us, event | category | flops | bytes accessed | tf_op | source)
XLA Modules:
  0.0 683.1 jit_solution(8922119833336385026)
XLA Ops:
  7.2 1.4 copy.158
  9.6 1.3 copy.145
  13.4 1.8 reshape.419.ups_ref
  17.0 82.9 %gather_weights.1 = (bf16[4,2,4,64,2176]{4,3,2,1,0:T(8,128)(2,1)}, bf16[2,4,64,2816]{3,2,1,0:T(8,128)(2,1)}, bf16[4,64,1408]{2,1,0:T(8,128)(2,1)}, bf16[2,512,128]{2,1,0:T(8,128)(2,1)}) custom-call(bf16[2,64,2176]{2,1,0:T(8,128)(2,1)} %pad_maximum_fusion.x_ref, bf16[4,64,2816]{2,1,0:T(8,128)(2,1)} %reshape.419.ups_ref, bf16[4,64,1408]{2,1,0:T(8,128)(2,1)} %bitcast.155, ...), custom_call_target="tpu_custom_call" | custom-call | tf_op jit(solution)/shard_map/gather_weights/pallas_call | solution.py:192
  104.5 1.9 fusion.38
  107.4 6.2 convolution_convert_fusion.3
  113.7 5.0 all-to-all-start
  119.3 3.7 fusion.4
  123.8 9.8 %fusion.10.k_ref.v_ref.q0.q1.q2 = f32[1024,1408]{1,0:T(8,128)S(1)} fusion(bf16[2048,2176]{1,0:T(8,128)(2,1)} %bitcast.160, bf16[1024,2048]{1,0:T(8,128)(2,1)S(1)} %copy-done.21, f32[2048]{0:T(1024)S(1)} %bitcast.178, f32[1024]{0:T(1024)S(1)} %add_rsqrt_fusion), kind=kOutput, calls=%fused_computation.18 | convolution fusion | flops 5913968640 | bytes 15740928 | tf_op jit(solution)/shard_map/dot_general | solution.py:894
  133.6 2.5 copy-done.19
  139.6 15.5 %attention_forward.1 = (bf16[1024,256]{1,0:T(8,128)(2,1)S(1)}, bf16[1024,256]{1,0:T(8,128)(2,1)S(1)}, bf16[1024,768]{1,0:T(8,128)(2,1)S(1)}, bf16[1024,768]{1,0:...) custom-call(f32[1024,1408]{1,0:T(8,128)} %copy-done.19, f32[1024,1408]{1,0:T(8,128)} %copy-done.19, ...), custom_call_target="tpu_custom_call" | custom-call | tf_op jit(solution)/shard_map/attention_forward/pallas_call | solution.py:1175
  155.2 6.2 convolution_convert_fusion.4
  161.4 41.5 %middle_and_unit.1 = (f32[128,2048]{1,0:T(8,128)S(1)}, bf16[4,128,2048]{2,1,0:T(8,128)(2,1)S(1)}) custom-call(bf16[2,2,2,128,2048]{4,3,2,1,0:T(8,128)(2,1)S(1)} %bitcast.125, bf16[128,2048]{1,0:T(8,128)(2,1)S(1)} %copy-done.1, f32[1,2048]{1,0:T(1,128)S(1)} %get-tuple-element.153.gain_ref), custom_call_target="tpu_custom_call" | custom-call | tf_op jit(solution)/shard_map/middle_and_unit/pallas_call | solution.py:468
  202.9 1.5 copy-done.2
  204.4 1.9 fusion.36
  206.6 6.8 convolution_convert_fusion
  213.4 46.5 %rows_to_experts.1 = bf16[4,320,2176]{2,1,0:T(8,128)(2,1)} custom-call(bf16[4,320,2176]{2,1,0:T(8,128)(2,1)} %bitcast.128), custom_call_target="tpu_custom_call" | custom-call | tf_op jit(solution)/shard_map/rows_to_experts/pallas_call | solution.py:597
  260.0 1.2 multiply_reduce_fusion.2
  262.3 2.6 copy-done
  264.9 20.2 %joined_rows.1 = (f32[1280,1408]{1,0:T(8,128)}, f32[1280,1408]{1,0:T(8,128)}) custom-call(bf16[1280,2176]{1,0:T(8,128)(2,1)S(1)} %bitcast.121, bf16[2048,2816]{1,0:T(8,128)(2,1)} %all-gather.11.cloned.1.call-done.gate_up_ref.linear_up_ref.up_ref, bf16[2048,2816]{1,0:T(8,128)(2,1)} %all-gather.11.cloned.1.call-done.gate_up_ref.linear_up_ref.up_ref), custom_call_target="tpu_custom_call" | custom-call | tf_op jit(solution)/shard_map/joined_rows/pallas_call | solution.py:908
  285.1 58.8 %all-gather.9.cloned.1.call-done.down_ref = bf16[2048,1408]{1,0:T(8,128)(2,1)} async-done(((bf16[256,1408]{1,0:T(8,128)(2,1)}), bf16[2048,1408]{1,0:T(8,128)(2,1)}) %all-gather.9.cloned.1.call-update) | async-done | bytes 5767184 | tf_op jit(solution)/shard_map/all_gather | solution.py:1358
  343.9 19.4 %experts.1 = (bf16[1280,1408]{1,0:T(8,128)(2,1)}, bf16[1280,1408]{1,0:T(8,128)(2,1)}, bf16[1280,1408]{1,0:T(8,128)(2,1)}, bf16[1280,1408]{1,0:T(8,128)(2,1)}, f32[1280,128]{1,0:T(8,128)}) custom-call(bf16[1280,2048]{1,0:T(8,128)(2,1)} %bitcast.20.grad_ref, bf16[2048,1408]{1,0:T(8,128)(2,1)} %all-gather.9.cloned.1.call-done.down_ref, ...), custom_call_target="tpu_custom_call" | custom-call | tf_op jit(solution)/shard_map/experts/pallas_call | solution.py:953
  363.3 13.1 %convolution_convert_fusion.2 = bf16[2048,1408]{1,0:T(8,128)(2,1)} fusion(bf16[1280,2048]{1,0:T(8,128)(2,1)} %bitcast.20.grad_ref, bf16[1280,1408]{1,0:T(8,128)(2,1)} %get-tuple-element.64), kind=kOutput, calls=%fused_computation.10 | convolution fusion | flops 7384858624 | bytes 14614528 | tf_op jit(solution)/shard_map/dot_general | solution.py:894
  376.7 53.8 %return_rows.1 = (bf16[4,160,2048]{2,1,0:T(8,128)(2,1)}, f32[4,160,128]{2,1,0:T(8,128)}, bf16[2048,2816]{1,0:T(8,128)(2,1)}) custom-call(bf16[1280,1408]{1,0:T(8,128)(2,1)} %get-tuple-element.61.dgate_pre_ref, bf16[1280,1408]{1,0:T(8,128)(2,1)} %get-tuple-element.62.dlinear_ref, ...), custom_call_target="tpu_custom_call" | custom-call | tf_op jit(solution)/shard_map/return_rows/pallas_call | solution.py:1082
  432.5 1.5 iota_compare_fusion.2
  435.0 2.1 fusion.34
  437.1 1.9 fusion.13
  439.0 40.3 %middle_back.1 = (f32[128,2048]{1,0:T(8,128)S(1)}, f32[1,2048]{1,0:T(1,128)S(1)}, bf16[2,2,2,128,2048]{4,3,2,1,0:T(8,128)(2,1)}, bf16[4,320,2048]{2,1,0:T(8,128)(2,1)}) custom-call(bf16[4,128,2048]{2,1,0:T(8,128)(2,1)S(1)} %bitcast.126, f32[128,2048]{1,0:T(8,128)S(1)} %copy-done.11, bf16[128,2048]{1,0:T(8,128)(2,1)S(1)} %copy-done.13, ...), custom_call_target="tpu_custom_call" | custom-call | tf_op jit(solution)/shard_map/middle_back/pallas_call | solution.py:539
  480.3 5.3 all-to-all-start.1
  485.6 8.8 %fusion.19.h0.h1.h2 = f32[1024,768]{1,0:T(8,128)} fusion(bf16[1024,2048]{1,0:T(8,128)(2,1)} %bitcast.183, bf16[2048,2176]{1,0:T(8,128)(2,1)} %bitcast.164), kind=kOutput, calls=%fused_computation.31 | convolution fusion | flops 3221225472 | bytes 10485760 | tf_op jit(solution)/shard_map/dot_general | solution.py:894
  494.4 13.6 %attention_back.1 = (bf16[1024,1280]{1,0:T(8,128)(2,1)}, f32[1024,128]{1,0:T(8,128)S(1)}) custom-call(bf16[1024,256]{1,0:T(8,128)(2,1)S(1)} %copy-done.16, bf16[1024,256]{1,0:T(8,128)(2,1)S(1)} %copy-done.18, bf16[1024,768]{1,0:T(8,128)(2,1)S(1)} %get-tuple-element.52.q0.q1.q2, bf16[1024,768]{1,0:T(8,128)(2,1)S(1)} %get-tuple-element.52.q0.q1.q2, ...), custom_call_target="tpu_custom_call" | custom-call | tf_op jit(solution)/shard_map/attention_back/pallas_call | solution.py:1251
  508.5 12.4 %fusion.59 = (bf16[1024,2048]{1,0:T(8,128)(2,1)}, bf16[2048]{0:T(1024)(128)(2,1)S(1)}) fusion(f32[1024]{0:T(1024)S(1)} %add_rsqrt_fusion, bf16[1024,2048]{1,0:T(8,128)(2,1)} %all-gather.5.cloned.1.call-done, bf16[2048,2176]{1,0:T(8,128)(2,1)} %bitcast.165, bf16[1024,3]{1,0:T(8,128)(2,1)S(1)} %copy.166, bf16[1024,1280]{1,0:T(8,128)(2,1)} %get-tuple-element.72), kind=kOutput, calls=%fused_computation.127 | convolution fusion | flops 5924714496 | bytes 16791552 | tf_op jit(solution)/shard_map/dot_general | solution.py:894
  521.4 1.2 convolution_convert_fusion.7
  523.8 7.7 %convolution_convert_fusion.5 = bf16[2048,768]{1,0:T(8,128)(2,1)} fusion(bf16[1024,2048]{1,0:T(8,128)(2,1)} %bitcast.184, bf16[1024,768]{1,0:T(8,128)(2,1)S(1)} %copy-done.45), kind=kOutput, calls=%fused_computation.26 | convolution fusion | flops 3222798336 | bytes 8912896 | tf_op jit(solution)/shard_map/dot_general | solution.py:894
  531.5 7.8 %convolution_convert_fusion.1 = bf16[2048,1280]{1,0:T(8,128)(2,1)} fusion(bf16[1024,1280]{1,0:T(8,128)(2,1)S(1)} %copy-done.44, bf16[1024,2048]{1,0:T(8,128)(2,1)S(1)} %copy-done.23, f32[2048]{0:T(1024)S(1)} %bitcast.180, f32[1024]{0:T(1024)S(1)} %add_rsqrt_fusion), kind=kOutput, calls=%fused_computation.9 | convolution fusion | flops 5379719168 | bytes 12070912 | tf_op jit(solution)/shard_map/dot_general | solution.py:894
  539.4 1.2 dynamic-slice_bitcast_fusion
  540.5 1.3 collective-permute-start
  541.8 4.0 all-to-all-done.1
  545.8 7.1 %bitcast_convert_fusion = bf16[512,2048]{1,0:T(8,128)(2,1)} fusion(bf16[4,320,2048]{2,1,0:T(8,128)(2,1)} %all-to-all-done.1, f32[4,320]{1,0:T(4,128)S(1)} %multiply_reduce_fusion, s32[4,512]{1,0:T(4,128)S(1)} %fusion.33), kind=kOutput, calls=%fused_computation.22 | convolution fusion | flops 2693922816 | bytes 7353344 | tf_op jit(solution)/shard_map/dot_general | solution.py:894
  552.8 5.4 collective-permute-done
  559.3 95.7 %finish.1 = (f32[2,64,2176]{2,1,0:T(8,128)}, bf16[4,64,2816]{2,1,0:T(8,128)(2,1)}, bf16[4,64,1408]{2,1,0:T(8,128)(2,1)}, bf16[128,2048]{1,0:T(8,128)(2,1)}, f32[128,2048]{1,0:T(8,128)}, /*index=5*/f32[64,128]{1,0:T(8,128)}) custom-call(bf16[4,2,4,64,1280]{4,3,2,1,0:T(8,128)(2,1)} %bitcast.130, bf16[4,2,4,64,128]{4,3,2,1,0:T(8,128)(2,1)} %bitcast.143, ...), custom_call_target="tpu_custom_call" | custom-call | tf_op jit(solution)/shard_map/finish/pallas_call | solution.py:832
  655.0 1.2 fusion.60
  658.0 1.5 slice_reduce_fusion
  659.5 1.5 copy.171
  661.2 1.3 copy.177
  662.5 4.3 reshape.456
  670.0 1.3 copy.169
  672.4 1.2 convert_bitcast_fusion
  (212 shorter events, 32.6 us)
Async XLA Ops:
  7.2 4.9 copy-start.33
  7.2 5.4 copy-start.34
  7.2 100.2 %all-gather.7.cloned.1.call-start = ((), (), s32[]{:S(2)}) async-start(), calls=%async_computation.5 | async-start | bytes 2621440 | tf_op jit(solution)/shard_map/all_gather | solution.py:1345
  8.7 4.4 copy-start.35
  8.7 4.6 copy-start.39
  8.7 4.6 copy-start.40
  8.7 4.6 copy-start.41
  8.7 4.6 copy-start.42
  8.7 4.7 copy-start.24
  9.6 109.6 %all-gather.5.cloned.1.call-start = ((), (), s32[]{:S(2)}) async-start(), calls=%async_computation.4 | async-start | bytes 4718592 | tf_op jit(solution)/shard_map/all_gather | solution.py:1344
  11.0 4.3 copy-start.38
  11.0 4.3 copy-start.37
  12.1 250.2 %all-gather.11.cloned.1.call-start = ((), (), s32[]{:S(2)}) async-start(), calls=%async_computation.7 | async-start | bytes 14417920 | tf_op jit(solution)/shard_map/all_gather | solution.py:1354
  99.9 2.1 copy-start.32
  100.0 3.8 copy-start.36
  100.0 243.9 %all-gather.9.cloned.1.call-start = ((), (), s32[]{:S(2)}) async-start(), calls=%async_computation.6 | async-start | bytes 6488064 | tf_op jit(solution)/shard_map/all_gather | solution.py:1358
  104.4 9.2 %copy-start.27 = (pred[1280,512]{1,0:T(32,128)(4,1)}, pred[1280,512]{1,0:T(32,128)(4,1)S(1)}, u32[]{:S(2)}) copy-start(pred[1280,512]{1,0:T(32,128)(4,1)S(1)} %bitcast_compare_fusion) | copy-start | bytes 1966084
  106.7 30.8 %copy-start.4 = (f32[1024,128]{1,0:T(8,128)}, f32[1024,128]{1,0:T(8,128)S(1)}, u32[]{:S(2)}) copy-start(f32[1024,128]{1,0:T(8,128)S(1)} %get-tuple-element.161.cos_ref) | copy-start | bytes 1572868
  106.8 30.8 %copy-start.6 = (f32[1024,128]{1,0:T(8,128)}, f32[1024,128]{1,0:T(8,128)S(1)}, u32[]{:S(2)}) copy-start(f32[1024,128]{1,0:T(8,128)S(1)} %get-tuple-element.162.sin_ref) | copy-start | bytes 1572868
  113.7 171.4 %all-to-all-start = ((bf16[4,320,2048]{2,1,0:T(8,128)(2,1)}), bf16[4,320,2048]{2,1,0:T(8,128)(2,1)}, u32[]{:S(2)}, u32[]{:S(2)}) async-start(bf16[4,320,2048]{2,1,0:T(8,128)(2,1)} %bitcast.129), calls=%async_computation | async-start | bytes 10485760 | tf_op jit(solution)/shard_map/all_to_all | solution.py:1371
  118.7 420.7 %reduce-scatter.5.cloned.1.call-start = ((), (), s32[]{:S(2)}) async-start(), calls=%async_computation.9 | async-start | bytes 7208960 | tf_op jit(solution)/shard_map/reduce_scatter | solution.py:1414
  119.2 4.5 copy-start.21
  133.6 2.5 copy-start.19
  155.1 6.2 copy-start.15
  155.1 6.3 copy-start.17
  155.1 6.3 copy-start.1
  161.4 45.2 %copy-start.28 = (pred[1280,512]{1,0:T(32,128)(4,1)S(1)}, pred[1280,512]{1,0:T(32,128)(4,1)}, u32[]{:S(2)}) copy-start(pred[1280,512]{1,0:T(32,128)(4,1)} %copy-done.27) | copy-start | bytes 1966084
  202.9 3.3 copy-start.10
  262.3 2.6 copy-start
  376.4 182.9 %reduce-scatter.3.cloned.1.call-start = ((), (), s32[]{:S(2)}) async-start(), calls=%async_computation.8 | async-start | bytes 14417920 | tf_op jit(solution)/shard_map/reduce_scatter | solution.py:1418
  430.5 4.0 copy-start.31
  434.7 2.5 copy-start.29
  434.7 2.5 copy-start.43
  480.3 65.5 %all-to-all-start.1 = ((bf16[4,320,2048]{2,1,0:T(8,128)(2,1)}), bf16[4,320,2048]{2,1,0:T(8,128)(2,1)}, u32[]{:S(2)}, u32[]{:S(2)}) async-start(bf16[4,320,2048]{2,1,0:T(8,128)(2,1)} %get-tuple-element.77), calls=%async_computation.3 | async-start | bytes 10485760 | tf_op jit(solution)/shard_map/all_to_all | solution.py:1437
  485.6 8.8 %copy-start.5 = (f32[1024,128]{1,0:T(8,128)S(1)}, f32[1024,128]{1,0:T(8,128)}, u32[]{:S(2)}) copy-start(f32[1024,128]{1,0:T(8,128)} %copy-done.4) | copy-start | bytes 1572868
  485.6 8.8 %copy-start.7 = (f32[1024,128]{1,0:T(8,128)S(1)}, f32[1024,128]{1,0:T(8,128)}, u32[]{:S(2)}) copy-start(f32[1024,128]{1,0:T(8,128)} %copy-done.6) | copy-start | bytes 1572868
  485.6 8.8 %copy-start.9 = (f32[1024,3]{1,0:T(8,128)S(1)}, f32[1024,3]{1,0:T(8,128)}, u32[]{:S(2)}) copy-start(f32[1024,3]{1,0:T(8,128)} %copy.157.gate_ref) | copy-start | bytes 36868
  485.6 8.8 %copy-start.16 = (bf16[1024,256]{1,0:T(8,128)(2,1)S(1)}, bf16[1024,256]{1,0:T(8,128)(2,1)}, u32[]{:S(2)}) copy-start(bf16[1024,256]{1,0:T(8,128)(2,1)} %copy-done.15) | copy-start | bytes 1572868
  485.6 8.8 %copy-start.18 = (bf16[1024,256]{1,0:T(8,128)(2,1)S(1)}, bf16[1024,256]{1,0:T(8,128)(2,1)}, u32[]{:S(2)}) copy-start(bf16[1024,256]{1,0:T(8,128)(2,1)} %copy-done.17) | copy-start | bytes 1572868
  508.5 12.4 %copy-start.3 = (bf16[4,128,2048]{2,1,0:T(8,128)(2,1)S(1)}, bf16[4,128,2048]{2,1,0:T(8,128)(2,1)}, u32[]{:S(2)}) copy-start(bf16[4,128,2048]{2,1,0:T(8,128)(2,1)} %copy-done.2) | copy-start | bytes 6291460
  508.5 12.8 %copy-start.22 = (bf16[1024,2048]{1,0:T(8,128)(2,1)S(1)}, bf16[1024,2048]{1,0:T(8,128)(2,1)}, u32[]{:S(2)}) copy-start(bf16[1024,2048]{1,0:T(8,128)(2,1)} %all-gather.5.cloned.1.call-done) | copy-start | bytes 12582916
  521.4 2.5 copy-start.45
  523.8 7.7 %copy-start.23 = (bf16[1024,2048]{1,0:T(8,128)(2,1)S(1)}, bf16[1024,2048]{1,0:T(8,128)(2,1)}, u32[]{:S(2)}) copy-start(bf16[1024,2048]{1,0:T(8,128)(2,1)} %all-gather.5.cloned.1.call-done) | copy-start | bytes 12582916
  523.8 7.7 %copy-start.44 = (bf16[1024,1280]{1,0:T(8,128)(2,1)S(1)}, bf16[1024,1280]{1,0:T(8,128)(2,1)}, u32[]{:S(2)}) copy-start(bf16[1024,1280]{1,0:T(8,128)(2,1)} %get-tuple-element.72) | copy-start | bytes 7864324
  540.5 17.7 %copy-start.25 = (bf16[512,1408]{1,0:T(8,128)(2,1)S(1)}, bf16[512,1408]{1,0:T(8,128)(2,1)}, u32[]{:S(2)}) copy-start(bf16[512,1408]{1,0:T(8,128)(2,1)} %reduce-scatter.5.cloned.1.call-done) | copy-start | bytes 4325380
  540.5 17.7 %collective-permute-start = (bf16[256,1408]{1,0:T(8,128)(2,1)S(1)}, bf16[256,1408]{1,0:T(8,128)(2,1)S(1)}, u32[]{:S(2)}, u32[]{:S(2)}) collective-permute-start(bf16[256,1408]{1,0:T(8,128)(2,1)S(1)} %dynamic-slice_bitcast_fusion), channel_id=1, source_target_pairs={{0,16},{16,0},{1,17},{17,1},{2,18},{18,2},{3,19},{19,3},{4,20},{20... | collective-permute-start | bytes 2162696 | tf_op jit(solution)/shard_map/ppermute | solution.py:1421
  666.9 5.6 copy-start.26
  668.7 6.5 copy-start.30
  (7 other events, 9.4 us)
Sparse Core Ops, SparseCore 0:
  9.7 41.7 all-gather.6
  53.7 54.9 all-gather.4
  110.4 111.2 all-gather.10
  223.2 120.6 all-gather.8
  376.5 60.5 reduce-scatter.4
  439.4 105.7 reduce-scatter.2

commit v9 on v7

--- a/solution.py
+++ b/solution.py
@@ -124,8 +124,8 @@
 
     def send_second(h, k, first):
         block = slot(h, first, place[rings[h][1]], both, h * half, half)
-        send(block, block, s2.at[k, 0], r2m.at[k], neighbour(rings[h][1], 1))
-        send(block, block, s2.at[k, 1], r2p.at[k], neighbour(rings[h][1], -1))
+        send(block, block, s2.at[h, k, 0], r2m.at[h, k], neighbour(rings[h][1], 1))
+        send(block, block, s2.at[h, k, 1], r2p.at[h, k], neighbour(rings[h][1], -1))
 
     for h in (0, 1):
         first, second = place[rings[h][0]], place[rings[h][1]]
@@ -133,8 +133,7 @@
         arrived(block, xr.at[h])
         send(block, block, s1.at[h, 1, 0], r1m.at[h, 1], neighbour(rings[h][0], 1))
         send(block, block, s1.at[h, 1, 1], r1p.at[h, 1], neighbour(rings[h][0], -1))
-        if h == 1:
-            send_second(h, 0, first)
+        send_second(h, 0, first)
     for j, jx in ((0, xl), (1, other)):
         for h in (0, 1):
             first, second = place[rings[h][0]], place[rings[h][1]]
@@ -145,7 +144,8 @@
             block = slot(h, mod4(first + 1), second, jx, h * half + quarter, quarter)
             send(block, block, f1s.at[h, j, 1], f1r.at[h, j, 1], neighbour(rings[h][0], -1))
     for k, step in ((1, -1), (2, 1)):
-        send_second(1, k, mod4(place[rings[1][0]] + step))
+        for h in (0, 1):
+            send_second(h, k, mod4(place[rings[h][0]] + step))
     for n, (shards, expert) in enumerate(experts):
         for step in (1, 3, 2):
             landed = expert.at[xl, mod4(y - step)]
@@ -157,24 +157,23 @@
             for p in (0, 1):
                 block = slot(h, mod4(first + 2), second, jx, h * half + p * quarter, quarter)
                 arrived(block, f1r.at[h, j, p])
-        if h == 1:
-            send_second(h, 3, mod4(first + 2))
+        send_second(h, 3, mod4(first + 2))
     steps = ((0, 0), (1, -1), (2, 1), (3, 2))
-    h = 1
-    second = place[rings[h][1]]
     for k, step in steps:
-        first = mod4(place[rings[h][0]] + step)
-        arrived(slot(h, first, mod4(second - 1), both, half, half), r2m.at[k])
-        block = slot(h, first, mod4(second - 1), both, half, quarter)
-        send(block, block, f2s.at[k, 0], f2r.at[k, 0], neighbour(rings[h][1], 1))
-        arrived(slot(h, first, mod4(second + 1), both, half, half), r2p.at[k])
-        block = slot(h, first, mod4(second + 1), both, half + quarter, quarter)
-        send(block, block, f2s.at[k, 1], f2r.at[k, 1], neighbour(rings[h][1], -1))
+        for h in (0, 1):
+            first, second = mod4(place[rings[h][0]] + step), place[rings[h][1]]
+            arrived(slot(h, first, mod4(second - 1), both, h * half, half), r2m.at[h, k])
+            block = slot(h, first, mod4(second - 1), both, h * half, quarter)
+            send(block, block, f2s.at[h, k, 0], f2r.at[h, k, 0], neighbour(rings[h][1], 1))
+            arrived(slot(h, first, mod4(second + 1), both, h * half, half), r2p.at[h, k])
+            block = slot(h, first, mod4(second + 1), both, h * half + quarter, quarter)
+            send(block, block, f2s.at[h, k, 1], f2r.at[h, k, 1], neighbour(rings[h][1], -1))
     for k, step in steps:
-        first = mod4(place[rings[h][0]] + step)
-        for p in (0, 1):
-            block = slot(h, first, mod4(second + 2), both, half + p * quarter, quarter)
-            arrived(block, f2r.at[k, p])
+        for h in (0, 1):
+            first, second = mod4(place[rings[h][0]] + step), place[rings[h][1]]
+            for p in (0, 1):
+                block = slot(h, first, mod4(second + 2), both, h * half + p * quarter, quarter)
+                arrived(block, f2r.at[h, k, p])
     for n, (shards, expert) in enumerate(experts):
         for step in (0, 1, 3, 2):
             arrived(expert.at[other, mod4(y - step)], ey.at[n, step])
@@ -182,55 +181,6 @@
     arrived(marks_out.at[other], mr)
     own_marks.wait()
     sends.finish()
-
-
-def gather_rest_body(start_ref, out_ref, s2, r2m, r2p, f2s, f2r):
-    y, z = lax.axis_index("y"), lax.axis_index("z")
-    half = out_ref.shape[3] // 2
-    quarter = half // 2
-    ahead, behind = neighbour("y", 1), neighbour("y", -1)
-    greet(ahead, behind)
-    sends = Sends()
-    both = pl.ds(0, 2)
-
-    def slot(ref, zz, yy, start, count):
-        return ref.at[zz, both, yy, pl.ds(start, count)]
-
-    steps = ((0, 0), (1, -1), (2, 1), (3, 2))
-    for k, step in steps:
-        zz = mod4(z + step)
-        src, dst = slot(start_ref, zz, y, 0, half), slot(out_ref, zz, y, 0, half)
-        sends(src, dst, s2.at[k, 0], r2m.at[k], ahead)
-        sends(src, dst, s2.at[k, 1], r2p.at[k], behind)
-    for k, step in steps:
-        zz = mod4(z + step)
-        arrived(slot(out_ref, zz, mod4(y - 1), 0, half), r2m.at[k])
-        block = slot(out_ref, zz, mod4(y - 1), 0, quarter)
-        sends(block, block, f2s.at[k, 0], f2r.at[k, 0], ahead)
-        arrived(slot(out_ref, zz, mod4(y + 1), 0, half), r2p.at[k])
-        block = slot(out_ref, zz, mod4(y + 1), quarter, quarter)
-        sends(block, block, f2s.at[k, 1], f2r.at[k, 1], behind)
-    for k, step in steps:
-        for p in (0, 1):
-            arrived(slot(out_ref, mod4(z + step), mod4(y + 2), p * quarter, quarter), f2r.at[k, p])
-    sends.finish()
-
-
-def gather_rest(whole, rows):
-    dma = pltpu.SemaphoreType.DMA
-    cols = whole.shape[1]
-    anywhere = pl.BlockSpec(memory_space=pl.ANY)
-    out = pl.pallas_call(
-        gather_rest_body,
-        out_shape=jax.ShapeDtypeStruct((4, 2, 4, rows, cols), whole.dtype),
-        in_specs=[anywhere],
-        out_specs=anywhere,
-        scratch_shapes=[dma((4, 2)), dma((4,)), dma((4,)), dma((4, 2)), dma((4, 2))],
-        input_output_aliases={0: 0},
-        compiler_params=pltpu.CompilerParams(collective_id=6, has_side_effects=True),
-        name="gather_rest",
-    )(whole.reshape(4, 2, 4, rows, cols))
-    return out.reshape(whole.shape)
 
 
 def gather_dp(shard, ups, downs, marks):
@@ -255,11 +205,11 @@
             dma((2, 2)),
             dma((2, 2, 2)),
             dma((2, 2, 2)),
-            dma((4, 2)),
-            dma((4,)),
-            dma((4,)),
-            dma((4, 2)),
-            dma((4, 2)),
+            dma((2, 4, 2)),
+            dma((2, 4)),
+            dma((2, 4)),
+            dma((2, 4, 2)),
+            dma((2, 4, 2)),
             dma((2, 3)),
             dma((2, 3)),
             dma((2, 4)),
@@ -531,27 +481,55 @@
 
 def back_body(
     part_ref, middle_ref, grad_ref, gain_ref, hidden_ref, down_ref, dmiddle_ref, dgain_ref, spread_ref, branch_out,
-    hidden, down, branch, loc, out_sem, *scratch,
+    hidden, down, branch, branch_buf, branch_sum, loc, cs, cr, ys, yr, *scratch,
 ):
     sends = Sends()
+    y, core = lax.axis_index("y"), lax.axis_index("core")
     loads = []
     for n, (src, dst) in enumerate(((hidden_ref, hidden), (down_ref, down))):
         loads.append(pltpu.make_async_copy(src, dst, loc.at[n]))
         loads[-1].start()
-    greet(*along_x())
+    greet(*along_x(), *(neighbour("y", step) for step in (1, 2, 3)))
     stages = reduce_stages(CHUNKS, [part_ref], *scratch[:7], sends)
     next(stages)
+    slots = branch_out.shape[1]
+    mine = pl.ds(pl.multiple_of(core * slots, slots), slots)
+    theirs = pl.ds(pl.multiple_of((1 - core) * slots, slots), slots)
+
+    def output(step):
+        target = mod4(y + step)
+        branch[step] = dot(hidden[target], down[...], ((1,), (1,))).astype(BF16)
+        sends(
+            branch.at[step, theirs], branch_buf.at[step], cs.at[step], cr.at[step], neighbour("core", 1)
+        )
+
+    def pass_on(step):
+        arrived(branch_buf.at[step], cr.at[step])
+        value = (branch[step, mine, :].astype(F32) + branch_buf[step].astype(F32)).astype(BF16)
+        if step == 0:
+            branch_out[y] = value
+        else:
+            branch_sum[step - 1] = value
+            sends(
+                branch_sum.at[step - 1],
+                branch_out.at[y],
+                ys.at[step - 1],
+                yr.at[step - 1],
+                neighbour("y", step),
+            )
+
     next(stages)
     for load in loads:
         load.wait()
-    slots = branch.shape[1]
-    outs = []
-    for n in range(4):
-        branch[n] = dot(hidden[n * slots : (n + 1) * slots, :], down[...], ((1,), (1,))).astype(BF16)
-        outs.append(pltpu.make_async_copy(branch.at[n], branch_out.at[n], out_sem.at[n]))
-        outs[-1].start()
+    output(2)
+    output(1)
+    pass_on(2)
+    output(3)
+    pass_on(1)
+    output(0)
+    pass_on(3)
     total = next(stages)
-    xl, xh, core = lax.axis_index("xl"), lax.axis_index("xh"), lax.axis_index("core")
+    xl, xh = lax.axis_index("xl"), lax.axis_index("xh")
     step = middle_ref.shape[0] // CHUNKS
     for n in range(CHUNKS):
         rows = slice(n * step, (n + 1) * step)
@@ -571,9 +549,10 @@
         spread_ref[xl, xh, core, rows, :] = dmiddle.astype(BF16)
         if n % 2 == 1:
             ring_spread(spread_ref, n // 2, *scratch[7:], sends)
+    pass_on(0)
     ring_spread_finish(spread_ref, *scratch[7:], sends)
-    for out in outs:
-        out.wait()
+    for step in (1, 3, 2):
+        arrived(branch_out.at[mod4(y - step)], yr.at[step - 1])
     sends.finish()
 
 
@@ -589,24 +568,29 @@
             jax.ShapeDtypeStruct((rows, width), F32),
             jax.ShapeDtypeStruct((1, width), F32),
             jax.ShapeDtypeStruct((2, 2, 2, rows, width), BF16),
-            jax.ShapeDtypeStruct((4, slots, width), BF16),
+            jax.ShapeDtypeStruct((4, slots // 2, width), BF16),
         ],
         in_specs=vmem(4) + [anywhere] * 2,
-        out_specs=vmem(3) + [anywhere],
+        out_specs=vmem(4),
         scratch_shapes=[
-            pltpu.VMEM((count, inner), BF16),
+            pltpu.VMEM((4, slots, inner), BF16),
             pltpu.VMEM(down.shape, BF16),
             pltpu.VMEM((4, slots, width), BF16),
+            pltpu.VMEM((4, slots // 2, width), BF16),
+            pltpu.VMEM((3, slots // 2, width), BF16),
             dma((2,)),
             dma((4,)),
+            dma((4,)),
+            dma((3,)),
+            dma((3,)),
         ]
         + reduce_scratch(1, rows, width)
         + ring_spread_scratch(),
         compiler_params=pltpu.CompilerParams(
-            collective_id=2, has_side_effects=True, vmem_limit_bytes=48 * MIB
+            collective_id=2, has_side_effects=True, vmem_limit_bytes=56 * MIB
         ),
         name="middle_back",
-    )(part.reshape(4, rows, width), middle, grad, gain[None], hidden, down)
+    )(part.reshape(4, rows, width), middle, grad, gain[None], hidden.reshape(4, slots, inner), down)
     return dmiddle, dgain[0], spread.reshape(8 * rows, width), branch
 
 
@@ -1411,7 +1395,6 @@
         jnp.swapaxes(down_proj, 1, 2),
         marks,
     )
-    weights, up_parts, down_parts = lax.optimization_barrier((weights, up_parts, down_parts))
     marks = marks[:, :, :3].astype(jnp.int32)
     up_whole = lax.all_gather(
         up_parts.reshape(2 * mlp_count * share, -1), "z", axis=0, tiled=True
@@ -1419,8 +1402,6 @@
     down_whole = lax.all_gather(
         down_parts.reshape(2 * mlp_count * share, -1), "z", axis=0, tiled=True
     )
-
-    weights = gather_rest(weights, share)
 
     tokens = segments.shape[0]
     match = jnp.sum((mlp_routes[:, :, None] == jnp.arange(mlp_count, dtype=jnp.int32)).astype(BF16), 1)
@@ -1478,14 +1459,6 @@
         dgate_pre, dlinear, up_whole, dgate_part.reshape(mlp_count, CAP, LANES), rows_ext
     )
     grad_up_sum = lax.psum_scatter(grad_up_whole, "z", scatter_dimension=0, tiled=True)
-    halves = grad_down_sum.reshape(2, mlp_count * share, hidden_local)
-    xl = lax.axis_index("xl")
-    theirs = lax.ppermute(
-        lax.dynamic_index_in_dim(halves, 1 - xl, 0, keepdims=False), "xl", ((0, 1), (1, 0))
-    )
-    grad_down_sum = (
-        lax.dynamic_index_in_dim(halves, xl, 0, keepdims=False).astype(F32) + theirs.astype(F32)
-    ).astype(BF16)
     pick_half = lax.dynamic_slice_in_dim(pick, lax.axis_index("core") * (CAP // 2), CAP // 2, 1)
     dgate_two = jnp.sum(pick_half.astype(F32) * jnp.sum(dgate_back, -1, keepdims=True), 1).T
     dlogit_mlp = router_back(dgate_two, weights_mlp, onehot_mlp)
@@ -1493,15 +1466,23 @@
         pick_half.reshape(-1, tokens), dunit_back.reshape(-1, width), ((0,), (0,))
     ) + dot(dlogit_mlp, router_two, ((1,), (1,)))
     grad_rmlp = dot(unit_two, dlogit_mlp, ((0,), (0,)))
-    dmiddle, grad_gain_two, dattention, branch_part = middle_back(
+    dmiddle, grad_gain_two, dattention, branch_back = middle_back(
         dunit_two.astype(BF16), middle, out_grad, gain_two, hidden, down_whole
     )
-    branch_back = lax.all_to_all(branch_part, "y", 0, 0, tiled=True)
 
     raw = dot(dattention, out_weights, ((1,), (0,)))
     grad_qkv, dgate_one = attention_back(
         key_rot, val_rows, queries, mixed, raw, prob, cosine, sine, gate_att
     )
+    halves = grad_down_sum.reshape(2, mlp_count * share, hidden_local)
+    xl = lax.axis_index("xl")
+    theirs = lax.ppermute(
+        lax.dynamic_index_in_dim(halves, 1 - xl, 0, keepdims=False), "xl", ((0, 1), (1, 0))
+    )
+    theirs, grad_qkv = lax.optimization_barrier((theirs, grad_qkv))
+    grad_down_sum = (
+        lax.dynamic_index_in_dim(halves, xl, 0, keepdims=False).astype(F32) + theirs.astype(F32)
+    ).astype(BF16)
     dlogit_att = router_back(dgate_one[:, :att_count], weights_att, onehot_att)
     grad_joined = jnp.concatenate([grad_qkv, pad_to(dlogit_att, 128)], 1)
     dunit_one = dot(grad_joined, weights[:, :out_at], ((1,), (1,)))
@@ -1515,9 +1496,9 @@
         ],
         1,
     )
-    gate_slots = jnp.sum(pick.astype(F32) * gate_mlp.T[:, None, :], -1, keepdims=True)
+    gate_slots = jnp.sum(pick_half.astype(F32) * gate_mlp.T[:, None, :], -1, keepdims=True)
     feed = dot(
-        pick_rows,
+        pick_half.reshape(-1, tokens),
         (branch_back.astype(F32) * gate_slots).astype(BF16).reshape(-1, width),
         ((0,), (0,)),
     )

time: 657 us -> 643 us (0.979)
  Pallas kernels: 457 us -> 429 us
  waiting for transfers between devices: 10.3 us -> 31.5 us
    pallas_call x1 -> x0, Pallas kernels: 36 us -> none  [gather_rest(): pl.pallas_call(gather_rest_body, out_shape=jax.ShapeDtypeStruct((4, 2, 4,...]
    all_gather x1, waiting for transfers between devices: 0.01 us -> 21.3 us  [on_device(): lax.all_gather(up_parts.reshape(2 * mlp_count * share, -1), 'z', axis=0,...]
    unnamed x108 -> x106, local copies, waits for them, and re-layouts: 18 us -> 16.9 us
  transfers between devices with their start and end apart: 9 -> 8, of which waited for: 2 -> 2; matrix products, arithmetic and copies ran while one was open for 17% -> 17% of each run, Pallas kernels for 52% -> 49%
where the time goes in v9:
time: 643 us; the launch traced here: 635 us
  Pallas kernels  429 us (67%)
  matrix products  94.4 us (15%)
  local copies, waits for them, and re-layouts  46.4 us (7%)
  waiting for transfers between devices  31.5 us (5%)
  between operations  15.6 us (2%)
  other arithmetic  11.1 us (2%)
    pallas_call x1, Pallas kernels, gather_dp(): pl.pallas_call(gather_body, out_shape=[jax.ShapeDtypeStruct((4, 2, 4, row...  97.8 us
    pallas_call x1, Pallas kernels, finish(): pl.pallas_call(finish_body, out_shape=[jax.ShapeDtypeStruct((2, share, co...  96.6 us
    dot_general x16, matrix products, dot(): return lax.dot_general(a, b, (dims, ((), ())), preferred_element_type=F32)  94.4 us
    pallas_call x1, Pallas kernels, return_rows(): pl.pallas_call(return_body, out_shape=[jax.ShapeDtypeStruct((4, half, wid...  53.8 us
    pallas_call x1, Pallas kernels, middle_back(): pl.pallas_call(back_body, out_shape=[jax.ShapeDtypeStruct((rows, width),...  45.7 us
    pallas_call x1, Pallas kernels, middle_and_unit(): pl.pallas_call(middle_body, out_shape=[jax.ShapeDtypeStruct((rows, width)...  41.8 us
    pallas_call x1, Pallas kernels, rows_to_experts(): pl.pallas_call(rows_body, out_shape=[jax.ShapeDtypeStruct(rows.shape, row...  39.6 us
    pallas_call x1, Pallas kernels, experts(): pl.pallas_call(experts_body, grid=(chunks,), in_specs=[pl.BlockSpec((coun...  24.7 us
  transfers between devices with their start and end apart: 8, of which 2 were waited for; matrix products, arithmetic and copies ran while one was open for 17% of the time, Pallas kernels for 49%

profile of v9, /device:TPU:1, one launch (start us, length us, event | category | flops | bytes accessed | tf_op | source)
XLA Modules:
  0.0 634.6 jit_solution(14894841846556423385)
XLA Ops:
  7.3 1.5 copy.160
  9.7 1.3 copy.145
  13.5 1.8 reshape.423.ups_ref
  17.1 97.8 %gather_weights.1 = (bf16[4,2,4,64,2176]{4,3,2,1,0:T(8,128)(2,1)}, bf16[2,4,64,2816]{3,2,1,0:T(8,128)(2,1)}, bf16[2,4,64,1408]{3,2,1,0:T(8,128)(2,1)}, bf16[2,512,128]{2,1,0:T(8,128)(2,1)}) custom-call(bf16[2,64,2176]{2,1,0:T(8,128)(2,1)} %pad_maximum_fusion.x_ref, bf16[4,64,2816]{2,1,0:T(8,128)(2,1)} %reshape.423.ups_ref, bf16[4,64,1408]{2,1,0:T(8,128)(2,1)} %bitcast.157, ...), custom_call_target="tpu_custom_call" | custom-call | tf_op jit(solution)/shard_map/gather_weights/pallas_call | solution.py:189
  115.5 1.1 slice.77
  119.4 1.9 fusion.38
  122.3 6.3 convolution_convert_fusion.3
  128.6 5.1 all-to-all-start
  134.0 3.2 fusion.4
  137.5 9.4 %fusion.8.k_ref.v_ref.q0.q1.q2 = f32[1024,1408]{1,0:T(8,128)S(1)} fusion(bf16[2048,2176]{1,0:T(8,128)(2,1)} %bitcast.162, bf16[1024,2048]{1,0:T(8,128)(2,1)S(1)} %copy-done.18, f32[2048]{0:T(1024)S(1)} %bitcast.182, f32[1024]{0:T(1024)S(1)} %add_rsqrt_fusion), kind=kOutput, calls=%fused_computation.16 | convolution fusion | flops 5913968640 | bytes 15740928 | tf_op jit(solution)/shard_map/dot_general | solution.py:965
  146.9 2.4 copy-done.16
  149.7 1.1 copy.157.gate_ref
  152.9 15.9 %attention_forward.1 = (bf16[1024,256]{1,0:T(8,128)(2,1)S(1)}, bf16[1024,256]{1,0:T(8,128)(2,1)S(1)}, bf16[1024,768]{1,0:T(8,128)(2,1)S(1)}, bf16[1024,768]{1,0:...) custom-call(f32[1024,1408]{1,0:T(8,128)} %copy-done.16, f32[1024,1408]{1,0:T(8,128)} %copy-done.16, ...), custom_call_target="tpu_custom_call" | custom-call | tf_op jit(solution)/shard_map/attention_forward/pallas_call | solution.py:1220
  168.9 6.2 convolution_convert_fusion.4
  175.1 41.8 %middle_and_unit.1 = (f32[128,2048]{1,0:T(8,128)S(1)}, bf16[4,128,2048]{2,1,0:T(8,128)(2,1)S(1)}) custom-call(bf16[2,2,2,128,2048]{4,3,2,1,0:T(8,128)(2,1)S(1)} %bitcast.126, bf16[128,2048]{1,0:T(8,128)(2,1)S(1)} %copy-done.1, f32[1,2048]{1,0:T(1,128)S(1)} %get-tuple-element.157.gain_ref), custom_call_target="tpu_custom_call" | custom-call | tf_op jit(solution)/shard_map/middle_and_unit/pallas_call | solution.py:465
  216.9 1.3 copy-done.2
  218.2 1.9 fusion.34
  220.4 7.4 %convolution_convert_fusion = bf16[1280,2176]{1,0:T(8,128)(2,1)} fusion(pred[1280,512]{1,0:T(32,128)(4,1)} %copy-done.24, bf16[512,8]{1,0:T(8,128)(2,1)S(1)} %copy.182, bf16[512,2048]{1,0:T(8,128)(2,1)} %bitcast.124), kind=kOutput, calls=%fused_computation | convolution fusion | flops 2861596672 | bytes 8331264 | tf_op jit(solution)/shard_map/dot_general | solution.py:965
  227.8 39.6 %rows_to_experts.1 = (bf16[4,320,2176]{2,1,0:T(8,128)(2,1)S(1)}, f32[1280,1408]{1,0:T(8,128)}) custom-call(bf16[4,320,2176]{2,1,0:T(8,128)(2,1)} %bitcast.128, bf16[1280,2048]{1,0:T(8,128)(2,1)} %bitcast.24.grad_ref, bf16[2048,1408]{1,0:T(8,128)(2,1)} %all-gather.9.cloned.1.call-done.down_ref), custom_call_target="tpu_custom_call" | custom-call | tf_op jit(solution)/shard_map/rows_to_experts/pallas_call | solution.py:653
  267.4 2.4 copy-done
  270.1 1.1 broadcast_in_dim.87.gate_ref
  271.1 21.3 %all-gather.11.cloned.1.call-done.gate_up_ref.linear_up_ref.up_ref = bf16[2048,2816]{1,0:T(8,128)(2,1)} async-done(((bf16[512,2816]{1,0:T(8,128)(2,1)}), bf16[2048,2816]{1,0:T(8,128)(2,1)}) %all-gather.11.cloned.1.call-update) | async-done | bytes 11534352 | tf_op jit(solution)/shard_map/all_gather | solution.py:1399
  292.5 24.7 %experts.1 = (bf16[1280,1408]{1,0:T(8,128)(2,1)}, bf16[1280,1408]{1,0:T(8,128)(2,1)}, bf16[1280,1408]{1,0:T(8,128)(2,1)}, bf16[1280,1408]{1,0:T(8,128)(2,1)}, f32[1280,128]{1,0:T(8,128)}) custom-call(bf16[1280,2176]{1,0:T(8,128)(2,1)} %bitcast.121, f32[1280,1408]{1,0:T(8,128)} %get-tuple-element.55.raw_ref, ...), custom_call_target="tpu_custom_call" | custom-call | tf_op jit(solution)/shard_map/experts/pallas_call | solution.py:998
  317.2 13.0 %convolution_convert_fusion.2 = bf16[2048,1408]{1,0:T(8,128)(2,1)} fusion(bf16[1280,2048]{1,0:T(8,128)(2,1)} %bitcast.24.grad_ref, bf16[1280,1408]{1,0:T(8,128)(2,1)} %get-tuple-element.58), kind=kOutput, calls=%fused_computation.9 | convolution fusion | flops 7384858624 | bytes 14614528 | tf_op jit(solution)/shard_map/dot_general | solution.py:965
  330.4 53.8 %return_rows.1 = (bf16[4,160,2048]{2,1,0:T(8,128)(2,1)}, f32[4,160,128]{2,1,0:T(8,128)}, bf16[2048,2816]{1,0:T(8,128)(2,1)}) custom-call(bf16[1280,1408]{1,0:T(8,128)(2,1)} %get-tuple-element.64.dgate_pre_ref, bf16[1280,1408]{1,0:T(8,128)(2,1)} %get-tuple-element.65.dlinear_ref, ...), custom_call_target="tpu_custom_call" | custom-call | tf_op jit(solution)/shard_map/return_rows/pallas_call | solution.py:1127
  387.4 2.2 fusion.32
  389.6 3.3 fusion.11
  392.9 45.7 %middle_back.1 = (f32[128,2048]{1,0:T(8,128)}, f32[1,2048]{1,0:T(1,128)}, bf16[2,2,2,128,2048]{4,3,2,1,0:T(8,128)(2,1)}, bf16[4,160,2048]{2,1,0:T(8,128)(2,1)}) custom-call(bf16[4,128,2048]{2,1,0:T(8,128)(2,1)} %bitcast.150, f32[128,2048]{1,0:T(8,128)} %copy-done.9, bf16[128,2048]{1,0:T(8,128)(2,1)} %copy.163.grad_ref, f32[1,2048]{1,0:T(1,128)} %copy-done.15, ...), custom_call_target="tpu_custom_call" | custom-call | tf_op jit(solution)/shard_map/middle_back/pallas_call | solution.py:565
  438.6 8.6 %fusion.17.h0.h1.h2 = f32[1024,768]{1,0:T(8,128)} fusion(bf16[1024,2048]{1,0:T(8,128)(2,1)} %bitcast.187, bf16[2048,2176]{1,0:T(8,128)(2,1)} %bitcast.166), kind=kOutput, calls=%fused_computation.29 | convolution fusion | flops 3221225472 | bytes 10485760 | tf_op jit(solution)/shard_map/dot_general | solution.py:965
  447.3 13.5 %attention_back.1 = (bf16[1024,1280]{1,0:T(8,128)(2,1)}, f32[1024,128]{1,0:T(8,128)S(1)}) custom-call(bf16[1024,256]{1,0:T(8,128)(2,1)S(1)} %copy-done.12, bf16[1024,256]{1,0:T(8,128)(2,1)S(1)} %copy-done.14, bf16[1024,768]{1,0:T(8,128)(2,1)S(1)} %get-tuple-element.62.q0.q1.q2, bf16[1024,768]{1,0:T(8,128)(2,1)S(1)} %get-tuple-element.62.q0.q1.q2, ...), custom_call_target="tpu_custom_call" | custom-call | tf_op jit(solution)/shard_map/attention_back/pallas_call | solution.py:1296
  461.4 2.0 convolution_convert_fusion.6
  463.4 3.6 convolution_convert_fusion.7
  467.0 3.3 bitcast_convert_fusion
  470.3 1.3 dynamic-slice_bitcast_fusion
  472.1 8.3 %convolution_convert_fusion.5 = bf16[2048,768]{1,0:T(8,128)(2,1)} fusion(bf16[1024,2048]{1,0:T(8,128)(2,1)} %bitcast.188, bf16[1024,768]{1,0:T(8,128)(2,1)} %get-tuple-element.51), kind=kOutput, calls=%fused_computation.24 | convolution fusion | flops 3222798336 | bytes 8912896 | tf_op jit(solution)/shard_map/dot_general | solution.py:965
  480.4 9.5 %collective-permute-done = bf16[256,1408]{1,0:T(8,128)(2,1)S(1)} collective-permute-done((bf16[256,1408]{1,0:T(8,128)(2,1)S(1)}, bf16[256,1408]{1,0:T(8,128)(2,1)S(1)}, u32[]{:S(2)}, u32[]{:S(2)}) %collective-permute-start) | collective-permute-done | bytes 720928 | tf_op jit(solution)/shard_map/ppermute | solution.py:1479
  490.0 8.4 %fusion.60 = (bf16[1024,2048]{1,0:T(8,128)(2,1)}, bf16[2048]{0:T(1024)(128)(2,1)S(1)}) fusion(f32[1024]{0:T(1024)S(1)} %add_rsqrt_fusion, bf16[1024,2048]{1,0:T(8,128)(2,1)S(1)} %copy-done.19, bf16[2048,2176]{1,0:T(8,128)(2,1)S(1)} %bitcast.169, bf16[1024,3]{1,0:T(8,128)(2,1)S(1)} %copy.166, bf16[1024,1280]{1,0:T(8,128)(2,1)S(1)} %copy-done.39), kind=kOutput, calls=%fused_computation.128 | convolution fusion | flops 5924714496 | bytes 17047552 | tf_op jit(solution)/shard_map/dot_general | solution.py:965
  500.7 10.3 %convolution_convert_fusion.1 = bf16[2048,1280]{1,0:T(8,128)(2,1)} fusion(bf16[1024,1280]{1,0:T(8,128)(2,1)} %get-tuple-element.74, bf16[1024,2048]{1,0:T(8,128)(2,1)} %all-gather.5.cloned.1.call-done, f32[2048]{0:T(1024)S(1)} %bitcast.184, f32[1024]{0:T(1024)S(1)} %add_rsqrt_fusion), kind=kOutput, calls=%fused_computation.8 | convolution fusion | flops 5379719168 | bytes 12070912 | tf_op jit(solution)/shard_map/dot_general | solution.py:965
  511.0 96.6 %finish.1 = (f32[2,64,2176]{2,1,0:T(8,128)}, bf16[4,64,2816]{2,1,0:T(8,128)(2,1)}, bf16[4,64,1408]{2,1,0:T(8,128)(2,1)}, bf16[128,2048]{1,0:T(8,128)(2,1)}, f32[128,2048]{1,0:T(8,128)}, /*index=5*/f32[64,128]{1,0:T(8,128)}) custom-call(bf16[4,2,4,64,1280]{4,3,2,1,0:T(8,128)(2,1)} %bitcast.130, bf16[4,2,4,64,128]{4,3,2,1,0:T(8,128)(2,1)} %bitcast.144, ...), custom_call_target="tpu_custom_call" | custom-call | tf_op jit(solution)/shard_map/finish/pallas_call | solution.py:903
  607.6 1.1 slice.70
  608.6 1.2 fusion.61
  609.8 1.5 slice_reduce_fusion
  612.2 1.3 copy.169
  615.0 1.3 copy.177
  617.8 1.1 reshape.454
  619.4 1.1 reshape.456
  621.1 4.3 reshape.461
  625.4 1.2 convert_bitcast_fusion
  (207 shorter events, 25.1 us)
Async XLA Ops:
  7.2 5.0 copy-start.28
  7.2 5.4 copy-start.37
  7.2 5.4 copy-start.38
  7.2 5.4 copy-start.35
  7.2 5.4 copy-start.36
  7.2 5.6 copy-start.29
  7.2 115.1 %all-gather.7.cloned.1.call-start = ((), (), s32[]{:S(2)}) async-start(), calls=%async_computation.4 | async-start | bytes 2621440 | tf_op jit(solution)/shard_map/all_gather | solution.py:1390
  8.7 4.5 copy-start.30
  8.8 4.7 copy-start.20
  9.6 124.4 %all-gather.5.cloned.1.call-start = ((), (), s32[]{:S(2)}) async-start(), calls=%async_computation.3 | async-start | bytes 4718592 | tf_op jit(solution)/shard_map/all_gather | solution.py:1389
  11.0 4.3 copy-start.33
  11.0 4.3 copy-start.34
  12.1 215.7 %all-gather.9.cloned.1.call-start = ((), (), s32[]{:S(2)}) async-start(), calls=%async_computation.5 | async-start | bytes 7208960 | tf_op jit(solution)/shard_map/all_gather | solution.py:1402
  114.9 3.7 copy-start.31
  114.9 177.6 %all-gather.11.cloned.1.call-start = ((), (), s32[]{:S(2)}) async-start(), calls=%async_computation.6 | async-start | bytes 14417920 | tf_op jit(solution)/shard_map/all_gather | solution.py:1399
  119.3 9.3 %copy-start.24 = (pred[1280,512]{1,0:T(32,128)(4,1)}, pred[1280,512]{1,0:T(32,128)(4,1)S(1)}, u32[]{:S(2)}) copy-start(pred[1280,512]{1,0:T(32,128)(4,1)S(1)} %bitcast_compare_fusion) | copy-start | bytes 1966084
  121.6 29.1 %copy-start.3 = (f32[1024,128]{1,0:T(8,128)}, f32[1024,128]{1,0:T(8,128)S(1)}, u32[]{:S(2)}) copy-start(f32[1024,128]{1,0:T(8,128)S(1)} %get-tuple-element.163.cos_ref) | copy-start | bytes 1572868
  121.6 29.1 %copy-start.5 = (f32[1024,128]{1,0:T(8,128)}, f32[1024,128]{1,0:T(8,128)S(1)}, u32[]{:S(2)}) copy-start(f32[1024,128]{1,0:T(8,128)S(1)} %get-tuple-element.164.sin_ref) | copy-start | bytes 1572868
  122.3 52.8 %copy-start.15 = (f32[1,2048]{1,0:T(1,128)}, f32[1,2048]{1,0:T(1,128)S(1)}, u32[]{:S(2)}) copy-start(f32[1,2048]{1,0:T(1,128)S(1)} %get-tuple-element.157.gain_ref) | copy-start | bytes 24580
  128.6 99.2 %all-to-all-start = ((bf16[4,320,2048]{2,1,0:T(8,128)(2,1)}), bf16[4,320,2048]{2,1,0:T(8,128)(2,1)}, u32[]{:S(2)}, u32[]{:S(2)}) async-start(bf16[4,320,2048]{2,1,0:T(8,128)(2,1)} %bitcast.129), calls=%async_computation | async-start | bytes 10485760 | tf_op jit(solution)/shard_map/all_to_all | solution.py:1415
  133.7 336.6 %reduce-scatter.3.cloned.1.call-start = ((), (), s32[]{:S(2)}) async-start(), calls=%async_computation.7 | async-start | bytes 7208960 | tf_op jit(solution)/shard_map/reduce_scatter | solution.py:1457
  134.0 3.5 copy-start.18
  146.9 2.4 copy-start.16
  168.8 6.2 copy-start.11
  168.8 6.2 copy-start.13
  168.8 6.2 copy-start.1
  216.9 3.2 copy-start.9
  267.4 2.4 copy-start
  330.2 180.8 %reduce-scatter.5.cloned.1.call-start = ((), (), s32[]{:S(2)}) async-start(), calls=%async_computation.8 | async-start | bytes 14417920 | tf_op jit(solution)/shard_map/reduce_scatter | solution.py:1461
  384.2 2.4 copy-start.26
  386.8 2.8 copy-start.40
  438.6 8.7 %copy-start.4 = (f32[1024,128]{1,0:T(8,128)S(1)}, f32[1024,128]{1,0:T(8,128)}, u32[]{:S(2)}) copy-start(f32[1024,128]{1,0:T(8,128)} %copy-done.3) | copy-start | bytes 1572868
  438.6 8.7 %copy-start.6 = (f32[1024,128]{1,0:T(8,128)S(1)}, f32[1024,128]{1,0:T(8,128)}, u32[]{:S(2)}) copy-start(f32[1024,128]{1,0:T(8,128)} %copy-done.5) | copy-start | bytes 1572868
  438.6 8.7 %copy-start.8 = (f32[1024,3]{1,0:T(8,128)S(1)}, f32[1024,3]{1,0:T(8,128)}, u32[]{:S(2)}) copy-start(f32[1024,3]{1,0:T(8,128)} %copy.157.gate_ref) | copy-start | bytes 36868
  438.6 8.7 %copy-start.12 = (bf16[1024,256]{1,0:T(8,128)(2,1)S(1)}, bf16[1024,256]{1,0:T(8,128)(2,1)}, u32[]{:S(2)}) copy-start(bf16[1024,256]{1,0:T(8,128)(2,1)} %copy-done.11) | copy-start | bytes 1572868
  438.6 8.7 %copy-start.14 = (bf16[1024,256]{1,0:T(8,128)(2,1)S(1)}, bf16[1024,256]{1,0:T(8,128)(2,1)}, u32[]{:S(2)}) copy-start(bf16[1024,256]{1,0:T(8,128)(2,1)} %copy-done.13) | copy-start | bytes 1572868
  463.4 3.6 copy-start.32
  463.4 3.6 copy-start.41
  470.3 19.7 %slice-start = ((s8[8912896]{0:T(1024)(128)(4,1)}), s8[4194304]{0:T(1024)(128)(4,1)S(1)}, s32[]{:S(2)}) async-start(s8[8912896]{0:T(1024)(128)(4,1)} %bitcast.167), calls=%async_computation.9 | async-start | bytes 8388608
  471.6 18.3 %copy-start.19 = (bf16[1024,2048]{1,0:T(8,128)(2,1)S(1)}, bf16[1024,2048]{1,0:T(8,128)(2,1)}, u32[]{:S(2)}) copy-start(bf16[1024,2048]{1,0:T(8,128)(2,1)} %all-gather.5.cloned.1.call-done) | copy-start | bytes 12582916
  471.6 18.3 %slice-start.1 = ((s8[8912896]{0:T(1024)(128)(4,1)}), s8[4194304]{0:T(1024)(128)(4,1)S(1)}, s32[]{:S(2)}) async-start(s8[8912896]{0:T(1024)(128)(4,1)} %bitcast.167), calls=%async_computation.10 | async-start | bytes 8388608
  471.6 18.3 %slice-start.2 = ((s8[8912896]{0:T(1024)(128)(4,1)}), s8[524288]{0:T(1024)(128)(4,1)S(1)}, s32[]{:S(2)}) async-start(s8[8912896]{0:T(1024)(128)(4,1)} %bitcast.167), calls=%async_computation.11 | async-start | bytes 1048576
  471.6 18.3 %copy-start.39 = (bf16[1024,1280]{1,0:T(8,128)(2,1)S(1)}, bf16[1024,1280]{1,0:T(8,128)(2,1)}, u32[]{:S(2)}) copy-start(bf16[1024,1280]{1,0:T(8,128)(2,1)} %get-tuple-element.74) | copy-start | bytes 7864324
  471.6 18.3 %collective-permute-start = (bf16[256,1408]{1,0:T(8,128)(2,1)S(1)}, bf16[256,1408]{1,0:T(8,128)(2,1)S(1)}, u32[]{:S(2)}, u32[]{:S(2)}) collective-permute-start(bf16[256,1408]{1,0:T(8,128)(2,1)S(1)} %dynamic-slice_bitcast_fusion), channel_id=1, source_target_pairs={{0,16},{16,0},{1,17},{17,1},{2,18},{18,2},{3,19},{19,3},{4,20},{20... | collective-permute-start | bytes 2162696 | tf_op jit(solution)/shard_map/ppermute | solution.py:1479
  490.0 9.7 %copy-start.21 = (bf16[512,1408]{1,0:T(8,128)(2,1)S(1)}, bf16[512,1408]{1,0:T(8,128)(2,1)}, u32[]{:S(2)}) copy-start(bf16[512,1408]{1,0:T(8,128)(2,1)} %reduce-scatter.3.cloned.1.call-done) | copy-start | bytes 4325380
  607.6 7.0 %copy-start.22 = (f32[128,2048]{1,0:T(8,128)S(1)}, f32[128,2048]{1,0:T(8,128)}, u32[]{:S(2)}) copy-start(f32[128,2048]{1,0:T(8,128)} %get-tuple-element.82) | copy-start | bytes 3145732
  615.0 5.4 copy-start.25
  617.5 8.0 %copy-start.23 = (bf16[4,64,1408]{2,1,0:T(8,128)(2,1)S(1)}, bf16[4,64,1408]{2,1,0:T(8,128)(2,1)}, u32[]{:S(2)}) copy-start(bf16[4,64,1408]{2,1,0:T(8,128)(2,1)} %get-tuple-element.86) | copy-start | bytes 2162692
  (5 other events, 6.6 us)
Sparse Core Ops, SparseCore 0:
  9.8 41.7 all-gather.6
  53.7 65.0 all-gather.4
  120.5 60.1 all-gather.8
  182.2 110.2 all-gather.10
  330.3 60.8 reduce-scatter.2
  393.5 105.7 reduce-scatter.4

commit v10 on v8

--- a/solution.py
+++ b/solution.py
@@ -484,27 +484,55 @@
 
 def back_body(
     part_ref, middle_ref, grad_ref, gain_ref, hidden_ref, down_ref, dmiddle_ref, dgain_ref, spread_ref, branch_out,
-    hidden, down, branch, loc, out_sem, *scratch,
+    hidden, down, branch, branch_buf, branch_sum, loc, cs, cr, ys, yr, *scratch,
 ):
     sends = Sends()
+    y, core = lax.axis_index("y"), lax.axis_index("core")
     loads = []
     for n, (src, dst) in enumerate(((hidden_ref, hidden), (down_ref, down))):
         loads.append(pltpu.make_async_copy(src, dst, loc.at[n]))
         loads[-1].start()
-    greet(*along_x())
+    greet(*along_x(), *(neighbour("y", step) for step in (1, 2, 3)))
     stages = reduce_stages(CHUNKS, [part_ref], *scratch[:7], sends)
     next(stages)
+    slots = branch_out.shape[1]
+    mine = pl.ds(pl.multiple_of(core * slots, slots), slots)
+    theirs = pl.ds(pl.multiple_of((1 - core) * slots, slots), slots)
+
+    def output(step):
+        target = mod4(y + step)
+        branch[step] = dot(hidden[target], down[...], ((1,), (1,))).astype(BF16)
+        sends(
+            branch.at[step, theirs], branch_buf.at[step], cs.at[step], cr.at[step], neighbour("core", 1)
+        )
+
+    def pass_on(step):
+        arrived(branch_buf.at[step], cr.at[step])
+        value = (branch[step, mine, :].astype(F32) + branch_buf[step].astype(F32)).astype(BF16)
+        if step == 0:
+            branch_out[y] = value
+        else:
+            branch_sum[step - 1] = value
+            sends(
+                branch_sum.at[step - 1],
+                branch_out.at[y],
+                ys.at[step - 1],
+                yr.at[step - 1],
+                neighbour("y", step),
+            )
+
     next(stages)
     for load in loads:
         load.wait()
-    slots = branch.shape[1]
-    outs = []
-    for n in range(4):
-        branch[n] = dot(hidden[n * slots : (n + 1) * slots, :], down[...], ((1,), (1,))).astype(BF16)
-        outs.append(pltpu.make_async_copy(branch.at[n], branch_out.at[n], out_sem.at[n]))
-        outs[-1].start()
+    output(2)
+    output(1)
+    pass_on(2)
+    output(3)
+    pass_on(1)
+    output(0)
+    pass_on(3)
     total = next(stages)
-    xl, xh, core = lax.axis_index("xl"), lax.axis_index("xh"), lax.axis_index("core")
+    xl, xh = lax.axis_index("xl"), lax.axis_index("xh")
     step = middle_ref.shape[0] // CHUNKS
     for n in range(CHUNKS):
         rows = slice(n * step, (n + 1) * step)
@@ -524,9 +552,10 @@
         spread_ref[xl, xh, core, rows, :] = dmiddle.astype(BF16)
         if n % 2 == 1:
             ring_spread(spread_ref, n // 2, *scratch[7:], sends)
+    pass_on(0)
     ring_spread_finish(spread_ref, *scratch[7:], sends)
-    for out in outs:
-        out.wait()
+    for step in (1, 3, 2):
+        arrived(branch_out.at[mod4(y - step)], yr.at[step - 1])
     sends.finish()
 
 
@@ -542,24 +571,29 @@
             jax.ShapeDtypeStruct((rows, width), F32),
             jax.ShapeDtypeStruct((1, width), F32),
             jax.ShapeDtypeStruct((2, 2, 2, rows, width), BF16),
-            jax.ShapeDtypeStruct((4, slots, width), BF16),
+            jax.ShapeDtypeStruct((4, slots // 2, width), BF16),
         ],
         in_specs=vmem(4) + [anywhere] * 2,
-        out_specs=vmem(3) + [anywhere],
+        out_specs=vmem(4),
         scratch_shapes=[
-            pltpu.VMEM((count, inner), BF16),
+            pltpu.VMEM((4, slots, inner), BF16),
             pltpu.VMEM(down.shape, BF16),
             pltpu.VMEM((4, slots, width), BF16),
+            pltpu.VMEM((4, slots // 2, width), BF16),
+            pltpu.VMEM((3, slots // 2, width), BF16),
             dma((2,)),
             dma((4,)),
+            dma((4,)),
+            dma((3,)),
+            dma((3,)),
         ]
         + reduce_scratch(1, rows, width)
         + ring_spread_scratch(),
         compiler_params=pltpu.CompilerParams(
-            collective_id=2, has_side_effects=True, vmem_limit_bytes=48 * MIB
+            collective_id=2, has_side_effects=True, vmem_limit_bytes=56 * MIB
         ),
         name="middle_back",
-    )(part.reshape(4, rows, width), middle, grad, gain[None], hidden, down)
+    )(part.reshape(4, rows, width), middle, grad, gain[None], hidden.reshape(4, slots, inner), down)
     return dmiddle, dgain[0], spread.reshape(8 * rows, width), branch
 
 
@@ -600,7 +634,9 @@
         in_specs=[pl.BlockSpec(memory_space=pl.ANY)],
         out_specs=pl.BlockSpec(memory_space=pl.ANY),
         scratch_shapes=[dma, dma((3,)), dma((3,)), dma((3,)), dma((3,))],
-        compiler_params=pltpu.CompilerParams(collective_id=4, has_side_effects=True),
+        compiler_params=pltpu.CompilerParams(
+            collective_id=4, has_side_effects=True, vmem_limit_bytes=40 * MIB
+        ),
         name="rows_to_experts",
     )(rows)
 
@@ -1354,10 +1390,8 @@
     up_whole = lax.all_gather(
         up_parts.reshape(2 * mlp_count * share, -1), "z", axis=0, tiled=True
     )
-    up_parts, down_parts = lax.optimization_barrier((up_parts, down_parts))
-    down_whole = lax.all_gather(
-        down_parts.reshape(mlp_count * share, -1), ("z", "xl"), axis=0, tiled=True
-    )
+    xl = lax.axis_index("xl")
+    down_theirs = lax.ppermute(down_parts, "xl", ((0, 1), (1, 0)))
 
     tokens = segments.shape[0]
     match = jnp.sum((mlp_routes[:, :, None] == jnp.arange(mlp_count, dtype=jnp.int32)).astype(BF16), 1)
@@ -1388,6 +1422,13 @@
     )
     key_rot, val_rows, queries, mixed, gmixed, prob = attention_forward(
         joined_att, cosine, sine, segments, gate_att
+    )
+    down_theirs, gmixed = lax.optimization_barrier((down_theirs, gmixed))
+    down_pair = jnp.where(
+        xl == 0, jnp.stack([down_parts, down_theirs]), jnp.stack([down_theirs, down_parts])
+    )
+    down_whole = lax.all_gather(
+        down_pair.reshape(2 * mlp_count * share, -1), "z", axis=0, tiled=True
     )
     out_weights = weights[:, out_at:]
     attention = dot(gmixed, out_weights, ((1,), (1,))).astype(BF16)
@@ -1416,30 +1457,32 @@
         dgate_pre, dlinear, up_whole, dgate_part.reshape(mlp_count, CAP, LANES), rows_ext
     )
     grad_up_sum = lax.psum_scatter(grad_up_whole, "z", scatter_dimension=0, tiled=True)
-    halves = grad_down_sum.reshape(2, mlp_count * share, hidden_local)
-    xl = lax.axis_index("xl")
-    theirs = lax.ppermute(
-        lax.dynamic_index_in_dim(halves, 1 - xl, 0, keepdims=False), "xl", ((0, 1), (1, 0))
-    )
-    grad_down_sum = (
-        lax.dynamic_index_in_dim(halves, xl, 0, keepdims=False).astype(F32) + theirs.astype(F32)
-    ).astype(BF16)
     pick_half = lax.dynamic_slice_in_dim(pick, lax.axis_index("core") * (CAP // 2), CAP // 2, 1)
     dgate_two = jnp.sum(pick_half.astype(F32) * jnp.sum(dgate_back, -1, keepdims=True), 1).T
     dlogit_mlp = router_back(dgate_two, weights_mlp, onehot_mlp)
     dunit_two = dot(
         pick_half.reshape(-1, tokens), dunit_back.reshape(-1, width), ((0,), (0,))
     ) + dot(dlogit_mlp, router_two, ((1,), (1,)))
-    grad_rmlp = dot(unit_two, dlogit_mlp, ((0,), (0,)))
-    dmiddle, grad_gain_two, dattention, branch_part = middle_back(
+    dmiddle, grad_gain_two, dattention, branch_back = middle_back(
         dunit_two.astype(BF16), middle, out_grad, gain_two, hidden, down_whole
     )
-    branch_back = lax.all_to_all(branch_part, "y", 0, 0, tiled=True)
-
+
+    grad_down_sum, dattention = lax.optimization_barrier((grad_down_sum, dattention))
     raw = dot(dattention, out_weights, ((1,), (0,)))
     grad_qkv, dgate_one = attention_back(
         key_rot, val_rows, queries, mixed, raw, prob, cosine, sine, gate_att
     )
+    halves = grad_down_sum.reshape(2, mlp_count * share, hidden_local)
+    theirs = lax.ppermute(
+        lax.dynamic_index_in_dim(halves, 1 - xl, 0, keepdims=False), "xl", ((0, 1), (1, 0))
+    )
+    theirs, grad_qkv, gmixed, dattention, branch_back, dlogit_mlp = lax.optimization_barrier(
+        (theirs, grad_qkv, gmixed, dattention, branch_back, dlogit_mlp)
+    )
+    grad_rmlp = dot(unit_two, dlogit_mlp, ((0,), (0,)))
+    grad_down_sum = (
+        lax.dynamic_index_in_dim(halves, xl, 0, keepdims=False).astype(F32) + theirs.astype(F32)
+    ).astype(BF16)
     dlogit_att = router_back(dgate_one[:, :att_count], weights_att, onehot_att)
     grad_joined = jnp.concatenate([grad_qkv, pad_to(dlogit_att, 128)], 1)
     dunit_one = dot(grad_joined, weights[:, :out_at], ((1,), (1,)))
@@ -1453,9 +1496,9 @@
         ],
         1,
     )
-    gate_slots = jnp.sum(pick.astype(F32) * gate_mlp.T[:, None, :], -1, keepdims=True)
+    gate_slots = jnp.sum(pick_half.astype(F32) * gate_mlp.T[:, None, :], -1, keepdims=True)
     feed = dot(
-        pick_rows,
+        pick_half.reshape(-1, tokens),
         (branch_back.astype(F32) * gate_slots).astype(BF16).reshape(-1, width),
         ((0,), (0,)),
     )

time: 692 us -> 616 us (0.89)
  waiting for transfers between devices: 68.7 us -> 2.52 us
  Pallas kernels: 429 us -> 420 us
    all_gather x1, waiting for transfers between devices: 58.8 us -> 2.36 us  [on_device(): lax.all_gather(down_pair.reshape(2 * mlp_count * share, -1), 'z', axis=0,...]
    pallas_call x1, Pallas kernels: 46.5 us -> 39.2 us  [rows_to_experts(): pl.pallas_call(rows_body, out_shape=jax.ShapeDtypeStruct(rows.shape, rows...]
    unnamed x108 -> x110, local copies, waits for them, and re-layouts: 18.9 us -> 23.1 us
  transfers between devices with their start and end apart: 9 -> 9, of which waited for: 3 -> 1; matrix products, arithmetic and copies ran while one was open for 16% -> 18% of each run, Pallas kernels for 46% -> 50%
where the time goes in v10:
time: 616 us; the launch traced here: 608 us
  Pallas kernels  420 us (68%)
  matrix products  89.8 us (15%)
  local copies, waits for them, and re-layouts  55.5 us (9%)
  other arithmetic  16.9 us (3%)
  between operations  15.5 us (3%)
  starting transfers between devices  7.47 us (1%)
    pallas_call x1, Pallas kernels, finish(): pl.pallas_call(finish_body, out_shape=[jax.ShapeDtypeStruct((2, share, co...  94 us
    dot_general x16, matrix products, dot(): return lax.dot_general(a, b, (dims, ((), ())), preferred_element_type=F32)  89.8 us
    pallas_call x1, Pallas kernels, gather_dp(): pl.pallas_call(gather_body, out_shape=[jax.ShapeDtypeStruct((4, 2, 4, row...  76.1 us
    pallas_call x1, Pallas kernels, return_rows(): pl.pallas_call(return_body, out_shape=[jax.ShapeDtypeStruct((4, half, wid...  53.9 us
    pallas_call x1, Pallas kernels, middle_back(): pl.pallas_call(back_body, out_shape=[jax.ShapeDtypeStruct((rows, width),...  45.7 us
    pallas_call x1, Pallas kernels, middle_and_unit(): pl.pallas_call(middle_body, out_shape=[jax.ShapeDtypeStruct((rows, width)...  42.5 us
    pallas_call x1, Pallas kernels, rows_to_experts(): pl.pallas_call(rows_body, out_shape=jax.ShapeDtypeStruct(rows.shape, rows...  39.2 us
    unnamed x110, local copies, waits for them, and re-layouts  23.1 us
  transfers between devices with their start and end apart: 9, of which 1 were waited for; matrix products, arithmetic and copies ran while one was open for 18% of the time, Pallas kernels for 50%

profile of v10, /device:TPU:1, one launch (start us, length us, event | category | flops | bytes accessed | tf_op | source)
XLA Modules:
  0.0 608.1 jit_solution(13304847851128166384)
XLA Ops:
  7.2 1.4 copy.145
  9.9 1.3 copy.154
  13.4 1.8 reshape.425.ups_ref
  17.0 76.1 %gather_weights.1 = (bf16[4,2,4,64,2176]{4,3,2,1,0:T(8,128)(2,1)}, bf16[2,4,64,2816]{3,2,1,0:T(8,128)(2,1)}, bf16[4,64,1408]{2,1,0:T(8,128)(2,1)}, bf16[2,512,128]{2,1,0:T(8,128)(2,1)}) custom-call(bf16[2,64,2176]{2,1,0:T(8,128)(2,1)} %pad_maximum_fusion.x_ref, bf16[4,64,2816]{2,1,0:T(8,128)(2,1)} %reshape.425.ups_ref, bf16[4,64,1408]{2,1,0:T(8,128)(2,1)} %bitcast.159, ...), custom_call_target="tpu_custom_call" | custom-call | tf_op jit(solution)/shard_map/gather_weights/pallas_call | solution.py:192
  93.2 1.3 collective-permute-start
  98.0 1.9 fusion.38
  100.3 3.5 fusion.4
  104.1 9.6 %fusion.8.k_ref.v_ref.q0.q1.q2 = f32[1024,1408]{1,0:T(8,128)S(1)} fusion(bf16[2048,2176]{1,0:T(8,128)(2,1)} %bitcast.165, bf16[1024,2048]{1,0:T(8,128)(2,1)S(1)} %copy-done.20, f32[2048]{0:T(1024)S(1)} %bitcast.183, f32[1024]{0:T(1024)S(1)} %add_rsqrt_fusion), kind=kOutput, calls=%fused_computation.16 | convolution fusion | flops 5913968640 | bytes 15740928 | tf_op jit(solution)/shard_map/dot_general | solution.py:930
  113.7 2.6 copy-done.18
  117.8 1.1 copy-done.9
  120.0 15.7 %attention_forward.1 = (bf16[1024,256]{1,0:T(8,128)(2,1)S(1)}, bf16[1024,256]{1,0:T(8,128)(2,1)S(1)}, bf16[1024,768]{1,0:T(8,128)(2,1)S(1)}, bf16[1024,768]{1,0:...) custom-call(f32[1024,1408]{1,0:T(8,128)} %copy-done.18, f32[1024,1408]{1,0:T(8,128)} %copy-done.18, ...), custom_call_target="tpu_custom_call" | custom-call | tf_op jit(solution)/shard_map/attention_forward/pallas_call | solution.py:1211
  137.3 2.8 maximum_select_fusion
  140.9 6.3 %convolution_convert_fusion.3 = bf16[1280,2048]{1,0:T(8,128)(2,1)} fusion(pred[1280,512]{1,0:T(32,128)(4,1)S(1)} %bitcast_compare_fusion, bf16[512,2048]{0,1:T(8,128)(2,1)} %all-gather.7.cloned.1.call-done), kind=kOutput, calls=%fused_computation.10 | convolution fusion | flops 2686976000 | bytes 7995392 | tf_op jit(solution)/shard_map/dot_general | solution.py:930
  147.2 5.2 all-to-all-start
  153.5 1.5 slice_bitcast_fusion.1
  155.0 6.0 convolution_convert_fusion.4
  161.0 42.5 %middle_and_unit.1 = (f32[128,2048]{1,0:T(8,128)S(1)}, bf16[4,128,2048]{2,1,0:T(8,128)(2,1)S(1)}) custom-call(bf16[2,2,2,128,2048]{4,3,2,1,0:T(8,128)(2,1)S(1)} %bitcast.129, bf16[128,2048]{1,0:T(8,128)(2,1)S(1)} %copy-done.2, f32[1,2048]{1,0:T(1,128)S(1)} %get-tuple-element.173.gain_ref), custom_call_target="tpu_custom_call" | custom-call | tf_op jit(solution)/shard_map/middle_and_unit/pallas_call | solution.py:468
  203.6 1.5 copy-done.3
  205.0 1.9 fusion.34
  207.2 5.5 convolution_convert_fusion
  212.7 39.2 %rows_to_experts.1 = bf16[4,320,2176]{2,1,0:T(8,128)(2,1)S(1)} custom-call(bf16[4,320,2176]{2,1,0:T(8,128)(2,1)S(1)} %bitcast.128), custom_call_target="tpu_custom_call" | custom-call | tf_op jit(solution)/shard_map/rows_to_experts/pallas_call | solution.py:631
  252.2 2.4 copy-done
  255.6 2.6 copy-done.1
  258.2 20.3 %joined_rows.1 = (f32[1280,1408]{1,0:T(8,128)}, f32[1280,1408]{1,0:T(8,128)}) custom-call(bf16[1280,2176]{1,0:T(8,128)(2,1)S(1)} %bitcast.124, bf16[2048,2816]{1,0:T(8,128)(2,1)} %all-gather.11.cloned.1.call-done.gate_up_ref.linear_up_ref.up_ref, bf16[2048,2816]{1,0:T(8,128)(2,1)} %all-gather.11.cloned.1.call-done.gate_up_ref.linear_up_ref.up_ref), custom_call_target="tpu_custom_call" | custom-call | tf_op jit(solution)/shard_map/joined_rows/pallas_call | solution.py:944
  278.5 2.4 all-gather.9.cloned.1.call-done.down_ref
  280.9 19.4 %experts.1 = (bf16[1280,1408]{1,0:T(8,128)(2,1)}, bf16[1280,1408]{1,0:T(8,128)(2,1)}, bf16[1280,1408]{1,0:T(8,128)(2,1)}, bf16[1280,1408]{1,0:T(8,128)(2,1)}, f32[1280,128]{1,0:T(8,128)}) custom-call(bf16[1280,2048]{1,0:T(8,128)(2,1)} %bitcast.17.grad_ref, bf16[2048,1408]{1,0:T(8,128)(2,1)} %all-gather.9.cloned.1.call-done.down_ref, ...), custom_call_target="tpu_custom_call" | custom-call | tf_op jit(solution)/shard_map/experts/pallas_call | solution.py:989
  300.3 13.1 %convolution_convert_fusion.2 = bf16[2048,1408]{1,0:T(8,128)(2,1)} fusion(bf16[1280,2048]{1,0:T(8,128)(2,1)} %bitcast.17.grad_ref, bf16[1280,1408]{1,0:T(8,128)(2,1)} %get-tuple-element.68), kind=kOutput, calls=%fused_computation.9 | convolution fusion | flops 7384858624 | bytes 14614528 | tf_op jit(solution)/shard_map/dot_general | solution.py:930
  313.6 53.9 %return_rows.1 = (bf16[4,160,2048]{2,1,0:T(8,128)(2,1)}, f32[4,160,128]{2,1,0:T(8,128)}, bf16[2048,2816]{1,0:T(8,128)(2,1)}) custom-call(bf16[1280,1408]{1,0:T(8,128)(2,1)} %get-tuple-element.70.dgate_pre_ref, bf16[1280,1408]{1,0:T(8,128)(2,1)} %get-tuple-element.71.dlinear_ref, ...), custom_call_target="tpu_custom_call" | custom-call | tf_op jit(solution)/shard_map/return_rows/pallas_call | solution.py:1118
  370.6 2.2 fusion.32
  372.8 3.3 fusion.11
  376.1 45.7 %middle_back.1 = (f32[128,2048]{1,0:T(8,128)}, f32[1,2048]{1,0:T(1,128)}, bf16[2,2,2,128,2048]{4,3,2,1,0:T(8,128)(2,1)}, bf16[4,160,2048]{2,1,0:T(8,128)(2,1)}) custom-call(bf16[4,128,2048]{2,1,0:T(8,128)(2,1)} %bitcast.153, f32[128,2048]{1,0:T(8,128)} %copy-done.11, bf16[128,2048]{1,0:T(8,128)(2,1)} %copy.163.grad_ref, f32[1,2048]{1,0:T(1,128)} %copy-done.17, ...), custom_call_target="tpu_custom_call" | custom-call | tf_op jit(solution)/shard_map/middle_back/pallas_call | solution.py:568
  422.5 2.0 dynamic-slice_bitcast_fusion
  425.1 8.7 %fusion.17.h0.h1.h2 = f32[1024,768]{1,0:T(8,128)} fusion(bf16[1024,2048]{1,0:T(8,128)(2,1)} %bitcast.188, bf16[2048,2176]{1,0:T(8,128)(2,1)} %bitcast.169), kind=kOutput, calls=%fused_computation.29 | convolution fusion | flops 3221225472 | bytes 10485760 | tf_op jit(solution)/shard_map/dot_general | solution.py:930
  433.9 13.7 %attention_back.1 = (bf16[1024,1280]{1,0:T(8,128)(2,1)}, f32[1024,128]{1,0:T(8,128)S(1)}) custom-call(bf16[1024,256]{1,0:T(8,128)(2,1)S(1)} %copy-done.14, bf16[1024,256]{1,0:T(8,128)(2,1)S(1)} %copy-done.16, bf16[1024,768]{1,0:T(8,128)(2,1)S(1)} %get-tuple-element.81.q0.q1.q2, bf16[1024,768]{1,0:T(8,128)(2,1)S(1)} %get-tuple-element.81.q0.q1.q2, ...), custom_call_target="tpu_custom_call" | custom-call | tf_op jit(solution)/shard_map/attention_back/pallas_call | solution.py:1287
  448.1 3.5 convolution_convert_fusion.7
  452.5 11.2 %fusion.58 = (bf16[1024,2048]{1,0:T(8,128)(2,1)}, bf16[2048]{0:T(1024)(128)(2,1)S(1)}) fusion(f32[1024]{0:T(1024)S(1)} %add_rsqrt_fusion, bf16[1024,2048]{1,0:T(8,128)(2,1)S(1)} %copy-done.21, bf16[2048,2176]{1,0:T(8,128)(2,1)} %bitcast.170, bf16[1024,3]{1,0:T(8,128)(2,1)S(1)} %copy.166, bf16[1024,1280]{1,0:T(8,128)(2,1)S(1)} %copy-done.44), kind=kOutput, calls=%fused_computation.127 | convolution fusion | flops 5924714496 | bytes 16791552 | tf_op jit(solution)/shard_map/dot_general | solution.py:930
  465.4 2.1 fusion.27
  467.5 5.2 bitcast_convert_fusion
  472.7 5.0 convolution_convert_fusion.5
  477.7 8.0 %convolution_convert_fusion.1 = bf16[2048,1280]{1,0:T(8,128)(2,1)} fusion(bf16[1024,1280]{1,0:T(8,128)(2,1)S(1)} %copy-done.45, bf16[1024,2048]{1,0:T(8,128)(2,1)S(1)} %copy-done.22, f32[2048]{0:T(1024)S(1)} %bitcast.185, f32[1024]{0:T(1024)S(1)} %add_rsqrt_fusion), kind=kOutput, calls=%fused_computation.8 | convolution fusion | flops 5379719168 | bytes 12070912 | tf_op jit(solution)/shard_map/dot_general | solution.py:930
  485.6 94.0 %finish.1 = (f32[2,64,2176]{2,1,0:T(8,128)}, bf16[4,64,2816]{2,1,0:T(8,128)(2,1)}, bf16[4,64,1408]{2,1,0:T(8,128)(2,1)}, bf16[128,2048]{1,0:T(8,128)(2,1)}, f32[128,2048]{1,0:T(8,128)}, /*index=5*/f32[64,128]{1,0:T(8,128)}) custom-call(bf16[4,2,4,64,1280]{4,3,2,1,0:T(8,128)(2,1)} %bitcast.133, bf16[4,2,4,64,128]{4,3,2,1,0:T(8,128)(2,1)} %bitcast.147, ...), custom_call_target="tpu_custom_call" | custom-call | tf_op jit(solution)/shard_map/finish/pallas_call | solution.py:868
  579.7 1.2 fusion.59
  582.7 1.5 slice_reduce_fusion
  584.2 1.5 copy.171
  585.9 1.3 copy.177
  587.2 4.6 reshape.462
  595.0 1.3 copy.169
  597.3 1.2 convert_bitcast_fusion
  (214 shorter events, 33.0 us)
Async XLA Ops:
  7.2 4.9 copy-start.32
  7.2 5.4 copy-start.33
  7.2 93.1 %all-gather.5.cloned.1.call-start = ((), (), s32[]{:S(2)}) async-start(), calls=%async_computation.3 | async-start | bytes 4718592 | tf_op jit(solution)/shard_map/all_gather | solution.py:1380
  8.7 4.4 copy-start.34
  8.7 4.6 copy-start.38
  8.7 4.6 copy-start.39
  8.7 4.6 copy-start.40
  8.7 4.6 copy-start.41
  8.7 4.7 copy-start.25
  9.8 5.4 copy-start.37
  9.8 5.4 copy-start.36
  9.8 131.1 %all-gather.7.cloned.1.call-start = ((), (), s32[]{:S(2)}) async-start(), calls=%async_computation.4 | async-start | bytes 2621440 | tf_op jit(solution)/shard_map/all_gather | solution.py:1381
  12.1 243.6 %all-gather.11.cloned.1.call-start = ((), (), s32[]{:S(2)}) async-start(), calls=%async_computation.6 | async-start | bytes 14417920 | tf_op jit(solution)/shard_map/all_gather | solution.py:1390
  93.1 2.7 copy-start.31
  93.1 187.7 %all-gather.9.cloned.1.call-start = ((), (), s32[]{:S(2)}) async-start(), calls=%async_computation.5 | async-start | bytes 7208960 | tf_op jit(solution)/shard_map/all_gather | solution.py:1430
  93.2 44.1 %collective-permute-start = (bf16[4,64,1408]{2,1,0:T(8,128)(2,1)}, bf16[4,64,1408]{2,1,0:T(8,128)(2,1)}, u32[]{:S(2)}, u32[]{:S(2)}) collective-permute-start(bf16[4,64,1408]{2,1,0:T(8,128)(2,1)} %get-tuple-element.58), channel_id=1, source_target_pairs={{0,16},{16,0},{1,17},{17,1},{2,18},{18,2},{3,19},{19,3},{4,20},{20... | collective-permute-start | bytes 2162696 | tf_op jit(solution)/shard_map/ppermute | solution.py:1394
  100.3 17.5 %copy-start.5 = (f32[1024,128]{1,0:T(8,128)}, f32[1024,128]{1,0:T(8,128)S(1)}, u32[]{:S(2)}) copy-start(f32[1024,128]{1,0:T(8,128)S(1)} %get-tuple-element.179.cos_ref) | copy-start | bytes 1572868
  100.3 17.5 %copy-start.7 = (f32[1024,128]{1,0:T(8,128)}, f32[1024,128]{1,0:T(8,128)S(1)}, u32[]{:S(2)}) copy-start(f32[1024,128]{1,0:T(8,128)S(1)} %get-tuple-element.180.sin_ref) | copy-start | bytes 1572868
  100.3 3.8 copy-start.20
  113.7 2.6 copy-start.18
  120.0 17.3 %copy-start.28 = (bf16[4,64,1408]{2,1,0:T(8,128)(2,1)S(1)}, bf16[4,64,1408]{2,1,0:T(8,128)(2,1)}, u32[]{:S(2)}) copy-start(bf16[4,64,1408]{2,1,0:T(8,128)(2,1)} %get-tuple-element.58) | copy-start | bytes 2162692
  137.3 2.9 copy-start.35
  147.2 5.3 copy-start.24
  147.2 131.3 %all-to-all-start = ((bf16[4,320,2048]{2,1,0:T(8,128)(2,1)}), bf16[4,320,2048]{2,1,0:T(8,128)(2,1)}, u32[]{:S(2)}, u32[]{:S(2)}) async-start(bf16[4,320,2048]{2,1,0:T(8,128)(2,1)} %bitcast.132), calls=%async_computation | async-start | bytes 10485760 | tf_op jit(solution)/shard_map/all_to_all | solution.py:1405
  152.4 270.1 %reduce-scatter.3.cloned.1.call-start = ((), (), s32[]{:S(2)}) async-start(), calls=%async_computation.7 | async-start | bytes 7208960 | tf_op jit(solution)/shard_map/reduce_scatter | solution.py:1455
  155.0 6.0 copy-start.17
  155.0 6.0 copy-start.2
  203.5 3.3 copy-start.11
  252.2 2.4 copy-start
  255.6 2.6 copy-start.1
  313.4 172.3 %reduce-scatter.5.cloned.1.call-start = ((), (), s32[]{:S(2)}) async-start(), calls=%async_computation.8 | async-start | bytes 14417920 | tf_op jit(solution)/shard_map/reduce_scatter | solution.py:1459
  367.5 2.4 copy-start.30
  370.1 2.7 copy-start.43
  424.6 9.3 %copy-start.6 = (f32[1024,128]{1,0:T(8,128)S(1)}, f32[1024,128]{1,0:T(8,128)}, u32[]{:S(2)}) copy-start(f32[1024,128]{1,0:T(8,128)} %copy-done.5) | copy-start | bytes 1572868
  424.6 9.3 %copy-start.8 = (f32[1024,128]{1,0:T(8,128)S(1)}, f32[1024,128]{1,0:T(8,128)}, u32[]{:S(2)}) copy-start(f32[1024,128]{1,0:T(8,128)} %copy-done.7) | copy-start | bytes 1572868
  424.6 9.3 %copy-start.10 = (f32[1024,3]{1,0:T(8,128)S(1)}, f32[1024,3]{1,0:T(8,128)}, u32[]{:S(2)}) copy-start(f32[1024,3]{1,0:T(8,128)} %copy.159.gate_ref) | copy-start | bytes 36868
  424.6 9.3 %copy-start.14 = (bf16[1024,256]{1,0:T(8,128)(2,1)S(1)}, bf16[1024,256]{1,0:T(8,128)(2,1)}, u32[]{:S(2)}) copy-start(bf16[1024,256]{1,0:T(8,128)(2,1)} %copy-done.13) | copy-start | bytes 1572868
  424.6 9.3 %copy-start.16 = (bf16[1024,256]{1,0:T(8,128)(2,1)S(1)}, bf16[1024,256]{1,0:T(8,128)(2,1)}, u32[]{:S(2)}) copy-start(bf16[1024,256]{1,0:T(8,128)(2,1)} %copy-done.15) | copy-start | bytes 1572868
  424.6 27.0 %collective-permute-start.1 = (bf16[256,1408]{1,0:T(8,128)(2,1)}, bf16[256,1408]{1,0:T(8,128)(2,1)}, u32[]{:S(2)}, u32[]{:S(2)}) collective-permute-start(bf16[256,1408]{1,0:T(8,128)(2,1)} %dynamic-slice_bitcast_fusion), channel_id=1, source_target_pairs={{0,16},{16,0},{1,17},{17,1},{2,18},{18,2},{3,19},{19,3},{4,20},{20... | collective-permute-start | bytes 2162696 | tf_op jit(solution)/shard_map/ppermute | solution.py:1476
  448.1 3.5 copy-start.21
  448.1 4.4 copy-start.44
  452.5 11.2 %copy-start.4 = (bf16[4,128,2048]{2,1,0:T(8,128)(2,1)S(1)}, bf16[4,128,2048]{2,1,0:T(8,128)(2,1)}, u32[]{:S(2)}) copy-start(bf16[4,128,2048]{2,1,0:T(8,128)(2,1)} %copy-done.3) | copy-start | bytes 6291460
  467.5 5.2 copy-start.42
  467.5 5.2 copy-start.46
  472.7 5.0 copy-start.22
  472.7 5.0 copy-start.45
  591.8 5.6 copy-start.27
  593.6 6.5 %copy-start.29 = (f32[64,128]{1,0:T(8,128)S(1)}, f32[64,128]{1,0:T(8,128)}, u32[]{:S(2)}) copy-start(f32[64,128]{1,0:T(8,128)} %get-tuple-element.100) | copy-start | bytes 98308
  (8 other events, 8.8 us)
Sparse Core Ops, SparseCore 0:
  10.2 58.2 all-gather.4
  70.2 35.2 all-gather.6
  107.1 109.0 all-gather.10
  218.3 62.4 all-gather.8
  313.5 60.3 reduce-scatter.2
  376.2 105.7 reduce-scatter.4

commit v11 on v10

--- a/solution.py
+++ b/solution.py
@@ -728,7 +728,30 @@
                 )
     next(ring_stages)
     next(feed_stages)
-    for k in range(4):
+    for part in parts[3:]:
+        part.wait()
+    for step in (2, 1, 3):
+        sends(
+            downs_ref.at[mod4(my_y + step)],
+            down_out.at[my_y],
+            es.at[1, step - 1],
+            er.at[1, step - 1],
+            neighbour("y", step),
+        )
+    for k, step in enumerate((2, 1, 3, 0)):
+        arrived(up_buf.at[step], ey.at[step])
+        value = (up_own[mod4(my_y + step)].astype(F32) + up_buf[step].astype(F32)).astype(BF16)
+        if step == 0:
+            up_out[my_y] = value
+        else:
+            up_sum[step - 1] = value
+            sends(
+                up_sum.at[step - 1],
+                up_out.at[my_y],
+                es.at[0, step - 1],
+                er.at[0, step - 1],
+                neighbour("y", step),
+            )
         for h in (0, 1):
             second = place[rings[h][1]]
             for d, way in ((0, 1), (1, -1)):
@@ -746,31 +769,6 @@
                     neighbour(rings[h][1], way),
                 )
     total = next(ring_stages)
-    for step in (2, 1, 3):
-        sends(
-            downs_ref.at[mod4(my_y + step)],
-            down_out.at[my_y],
-            es.at[1, step - 1],
-            er.at[1, step - 1],
-            neighbour("y", step),
-        )
-    for part in parts[3:]:
-        part.wait()
-    for step in (2, 1, 3, 0):
-        target = mod4(my_y + step)
-        arrived(up_buf.at[step], ey.at[step])
-        value = (up_own[target].astype(F32) + up_buf[step].astype(F32)).astype(BF16)
-        if step == 0:
-            up_out[my_y] = value
-        else:
-            up_sum[step - 1] = value
-            sends(
-                up_sum.at[step - 1],
-                up_out.at[my_y],
-                es.at[0, step - 1],
-                er.at[0, step - 1],
-                neighbour("y", step),
-            )
     for k in range(4):
         for h in (0, 1):
             second = place[rings[h][1]]

time: 616 us -> 615 us (level)
  transfers between devices with their start and end apart: 9 -> 9, of which waited for: 1 -> 1; matrix products, arithmetic and copies ran while one was open for 18% -> 18% of each run, Pallas kernels for 50% -> 51%
where the time goes in v11:
time: 615 us; the launch traced here: 608 us
  Pallas kernels  420 us (68%)
  matrix products  89.8 us (15%)
  local copies, waits for them, and re-layouts  55.5 us (9%)
  other arithmetic  16.9 us (3%)
  between operations  15.5 us (3%)
  starting transfers between devices  7.47 us (1%)
    pallas_call x1, Pallas kernels, finish(): pl.pallas_call(finish_body, out_shape=[jax.ShapeDtypeStruct((2, share, co...  93.7 us
    dot_general x16, matrix products, dot(): return lax.dot_general(a, b, (dims, ((), ())), preferred_element_type=F32)  89.8 us
    pallas_call x1, Pallas kernels, gather_dp(): pl.pallas_call(gather_body, out_shape=[jax.ShapeDtypeStruct((4, 2, 4, row...  76.1 us
    pallas_call x1, Pallas kernels, return_rows(): pl.pallas_call(return_body, out_shape=[jax.ShapeDtypeStruct((4, half, wid...  53.9 us
    pallas_call x1, Pallas kernels, middle_back(): pl.pallas_call(back_body, out_shape=[jax.ShapeDtypeStruct((rows, width),...  45.7 us
    pallas_call x1, Pallas kernels, middle_and_unit(): pl.pallas_call(middle_body, out_shape=[jax.ShapeDtypeStruct((rows, width)...  42.5 us
    pallas_call x1, Pallas kernels, rows_to_experts(): pl.pallas_call(rows_body, out_shape=jax.ShapeDtypeStruct(rows.shape, rows...  39.2 us
    unnamed x110, local copies, waits for them, and re-layouts  23.1 us
  transfers between devices with their start and end apart: 9, of which 1 were waited for; matrix products, arithmetic and copies ran while one was open for 18% of the time, Pallas kernels for 51%

profile of v11, /device:TPU:1, one launch (start us, length us, event | category | flops | bytes accessed | tf_op | source)
XLA Modules:
  0.0 607.7 jit_solution(17252868552691634003)
XLA Ops:
  7.2 1.4 copy.145
  9.9 1.3 copy.154
  13.4 1.8 reshape.425.ups_ref
  17.0 76.1 %gather_weights.1 = (bf16[4,2,4,64,2176]{4,3,2,1,0:T(8,128)(2,1)}, bf16[2,4,64,2816]{3,2,1,0:T(8,128)(2,1)}, bf16[4,64,1408]{2,1,0:T(8,128)(2,1)}, bf16[2,512,128]{2,1,0:T(8,128)(2,1)}) custom-call(bf16[2,64,2176]{2,1,0:T(8,128)(2,1)} %pad_maximum_fusion.x_ref, bf16[4,64,2816]{2,1,0:T(8,128)(2,1)} %reshape.425.ups_ref, bf16[4,64,1408]{2,1,0:T(8,128)(2,1)} %bitcast.159, ...), custom_call_target="tpu_custom_call" | custom-call | tf_op jit(solution)/shard_map/gather_weights/pallas_call | solution.py:192
  93.2 1.3 collective-permute-start
  98.0 1.9 fusion.38
  100.3 3.5 fusion.4
  104.1 9.6 %fusion.8.k_ref.v_ref.q0.q1.q2 = f32[1024,1408]{1,0:T(8,128)S(1)} fusion(bf16[2048,2176]{1,0:T(8,128)(2,1)} %bitcast.165, bf16[1024,2048]{1,0:T(8,128)(2,1)S(1)} %copy-done.20, f32[2048]{0:T(1024)S(1)} %bitcast.183, f32[1024]{0:T(1024)S(1)} %add_rsqrt_fusion), kind=kOutput, calls=%fused_computation.16 | convolution fusion | flops 5913968640 | bytes 15740928 | tf_op jit(solution)/shard_map/dot_general | solution.py:928
  113.7 2.6 copy-done.18
  117.8 1.1 copy-done.9
  120.0 15.7 %attention_forward.1 = (bf16[1024,256]{1,0:T(8,128)(2,1)S(1)}, bf16[1024,256]{1,0:T(8,128)(2,1)S(1)}, bf16[1024,768]{1,0:T(8,128)(2,1)S(1)}, bf16[1024,768]{1,0:...) custom-call(f32[1024,1408]{1,0:T(8,128)} %copy-done.18, f32[1024,1408]{1,0:T(8,128)} %copy-done.18, ...), custom_call_target="tpu_custom_call" | custom-call | tf_op jit(solution)/shard_map/attention_forward/pallas_call | solution.py:1209
  137.3 2.8 maximum_select_fusion
  140.9 6.3 %convolution_convert_fusion.3 = bf16[1280,2048]{1,0:T(8,128)(2,1)} fusion(pred[1280,512]{1,0:T(32,128)(4,1)S(1)} %bitcast_compare_fusion, bf16[512,2048]{0,1:T(8,128)(2,1)} %all-gather.7.cloned.1.call-done), kind=kOutput, calls=%fused_computation.10 | convolution fusion | flops 2686976000 | bytes 7995392 | tf_op jit(solution)/shard_map/dot_general | solution.py:928
  147.2 5.2 all-to-all-start
  153.5 1.5 slice_bitcast_fusion.1
  155.0 6.0 convolution_convert_fusion.4
  161.0 42.5 %middle_and_unit.1 = (f32[128,2048]{1,0:T(8,128)S(1)}, bf16[4,128,2048]{2,1,0:T(8,128)(2,1)S(1)}) custom-call(bf16[2,2,2,128,2048]{4,3,2,1,0:T(8,128)(2,1)S(1)} %bitcast.129, bf16[128,2048]{1,0:T(8,128)(2,1)S(1)} %copy-done.2, f32[1,2048]{1,0:T(1,128)S(1)} %get-tuple-element.173.gain_ref), custom_call_target="tpu_custom_call" | custom-call | tf_op jit(solution)/shard_map/middle_and_unit/pallas_call | solution.py:468
  203.6 1.5 copy-done.3
  205.0 1.9 fusion.34
  207.2 5.5 convolution_convert_fusion
  212.7 39.2 %rows_to_experts.1 = bf16[4,320,2176]{2,1,0:T(8,128)(2,1)S(1)} custom-call(bf16[4,320,2176]{2,1,0:T(8,128)(2,1)S(1)} %bitcast.128), custom_call_target="tpu_custom_call" | custom-call | tf_op jit(solution)/shard_map/rows_to_experts/pallas_call | solution.py:631
  252.2 2.4 copy-done
  255.6 2.6 copy-done.1
  258.2 20.3 %joined_rows.1 = (f32[1280,1408]{1,0:T(8,128)}, f32[1280,1408]{1,0:T(8,128)}) custom-call(bf16[1280,2176]{1,0:T(8,128)(2,1)S(1)} %bitcast.124, bf16[2048,2816]{1,0:T(8,128)(2,1)} %all-gather.11.cloned.1.call-done.gate_up_ref.linear_up_ref.up_ref, bf16[2048,2816]{1,0:T(8,128)(2,1)} %all-gather.11.cloned.1.call-done.gate_up_ref.linear_up_ref.up_ref), custom_call_target="tpu_custom_call" | custom-call | tf_op jit(solution)/shard_map/joined_rows/pallas_call | solution.py:942
  278.5 2.4 all-gather.9.cloned.1.call-done.down_ref
  280.9 19.4 %experts.1 = (bf16[1280,1408]{1,0:T(8,128)(2,1)}, bf16[1280,1408]{1,0:T(8,128)(2,1)}, bf16[1280,1408]{1,0:T(8,128)(2,1)}, bf16[1280,1408]{1,0:T(8,128)(2,1)}, f32[1280,128]{1,0:T(8,128)}) custom-call(bf16[1280,2048]{1,0:T(8,128)(2,1)} %bitcast.17.grad_ref, bf16[2048,1408]{1,0:T(8,128)(2,1)} %all-gather.9.cloned.1.call-done.down_ref, ...), custom_call_target="tpu_custom_call" | custom-call | tf_op jit(solution)/shard_map/experts/pallas_call | solution.py:987
  300.3 13.1 %convolution_convert_fusion.2 = bf16[2048,1408]{1,0:T(8,128)(2,1)} fusion(bf16[1280,2048]{1,0:T(8,128)(2,1)} %bitcast.17.grad_ref, bf16[1280,1408]{1,0:T(8,128)(2,1)} %get-tuple-element.68), kind=kOutput, calls=%fused_computation.9 | convolution fusion | flops 7384858624 | bytes 14614528 | tf_op jit(solution)/shard_map/dot_general | solution.py:928
  313.6 53.9 %return_rows.1 = (bf16[4,160,2048]{2,1,0:T(8,128)(2,1)}, f32[4,160,128]{2,1,0:T(8,128)}, bf16[2048,2816]{1,0:T(8,128)(2,1)}) custom-call(bf16[1280,1408]{1,0:T(8,128)(2,1)} %get-tuple-element.70.dgate_pre_ref, bf16[1280,1408]{1,0:T(8,128)(2,1)} %get-tuple-element.71.dlinear_ref, ...), custom_call_target="tpu_custom_call" | custom-call | tf_op jit(solution)/shard_map/return_rows/pallas_call | solution.py:1116
  370.6 2.2 fusion.32
  372.8 3.3 fusion.11
  376.1 45.7 %middle_back.1 = (f32[128,2048]{1,0:T(8,128)}, f32[1,2048]{1,0:T(1,128)}, bf16[2,2,2,128,2048]{4,3,2,1,0:T(8,128)(2,1)}, bf16[4,160,2048]{2,1,0:T(8,128)(2,1)}) custom-call(bf16[4,128,2048]{2,1,0:T(8,128)(2,1)} %bitcast.153, f32[128,2048]{1,0:T(8,128)} %copy-done.11, bf16[128,2048]{1,0:T(8,128)(2,1)} %copy.163.grad_ref, f32[1,2048]{1,0:T(1,128)} %copy-done.17, ...), custom_call_target="tpu_custom_call" | custom-call | tf_op jit(solution)/shard_map/middle_back/pallas_call | solution.py:568
  422.5 2.0 dynamic-slice_bitcast_fusion
  425.1 8.7 %fusion.17.h0.h1.h2 = f32[1024,768]{1,0:T(8,128)} fusion(bf16[1024,2048]{1,0:T(8,128)(2,1)} %bitcast.188, bf16[2048,2176]{1,0:T(8,128)(2,1)} %bitcast.169), kind=kOutput, calls=%fused_computation.29 | convolution fusion | flops 3221225472 | bytes 10485760 | tf_op jit(solution)/shard_map/dot_general | solution.py:928
  433.9 13.7 %attention_back.1 = (bf16[1024,1280]{1,0:T(8,128)(2,1)}, f32[1024,128]{1,0:T(8,128)S(1)}) custom-call(bf16[1024,256]{1,0:T(8,128)(2,1)S(1)} %copy-done.14, bf16[1024,256]{1,0:T(8,128)(2,1)S(1)} %copy-done.16, bf16[1024,768]{1,0:T(8,128)(2,1)S(1)} %get-tuple-element.81.q0.q1.q2, bf16[1024,768]{1,0:T(8,128)(2,1)S(1)} %get-tuple-element.81.q0.q1.q2, ...), custom_call_target="tpu_custom_call" | custom-call | tf_op jit(solution)/shard_map/attention_back/pallas_call | solution.py:1285
  448.1 3.5 convolution_convert_fusion.7
  452.5 11.2 %fusion.58 = (bf16[1024,2048]{1,0:T(8,128)(2,1)}, bf16[2048]{0:T(1024)(128)(2,1)S(1)}) fusion(f32[1024]{0:T(1024)S(1)} %add_rsqrt_fusion, bf16[1024,2048]{1,0:T(8,128)(2,1)S(1)} %copy-done.21, bf16[2048,2176]{1,0:T(8,128)(2,1)} %bitcast.170, bf16[1024,3]{1,0:T(8,128)(2,1)S(1)} %copy.166, bf16[1024,1280]{1,0:T(8,128)(2,1)S(1)} %copy-done.44), kind=kOutput, calls=%fused_computation.127 | convolution fusion | flops 5924714496 | bytes 16791552 | tf_op jit(solution)/shard_map/dot_general | solution.py:928
  465.4 2.1 fusion.27
  467.5 5.2 bitcast_convert_fusion
  472.7 5.0 convolution_convert_fusion.5
  477.7 8.0 %convolution_convert_fusion.1 = bf16[2048,1280]{1,0:T(8,128)(2,1)} fusion(bf16[1024,1280]{1,0:T(8,128)(2,1)S(1)} %copy-done.45, bf16[1024,2048]{1,0:T(8,128)(2,1)S(1)} %copy-done.22, f32[2048]{0:T(1024)S(1)} %bitcast.185, f32[1024]{0:T(1024)S(1)} %add_rsqrt_fusion), kind=kOutput, calls=%fused_computation.8 | convolution fusion | flops 5379719168 | bytes 12070912 | tf_op jit(solution)/shard_map/dot_general | solution.py:928
  485.6 93.7 %finish.1 = (f32[2,64,2176]{2,1,0:T(8,128)}, bf16[4,64,2816]{2,1,0:T(8,128)(2,1)}, bf16[4,64,1408]{2,1,0:T(8,128)(2,1)}, bf16[128,2048]{1,0:T(8,128)(2,1)}, f32[128,2048]{1,0:T(8,128)}, /*index=5*/f32[64,128]{1,0:T(8,128)}) custom-call(bf16[4,2,4,64,1280]{4,3,2,1,0:T(8,128)(2,1)} %bitcast.133, bf16[4,2,4,64,128]{4,3,2,1,0:T(8,128)(2,1)} %bitcast.147, ...), custom_call_target="tpu_custom_call" | custom-call | tf_op jit(solution)/shard_map/finish/pallas_call | solution.py:866
  579.3 1.2 fusion.59
  582.3 1.5 slice_reduce_fusion
  583.9 1.5 copy.171
  585.6 1.3 copy.177
  586.9 4.6 reshape.462
  594.6 1.3 copy.169
  597.0 1.2 convert_bitcast_fusion
  (214 shorter events, 33.0 us)
Async XLA Ops:
  7.2 4.9 copy-start.32
  7.2 5.4 copy-start.33
  7.2 93.1 %all-gather.5.cloned.1.call-start = ((), (), s32[]{:S(2)}) async-start(), calls=%async_computation.3 | async-start | bytes 4718592 | tf_op jit(solution)/shard_map/all_gather | solution.py:1378
  8.7 4.4 copy-start.34
  8.7 4.6 copy-start.38
  8.7 4.6 copy-start.39
  8.7 4.6 copy-start.40
  8.7 4.6 copy-start.41
  8.7 4.7 copy-start.25
  9.8 5.4 copy-start.37
  9.8 5.4 copy-start.36
  9.8 131.1 %all-gather.7.cloned.1.call-start = ((), (), s32[]{:S(2)}) async-start(), calls=%async_computation.4 | async-start | bytes 2621440 | tf_op jit(solution)/shard_map/all_gather | solution.py:1379
  12.1 243.6 %all-gather.11.cloned.1.call-start = ((), (), s32[]{:S(2)}) async-start(), calls=%async_computation.6 | async-start | bytes 14417920 | tf_op jit(solution)/shard_map/all_gather | solution.py:1388
  93.1 2.7 copy-start.31
  93.1 187.7 %all-gather.9.cloned.1.call-start = ((), (), s32[]{:S(2)}) async-start(), calls=%async_computation.5 | async-start | bytes 7208960 | tf_op jit(solution)/shard_map/all_gather | solution.py:1428
  93.2 44.1 %collective-permute-start = (bf16[4,64,1408]{2,1,0:T(8,128)(2,1)}, bf16[4,64,1408]{2,1,0:T(8,128)(2,1)}, u32[]{:S(2)}, u32[]{:S(2)}) collective-permute-start(bf16[4,64,1408]{2,1,0:T(8,128)(2,1)} %get-tuple-element.58), channel_id=1, source_target_pairs={{0,16},{16,0},{1,17},{17,1},{2,18},{18,2},{3,19},{19,3},{4,20},{20... | collective-permute-start | bytes 2162696 | tf_op jit(solution)/shard_map/ppermute | solution.py:1392
  100.3 17.5 %copy-start.5 = (f32[1024,128]{1,0:T(8,128)}, f32[1024,128]{1,0:T(8,128)S(1)}, u32[]{:S(2)}) copy-start(f32[1024,128]{1,0:T(8,128)S(1)} %get-tuple-element.179.cos_ref) | copy-start | bytes 1572868
  100.3 17.5 %copy-start.7 = (f32[1024,128]{1,0:T(8,128)}, f32[1024,128]{1,0:T(8,128)S(1)}, u32[]{:S(2)}) copy-start(f32[1024,128]{1,0:T(8,128)S(1)} %get-tuple-element.180.sin_ref) | copy-start | bytes 1572868
  100.3 3.8 copy-start.20
  113.7 2.6 copy-start.18
  120.0 17.3 %copy-start.28 = (bf16[4,64,1408]{2,1,0:T(8,128)(2,1)S(1)}, bf16[4,64,1408]{2,1,0:T(8,128)(2,1)}, u32[]{:S(2)}) copy-start(bf16[4,64,1408]{2,1,0:T(8,128)(2,1)} %get-tuple-element.58) | copy-start | bytes 2162692
  137.3 2.9 copy-start.35
  147.2 5.3 copy-start.24
  147.2 131.3 %all-to-all-start = ((bf16[4,320,2048]{2,1,0:T(8,128)(2,1)}), bf16[4,320,2048]{2,1,0:T(8,128)(2,1)}, u32[]{:S(2)}, u32[]{:S(2)}) async-start(bf16[4,320,2048]{2,1,0:T(8,128)(2,1)} %bitcast.132), calls=%async_computation | async-start | bytes 10485760 | tf_op jit(solution)/shard_map/all_to_all | solution.py:1403
  152.4 270.1 %reduce-scatter.3.cloned.1.call-start = ((), (), s32[]{:S(2)}) async-start(), calls=%async_computation.7 | async-start | bytes 7208960 | tf_op jit(solution)/shard_map/reduce_scatter | solution.py:1453
  155.0 6.0 copy-start.17
  155.0 6.0 copy-start.2
  203.5 3.3 copy-start.11
  252.2 2.4 copy-start
  255.6 2.6 copy-start.1
  313.4 172.3 %reduce-scatter.5.cloned.1.call-start = ((), (), s32[]{:S(2)}) async-start(), calls=%async_computation.8 | async-start | bytes 14417920 | tf_op jit(solution)/shard_map/reduce_scatter | solution.py:1457
  367.5 2.4 copy-start.30
  370.1 2.7 copy-start.43
  424.6 9.3 %copy-start.6 = (f32[1024,128]{1,0:T(8,128)S(1)}, f32[1024,128]{1,0:T(8,128)}, u32[]{:S(2)}) copy-start(f32[1024,128]{1,0:T(8,128)} %copy-done.5) | copy-start | bytes 1572868
  424.6 9.3 %copy-start.8 = (f32[1024,128]{1,0:T(8,128)S(1)}, f32[1024,128]{1,0:T(8,128)}, u32[]{:S(2)}) copy-start(f32[1024,128]{1,0:T(8,128)} %copy-done.7) | copy-start | bytes 1572868
  424.6 9.3 %copy-start.10 = (f32[1024,3]{1,0:T(8,128)S(1)}, f32[1024,3]{1,0:T(8,128)}, u32[]{:S(2)}) copy-start(f32[1024,3]{1,0:T(8,128)} %copy.159.gate_ref) | copy-start | bytes 36868
  424.6 9.3 %copy-start.14 = (bf16[1024,256]{1,0:T(8,128)(2,1)S(1)}, bf16[1024,256]{1,0:T(8,128)(2,1)}, u32[]{:S(2)}) copy-start(bf16[1024,256]{1,0:T(8,128)(2,1)} %copy-done.13) | copy-start | bytes 1572868
  424.6 9.3 %copy-start.16 = (bf16[1024,256]{1,0:T(8,128)(2,1)S(1)}, bf16[1024,256]{1,0:T(8,128)(2,1)}, u32[]{:S(2)}) copy-start(bf16[1024,256]{1,0:T(8,128)(2,1)} %copy-done.15) | copy-start | bytes 1572868
  424.6 27.0 %collective-permute-start.1 = (bf16[256,1408]{1,0:T(8,128)(2,1)}, bf16[256,1408]{1,0:T(8,128)(2,1)}, u32[]{:S(2)}, u32[]{:S(2)}) collective-permute-start(bf16[256,1408]{1,0:T(8,128)(2,1)} %dynamic-slice_bitcast_fusion), channel_id=1, source_target_pairs={{0,16},{16,0},{1,17},{17,1},{2,18},{18,2},{3,19},{19,3},{4,20},{20... | collective-permute-start | bytes 2162696 | tf_op jit(solution)/shard_map/ppermute | solution.py:1474
  448.1 3.5 copy-start.21
  448.1 4.4 copy-start.44
  452.5 11.2 %copy-start.4 = (bf16[4,128,2048]{2,1,0:T(8,128)(2,1)S(1)}, bf16[4,128,2048]{2,1,0:T(8,128)(2,1)}, u32[]{:S(2)}) copy-start(bf16[4,128,2048]{2,1,0:T(8,128)(2,1)} %copy-done.3) | copy-start | bytes 6291460
  467.5 5.2 copy-start.42
  467.5 5.2 copy-start.46
  472.7 5.0 copy-start.22
  472.7 5.0 copy-start.45
  591.4 5.6 copy-start.27
  593.2 6.5 %copy-start.29 = (f32[64,128]{1,0:T(8,128)S(1)}, f32[64,128]{1,0:T(8,128)}, u32[]{:S(2)}) copy-start(f32[64,128]{1,0:T(8,128)} %get-tuple-element.100) | copy-start | bytes 98308
  (8 other events, 8.8 us)
Sparse Core Ops, SparseCore 0:
  10.2 58.2 all-gather.4
  70.2 35.2 all-gather.6
  107.1 109.0 all-gather.10
  218.3 62.4 all-gather.8
  313.5 60.3 reduce-scatter.2
  376.2 105.7 reduce-scatter.4
